TPU v7x, 32 devices: a whole 2x2x4 slice. The times are simulated.
32 devices in a mesh: gx: 8 (over z, x), gy: 4 (over y, core).
Axes of the slice: x: 2, y: 2, z: 4, core: 2. Of those that a mesh axis runs over, the one named last changes fastest.
Arguments:
- fields: float32 [4, 16, 8, 8, 8, 128], P(None, 'gx', None, 'gy'), may hold values from -6 to 6
- viscosity: float32 [16, 8, 8, 8, 128], P('gx', None, 'gy'), may hold values from 0.002 to 0.02
- inv_density: float32 [16, 8, 16], P('gx', 'gy'), may hold values from 0.5 to 2
- elem_group: int32 [16, 8, 16], P('gx', 'gy'), may hold values from 0 to 3
- coarse_inverse: float32 [128, 128], P(('gx', 'gy')), as said below
Outputs:
- fields_new: float32 [4, 16, 8, 8, 8, 128], P(None, 'gx', None, 'gy')
- pressure: float32 [16, 8, 8, 8, 128], P('gx', None, 'gy')
Inputs may be any that keep to these rules, and one draw needn't show every extreme that they name: `elem_group`: the coarse unknown of an element among the 4 of its own device. `coarse_inverse`: symmetric and positive definite.
All inputs are finite; a program needn't handle non-finite values.
Results may differ from a plain program's by a relative error of at most 0.0015.
Values sent between devices are 32-bit elements; how exact they have to be, the bound alone decides.
No kernel may reach another device: no remote copies, remote signals or barrier semaphores. Data moves between devices by JAX's collectives and lax.ppermute only.
A program may use at most 64 MiB of HBM per device.

v0:
```python
import jax
import jax.numpy as jnp
import numpy as np
from jax import lax
from jax.sharding import PartitionSpec as P

ORDER = 7
ITERS = 2
NCD = 4


dt_step = 0.01
sigma_p = 4.0
prandtl = 0.7
cheb_ratio = 0.1


def with_halo(cells, sides, width):
    for axis, dim in sides:
        count = lax.axis_size(axis)
        ends = count - 1
        head = lax.slice_in_dim(cells, 0, width, axis=dim)
        tail = lax.slice_in_dim(cells, cells.shape[dim] - width, cells.shape[dim], axis=dim)
        cells = jnp.concatenate(
            [
                lax.ppermute(tail, axis, [(i, (i + 1) % count) for i in range(ends)]),
                cells,
                lax.ppermute(head, axis, [((i + 1) % count, i) for i in range(ends)]),
            ],
            axis=dim,
        )
    return cells


def tables():
    points = np.array(
        [
            -1.0,
            -0.8717401485096066,
            -0.5917001814331423,
            -0.2092992179024789,
            0.2092992179024789,
            0.5917001814331423,
            0.8717401485096066,
            1.0,
        ]
    )
    weights = np.array(
        [
            1.0 / 28.0,
            0.2107042271435061,
            0.3411226924835044,
            0.4124587946587038,
            0.4124587946587038,
            0.3411226924835044,
            0.2107042271435061,
            1.0 / 28.0,
        ]
    )
    identity = np.eye(8)
    differ = points[:, None] - points[None, :] + identity
    barycentric = 1.0 / np.prod(differ, axis=1)
    offdiag = barycentric[None, :] / barycentric[:, None] / differ * (1.0 - identity)
    derivative = offdiag - identity * np.sum(offdiag, axis=1)[:, None]
    mass_one = identity * weights[None, :]
    stiff_one = derivative.T @ mass_one @ derivative
    stiff_three = (
        np.kron(np.kron(stiff_one, mass_one), mass_one)
        + np.kron(np.kron(mass_one, stiff_one), mass_one)
        + np.kron(np.kron(mass_one, mass_one), stiff_one)
    )
    three_diag = np.sum(stiff_three * np.eye(512), axis=1)
    spectral_bound = float(np.max(np.sum(np.abs(stiff_three), axis=1) / three_diag))
    return (derivative, weights, np.sum(stiff_one * identity, axis=1), spectral_bound)


def join_pairs(field, elem_axis):
    node_axis = elem_axis + 1
    top_node = field.shape[node_axis] - 1
    last_face = lax.index_in_dim(field, top_node, node_axis, keepdims=False)
    first_face = lax.index_in_dim(field, 0, node_axis, keepdims=False)
    elem_count = field.shape[elem_axis]
    summed = lax.slice_in_dim(last_face, 0, elem_count - 1, axis=elem_axis) + lax.slice_in_dim(
        first_face, 1, elem_count, axis=elem_axis
    )
    new_last = jnp.concatenate(
        [summed, lax.slice_in_dim(last_face, elem_count - 1, elem_count, axis=elem_axis)], elem_axis
    )
    new_first = jnp.concatenate(
        [lax.slice_in_dim(first_face, 0, 1, axis=elem_axis), summed], elem_axis
    )
    middle = lax.slice_in_dim(field, 1, top_node, axis=node_axis)
    return jnp.concatenate(
        [jnp.expand_dims(new_first, node_axis), middle, jnp.expand_dims(new_last, node_axis)],
        node_axis,
    )


def add_edges(grid, extra_first, extra_last, edge_dim):
    extent = grid.shape[edge_dim]
    return jnp.concatenate(
        [
            lax.slice_in_dim(grid, 0, 1, axis=edge_dim) + extra_first,
            lax.slice_in_dim(grid, 1, extent - 1, axis=edge_dim),
            lax.slice_in_dim(grid, extent - 1, extent, axis=edge_dim) + extra_last,
        ],
        edge_dim,
    )


def per_device(fields, viscosity, inv_density, elem_group, coarse_inverse):
    precision = lax.Precision.HIGHEST
    derivative_np, weights_np, stiff_np, spectral_bound = tables()
    line_nodes = ORDER + 1
    elems_x = fields.shape[1]
    elems_y = fields.shape[3]
    length = fields.shape[5]
    elems_z = length // line_nodes
    rows_x = elems_x * line_nodes
    rows_y = elems_y * line_nodes
    derivative = jnp.asarray(derivative_np, jnp.float32)
    weights_line = jnp.asarray(weights_np, jnp.float32)
    stiff_line = jnp.asarray(stiff_np, jnp.float32)
    band_np = np.kron(np.eye(elems_z), derivative_np)
    band_matrix = jnp.asarray(band_np, jnp.float32)
    band_trans = jnp.asarray(band_np.T, jnp.float32)
    pair_np = np.eye(length)
    joints = np.arange(elems_z - 1) * line_nodes + ORDER
    pair_np[joints, joints + 1] = 1.0
    pair_np[joints + 1, joints] = 1.0
    pair_table = jnp.asarray(pair_np, jnp.float32)
    block_np = np.kron(np.eye(elems_z), np.ones((line_nodes, 1)))
    block_table = jnp.asarray(block_np, jnp.float32)
    block_trans = jnp.asarray(block_np.T, jnp.float32)

    def gradient(field):
        along_x = jnp.einsum("ia,cxaybl->cxiybl", derivative, field, precision=precision)
        along_y = jnp.einsum("jb,cxaybl->cxayjl", derivative, field, precision=precision)
        along_z = jnp.matmul(field, band_trans, precision=precision)
        return (along_x, along_y, along_z)

    def adjoint(first_part, second_part, third_part):
        result = jnp.einsum("ai,cxaybl->cxiybl", derivative, first_part, precision=precision)
        result = result + jnp.einsum(
            "bj,cxaybl->cxayjl", derivative, second_part, precision=precision
        )
        return result + jnp.matmul(third_part, band_matrix, precision=precision)

    def assemble(field):
        channels = field.shape[0]
        field = join_pairs(field, 1)
        grid = field.reshape(channels, rows_x, rows_y, length)
        border = with_halo(grid, (("gx", 1),), 1)
        grid = add_edges(grid, border[:, 0:1], border[:, -1:], 1)
        field = join_pairs(
            grid.reshape(channels, elems_x, line_nodes, elems_y, line_nodes, length), 3
        )
        grid = field.reshape(channels, rows_x, rows_y, length)
        border = with_halo(grid, (("gy", 2),), 1)
        grid = add_edges(grid, border[:, :, 0:1], border[:, :, -1:], 2)
        field = grid.reshape(channels, elems_x, line_nodes, elems_y, line_nodes, length)
        return jnp.matmul(field, pair_table, precision=precision)

    def on_x(values):
        return values[None, :, None, None, None]

    def on_y(values):
        return values[None, None, None, :, None]

    weights_z = jnp.tile(weights_line, elems_z)
    stiff_z = jnp.tile(stiff_line, elems_z)
    weight = on_x(weights_line) * on_y(weights_line) * weights_z
    diag_stiff = (
        on_x(stiff_line) * on_y(weights_line) * weights_z
        + on_x(weights_line) * on_y(stiff_line) * weights_z
        + on_x(weights_line) * on_y(weights_line) * stiff_z
    )
    kappa = jnp.dot(inv_density, block_trans, precision=precision)[:, None, :, None, :]
    unit = jnp.ones((1, elems_x, line_nodes, elems_y, line_nodes, length), jnp.float32)
    stacked = jnp.concatenate(
        [unit, unit * weight, (kappa * diag_stiff + sigma_p * weight)[None], fields * weight], 0
    )
    summed = assemble(stacked)
    multiplicity = summed[0]
    mass_sum = summed[1]
    pdiag = summed[2]
    start = summed[3:] / mass_sum
    along_x, along_y, along_z = gradient(start)
    advect = start[0] * along_x + start[1] * along_y + start[2] * along_z
    factors = jnp.asarray([1.0, 1.0, 1.0, 1.0 / prandtl], jnp.float32)[
        :, None, None, None, None, None
    ]
    scaled = factors * viscosity * weight
    rhs = -weight * advect - adjoint(scaled * along_x, scaled * along_y, scaled * along_z)
    fields_new = start + dt_step * assemble(rhs) / mass_sum
    div_x = jnp.einsum("ia,xaybl->xiybl", derivative, fields_new[0], precision=precision)
    div_y = jnp.einsum("jb,xaybl->xayjl", derivative, fields_new[1], precision=precision)
    div_z = jnp.matmul(fields_new[2], band_trans, precision=precision)
    rhs_p = assemble((-weight * (div_x + div_y + div_z))[None])[0]
    inv_mult = 1.0 / multiplicity
    inv_diag = 1.0 / pdiag
    kappa_weight = kappa * weight
    one_hot = (elem_group[..., None] == jnp.arange(NCD, dtype=jnp.int32)).astype(jnp.float32)

    def op_local(field):
        grad_x, grad_y, grad_z = gradient(field[None])
        return (
            adjoint(kappa_weight * grad_x, kappa_weight * grad_y, kappa_weight * grad_z)[0]
            + sigma_p * weight * field
        )

    def restrict(resid):
        node_sums = (resid * inv_mult).sum(axis=(1, 3))
        elem_sums = jnp.dot(node_sums, block_table, precision=precision)
        return jnp.einsum("xyz,xyzk->k", elem_sums, one_hot, precision=precision)

    def gather_rest(resid):
        return lax.all_gather(restrict(resid), ("gx", "gy"), axis=0, tiled=True)

    def total(value):
        return lax.psum(value, ("gx", "gy"))

    lower = cheb_ratio * spectral_bound
    cheb_theta = 0.5 * (spectral_bound + lower)
    cheb_delta = 0.5 * (spectral_bound - lower)

    def precondition(resid, restricted_all):
        coarse_values = jnp.dot(coarse_inverse, restricted_all, precision=precision)
        elem_values = jnp.einsum("xyzk,k->xyz", one_hot, coarse_values, precision=precision)
        spread = jnp.dot(elem_values, block_trans, precision=precision)[:, None, :, None, :]
        coarse_local = spread * inv_mult
        update = resid * inv_diag / cheb_theta
        smoothed = update
        cheb_rho = cheb_delta / cheb_theta
        local = op_local(smoothed)
        both = assemble(jnp.stack([local, coarse_local], 0))
        applied = both[0]
        coarse_term = both[1]
        defect = resid - applied
        rho_next = 1.0 / (2.0 * cheb_theta / cheb_delta - cheb_rho)
        update = rho_next * cheb_rho * update + 2.0 * rho_next / cheb_delta * defect * inv_diag
        smoothed = smoothed + update
        return smoothed + coarse_term

    pressure = jnp.zeros_like(rhs_p)
    resid = rhs_p
    restricted_all = gather_rest(resid)
    precond_r = precondition(resid, restricted_all)
    rz_value = total(jnp.sum(resid * precond_r * inv_mult))
    direction = precond_r
    for iteration in range(ITERS):
        last_turn = iteration + 1 == ITERS
        image = assemble(op_local(direction)[None])[0]
        partial_sum = jnp.sum(direction * image * inv_mult)
        curvature = total(partial_sum)
        step_size = rz_value / curvature
        pressure = pressure + step_size * direction
        if not last_turn:
            resid = resid - step_size * image
            restricted_all = gather_rest(resid)
            precond_r = precondition(resid, restricted_all)
            rz_next = total(jnp.sum(resid * precond_r * inv_mult))
            direction = precond_r + rz_next / rz_value * direction
            rz_value = rz_next
    return (fields_new, pressure)


def solution(mesh):
    placed = (
        P(None, "gx", None, "gy", None, None),
        P("gx", None, "gy", None, None),
        P("gx", "gy", None),
        P("gx", "gy", None),
        P(("gx", "gy"), None),
    )
    return jax.shard_map(
        per_device,
        mesh=mesh,
        in_specs=placed,
        out_specs=(P(None, "gx", None, "gy", None, None), P("gx", None, "gy", None, None)),
        check_vma=False,
    )
```

profile of v0, /device:TPU:0, one launch (start us, length us, event | category | flops | bytes accessed | tf_op | source)
XLA Modules:
  0.0 363.7 jit_solution(13373132914196396933)
XLA Ops:
  5.3 4.8 %collective-permute-start = (f32[7,1,16,128]{3,2,1,0:T(8,128)S(1)}, f32[7,1,16,128]{3,2,1,0:T(8,128)S(1)}, u32[]{:S(2)}, u32[]{:S(2)}) collective-permute-start(f32[7,1,16,128]{3,2,1,0:T(8,128)S(1)} %get-tuple-element.18), channel_id=1, source_target_pairs={{0,4},{4,8},{8,12},{12,16},{16,20},{20,24},{24,28},{1,5},{5,9},{9,... | collective-permute-start | bytes 172040 | tf_op jit(solution)/shard_map/ppermute | solution.py:26
  12.0 4.3 %collective-permute-done.1 = f32[7,1,16,128]{3,2,1,0:T(8,128)S(1)} collective-permute-done((f32[7,1,16,128]{3,2,1,0:T(8,128)S(1)}, f32[7,1,16,128]{3,2,1,0:T(8,128)S(1)}, u32[]{:S(2)}, u32[]{:S(2)}) %collective-permute-start.1) | collective-permute-done | bytes 57376 | tf_op jit(solution)/shard_map/ppermute | solution.py:28
  17.4 1.3 collective-permute-start.2
  20.2 3.4 collective-permute-done.3
  32.4 4.4 %collective-permute-start.4 = (f32[4,1,16,128]{3,2,1,0:T(8,128)S(1)}, f32[4,1,16,128]{3,2,1,0:T(8,128)S(1)}, u32[]{:S(2)}, u32[]{:S(2)}) collective-permute-start(f32[4,1,16,128]{3,2,1,0:T(8,128)S(1)} %get-tuple-element.32), channel_id=1, source_target_pairs={{0,4},{4,8},{8,12},{12,16},{16,20},{20,24},{24,28},{1,5},{5,9},{9,... | collective-permute-start | bytes 98312 | tf_op jit(solution)/shard_map/ppermute | solution.py:26
  38.4 4.2 %collective-permute-done.5 = f32[4,1,16,128]{3,2,1,0:T(8,128)S(1)} collective-permute-done((f32[4,1,16,128]{3,2,1,0:T(8,128)S(1)}, f32[4,1,16,128]{3,2,1,0:T(8,128)S(1)}, u32[]{:S(2)}, u32[]{:S(2)}) %collective-permute-start.5) | collective-permute-done | bytes 32800 | tf_op jit(solution)/shard_map/ppermute | solution.py:28
  43.3 3.3 collective-permute-start.6
  46.6 1.5 collective-permute-start.7
  48.1 2.5 collective-permute-done.7
  53.7 3.4 collective-permute-start.8
  58.4 4.2 %collective-permute-done.9 = f32[1,1,16,128]{3,2,1,0:T(8,128)S(1)} collective-permute-done((f32[1,1,16,128]{3,2,1,0:T(8,128)S(1)}, f32[1,1,16,128]{3,2,1,0:T(8,128)S(1)}, u32[]{:S(2)}, u32[]{:S(2)}) %collective-permute-start.9) | collective-permute-done | bytes 8224 | tf_op jit(solution)/shard_map/ppermute | solution.py:28
  62.8 3.1 collective-permute-start.10
  67.3 2.7 collective-permute-done.11
  73.9 42.1 %all-reduce = f32[128]{0:T(128)S(1)} all-reduce(f32[128]{0:T(128)S(1)} %dynamic-update-slice), channel_id=1, replica_groups=mesh['gx'=8,'gy'=4] {'gx','gy'}, use_global_device_ids=true, to_apply=%add | all-reduce | flops 128 | bytes 1024
  118.2 4.2 %collective-permute-start.12 = (f32[2,1,16,128]{3,2,1,0:T(8,128)S(1)}, f32[2,1,16,128]{3,2,1,0:T(8,128)S(1)}, u32[]{:S(2)}, u32[]{:S(2)}) collective-permute-start(f32[2,1,16,128]{3,2,1,0:T(8,128)S(1)} %get-tuple-element.59), channel_id=1, source_target_pairs={{0,4},{4,8},{8,12},{12,16},{16,20},{20,24},{24,28},{1,5},{5,9},{9,... | collective-permute-start | bytes 49160 | tf_op jit(solution)/shard_map/ppermute | solution.py:26
  123.8 4.2 %collective-permute-done.13 = f32[2,1,16,128]{3,2,1,0:T(8,128)S(1)} collective-permute-done((f32[2,1,16,128]{3,2,1,0:T(8,128)S(1)}, f32[2,1,16,128]{3,2,1,0:T(8,128)S(1)}, u32[]{:S(2)}, u32[]{:S(2)}) %collective-permute-start.13) | collective-permute-done | bytes 16416 | tf_op jit(solution)/shard_map/ppermute | solution.py:28
  131.0 2.0 collective-permute-done.15
  136.9 4.6 %collective-permute-start.16 = (f32[1,1,16,128]{3,2,1,0:T(8,128)S(1)}, f32[1,1,16,128]{3,2,1,0:T(8,128)S(1)}, u32[]{:S(2)}, u32[]{:S(2)}) collective-permute-start(f32[1,1,16,128]{3,2,1,0:T(8,128)S(1)} %get-tuple-element.83), channel_id=1, source_target_pairs={{0,4},{4,8},{8,12},{12,16},{16,20},{20,24},{24,28},{1,5},{5,9},{9,... | collective-permute-start | bytes 24584 | tf_op jit(solution)/shard_map/ppermute | solution.py:26
  142.9 4.2 %collective-permute-done.17 = f32[1,1,16,128]{3,2,1,0:T(8,128)S(1)} collective-permute-done((f32[1,1,16,128]{3,2,1,0:T(8,128)S(1)}, f32[1,1,16,128]{3,2,1,0:T(8,128)S(1)}, u32[]{:S(2)}, u32[]{:S(2)}) %collective-permute-start.17) | collective-permute-done | bytes 8224 | tf_op jit(solution)/shard_map/ppermute | solution.py:28
  147.3 3.0 collective-permute-start.18
  151.6 2.7 collective-permute-done.19
  155.3 40.1 %all-reduce.2 = (f32[]{:T(128)}, f32[]{:T(128)}) all-reduce(f32[]{:T(128)} %get-tuple-element.3, f32[]{:T(128)} %get-tuple-element.2), channel_id=1, replica_groups=mesh['gx'=8,'gy'=4] {'gx','gy'}, use_global_device_ids=true, to_apply=%region_2.0 | all-reduce | flops 2 | bytes 16 | tf_op jit(solution)/shard_map/psum | solution.py:221
  198.5 40.5 %all-reduce.1 = f32[128]{0:T(128)S(1)} all-reduce(f32[128]{0:T(128)S(1)} %dynamic-update-slice.1), channel_id=1, replica_groups=mesh['gx'=8,'gy'=4] {'gx','gy'}, use_global_device_ids=true, to_apply=%add.1 | all-reduce | flops 128 | bytes 1024
  240.4 4.2 %collective-permute-start.20 = (f32[2,1,16,128]{3,2,1,0:T(8,128)S(1)}, f32[2,1,16,128]{3,2,1,0:T(8,128)S(1)}, u32[]{:S(2)}, u32[]{:S(2)}) collective-permute-start(f32[2,1,16,128]{3,2,1,0:T(8,128)S(1)} %get-tuple-element.47), channel_id=1, source_target_pairs={{0,4},{4,8},{8,12},{12,16},{16,20},{20,24},{24,28},{1,5},{5,9},{9,... | collective-permute-start | bytes 49160 | tf_op jit(solution)/shard_map/ppermute | solution.py:26
  246.0 4.2 %collective-permute-done.21 = f32[2,1,16,128]{3,2,1,0:T(8,128)S(1)} collective-permute-done((f32[2,1,16,128]{3,2,1,0:T(8,128)S(1)}, f32[2,1,16,128]{3,2,1,0:T(8,128)S(1)}, u32[]{:S(2)}, u32[]{:S(2)}) %collective-permute-start.21) | collective-permute-done | bytes 16416 | tf_op jit(solution)/shard_map/ppermute | solution.py:28
  251.9 1.5 collective-permute-start.23
  253.4 2.7 collective-permute-done.23
  257.2 42.0 %psum.30 = f32[]{:T(128)} all-reduce(f32[]{:T(128)} %fusion.82), channel_id=1, replica_groups=mesh['gx'=8,'gy'=4] {'gx','gy'}, use_global_device_ids=true, to_apply=%region_7.0 | all-reduce | flops 1 | bytes 8 | tf_op jit(solution)/shard_map/psum | solution.py:221
  304.0 4.2 %collective-permute-start.24 = (f32[1,1,16,128]{3,2,1,0:T(8,128)S(1)}, f32[1,1,16,128]{3,2,1,0:T(8,128)S(1)}, u32[]{:S(2)}, u32[]{:S(2)}) collective-permute-start(f32[1,1,16,128]{3,2,1,0:T(8,128)S(1)} %get-tuple-element.71), channel_id=1, source_target_pairs={{0,4},{4,8},{8,12},{12,16},{16,20},{20,24},{24,28},{1,5},{5,9},{9,... | collective-permute-start | bytes 24584 | tf_op jit(solution)/shard_map/ppermute | solution.py:26
  309.5 4.2 %collective-permute-done.25 = f32[1,1,16,128]{3,2,1,0:T(8,128)S(1)} collective-permute-done((f32[1,1,16,128]{3,2,1,0:T(8,128)S(1)}, f32[1,1,16,128]{3,2,1,0:T(8,128)S(1)}, u32[]{:S(2)}, u32[]{:S(2)}) %collective-permute-start.25) | collective-permute-done | bytes 8224 | tf_op jit(solution)/shard_map/ppermute | solution.py:28
  316.6 2.3 collective-permute-done.27
  319.8 41.9 %psum.31 = f32[]{:T(128)} all-reduce(f32[]{:T(128)} %fusion.37), channel_id=1, replica_groups=mesh['gx'=8,'gy'=4] {'gx','gy'}, use_global_device_ids=true, to_apply=%region_9.0 | all-reduce | flops 1 | bytes 8 | tf_op jit(solution)/shard_map/psum | solution.py:221
  (289 shorter events, 59.6 us)
Async XLA Ops:
  0.6 1.7 copy-start
  5.3 6.7 %collective-permute-start = (f32[7,1,16,128]{3,2,1,0:T(8,128)S(1)}, f32[7,1,16,128]{3,2,1,0:T(8,128)S(1)}, u32[]{:S(2)}, u32[]{:S(2)}) collective-permute-start(f32[7,1,16,128]{3,2,1,0:T(8,128)S(1)} %get-tuple-element.18), channel_id=1, source_target_pairs={{0,4},{4,8},{8,12},{12,16},{16,20},{20,24},{24,28},{1,5},{5,9},{9,... | collective-permute-start | bytes 172040 | tf_op jit(solution)/shard_map/ppermute | solution.py:26
  10.2 6.1 %collective-permute-start.1 = (f32[7,1,16,128]{3,2,1,0:T(8,128)S(1)}, f32[7,1,16,128]{3,2,1,0:T(8,128)S(1)}, u32[]{:S(2)}, u32[]{:S(2)}) collective-permute-start(f32[7,1,16,128]{3,2,1,0:T(8,128)S(1)} %get-tuple-element.19), channel_id=1, source_target_pairs={{4,0},{8,4},{12,8},{16,12},{20,16},{24,20},{28,24},{5,1},{9,5},{13... | collective-permute-start | bytes 172040 | tf_op jit(solution)/shard_map/ppermute | solution.py:28
  17.3 2.7 copy-start.9
  17.4 2.8 collective-permute-start.2
  18.7 4.9 %collective-permute-start.3 = (f32[7,16,1,128]{3,2,1,0:T(1,128)S(1)}, f32[7,16,1,128]{3,2,1,0:T(1,128)S(1)}, u32[]{:S(2)}, u32[]{:S(2)}) collective-permute-start(f32[7,16,1,128]{3,2,1,0:T(1,128)S(1)} %get-tuple-element.13), channel_id=1, source_target_pairs={{1,0},{2,1},{3,2},{5,4},{6,5},{7,6},{9,8},{10,9},{11,10},{13,12},{... | collective-permute-start | bytes 172040 | tf_op jit(solution)/shard_map/ppermute | solution.py:28
  32.4 5.9 %collective-permute-start.4 = (f32[4,1,16,128]{3,2,1,0:T(8,128)S(1)}, f32[4,1,16,128]{3,2,1,0:T(8,128)S(1)}, u32[]{:S(2)}, u32[]{:S(2)}) collective-permute-start(f32[4,1,16,128]{3,2,1,0:T(8,128)S(1)} %get-tuple-element.32), channel_id=1, source_target_pairs={{0,4},{4,8},{8,12},{12,16},{16,20},{20,24},{24,28},{1,5},{5,9},{9,... | collective-permute-start | bytes 98312 | tf_op jit(solution)/shard_map/ppermute | solution.py:26
  36.8 5.8 %collective-permute-start.5 = (f32[4,1,16,128]{3,2,1,0:T(8,128)S(1)}, f32[4,1,16,128]{3,2,1,0:T(8,128)S(1)}, u32[]{:S(2)}, u32[]{:S(2)}) collective-permute-start(f32[4,1,16,128]{3,2,1,0:T(8,128)S(1)} %get-tuple-element.33), channel_id=1, source_target_pairs={{4,0},{8,4},{12,8},{16,12},{20,16},{24,20},{28,24},{5,1},{9,5},{13... | collective-permute-start | bytes 98312 | tf_op jit(solution)/shard_map/ppermute | solution.py:28
  43.3 4.9 %collective-permute-start.6 = (f32[4,16,1,128]{3,2,1,0:T(1,128)S(1)}, f32[4,16,1,128]{3,2,1,0:T(1,128)S(1)}, u32[]{:S(2)}, u32[]{:S(2)}) collective-permute-start(f32[4,16,1,128]{3,2,1,0:T(1,128)S(1)} %get-tuple-element.26), channel_id=1, source_target_pairs={{0,1},{1,2},{2,3},{4,5},{5,6},{6,7},{8,9},{9,10},{10,11},{12,13},{... | collective-permute-start | bytes 98312 | tf_op jit(solution)/shard_map/ppermute | solution.py:26
  46.6 4.0 %collective-permute-start.7 = (f32[4,16,1,128]{3,2,1,0:T(1,128)S(1)}, f32[4,16,1,128]{3,2,1,0:T(1,128)S(1)}, u32[]{:S(2)}, u32[]{:S(2)}) collective-permute-start(f32[4,16,1,128]{3,2,1,0:T(1,128)S(1)} %get-tuple-element.27), channel_id=1, source_target_pairs={{1,0},{2,1},{3,2},{5,4},{6,5},{7,6},{9,8},{10,9},{11,10},{13,12},{... | collective-permute-start | bytes 98312 | tf_op jit(solution)/shard_map/ppermute | solution.py:28
  51.4 1.3 copy-start.7
  53.7 4.8 %collective-permute-start.8 = (f32[1,1,16,128]{3,2,1,0:T(8,128)S(1)}, f32[1,1,16,128]{3,2,1,0:T(8,128)S(1)}, u32[]{:S(2)}, u32[]{:S(2)}) collective-permute-start(f32[1,1,16,128]{3,2,1,0:T(8,128)S(1)} %get-tuple-element.95), channel_id=1, source_target_pairs={{0,4},{4,8},{8,12},{12,16},{16,20},{20,24},{24,28},{1,5},{5,9},{9,... | collective-permute-start | bytes 24584 | tf_op jit(solution)/shard_map/ppermute | solution.py:26
  57.1 5.5 %collective-permute-start.9 = (f32[1,1,16,128]{3,2,1,0:T(8,128)S(1)}, f32[1,1,16,128]{3,2,1,0:T(8,128)S(1)}, u32[]{:S(2)}, u32[]{:S(2)}) collective-permute-start(f32[1,1,16,128]{3,2,1,0:T(8,128)S(1)} %get-tuple-element.96), channel_id=1, source_target_pairs={{4,0},{8,4},{12,8},{16,12},{20,16},{24,20},{28,24},{5,1},{9,5},{13... | collective-permute-start | bytes 24584 | tf_op jit(solution)/shard_map/ppermute | solution.py:28
  62.8 4.4 %collective-permute-start.10 = (f32[1,16,1,128]{3,2,1,0:T(1,128)S(1)}, f32[1,16,1,128]{3,2,1,0:T(1,128)S(1)}, u32[]{:S(2)}, u32[]{:S(2)}) collective-permute-start(f32[1,16,1,128]{3,2,1,0:T(1,128)S(1)} %get-tuple-element.89), channel_id=1, source_target_pairs={{0,1},{1,2},{2,3},{4,5},{5,6},{6,7},{8,9},{9,10},{10,11},{12,13},{... | collective-permute-start | bytes 24584 | tf_op jit(solution)/shard_map/ppermute | solution.py:26
  65.9 4.0 %collective-permute-start.11 = (f32[1,16,1,128]{3,2,1,0:T(1,128)S(1)}, f32[1,16,1,128]{3,2,1,0:T(1,128)S(1)}, u32[]{:S(2)}, u32[]{:S(2)}) collective-permute-start(f32[1,16,1,128]{3,2,1,0:T(1,128)S(1)} %get-tuple-element.90), channel_id=1, source_target_pairs={{1,0},{2,1},{3,2},{5,4},{6,5},{7,6},{9,8},{10,9},{11,10},{13,12},{... | collective-permute-start | bytes 24584 | tf_op jit(solution)/shard_map/ppermute | solution.py:28
  73.7 42.3 %copy-start.18 = (f32[4,128]{1,0:T(4,128)S(1)}, f32[4,128]{1,0:T(4,128)}, u32[]{:S(2)}) copy-start(f32[4,128]{1,0:T(4,128)} %param.18) | copy-start | bytes 6148
  118.2 5.6 %collective-permute-start.12 = (f32[2,1,16,128]{3,2,1,0:T(8,128)S(1)}, f32[2,1,16,128]{3,2,1,0:T(8,128)S(1)}, u32[]{:S(2)}, u32[]{:S(2)}) collective-permute-start(f32[2,1,16,128]{3,2,1,0:T(8,128)S(1)} %get-tuple-element.59), channel_id=1, source_target_pairs={{0,4},{4,8},{8,12},{12,16},{16,20},{20,24},{24,28},{1,5},{5,9},{9,... | collective-permute-start | bytes 49160 | tf_op jit(solution)/shard_map/ppermute | solution.py:26
  122.3 5.6 %collective-permute-start.13 = (f32[2,1,16,128]{3,2,1,0:T(8,128)S(1)}, f32[2,1,16,128]{3,2,1,0:T(8,128)S(1)}, u32[]{:S(2)}, u32[]{:S(2)}) collective-permute-start(f32[2,1,16,128]{3,2,1,0:T(8,128)S(1)} %get-tuple-element.60), channel_id=1, source_target_pairs={{4,0},{8,4},{12,8},{16,12},{20,16},{24,20},{28,24},{5,1},{9,5},{13... | collective-permute-start | bytes 49160 | tf_op jit(solution)/shard_map/ppermute | solution.py:28
  128.3 2.6 collective-permute-start.14
  129.6 3.4 collective-permute-start.15
  136.9 6.0 %collective-permute-start.16 = (f32[1,1,16,128]{3,2,1,0:T(8,128)S(1)}, f32[1,1,16,128]{3,2,1,0:T(8,128)S(1)}, u32[]{:S(2)}, u32[]{:S(2)}) collective-permute-start(f32[1,1,16,128]{3,2,1,0:T(8,128)S(1)} %get-tuple-element.83), channel_id=1, source_target_pairs={{0,4},{4,8},{8,12},{12,16},{16,20},{20,24},{24,28},{1,5},{5,9},{9,... | collective-permute-start | bytes 24584 | tf_op jit(solution)/shard_map/ppermute | solution.py:26
  141.6 5.5 %collective-permute-start.17 = (f32[1,1,16,128]{3,2,1,0:T(8,128)S(1)}, f32[1,1,16,128]{3,2,1,0:T(8,128)S(1)}, u32[]{:S(2)}, u32[]{:S(2)}) collective-permute-start(f32[1,1,16,128]{3,2,1,0:T(8,128)S(1)} %get-tuple-element.84), channel_id=1, source_target_pairs={{4,0},{8,4},{12,8},{16,12},{20,16},{24,20},{28,24},{5,1},{9,5},{13... | collective-permute-start | bytes 24584 | tf_op jit(solution)/shard_map/ppermute | solution.py:28
  147.3 4.3 %collective-permute-start.18 = (f32[1,16,1,128]{3,2,1,0:T(1,128)S(1)}, f32[1,16,1,128]{3,2,1,0:T(1,128)S(1)}, u32[]{:S(2)}, u32[]{:S(2)}) collective-permute-start(f32[1,16,1,128]{3,2,1,0:T(1,128)S(1)} %get-tuple-element.77), channel_id=1, source_target_pairs={{0,1},{1,2},{2,3},{4,5},{5,6},{6,7},{8,9},{9,10},{10,11},{12,13},{... | collective-permute-start | bytes 24584 | tf_op jit(solution)/shard_map/ppermute | solution.py:26
  150.3 4.0 %collective-permute-start.19 = (f32[1,16,1,128]{3,2,1,0:T(1,128)S(1)}, f32[1,16,1,128]{3,2,1,0:T(1,128)S(1)}, u32[]{:S(2)}, u32[]{:S(2)}) collective-permute-start(f32[1,16,1,128]{3,2,1,0:T(1,128)S(1)} %get-tuple-element.78), channel_id=1, source_target_pairs={{1,0},{2,1},{3,2},{5,4},{6,5},{7,6},{9,8},{10,9},{11,10},{13,12},{... | collective-permute-start | bytes 24584 | tf_op jit(solution)/shard_map/ppermute | solution.py:28
  240.4 5.6 %collective-permute-start.20 = (f32[2,1,16,128]{3,2,1,0:T(8,128)S(1)}, f32[2,1,16,128]{3,2,1,0:T(8,128)S(1)}, u32[]{:S(2)}, u32[]{:S(2)}) collective-permute-start(f32[2,1,16,128]{3,2,1,0:T(8,128)S(1)} %get-tuple-element.47), channel_id=1, source_target_pairs={{0,4},{4,8},{8,12},{12,16},{16,20},{20,24},{24,28},{1,5},{5,9},{9,... | collective-permute-start | bytes 49160 | tf_op jit(solution)/shard_map/ppermute | solution.py:26
  244.6 5.6 %collective-permute-start.21 = (f32[2,1,16,128]{3,2,1,0:T(8,128)S(1)}, f32[2,1,16,128]{3,2,1,0:T(8,128)S(1)}, u32[]{:S(2)}, u32[]{:S(2)}) collective-permute-start(f32[2,1,16,128]{3,2,1,0:T(8,128)S(1)} %get-tuple-element.48), channel_id=1, source_target_pairs={{4,0},{8,4},{12,8},{16,12},{20,16},{24,20},{28,24},{5,1},{9,5},{13... | collective-permute-start | bytes 49160 | tf_op jit(solution)/shard_map/ppermute | solution.py:28
  250.6 2.9 collective-permute-start.22
  251.9 4.2 %collective-permute-start.23 = (f32[2,16,1,128]{3,2,1,0:T(1,128)S(1)}, f32[2,16,1,128]{3,2,1,0:T(1,128)S(1)}, u32[]{:S(2)}, u32[]{:S(2)}) collective-permute-start(f32[2,16,1,128]{3,2,1,0:T(1,128)S(1)} %get-tuple-element.42), channel_id=1, source_target_pairs={{1,0},{2,1},{3,2},{5,4},{6,5},{7,6},{9,8},{10,9},{11,10},{13,12},{... | collective-permute-start | bytes 49160 | tf_op jit(solution)/shard_map/ppermute | solution.py:28
  304.0 5.5 %collective-permute-start.24 = (f32[1,1,16,128]{3,2,1,0:T(8,128)S(1)}, f32[1,1,16,128]{3,2,1,0:T(8,128)S(1)}, u32[]{:S(2)}, u32[]{:S(2)}) collective-permute-start(f32[1,1,16,128]{3,2,1,0:T(8,128)S(1)} %get-tuple-element.71), channel_id=1, source_target_pairs={{0,4},{4,8},{8,12},{12,16},{16,20},{20,24},{24,28},{1,5},{5,9},{9,... | collective-permute-start | bytes 24584 | tf_op jit(solution)/shard_map/ppermute | solution.py:26
  308.2 5.5 %collective-permute-start.25 = (f32[1,1,16,128]{3,2,1,0:T(8,128)S(1)}, f32[1,1,16,128]{3,2,1,0:T(8,128)S(1)}, u32[]{:S(2)}, u32[]{:S(2)}) collective-permute-start(f32[1,1,16,128]{3,2,1,0:T(8,128)S(1)} %get-tuple-element.72), channel_id=1, source_target_pairs={{4,0},{8,4},{12,8},{16,12},{20,16},{24,20},{28,24},{5,1},{9,5},{13... | collective-permute-start | bytes 24584 | tf_op jit(solution)/shard_map/ppermute | solution.py:28
  314.0 2.6 collective-permute-start.26
  315.2 3.7 %collective-permute-start.27 = (f32[1,16,1,128]{3,2,1,0:T(1,128)S(1)}, f32[1,16,1,128]{3,2,1,0:T(1,128)S(1)}, u32[]{:S(2)}, u32[]{:S(2)}) collective-permute-start(f32[1,16,1,128]{3,2,1,0:T(1,128)S(1)} %get-tuple-element.66), channel_id=1, source_target_pairs={{1,0},{2,1},{3,2},{5,4},{6,5},{7,6},{9,8},{10,9},{11,10},{13,12},{... | collective-permute-start | bytes 24584 | tf_op jit(solution)/shard_map/ppermute | solution.py:28
  (18 other events, 13.8 us)
where the time goes:
time: 366 us; the launch traced here: 364 us
  blocking collectives  207 us (57%)
  starting transfers between devices  62.8 us (17%)
  waiting for transfers between devices  48.8 us (13%)
  matrix products  18.2 us (5%)
  local copies, waits for them, and re-layouts  13.9 us (4%)
  other arithmetic  7.2 us (2%)
  between operations  6.35 us (2%)
    psum x3, blocking collectives, total(): return lax.psum(value, ('gx', 'gy'))  124 us
    unnamed x2, blocking collectives  82.6 us
    ppermute x14, waiting for transfers between devices, with_halo(): lax.ppermute(head, axis, [((i + 1) % count, i) for i in range(ends)])  47.8 us
    ppermute x14, starting transfers between devices, with_halo(): lax.ppermute(tail, axis, [(i, (i + 1) % count) for i in range(ends)])  44.3 us
    ppermute x14, starting transfers between devices, with_halo(): lax.ppermute(head, axis, [((i + 1) % count, i) for i in range(ends)])  18.5 us
    unnamed x45, local copies, waits for them, and re-layouts  9.75 us
  transfers between devices with their start and end apart: 28, of which 18 were waited for; matrix products, arithmetic and copies ran while one was open for 0% of the time, Pallas kernels for 0%

commit v1 on v0

--- a/solution.py
+++ b/solution.py
@@ -15,20 +15,22 @@
 cheb_ratio = 0.1
 
 
+def swap_faces(first_face, last_face, axis):
+    count = lax.axis_size(axis)
+    even = lax.axis_index(axis) % 2 == 0
+    first_pairs = [(i, i ^ 1) for i in range(count) if i ^ 1 < count]
+    second_pairs = [(i, ((i + 1) ^ 1) - 1) for i in range(1, count) if ((i + 1) ^ 1) - 1 < count]
+    got_first = lax.ppermute(jnp.where(even, last_face, first_face), axis, first_pairs)
+    got_second = lax.ppermute(jnp.where(even, first_face, last_face), axis, second_pairs)
+    return jnp.where(even, got_second, got_first), jnp.where(even, got_first, got_second)
+
+
 def with_halo(cells, sides, width):
     for axis, dim in sides:
-        count = lax.axis_size(axis)
-        ends = count - 1
         head = lax.slice_in_dim(cells, 0, width, axis=dim)
         tail = lax.slice_in_dim(cells, cells.shape[dim] - width, cells.shape[dim], axis=dim)
-        cells = jnp.concatenate(
-            [
-                lax.ppermute(tail, axis, [(i, (i + 1) % count) for i in range(ends)]),
-                cells,
-                lax.ppermute(head, axis, [((i + 1) % count, i) for i in range(ends)]),
-            ],
-            axis=dim,
-        )
+        before, after = swap_faces(head, tail, axis)
+        cells = jnp.concatenate([before, cells, after], axis=dim)
     return cells
 
 
@@ -214,11 +216,16 @@
         elem_sums = jnp.dot(node_sums, block_table, precision=precision)
         return jnp.einsum("xyz,xyzk->k", elem_sums, one_hot, precision=precision)
 
+    def spread_out(values):
+        count = lax.axis_size("gx") * lax.axis_size("gy")
+        copies = jnp.broadcast_to(values[None], (count,) + values.shape)
+        return lax.all_to_all(copies, ("gx", "gy"), 0, 0, tiled=True)
+
     def gather_rest(resid):
-        return lax.all_gather(restrict(resid), ("gx", "gy"), axis=0, tiled=True)
+        return spread_out(restrict(resid)).reshape(-1)
 
     def total(value):
-        return lax.psum(value, ("gx", "gy"))
+        return jnp.sum(spread_out(value[None]))
 
     lower = cheb_ratio * spectral_bound
     cheb_theta = 0.5 * (spectral_bound + lower)

time: 366 us -> 195 us (0.53)
  blocking collectives: 207 us -> 32.7 us
  waiting for transfers between devices: 48.8 us -> 36.4 us
  starting transfers between devices: 62.8 us -> 70.3 us
  local copies, waits for them, and re-layouts: 13.9 us -> 18.9 us
  other arithmetic: 7.2 us -> 11.3 us
    psum x3 -> x0, blocking collectives: 124 us -> none  [total(): return lax.psum(value, ('gx', 'gy'))]
    unnamed x2 -> x0, blocking collectives: 82.6 us -> none
    all_to_all x0 -> x3, blocking collectives: none -> 32.7 us  [spread_out(): return lax.all_to_all(copies, ('gx', 'gy'), 0, 0, tiled=True)]
    ppermute x28, waiting for transfers between devices: 48.8 us -> 18 us  [the longest x14 17.9 us: swap_faces(): lax.ppermute(jnp.where(even, last_face, first_face), axis, first_pairs)]
    all_to_all x0 -> x3, waiting for transfers between devices: none -> 18.5 us  [spread_out(): return lax.all_to_all(copies, ('gx', 'gy'), 0, 0, tiled=True)]
    all_to_all x0 -> x3, starting transfers between devices: none -> 11 us  [spread_out(): return lax.all_to_all(copies, ('gx', 'gy'), 0, 0, tiled=True)]
    broadcast_in_dim x0 -> x6, local copies, waits for them, and re-layouts: none -> 4.53 us  [spread_out(): copies = jnp.broadcast_to(values[None], (count,) + values.shape)]
    unnamed x45 -> x41, local copies, waits for them, and re-layouts: 9.75 us -> 9.76 us
  transfers between devices with their start and end apart: 28 -> 31, of which waited for: 18 -> 17; matrix products, arithmetic and copies ran while one was open for 0% -> 1% of each run, Pallas kernels for 0% -> 0%
where the time goes in v1:
time: 195 us; the launch traced here: 194 us
  starting transfers between devices  70.3 us (36%)
  waiting for transfers between devices  36.4 us (19%)
  blocking collectives  32.7 us (17%)
  local copies, waits for them, and re-layouts  18.9 us (10%)
  matrix products  18.2 us (9%)
  other arithmetic  11.3 us (6%)
  between operations  6.25 us (3%)
    ppermute x14, starting transfers between devices, swap_faces(): lax.ppermute(jnp.where(even, last_face, first_face), axis, first_pairs)  49.8 us
    all_to_all x3, blocking collectives, spread_out(): return lax.all_to_all(copies, ('gx', 'gy'), 0, 0, tiled=True)  32.7 us
    all_to_all x3, waiting for transfers between devices, spread_out(): return lax.all_to_all(copies, ('gx', 'gy'), 0, 0, tiled=True)  18.5 us
    ppermute x14, waiting for transfers between devices, swap_faces(): lax.ppermute(jnp.where(even, last_face, first_face), axis, first_pairs)  17.9 us
    all_to_all x3, starting transfers between devices, spread_out(): return lax.all_to_all(copies, ('gx', 'gy'), 0, 0, tiled=True)  11 us
    unnamed x41, local copies, waits for them, and re-layouts  9.76 us
    ppermute x14, starting transfers between devices, swap_faces(): lax.ppermute(jnp.where(even, first_face, last_face), axis, second_pairs)  9.45 us
    broadcast_in_dim x6, local copies, waits for them, and re-layouts, spread_out(): copies = jnp.broadcast_to(values[None], (count,) + values.shape)  4.53 us
  transfers between devices with their start and end apart: 31, of which 17 were waited for; matrix products, arithmetic and copies ran while one was open for 1% of the time, Pallas kernels for 0%

profile of v1, /device:TPU:0, one launch (start us, length us, event | category | flops | bytes accessed | tf_op | source)
XLA Modules:
  0.0 194.0 jit_solution(16856921637758985290)
XLA Ops:
  3.1 1.2 copy_multiply_fusion
  6.0 5.8 %collective-permute-start.1 = (f32[7,1,16,128]{3,2,1,0:T(8,128)S(1)}, f32[7,1,16,128]{3,2,1,0:T(8,128)S(1)}, u32[]{:S(2)}, u32[]{:S(2)}) collective-permute-start(f32[7,1,16,128]{3,2,1,0:T(8,128)S(1)} %get-tuple-element.17), channel_id=1, source_target_pairs={{0,4},{4,0},{8,12},{12,8},{16,20},{20,16},{24,28},{28,24},{1,5},{5... | collective-permute-start | bytes 172040 | tf_op jit(solution)/shard_map/ppermute | solution.py:23
  11.9 2.1 %collective-permute-done.1 = f32[7,1,16,128]{3,2,1,0:T(8,128)S(1)} collective-permute-done((f32[7,1,16,128]{3,2,1,0:T(8,128)S(1)}, f32[7,1,16,128]{3,2,1,0:T(8,128)S(1)}, u32[]{:S(2)}, u32[]{:S(2)}) %collective-permute-start.1) | collective-permute-done | bytes 57376 | tf_op jit(solution)/shard_map/ppermute | solution.py:23
  15.8 2.9 %collective-permute-start.3 = (f32[7,16,1,128]{3,2,1,0:T(1,128)S(1)}, f32[7,16,1,128]{3,2,1,0:T(1,128)S(1)}, u32[]{:S(2)}, u32[]{:S(2)}) collective-permute-start(f32[7,16,1,128]{3,2,1,0:T(1,128)S(1)} %get-tuple-element.13), channel_id=1, source_target_pairs={{0,1},{1,0},{2,3},{3,2},{4,5},{5,4},{6,7},{7,6},{8,9},{9,8},{10,11... | collective-permute-start | bytes 172040 | tf_op jit(solution)/shard_map/ppermute | solution.py:23
  29.2 4.8 %collective-permute-start.5 = (f32[4,1,16,128]{3,2,1,0:T(8,128)S(1)}, f32[4,1,16,128]{3,2,1,0:T(8,128)S(1)}, u32[]{:S(2)}, u32[]{:S(2)}) collective-permute-start(f32[4,1,16,128]{3,2,1,0:T(8,128)S(1)} %get-tuple-element.31), channel_id=1, source_target_pairs={{0,4},{4,0},{8,12},{12,8},{16,20},{20,16},{24,28},{28,24},{1,5},{5... | collective-permute-start | bytes 98312 | tf_op jit(solution)/shard_map/ppermute | solution.py:23
  34.1 2.1 %collective-permute-done.5 = f32[4,1,16,128]{3,2,1,0:T(8,128)S(1)} collective-permute-done((f32[4,1,16,128]{3,2,1,0:T(8,128)S(1)}, f32[4,1,16,128]{3,2,1,0:T(8,128)S(1)}, u32[]{:S(2)}, u32[]{:S(2)}) %collective-permute-start.5) | collective-permute-done | bytes 32800 | tf_op jit(solution)/shard_map/ppermute | solution.py:23
  37.7 3.7 %collective-permute-start.7 = (f32[4,16,1,128]{3,2,1,0:T(1,128)S(1)}, f32[4,16,1,128]{3,2,1,0:T(1,128)S(1)}, u32[]{:S(2)}, u32[]{:S(2)}) collective-permute-start(f32[4,16,1,128]{3,2,1,0:T(1,128)S(1)} %get-tuple-element.27), channel_id=1, source_target_pairs={{0,1},{1,0},{2,3},{3,2},{4,5},{5,4},{6,7},{7,6},{8,9},{9,8},{10,11... | collective-permute-start | bytes 98312 | tf_op jit(solution)/shard_map/ppermute | solution.py:23
  46.0 4.7 %collective-permute-start.9 = (f32[1,1,16,128]{3,2,1,0:T(8,128)S(1)}, f32[1,1,16,128]{3,2,1,0:T(8,128)S(1)}, u32[]{:S(2)}, u32[]{:S(2)}) collective-permute-start(f32[1,1,16,128]{3,2,1,0:T(8,128)S(1)} %get-tuple-element.94), channel_id=1, source_target_pairs={{0,4},{4,0},{8,12},{12,8},{16,20},{20,16},{24,28},{28,24},{1,5},{5... | collective-permute-start | bytes 24584 | tf_op jit(solution)/shard_map/ppermute | solution.py:23
  50.7 1.6 collective-permute-done.9
  53.2 3.5 %collective-permute-start.11 = (f32[1,16,1,128]{3,2,1,0:T(1,128)S(1)}, f32[1,16,1,128]{3,2,1,0:T(1,128)S(1)}, u32[]{:S(2)}, u32[]{:S(2)}) collective-permute-start(f32[1,16,1,128]{3,2,1,0:T(1,128)S(1)} %get-tuple-element.90), channel_id=1, source_target_pairs={{0,1},{1,0},{2,3},{3,2},{4,5},{5,4},{6,7},{7,6},{8,9},{9,8},{10,11... | collective-permute-start | bytes 24584 | tf_op jit(solution)/shard_map/ppermute | solution.py:23
  61.8 6.0 %all-to-all-start = ((f32[32,1,4]{2,1,0:T(1,128)}), f32[32,1,4]{2,1,0:T(1,128)S(1)}, u32[]{:S(2)}, u32[]{:S(2)}) async-start(f32[32,1,4]{2,1,0:T(1,128)} %broadcast_in_dim.178), calls=%async_computation | async-start | bytes 32768 | tf_op jit(solution)/shard_map/all_to_all | solution.py:222
  69.2 5.6 %all-to-all-done = f32[32,1,4]{2,1,0:T(1,128)S(1)} async-done(((f32[32,1,4]{2,1,0:T(1,128)}), f32[32,1,4]{2,1,0:T(1,128)S(1)}, u32[]{:S(2)}, u32[]{:S(2)}) %all-to-all-start) | async-done | bytes 544 | tf_op jit(solution)/shard_map/all_to_all | solution.py:222
  78.0 3.3 %collective-permute-start.13 = (f32[2,1,16,128]{3,2,1,0:T(8,128)S(1)}, f32[2,1,16,128]{3,2,1,0:T(8,128)S(1)}, u32[]{:S(2)}, u32[]{:S(2)}) collective-permute-start(f32[2,1,16,128]{3,2,1,0:T(8,128)S(1)} %get-tuple-element.58), channel_id=1, source_target_pairs={{0,4},{4,0},{8,12},{12,8},{16,20},{20,16},{24,28},{28,24},{1,5},{5... | collective-permute-start | bytes 49160 | tf_op jit(solution)/shard_map/ppermute | solution.py:23
  81.3 1.7 collective-permute-done.13
  84.1 2.0 %collective-permute-start.15 = (f32[2,16,1,128]{3,2,1,0:T(1,128)S(1)}, f32[2,16,1,128]{3,2,1,0:T(1,128)S(1)}, u32[]{:S(2)}, u32[]{:S(2)}) collective-permute-start(f32[2,16,1,128]{3,2,1,0:T(1,128)S(1)} %get-tuple-element.54), channel_id=1, source_target_pairs={{0,1},{1,0},{2,3},{3,2},{4,5},{5,4},{6,7},{7,6},{8,9},{9,8},{10,11... | collective-permute-start | bytes 49160 | tf_op jit(solution)/shard_map/ppermute | solution.py:23
  91.4 4.9 %collective-permute-start.17 = (f32[1,1,16,128]{3,2,1,0:T(8,128)S(1)}, f32[1,1,16,128]{3,2,1,0:T(8,128)S(1)}, u32[]{:S(2)}, u32[]{:S(2)}) collective-permute-start(f32[1,1,16,128]{3,2,1,0:T(8,128)S(1)} %get-tuple-element.86), channel_id=1, source_target_pairs={{0,4},{4,0},{8,12},{12,8},{16,20},{20,16},{24,28},{28,24},{1,5},{5... | collective-permute-start | bytes 24584 | tf_op jit(solution)/shard_map/ppermute | solution.py:23
  96.3 1.6 collective-permute-done.17
  98.8 3.6 %collective-permute-start.19 = (f32[1,16,1,128]{3,2,1,0:T(1,128)S(1)}, f32[1,16,1,128]{3,2,1,0:T(1,128)S(1)}, u32[]{:S(2)}, u32[]{:S(2)}) collective-permute-start(f32[1,16,1,128]{3,2,1,0:T(1,128)S(1)} %get-tuple-element.82), channel_id=1, source_target_pairs={{0,1},{1,0},{2,3},{3,2},{4,5},{5,4},{6,7},{7,6},{8,9},{9,8},{10,11... | collective-permute-start | bytes 24584 | tf_op jit(solution)/shard_map/ppermute | solution.py:23
  104.9 10.8 %all_to_all.36 = f32[32,1,1]{2,1,0:T(1,128)S(1)} all-to-all(f32[32,1,1]{2,1,0:T(1,128)S(1)} %broadcast_in_dim.189), channel_id=1, replica_groups=mesh['gx'=8,'gy'=4] {'gx','gy'}, dimensions={0} | all-to-all | bytes 256 | tf_op jit(solution)/shard_map/all_to_all | solution.py:222
  115.7 1.3 broadcast_in_dim.183
  117.0 2.5 %all-to-all-start.1 = ((f32[32,1,1]{2,1,0:T(1,128)}), f32[32,1,1]{2,1,0:T(1,128)S(1)}, u32[]{:S(2)}, u32[]{:S(2)}) async-start(f32[32,1,1]{2,1,0:T(1,128)} %broadcast_in_dim.183), calls=%async_computation.1 | async-start | bytes 32768 | tf_op jit(solution)/shard_map/all_to_all | solution.py:222
  120.2 6.4 %all-to-all-done.1 = f32[32,1,1]{2,1,0:T(1,128)S(1)} async-done(((f32[32,1,1]{2,1,0:T(1,128)}), f32[32,1,1]{2,1,0:T(1,128)S(1)}, u32[]{:S(2)}, u32[]{:S(2)}) %all-to-all-start.1) | async-done | bytes 160 | tf_op jit(solution)/shard_map/all_to_all | solution.py:222
  130.9 2.5 %all-to-all-start.3 = ((f32[32,1,4]{2,1,0:T(1,128)}), f32[32,1,4]{2,1,0:T(1,128)S(1)}, u32[]{:S(2)}, u32[]{:S(2)}) async-start(f32[32,1,4]{2,1,0:T(1,128)} %broadcast_in_dim.190), calls=%async_computation.3 | async-start | bytes 32768 | tf_op jit(solution)/shard_map/all_to_all | solution.py:222
  134.2 6.4 %all-to-all-done.3 = f32[32,1,4]{2,1,0:T(1,128)S(1)} async-done(((f32[32,1,4]{2,1,0:T(1,128)}), f32[32,1,4]{2,1,0:T(1,128)S(1)}, u32[]{:S(2)}, u32[]{:S(2)}) %all-to-all-start.3) | async-done | bytes 544 | tf_op jit(solution)/shard_map/all_to_all | solution.py:222
  142.7 3.3 %collective-permute-start.21 = (f32[2,1,16,128]{3,2,1,0:T(8,128)S(1)}, f32[2,1,16,128]{3,2,1,0:T(8,128)S(1)}, u32[]{:S(2)}, u32[]{:S(2)}) collective-permute-start(f32[2,1,16,128]{3,2,1,0:T(8,128)S(1)} %get-tuple-element.50), channel_id=1, source_target_pairs={{0,4},{4,0},{8,12},{12,8},{16,20},{20,16},{24,28},{28,24},{1,5},{5... | collective-permute-start | bytes 49160 | tf_op jit(solution)/shard_map/ppermute | solution.py:23
  146.1 1.7 collective-permute-done.21
  148.8 2.0 %collective-permute-start.23 = (f32[2,16,1,128]{3,2,1,0:T(1,128)S(1)}, f32[2,16,1,128]{3,2,1,0:T(1,128)S(1)}, u32[]{:S(2)}, u32[]{:S(2)}) collective-permute-start(f32[2,16,1,128]{3,2,1,0:T(1,128)S(1)} %get-tuple-element.46), channel_id=1, source_target_pairs={{0,1},{1,0},{2,3},{3,2},{4,5},{5,4},{6,7},{7,6},{8,9},{9,8},{10,11... | collective-permute-start | bytes 49160 | tf_op jit(solution)/shard_map/ppermute | solution.py:23
  153.4 11.0 %all_to_all.37 = f32[32,1,1]{2,1,0:T(1,128)S(1)} all-to-all(f32[32,1,1]{2,1,0:T(1,128)S(1)} %broadcast_in_dim.195), channel_id=1, replica_groups=mesh['gx'=8,'gy'=4] {'gx','gy'}, dimensions={0} | all-to-all | bytes 256 | tf_op jit(solution)/shard_map/all_to_all | solution.py:222
  170.4 3.3 %collective-permute-start.25 = (f32[1,1,16,128]{3,2,1,0:T(8,128)S(1)}, f32[1,1,16,128]{3,2,1,0:T(8,128)S(1)}, u32[]{:S(2)}, u32[]{:S(2)}) collective-permute-start(f32[1,1,16,128]{3,2,1,0:T(8,128)S(1)} %get-tuple-element.78), channel_id=1, source_target_pairs={{0,4},{4,0},{8,12},{12,8},{16,20},{20,16},{24,28},{28,24},{1,5},{5... | collective-permute-start | bytes 24584 | tf_op jit(solution)/shard_map/ppermute | solution.py:23
  173.7 1.6 collective-permute-done.25
  176.2 2.0 %collective-permute-start.27 = (f32[1,16,1,128]{3,2,1,0:T(1,128)S(1)}, f32[1,16,1,128]{3,2,1,0:T(1,128)S(1)}, u32[]{:S(2)}, u32[]{:S(2)}) collective-permute-start(f32[1,16,1,128]{3,2,1,0:T(1,128)S(1)} %get-tuple-element.74), channel_id=1, source_target_pairs={{0,1},{1,0},{2,3},{3,2},{4,5},{5,4},{6,7},{7,6},{8,9},{9,8},{10,11... | collective-permute-start | bytes 24584 | tf_op jit(solution)/shard_map/ppermute | solution.py:23
  180.6 10.9 %all_to_all.38 = f32[32,1,1]{2,1,0:T(1,128)S(1)} all-to-all(f32[32,1,1]{2,1,0:T(1,128)S(1)} %broadcast_in_dim.201), channel_id=1, replica_groups=mesh['gx'=8,'gy'=4] {'gx','gy'}, dimensions={0} | all-to-all | bytes 256 | tf_op jit(solution)/shard_map/all_to_all | solution.py:222
  (304 shorter events, 60.8 us)
Async XLA Ops:
  5.4 6.6 %collective-permute-start = (f32[7,1,16,128]{3,2,1,0:T(8,128)S(1)}, f32[7,1,16,128]{3,2,1,0:T(8,128)S(1)}, u32[]{:S(2)}, u32[]{:S(2)}) collective-permute-start(f32[7,1,16,128]{3,2,1,0:T(8,128)S(1)} %get-tuple-element.16), channel_id=1, source_target_pairs={{4,8},{8,4},{12,16},{16,12},{20,24},{24,20},{5,9},{9,5},{13,17},{1... | collective-permute-start | bytes 172040 | tf_op jit(solution)/shard_map/ppermute | solution.py:24
  6.0 8.0 %collective-permute-start.1 = (f32[7,1,16,128]{3,2,1,0:T(8,128)S(1)}, f32[7,1,16,128]{3,2,1,0:T(8,128)S(1)}, u32[]{:S(2)}, u32[]{:S(2)}) collective-permute-start(f32[7,1,16,128]{3,2,1,0:T(8,128)S(1)} %get-tuple-element.17), channel_id=1, source_target_pairs={{0,4},{4,0},{8,12},{12,8},{16,20},{20,16},{24,28},{28,24},{1,5},{5... | collective-permute-start | bytes 172040 | tf_op jit(solution)/shard_map/ppermute | solution.py:23
  15.0 3.7 %copy-start.8 = (f32[2,8,2,8,128]{4,3,2,1,0:T(8,128)S(1)}, f32[2,8,2,8,128]{4,3,2,1,0:T(8,128)}, u32[]{:S(2)}) copy-start(f32[2,8,2,8,128]{4,3,2,1,0:T(8,128)} %param.15) | copy-start | bytes 393220
  15.1 3.8 %collective-permute-start.2 = (f32[7,16,1,128]{3,2,1,0:T(1,128)S(1)}, f32[7,16,1,128]{3,2,1,0:T(1,128)S(1)}, u32[]{:S(2)}, u32[]{:S(2)}) collective-permute-start(f32[7,16,1,128]{3,2,1,0:T(1,128)S(1)} %get-tuple-element.12), channel_id=1, source_target_pairs={{1,2},{2,1},{5,6},{6,5},{9,10},{10,9},{13,14},{14,13},{17,18},{18,... | collective-permute-start | bytes 172040 | tf_op jit(solution)/shard_map/ppermute | solution.py:24
  15.8 3.8 %collective-permute-start.3 = (f32[7,16,1,128]{3,2,1,0:T(1,128)S(1)}, f32[7,16,1,128]{3,2,1,0:T(1,128)S(1)}, u32[]{:S(2)}, u32[]{:S(2)}) collective-permute-start(f32[7,16,1,128]{3,2,1,0:T(1,128)S(1)} %get-tuple-element.13), channel_id=1, source_target_pairs={{0,1},{1,0},{2,3},{3,2},{4,5},{5,4},{6,7},{7,6},{8,9},{9,8},{10,11... | collective-permute-start | bytes 172040 | tf_op jit(solution)/shard_map/ppermute | solution.py:23
  28.5 5.6 %collective-permute-start.4 = (f32[4,1,16,128]{3,2,1,0:T(8,128)S(1)}, f32[4,1,16,128]{3,2,1,0:T(8,128)S(1)}, u32[]{:S(2)}, u32[]{:S(2)}) collective-permute-start(f32[4,1,16,128]{3,2,1,0:T(8,128)S(1)} %get-tuple-element.30), channel_id=1, source_target_pairs={{4,8},{8,4},{12,16},{16,12},{20,24},{24,20},{5,9},{9,5},{13,17},{1... | collective-permute-start | bytes 98312 | tf_op jit(solution)/shard_map/ppermute | solution.py:24
  29.2 7.0 %collective-permute-start.5 = (f32[4,1,16,128]{3,2,1,0:T(8,128)S(1)}, f32[4,1,16,128]{3,2,1,0:T(8,128)S(1)}, u32[]{:S(2)}, u32[]{:S(2)}) collective-permute-start(f32[4,1,16,128]{3,2,1,0:T(8,128)S(1)} %get-tuple-element.31), channel_id=1, source_target_pairs={{0,4},{4,0},{8,12},{12,8},{16,20},{20,16},{24,28},{28,24},{1,5},{5... | collective-permute-start | bytes 98312 | tf_op jit(solution)/shard_map/ppermute | solution.py:23
  36.9 4.6 %collective-permute-start.6 = (f32[4,16,1,128]{3,2,1,0:T(1,128)S(1)}, f32[4,16,1,128]{3,2,1,0:T(1,128)S(1)}, u32[]{:S(2)}, u32[]{:S(2)}) collective-permute-start(f32[4,16,1,128]{3,2,1,0:T(1,128)S(1)} %get-tuple-element.26), channel_id=1, source_target_pairs={{1,2},{2,1},{5,6},{6,5},{9,10},{10,9},{13,14},{14,13},{17,18},{18,... | collective-permute-start | bytes 98312 | tf_op jit(solution)/shard_map/ppermute | solution.py:24
  37.7 4.5 %collective-permute-start.7 = (f32[4,16,1,128]{3,2,1,0:T(1,128)S(1)}, f32[4,16,1,128]{3,2,1,0:T(1,128)S(1)}, u32[]{:S(2)}, u32[]{:S(2)}) collective-permute-start(f32[4,16,1,128]{3,2,1,0:T(1,128)S(1)} %get-tuple-element.27), channel_id=1, source_target_pairs={{0,1},{1,0},{2,3},{3,2},{4,5},{5,4},{6,7},{7,6},{8,9},{9,8},{10,11... | collective-permute-start | bytes 98312 | tf_op jit(solution)/shard_map/ppermute | solution.py:23
  45.3 5.4 %collective-permute-start.8 = (f32[1,1,16,128]{3,2,1,0:T(8,128)S(1)}, f32[1,1,16,128]{3,2,1,0:T(8,128)S(1)}, u32[]{:S(2)}, u32[]{:S(2)}) collective-permute-start(f32[1,1,16,128]{3,2,1,0:T(8,128)S(1)} %get-tuple-element.93), channel_id=1, source_target_pairs={{4,8},{8,4},{12,16},{16,12},{20,24},{24,20},{5,9},{9,5},{13,17},{1... | collective-permute-start | bytes 24584 | tf_op jit(solution)/shard_map/ppermute | solution.py:24
  46.0 6.4 %collective-permute-start.9 = (f32[1,1,16,128]{3,2,1,0:T(8,128)S(1)}, f32[1,1,16,128]{3,2,1,0:T(8,128)S(1)}, u32[]{:S(2)}, u32[]{:S(2)}) collective-permute-start(f32[1,1,16,128]{3,2,1,0:T(8,128)S(1)} %get-tuple-element.94), channel_id=1, source_target_pairs={{0,4},{4,0},{8,12},{12,8},{16,20},{20,16},{24,28},{28,24},{1,5},{5... | collective-permute-start | bytes 24584 | tf_op jit(solution)/shard_map/ppermute | solution.py:23
  52.5 4.2 %collective-permute-start.10 = (f32[1,16,1,128]{3,2,1,0:T(1,128)S(1)}, f32[1,16,1,128]{3,2,1,0:T(1,128)S(1)}, u32[]{:S(2)}, u32[]{:S(2)}) collective-permute-start(f32[1,16,1,128]{3,2,1,0:T(1,128)S(1)} %get-tuple-element.89), channel_id=1, source_target_pairs={{1,2},{2,1},{5,6},{6,5},{9,10},{10,9},{13,14},{14,13},{17,18},{18,... | collective-permute-start | bytes 24584 | tf_op jit(solution)/shard_map/ppermute | solution.py:24
  53.2 4.4 %collective-permute-start.11 = (f32[1,16,1,128]{3,2,1,0:T(1,128)S(1)}, f32[1,16,1,128]{3,2,1,0:T(1,128)S(1)}, u32[]{:S(2)}, u32[]{:S(2)}) collective-permute-start(f32[1,16,1,128]{3,2,1,0:T(1,128)S(1)} %get-tuple-element.90), channel_id=1, source_target_pairs={{0,1},{1,0},{2,3},{3,2},{4,5},{5,4},{6,7},{7,6},{8,9},{9,8},{10,11... | collective-permute-start | bytes 24584 | tf_op jit(solution)/shard_map/ppermute | solution.py:23
  61.8 13.0 %all-to-all-start = ((f32[32,1,4]{2,1,0:T(1,128)}), f32[32,1,4]{2,1,0:T(1,128)S(1)}, u32[]{:S(2)}, u32[]{:S(2)}) async-start(f32[32,1,4]{2,1,0:T(1,128)} %broadcast_in_dim.178), calls=%async_computation | async-start | bytes 32768 | tf_op jit(solution)/shard_map/all_to_all | solution.py:222
  77.3 4.0 %collective-permute-start.12 = (f32[2,1,16,128]{3,2,1,0:T(8,128)S(1)}, f32[2,1,16,128]{3,2,1,0:T(8,128)S(1)}, u32[]{:S(2)}, u32[]{:S(2)}) collective-permute-start(f32[2,1,16,128]{3,2,1,0:T(8,128)S(1)} %get-tuple-element.57), channel_id=1, source_target_pairs={{4,8},{8,4},{12,16},{16,12},{20,24},{24,20},{5,9},{9,5},{13,17},{1... | collective-permute-start | bytes 49160 | tf_op jit(solution)/shard_map/ppermute | solution.py:24
  78.0 5.1 %collective-permute-start.13 = (f32[2,1,16,128]{3,2,1,0:T(8,128)S(1)}, f32[2,1,16,128]{3,2,1,0:T(8,128)S(1)}, u32[]{:S(2)}, u32[]{:S(2)}) collective-permute-start(f32[2,1,16,128]{3,2,1,0:T(8,128)S(1)} %get-tuple-element.58), channel_id=1, source_target_pairs={{0,4},{4,0},{8,12},{12,8},{16,20},{20,16},{24,28},{28,24},{1,5},{5... | collective-permute-start | bytes 49160 | tf_op jit(solution)/shard_map/ppermute | solution.py:23
  83.4 2.7 %collective-permute-start.14 = (f32[2,16,1,128]{3,2,1,0:T(1,128)S(1)}, f32[2,16,1,128]{3,2,1,0:T(1,128)S(1)}, u32[]{:S(2)}, u32[]{:S(2)}) collective-permute-start(f32[2,16,1,128]{3,2,1,0:T(1,128)S(1)} %get-tuple-element.53), channel_id=1, source_target_pairs={{1,2},{2,1},{5,6},{6,5},{9,10},{10,9},{13,14},{14,13},{17,18},{18,... | collective-permute-start | bytes 49160 | tf_op jit(solution)/shard_map/ppermute | solution.py:24
  84.1 2.8 %collective-permute-start.15 = (f32[2,16,1,128]{3,2,1,0:T(1,128)S(1)}, f32[2,16,1,128]{3,2,1,0:T(1,128)S(1)}, u32[]{:S(2)}, u32[]{:S(2)}) collective-permute-start(f32[2,16,1,128]{3,2,1,0:T(1,128)S(1)} %get-tuple-element.54), channel_id=1, source_target_pairs={{0,1},{1,0},{2,3},{3,2},{4,5},{5,4},{6,7},{7,6},{8,9},{9,8},{10,11... | collective-permute-start | bytes 49160 | tf_op jit(solution)/shard_map/ppermute | solution.py:23
  90.8 5.5 %collective-permute-start.16 = (f32[1,1,16,128]{3,2,1,0:T(8,128)S(1)}, f32[1,1,16,128]{3,2,1,0:T(8,128)S(1)}, u32[]{:S(2)}, u32[]{:S(2)}) collective-permute-start(f32[1,1,16,128]{3,2,1,0:T(8,128)S(1)} %get-tuple-element.85), channel_id=1, source_target_pairs={{4,8},{8,4},{12,16},{16,12},{20,24},{24,20},{5,9},{9,5},{13,17},{1... | collective-permute-start | bytes 24584 | tf_op jit(solution)/shard_map/ppermute | solution.py:24
  91.4 6.5 %collective-permute-start.17 = (f32[1,1,16,128]{3,2,1,0:T(8,128)S(1)}, f32[1,1,16,128]{3,2,1,0:T(8,128)S(1)}, u32[]{:S(2)}, u32[]{:S(2)}) collective-permute-start(f32[1,1,16,128]{3,2,1,0:T(8,128)S(1)} %get-tuple-element.86), channel_id=1, source_target_pairs={{0,4},{4,0},{8,12},{12,8},{16,20},{20,16},{24,28},{28,24},{1,5},{5... | collective-permute-start | bytes 24584 | tf_op jit(solution)/shard_map/ppermute | solution.py:23
  98.1 4.2 %collective-permute-start.18 = (f32[1,16,1,128]{3,2,1,0:T(1,128)S(1)}, f32[1,16,1,128]{3,2,1,0:T(1,128)S(1)}, u32[]{:S(2)}, u32[]{:S(2)}) collective-permute-start(f32[1,16,1,128]{3,2,1,0:T(1,128)S(1)} %get-tuple-element.81), channel_id=1, source_target_pairs={{1,2},{2,1},{5,6},{6,5},{9,10},{10,9},{13,14},{14,13},{17,18},{18,... | collective-permute-start | bytes 24584 | tf_op jit(solution)/shard_map/ppermute | solution.py:24
  98.8 4.4 %collective-permute-start.19 = (f32[1,16,1,128]{3,2,1,0:T(1,128)S(1)}, f32[1,16,1,128]{3,2,1,0:T(1,128)S(1)}, u32[]{:S(2)}, u32[]{:S(2)}) collective-permute-start(f32[1,16,1,128]{3,2,1,0:T(1,128)S(1)} %get-tuple-element.82), channel_id=1, source_target_pairs={{0,1},{1,0},{2,3},{3,2},{4,5},{5,4},{6,7},{7,6},{8,9},{9,8},{10,11... | collective-permute-start | bytes 24584 | tf_op jit(solution)/shard_map/ppermute | solution.py:23
  117.0 9.6 %all-to-all-start.1 = ((f32[32,1,1]{2,1,0:T(1,128)}), f32[32,1,1]{2,1,0:T(1,128)S(1)}, u32[]{:S(2)}, u32[]{:S(2)}) async-start(f32[32,1,1]{2,1,0:T(1,128)} %broadcast_in_dim.183), calls=%async_computation.1 | async-start | bytes 32768 | tf_op jit(solution)/shard_map/all_to_all | solution.py:222
  130.9 9.6 %all-to-all-start.3 = ((f32[32,1,4]{2,1,0:T(1,128)}), f32[32,1,4]{2,1,0:T(1,128)S(1)}, u32[]{:S(2)}, u32[]{:S(2)}) async-start(f32[32,1,4]{2,1,0:T(1,128)} %broadcast_in_dim.190), calls=%async_computation.3 | async-start | bytes 32768 | tf_op jit(solution)/shard_map/all_to_all | solution.py:222
  142.0 4.0 %collective-permute-start.20 = (f32[2,1,16,128]{3,2,1,0:T(8,128)S(1)}, f32[2,1,16,128]{3,2,1,0:T(8,128)S(1)}, u32[]{:S(2)}, u32[]{:S(2)}) collective-permute-start(f32[2,1,16,128]{3,2,1,0:T(8,128)S(1)} %get-tuple-element.49), channel_id=1, source_target_pairs={{4,8},{8,4},{12,16},{16,12},{20,24},{24,20},{5,9},{9,5},{13,17},{1... | collective-permute-start | bytes 49160 | tf_op jit(solution)/shard_map/ppermute | solution.py:24
  142.7 5.1 %collective-permute-start.21 = (f32[2,1,16,128]{3,2,1,0:T(8,128)S(1)}, f32[2,1,16,128]{3,2,1,0:T(8,128)S(1)}, u32[]{:S(2)}, u32[]{:S(2)}) collective-permute-start(f32[2,1,16,128]{3,2,1,0:T(8,128)S(1)} %get-tuple-element.50), channel_id=1, source_target_pairs={{0,4},{4,0},{8,12},{12,8},{16,20},{20,16},{24,28},{28,24},{1,5},{5... | collective-permute-start | bytes 49160 | tf_op jit(solution)/shard_map/ppermute | solution.py:23
  148.1 2.7 %collective-permute-start.22 = (f32[2,16,1,128]{3,2,1,0:T(1,128)S(1)}, f32[2,16,1,128]{3,2,1,0:T(1,128)S(1)}, u32[]{:S(2)}, u32[]{:S(2)}) collective-permute-start(f32[2,16,1,128]{3,2,1,0:T(1,128)S(1)} %get-tuple-element.45), channel_id=1, source_target_pairs={{1,2},{2,1},{5,6},{6,5},{9,10},{10,9},{13,14},{14,13},{17,18},{18,... | collective-permute-start | bytes 49160 | tf_op jit(solution)/shard_map/ppermute | solution.py:24
  148.8 2.8 %collective-permute-start.23 = (f32[2,16,1,128]{3,2,1,0:T(1,128)S(1)}, f32[2,16,1,128]{3,2,1,0:T(1,128)S(1)}, u32[]{:S(2)}, u32[]{:S(2)}) collective-permute-start(f32[2,16,1,128]{3,2,1,0:T(1,128)S(1)} %get-tuple-element.46), channel_id=1, source_target_pairs={{0,1},{1,0},{2,3},{3,2},{4,5},{5,4},{6,7},{7,6},{8,9},{9,8},{10,11... | collective-permute-start | bytes 49160 | tf_op jit(solution)/shard_map/ppermute | solution.py:23
  169.7 4.0 %collective-permute-start.24 = (f32[1,1,16,128]{3,2,1,0:T(8,128)S(1)}, f32[1,1,16,128]{3,2,1,0:T(8,128)S(1)}, u32[]{:S(2)}, u32[]{:S(2)}) collective-permute-start(f32[1,1,16,128]{3,2,1,0:T(8,128)S(1)} %get-tuple-element.77), channel_id=1, source_target_pairs={{4,8},{8,4},{12,16},{16,12},{20,24},{24,20},{5,9},{9,5},{13,17},{1... | collective-permute-start | bytes 24584 | tf_op jit(solution)/shard_map/ppermute | solution.py:24
  170.4 5.0 %collective-permute-start.25 = (f32[1,1,16,128]{3,2,1,0:T(8,128)S(1)}, f32[1,1,16,128]{3,2,1,0:T(8,128)S(1)}, u32[]{:S(2)}, u32[]{:S(2)}) collective-permute-start(f32[1,1,16,128]{3,2,1,0:T(8,128)S(1)} %get-tuple-element.78), channel_id=1, source_target_pairs={{0,4},{4,0},{8,12},{12,8},{16,20},{20,16},{24,28},{28,24},{1,5},{5... | collective-permute-start | bytes 24584 | tf_op jit(solution)/shard_map/ppermute | solution.py:23
  175.6 2.6 %collective-permute-start.26 = (f32[1,16,1,128]{3,2,1,0:T(1,128)S(1)}, f32[1,16,1,128]{3,2,1,0:T(1,128)S(1)}, u32[]{:S(2)}, u32[]{:S(2)}) collective-permute-start(f32[1,16,1,128]{3,2,1,0:T(1,128)S(1)} %get-tuple-element.73), channel_id=1, source_target_pairs={{1,2},{2,1},{5,6},{6,5},{9,10},{10,9},{13,14},{14,13},{17,18},{18,... | collective-permute-start | bytes 24584 | tf_op jit(solution)/shard_map/ppermute | solution.py:24
  176.2 2.8 %collective-permute-start.27 = (f32[1,16,1,128]{3,2,1,0:T(1,128)S(1)}, f32[1,16,1,128]{3,2,1,0:T(1,128)S(1)}, u32[]{:S(2)}, u32[]{:S(2)}) collective-permute-start(f32[1,16,1,128]{3,2,1,0:T(1,128)S(1)} %get-tuple-element.74), channel_id=1, source_target_pairs={{0,1},{1,0},{2,3},{3,2},{4,5},{5,4},{6,7},{7,6},{8,9},{9,8},{10,11... | collective-permute-start | bytes 24584 | tf_op jit(solution)/shard_map/ppermute | solution.py:23
  (21 other events, 17.3 us)

commit v2 on v0

v2 whole, which is shorter than its diff:
```python
import functools

import jax
import jax.numpy as jnp
import numpy as np
from jax import lax
from jax.experimental import pallas as pl
from jax.experimental.pallas import tpu as pltpu
from jax.sharding import PartitionSpec as P

NCD = 4
NODES = 8
LANES = 128
TILE = (8, 128)
BOTH = ("gx", "gy")

dt_step = 0.01
sigma_p = 4.0
prandtl = 0.7
cheb_ratio = 0.1


def tables():
    points = np.array(
        [
            -1.0,
            -0.8717401485096066,
            -0.5917001814331423,
            -0.2092992179024789,
            0.2092992179024789,
            0.5917001814331423,
            0.8717401485096066,
            1.0,
        ]
    )
    weights = np.array(
        [
            1.0 / 28.0,
            0.2107042271435061,
            0.3411226924835044,
            0.4124587946587038,
            0.4124587946587038,
            0.3411226924835044,
            0.2107042271435061,
            1.0 / 28.0,
        ]
    )
    identity = np.eye(8)
    differ = points[:, None] - points[None, :] + identity
    barycentric = 1.0 / np.prod(differ, axis=1)
    offdiag = barycentric[None, :] / barycentric[:, None] / differ * (1.0 - identity)
    derivative = offdiag - identity * np.sum(offdiag, axis=1)[:, None]
    mass_one = identity * weights[None, :]
    stiff_one = derivative.T @ mass_one @ derivative
    stiff_three = (
        np.kron(np.kron(stiff_one, mass_one), mass_one)
        + np.kron(np.kron(mass_one, stiff_one), mass_one)
        + np.kron(np.kron(mass_one, mass_one), stiff_one)
    )
    three_diag = np.sum(stiff_three * np.eye(512), axis=1)
    spectral_bound = float(np.max(np.sum(np.abs(stiff_three), axis=1) / three_diag))
    return (derivative, weights, stiff_one, spectral_bound)


DERIV, WEIGHTS, STIFF, BOUND = tables()
SCALED = STIFF / WEIGHTS[:, None]
LINE = np.diag(STIFF) / WEIGHTS
THETA = 0.5 * (BOUND + cheb_ratio * BOUND)
DELTA = 0.5 * (BOUND - cheb_ratio * BOUND)
RHO = DELTA / THETA
RHO_NEXT = 1.0 / (2.0 * THETA / DELTA - RHO)


def constant_tables(elems_z):
    def turned(matrix):
        rows = np.arange(8)
        return [np.repeat(matrix[rows, (rows - s) % 8][:, None], LANES, 1) for s in range(8)]

    wz = np.tile(WEIGHTS, elems_z)
    kz = np.tile(LINE, elems_z)
    tiles = turned(DERIV) + turned(DERIV.T) + turned(SCALED)
    tiles += [WEIGHTS[:, None] * wz[None, :], LINE[:, None] + kz[None, :]]
    eye = np.eye(elems_z)
    mats = [np.kron(eye, DERIV.T), np.kron(eye, DERIV), np.kron(eye, SCALED.T)]
    spread = np.kron(eye, np.ones((1, 8)))
    return (
        np.stack(tiles).astype(np.float32),
        np.stack(mats).astype(np.float32),
        spread.astype(np.float32),
    )


T_D, T_DT, T_K, T_W, T_LINE = 0, 8, 16, 24, 25


class Place:
    def __init__(self):
        self.ix = lax.axis_index("gx")
        self.iy = lax.axis_index("gy")
        self.nx = lax.axis_size("gx")
        self.ny = lax.axis_size("gy")
        self.even_x = self.ix % 2 == 0
        self.even_y = self.iy % 2 == 0
        self.row = lax.broadcasted_iota(jnp.int32, TILE, 0)
        self.lane = lax.broadcasted_iota(jnp.int32, TILE, 1)
        self.low_z = (self.lane % 8 == 0) & (self.lane > 0)
        self.high_z = (self.lane % 8 == 7) & (self.lane < LANES - 1)
        self.prev_x = self.ix > 0
        self.next_x = self.ix < self.nx - 1
        self.prev_y = self.iy > 0
        self.next_y = self.iy < self.ny - 1

    def mult_tile(self, ey):
        along_z = 1.0 + jnp.where(self.low_z | self.high_z, 1.0, 0.0)
        low = 1.0 if ey == 1 else jnp.where(self.prev_y, 1.0, 0.0)
        high = 1.0 if ey == 0 else jnp.where(self.next_y, 1.0, 0.0)
        along_y = 1.0 + jnp.where(self.row == 0, low, jnp.where(self.row == 7, high, 0.0))
        return along_y * along_z

    def inv_x(self, ex, a):
        if a == 0:
            return 0.5 if ex == 1 else jnp.where(self.prev_x, 0.5, 1.0)
        if a == 7:
            return 0.5 if ex == 0 else jnp.where(self.next_x, 0.5, 1.0)
        return 1.0

    def join_z(self, t):
        up = pltpu.roll(t, LANES - 1, 1)
        down = pltpu.roll(t, 1, 1)
        return t + jnp.where(self.high_z, up, jnp.where(self.low_z, down, 0.0))

    def to_low(self, below):
        return jnp.where(self.row == 0, pltpu.roll(below, 1, 0), 0.0)

    def to_high(self, above):
        return jnp.where(self.row == 7, pltpu.roll(above, 7, 0), 0.0)

    def join_y(self, below, above):
        return below + self.to_high(above), above + self.to_low(below)

    def before_x(self, first, second):
        return jnp.where(self.even_x, second, first)

    def after_x(self, first, second):
        return jnp.where(self.even_x, first, second)

    def before_y(self, first, second):
        return jnp.where(self.even_y, second, first)

    def after_y(self, first, second):
        return jnp.where(self.even_y, first, second)


def along_x(matrix, tiles):
    out = []
    for i in range(8):
        acc = None
        for a in range(8):
            term = float(matrix[i, a]) * tiles[a]
            acc = term if acc is None else acc + term
        out.append(acc)
    return out


def along_y(ctab, base, tile):
    acc = ctab[base] * tile
    for s in range(1, 8):
        acc = acc + ctab[base + s] * pltpu.roll(tile, s, 0)
    return acc


def along_z(rows, matrix):
    return jnp.dot(
        rows, matrix, precision=lax.Precision.HIGHEST, preferred_element_type=jnp.float32
    )


def total(tile):
    return jnp.sum(jnp.sum(tile, axis=0, keepdims=True), axis=1, keepdims=True)


def store_y_faces(place, field, first_out, second_out, lead, at):
    for ex in range(2):
        for a in range(8):
            low = field[lead + (ex, a, 0, pl.ds(0, 1), slice(None))]
            high = field[lead + (ex, a, 1, pl.ds(7, 1), slice(None))]
            row = at + ex * 8 + a
            first_out[pl.ds(row, 1), :] = place.after_y(high, low)
            second_out[pl.ds(row, 1), :] = place.after_y(low, high)


def join_own(place, tiles):
    for ex in range(2):
        for a in range(8):
            tiles[ex][a] = list(place.join_y(*tiles[ex][a]))
    for ey in range(2):
        both = tiles[0][7][ey] + tiles[1][0][ey]
        tiles[0][7][ey] = both
        tiles[1][0][ey] = both


def mass_kernel(pack_rows, fields, kappa, group, coarse, ctab, spread, out, xf, pack, first, second):
    place = Place()
    spread_v = spread[...]
    pack[...] = jnp.zeros(pack.shape, jnp.float32)
    pack[pl.ds(0, 4), :] = along_z(kappa[...], spread_v)
    pack[pl.ds(4, 4), :] = along_z(group[...].astype(jnp.float32), spread_v)
    pack[pl.ds(8, coarse.shape[0]), :] = coarse[...]
    first[pl.ds(64, pack_rows), :] = pack[...]
    second[pl.ds(64, pack_rows), :] = pack[...]
    weight = ctab[T_W]

    def channel(ch, carry):
        tiles = [
            [
                [
                    place.join_z(fields[ch, ex, a, ey] * (float(WEIGHTS[a]) * weight))
                    for ey in range(2)
                ]
                for a in range(8)
            ]
            for ex in range(2)
        ]
        join_own(place, tiles)
        for ex in range(2):
            for a in range(8):
                for ey in range(2):
                    out[ch, ex, a, ey] = tiles[ex][a][ey]
        for ey in range(2):
            xf[0, ch, ey] = tiles[0][0][ey]
            xf[1, ch, ey] = tiles[1][7][ey]
        store_y_faces(place, out, first, second, (ch,), ch * 16)
        return carry

    lax.fori_loop(0, 4, channel, 0)


def turn_faces_kernel(pack_rows, xf, *refs):
    place = Place()
    if pack_rows:
        pack, y_first, y_second, first, second = refs
    else:
        y_first, y_second, first, second = refs
    for ch in range(4):
        sides = []
        for side in range(2):
            row = pl.ds(ch * 16 + 15 * side, 1)
            got_a, got_b = y_first[row, :], y_second[row, :]
            low = xf[side, ch, 0] + jnp.where(place.row == 0, place.before_y(got_a, got_b), 0.0)
            high = xf[side, ch, 1] + jnp.where(place.row == 7, place.after_y(got_a, got_b), 0.0)
            sides.append((low, high))
        for ey in range(2):
            rows = pl.ds(ch * 16 + ey * 8, 8)
            first[rows, :] = place.after_x(sides[1][ey], sides[0][ey])
            second[rows, :] = place.after_x(sides[0][ey], sides[1][ey])
    if pack_rows:
        came = pl.ds(64, pack_rows)
        parts = (
            place.before_y(y_first[came, :], y_second[came, :]),
            pack[...],
            place.after_y(y_first[came, :], y_second[came, :]),
        )
        for k in range(3):
            rows = pl.ds(64 + k * pack_rows, pack_rows)
            first[rows, :] = parts[k]
            second[rows, :] = parts[k]


def setup_kernel(
    pack_rows, blocks, pack, y_first, y_second, x_first, x_second, ctab, inv_diag, kap, grp, coarse
):
    place = Place()
    came = pl.ds(64, pack_rows)
    packs = [[None] * 3 for _ in range(3)]
    packs[1][0] = place.before_y(y_first[came, :], y_second[came, :])
    packs[1][1] = pack[...]
    packs[1][2] = place.after_y(y_first[came, :], y_second[came, :])
    for k in range(3):
        rows = pl.ds(64 + k * pack_rows, pack_rows)
        packs[0][k] = place.before_x(x_first[rows, :], x_second[rows, :])
        packs[2][k] = place.after_x(x_first[rows, :], x_second[rows, :])
    for dx in range(3):
        for dy in range(3):
            at = (dx * 3 + dy) * NCD * blocks
            coarse[pl.ds(at, NCD * blocks), :] = packs[dx][dy][8 : 8 + NCD * blocks]
    there_x = [jnp.where(place.prev_x, 1.0, 0.0), 1.0, jnp.where(place.next_x, 1.0, 0.0)]
    there_y = [jnp.where(place.prev_y, 1.0, 0.0), 1.0, jnp.where(place.next_y, 1.0, 0.0)]

    def element_row(base, u, v):
        row = base + (u % 2) * 2 + v % 2
        return packs[u // 2][v // 2][row : row + 1]

    for x in range(4):
        for y in range(4):
            kap[pl.ds(x * 4 + y, 1), :] = element_row(0, x + 1, y + 1)
            grp[pl.ds(x * 4 + y, 1), :] = element_row(4, x + 1, y + 1)
    kappa = [
        [
            place.join_z(jnp.broadcast_to(element_row(0, u, v), TILE)) if True else None
            for v in range(6)
        ]
        for u in range(6)
    ]
    count_z = 1.0 + jnp.where(place.low_z | place.high_z, 1.0, 0.0)
    weight = ctab[T_W]
    line = ctab[T_LINE]

    def pick(values, y):
        low = values[y] + values[y + 1]
        high = values[y + 1] + values[y + 2]
        return jnp.where(place.row == 0, low, jnp.where(place.row == 7, high, values[y + 1]))

    for x in range(4):
        for kind in range(3):
            us = {0: (x, x + 1), 1: (x + 1,), 2: (x + 1, x + 2)}[kind]
            sums, counts = [], []
            for v in range(6):
                acc, num = None, 0.0
                for u in us:
                    acc = kappa[u][v] if acc is None else acc + kappa[u][v]
                    num = num + there_x[u // 2]
                sums.append(acc)
                counts.append(num * there_y[v // 2])
            for y in range(4):
                kappa_sum = pick(sums, y)
                mult = pick(counts, y) * count_z
                present = there_x[(x + 1) // 2] * there_y[(y + 1) // 2] > 0.5
                for a in {0: (0,), 1: range(1, 7), 2: (7,)}[kind]:
                    diag = (float(LINE[a]) + line) * kappa_sum + sigma_p * mult
                    diag = diag * (float(WEIGHTS[a]) * weight)
                    inv_diag[x, a, y] = jnp.where(present, 1.0 / diag, 0.0)


def got_face_sum(place, tile, ch, ex, a, ey, y_first, y_second, x_first, x_second):
    row = pl.ds(ch * 16 + ex * 8 + a, 1)
    got_a, got_b = y_first[row, :], y_second[row, :]
    if ey == 0:
        tile = tile + jnp.where(place.row == 0, place.before_y(got_a, got_b), 0.0)
    else:
        tile = tile + jnp.where(place.row == 7, place.after_y(got_a, got_b), 0.0)
    rows = pl.ds(pl.multiple_of(ch * 16 + ey * 8, 8), 8)
    if ex == 0 and a == 0:
        tile = tile + place.before_x(x_first[rows, :], x_second[rows, :])
    if ex == 1 and a == 7:
        tile = tile + place.after_x(x_first[rows, :], x_second[rows, :])
    return tile


def rhs_kernel(
    summed,
    visc,
    y_first,
    y_second,
    x_first,
    x_second,
    ctab,
    zmat,
    start,
    rhs,
    xf,
    first,
    second,
    grad_z,
    flux_z,
):
    place = Place()
    weight = ctab[T_W]
    inv_mass = [1.0 / (weight * place.mult_tile(ey)) for ey in range(2)]

    def begin(ch, carry):
        for ex in range(2):
            for a in range(8):
                for ey in range(2):
                    tile = got_face_sum(
                        place, summed[ch, ex, a, ey], ch, ex, a, ey,
                        y_first, y_second, x_first, x_second,
                    )
                    scale = place.inv_x(ex, a) * float(1.0 / WEIGHTS[a])
                    start[ch, ex, a, ey] = tile * (inv_mass[ey] * scale)
        return carry

    lax.fori_loop(0, 4, begin, 0)
    grad_z[...] = along_z(start[...].reshape(1024, LANES), zmat[0]).reshape(grad_z.shape)

    def column(index, carry):
        ch, ex, ey = index // 4, index // 2 % 2, index % 2
        coef = jnp.where(ch == 3, 1.0 / prandtl, 1.0)
        field = [start[ch, ex, a, ey] for a in range(8)]
        grad_x = along_x(DERIV, field)
        flux_x, parts = [], []
        for a in range(8):
            grad_y = along_y(ctab, T_D, field[a])
            slope = grad_z[ch, ex, a, ey]
            node = float(WEIGHTS[a]) * weight
            advect = (
                start[0, ex, a, ey] * grad_x[a]
                + start[1, ex, a, ey] * grad_y
                + start[2, ex, a, ey] * slope
            )
            nu = visc[ex, a, ey] * node * coef
            flux_x.append(nu * grad_x[a])
            flux_z[ch, ex, a, ey] = nu * slope
            parts.append(node * advect + along_y(ctab, T_DT, nu * grad_y))
        back = along_x(DERIV.T, flux_x)
        for a in range(8):
            rhs[ch, ex, a, ey] = parts[a] + back[a]
        return carry

    lax.fori_loop(0, 16, column, 0)
    grad_z[...] = along_z(flux_z[...].reshape(1024, LANES), zmat[1]).reshape(grad_z.shape)

    def finish(ch, carry):
        tiles = [
            [
                [
                    place.join_z(-(rhs[ch, ex, a, ey] + grad_z[ch, ex, a, ey]))
                    for ey in range(2)
                ]
                for a in range(8)
            ]
            for ex in range(2)
        ]
        join_own(place, tiles)
        for ex in range(2):
            for a in range(8):
                for ey in range(2):
                    rhs[ch, ex, a, ey] = tiles[ex][a][ey]
        for ey in range(2):
            xf[0, ch, ey] = tiles[0][0][ey]
            xf[1, ch, ey] = tiles[1][7][ey]
        store_y_faces(place, rhs, first, second, (ch,), ch * 16)
        return carry

    lax.fori_loop(0, 4, finish, 0)


def store_own(place, tiles, out, first, second):
    join_own(place, tiles)
    for ex in range(2):
        for a in range(8):
            low, high = tiles[ex][a]
            out[ex, a, 0] = low
            out[ex, a, 1] = high
            first[ex, a] = place.after_y(high, low)
            second[ex, a] = place.after_y(low, high)


def advance_kernel(
    start,
    rhs,
    y_first,
    y_second,
    x_first,
    x_second,
    ctab,
    zmat,
    fields_new,
    out,
    first,
    second,
    grad_z,
):
    place = Place()
    weight = ctab[T_W]
    inv_mass = [dt_step / (weight * place.mult_tile(ey)) for ey in range(2)]

    def step(ch, carry):
        for ex in range(2):
            for a in range(8):
                for ey in range(2):
                    tile = got_face_sum(
                        place, rhs[ch, ex, a, ey], ch, ex, a, ey,
                        y_first, y_second, x_first, x_second,
                    )
                    scale = place.inv_x(ex, a) * float(1.0 / WEIGHTS[a])
                    fields_new[ch, ex, a, ey] = start[ch, ex, a, ey] + tile * (
                        inv_mass[ey] * scale
                    )
        return carry

    lax.fori_loop(0, 4, step, 0)
    grad_z[...] = along_z(fields_new[2].reshape(256, LANES), zmat[0]).reshape(grad_z.shape)
    tiles = [[[None, None] for _ in range(8)] for _ in range(2)]
    for ex in range(2):
        for ey in range(2):
            slope = along_x(DERIV, [fields_new[0, ex, a, ey] for a in range(8)])
            for a in range(8):
                div = slope[a] + along_y(ctab, T_D, fields_new[1, ex, a, ey]) + grad_z[ex, a, ey]
                tiles[ex][a][ey] = place.join_z(div * (float(-WEIGHTS[a]) * weight))
    store_own(place, tiles, out, first, second)


def turn_columns_kernel(own, y_first, y_second, first, second):
    place = Place()

    def line(a, carry):
        for y in range(4):
            sides = []
            for ex in range(2):
                if y in (1, 2):
                    sides.append(own[ex, a, y - 1])
                elif y == 0:
                    sides.append(place.before_y(y_first[ex, a], y_second[ex, a]))
                else:
                    sides.append(place.after_y(y_first[ex, a], y_second[ex, a]))
            first[a, y] = place.after_x(sides[1], sides[0])
            second[a, y] = place.after_x(sides[0], sides[1])
        return carry

    lax.fori_loop(0, 8, line, 0)


def restricted(place, sums, grp):
    values = []
    for c in range(NCD):
        acc = jnp.zeros(TILE, jnp.float32)
        for ex in range(2):
            for ey in range(2):
                group = grp[pl.ds((ex + 1) * 4 + ey + 1, 1), :]
                acc = acc + jnp.where(group == float(c), sums[ex][ey], 0.0)
        values.append(total(acc))
    return values


def message(place, own_values, scalars):
    lane = lax.broadcasted_iota(jnp.int32, (1, LANES), 1)
    spot = (place.ix * place.ny + place.iy) % (LANES // NCD)
    after = (spot + 1) % (LANES // NCD)
    row = jnp.zeros((1, LANES), jnp.float32)
    for c, value in enumerate(own_values):
        row = row + jnp.where(lane == spot * NCD + c, value, 0.0)
    for c, value in enumerate(scalars):
        row = row + jnp.where(lane == after * NCD + c, value, 0.0)
    return row


def smooth_kernel(
    own,
    y_first,
    y_second,
    x_first,
    x_second,
    inv_diag,
    kap,
    grp,
    extra,
    ctab,
    zmat,
    resid,
    smoothed,
    msg,
    ext,
    scaled,
    local,
    edge,
):
    place = Place()
    weight = ctab[T_W]

    def raw(x, a, y):
        if x in (1, 2):
            if y in (1, 2):
                return own[x - 1, a, y - 1]
            if y == 0:
                return place.before_y(y_first[x - 1, a], y_second[x - 1, a])
            return place.after_y(y_first[x - 1, a], y_second[x - 1, a])
        if x == 0:
            return place.before_x(x_first[a, y], x_second[a, y])
        return place.after_x(x_first[a, y], x_second[a, y])

    def put(x, a, tiles):
        low = place.join_y(tiles[0], tiles[1])
        high = place.join_y(tiles[2], tiles[3])
        for y, tile in enumerate(low + high):
            ext[x, a, y] = tile
            scaled[x, a, y] = tile * inv_diag[x, a, y] * float(1.0 / THETA)

    joined = {}
    for x, a, x2, a2 in ((0, 7, 1, 0), (2, 7, 3, 0)):
        both = [raw(x, a, y) + raw(x2, a2, y) for y in range(4)]
        put(x, a, both)
        put(x2, a2, both)
        joined[(x, a)] = joined[(x2, a2)] = True

    for x in range(4):
        first = 1 if (x, 0) in joined else 0
        last = 7 if (x, 7) in joined else 8

        def fill(a, carry, x=x):
            put(x, a, [raw(x, a, y) for y in range(4)])
            return carry

        lax.fori_loop(first, last, fill, 0)

    local[...] = along_z(scaled[pl.ds(1, 2)].reshape(512, LANES), zmat[2]).reshape(local.shape)
    edge[pl.ds(0, 4)] = along_z(scaled[0, 7].reshape(32, LANES), zmat[2]).reshape(4, 8, LANES)
    edge[pl.ds(4, 4)] = along_z(scaled[3, 0].reshape(32, LANES), zmat[2]).reshape(4, 8, LANES)

    def finish_tile(tile, a, slope, x, y):
        kappa = kap[pl.ds(x * 4 + y, 1), :]
        stiff = slope + along_y(ctab, T_K, tile)
        return (kappa * stiff + sigma_p * tile) * (float(WEIGHTS[a]) * weight)

    def column(y, carry):
        for x in (1, 2):
            tiles = [scaled[x, a, y] for a in range(8)]
            slopes = along_x(SCALED, tiles)
            for a in range(8):
                local[x - 1, a, y] = finish_tile(tiles[a], a, slopes[a] + local[x - 1, a, y], x, y)
        for x, a, at in ((0, 7, 0), (3, 0, 4)):
            slope = edge[at + y]
            for k in range(8):
                slope = slope + float(SCALED[a, k]) * scaled[x, k, y]
            edge[at + y] = finish_tile(scaled[x, a, y], a, slope, x, y)
        return carry

    lax.fori_loop(0, 4, column, 0)
    inv_mult = [1.0 / place.mult_tile(ey) for ey in range(2)]
    sums = [[jnp.zeros(TILE, jnp.float32) for _ in range(2)] for _ in range(2)]
    for x in (1, 2):
        for a in range(8):
            if (x, a) == (1, 0):
                tiles = [local[0, 0, y] + edge[y] for y in range(4)]
            elif (x, a) == (2, 7):
                tiles = [local[1, 7, y] + edge[4 + y] for y in range(4)]
            elif (x, a) in ((1, 7), (2, 0)):
                tiles = [local[0, 7, y] + local[1, 0, y] for y in range(4)]
            else:
                tiles = [local[x - 1, a, y] for y in range(4)]
            low = tiles[1] + place.to_low(tiles[0]) + place.to_high(tiles[2])
            high = tiles[2] + place.to_low(tiles[1]) + place.to_high(tiles[3])
            for ey, image in enumerate((low, high)):
                image = place.join_z(image)
                value = ext[x, a, ey + 1]
                update = scaled[x, a, ey + 1]
                defect = (value - image) * inv_diag[x, a, ey + 1]
                resid[x - 1, a, ey] = value
                smoothed[x - 1, a, ey] = (
                    float(1.0 + RHO_NEXT * RHO) * update + float(2.0 * RHO_NEXT / DELTA) * defect
                )
                scale = place.inv_x(x - 1, a)
                sums[x - 1][ey] = sums[x - 1][ey] + value * (inv_mult[ey] * scale)
    row = message(place, restricted(place, sums, grp), []) + extra[...]
    for i in range(msg.shape[0]):
        msg[i] = row


def coarse_part(place, blocks, got, coarse, grp):
    lane = lax.broadcasted_iota(jnp.int32, (1, LANES), 1)
    values = [jnp.zeros((1, LANES), jnp.float32) for _ in range(blocks)]
    per = LANES // NCD
    for i in range(got.shape[0]):
        values[i // per] = jnp.where(lane // NCD == i % per, got[i], values[i // per])

    def solved(dx, dy, c):
        acc = None
        for j in range(blocks):
            term = coarse[pl.ds(((dx * 3 + dy) * NCD + c) * blocks + j, 1), :] * values[j]
            acc = term if acc is None else acc + term
        return jnp.sum(acc, axis=1, keepdims=True)

    device = [[[solved(dx, dy, c) for c in range(NCD)] for dy in range(3)] for dx in range(3)]
    inv_z = jnp.where(place.low_z | place.high_z, 0.5, 1.0)
    rows = []
    for x in range(4):
        line = []
        for y in range(4):
            group = grp[pl.ds(x * 4 + y, 1), :]
            acc = jnp.zeros((1, LANES), jnp.float32)
            for c in range(NCD):
                acc = acc + jnp.where(
                    group == float(c), device[(x + 1) // 2][(y + 1) // 2][c], 0.0
                )
            line.append(place.join_z(jnp.broadcast_to(acc, TILE)) * inv_z)
        rows.append(line)
    low_y = jnp.where(place.prev_y, 0.5, 1.0)
    high_y = jnp.where(place.next_y, 0.5, 1.0)

    def tile(ex, kind, ey):
        if kind == 1:
            vals = [rows[ex + 1][y] for y in range(4)]
        elif kind == 0:
            scale = place.inv_x(ex, 0)
            vals = [(rows[ex][y] + rows[ex + 1][y]) * scale for y in range(4)]
        else:
            scale = place.inv_x(ex, 7)
            vals = [(rows[ex + 1][y] + rows[ex + 2][y]) * scale for y in range(4)]
        mid = vals[ey + 1]
        low = (vals[ey] + mid) * (low_y if ey == 0 else 0.5)
        high = (mid + vals[ey + 2]) * (high_y if ey == 1 else 0.5)
        return jnp.where(place.row == 0, low, jnp.where(place.row == 7, high, mid))

    return tile


def kind_of(a):
    return 0 if a == 0 else (2 if a == 7 else 1)


def own_operator(ctab, kap, field, slope_z, ex, ey):
    weight = ctab[T_W]
    tiles = [field[ex, a, ey] for a in range(8)]
    slopes = along_x(SCALED, tiles)
    kappa = kap[pl.ds((ex + 1) * 4 + ey + 1, 1), :]
    out = []
    for a in range(8):
        stiff = slopes[a] + along_y(ctab, T_K, tiles[a]) + slope_z[ex, a, ey]
        out.append((kappa * stiff + sigma_p * tiles[a]) * (float(WEIGHTS[a]) * weight))
    return tiles, out


def first_direction_kernel(
    blocks, got, coarse, grp, kap, resid, smoothed, ctab, zmat, direction, out, first, second, extra, slope_z
):
    place = Place()
    inv_mult = [1.0 / place.mult_tile(ey) for ey in range(2)]
    part = coarse_part(place, blocks, got, coarse, grp)
    energy = jnp.zeros(TILE, jnp.float32)
    for ex in range(2):
        for ey in range(2):
            kinds = [part(ex, kind, ey) for kind in range(3)]
            for a in range(8):
                value = smoothed[ex, a, ey] + kinds[kind_of(a)]
                direction[ex, a, ey] = value
                scale = place.inv_x(ex, a)
                energy = energy + value * resid[ex, a, ey] * (inv_mult[ey] * scale)
    slope_z[...] = along_z(direction[...].reshape(256, LANES), zmat[2]).reshape(slope_z.shape)
    curvature = jnp.zeros(TILE, jnp.float32)
    tiles = [[[None, None] for _ in range(8)] for _ in range(2)]
    for ex in range(2):
        for ey in range(2):
            values, images = own_operator(ctab, kap, direction, slope_z, ex, ey)
            for a in range(8):
                curvature = curvature + values[a] * images[a]
                tiles[ex][a][ey] = place.join_z(images[a])
    store_own(place, tiles, out, first, second)
    extra[...] = message(place, [], [total(energy), total(curvature)])


def gathered_scalars(got, count):
    lane = lax.broadcasted_iota(jnp.int32, (1, LANES), 1)
    per = LANES // NCD
    sums = []
    for c in range(count):
        acc = jnp.zeros((1, LANES), jnp.float32)
        for i in range(got.shape[0]):
            acc = acc + jnp.where(lane == ((i + 1) % per) * NCD + c, got[i], 0.0)
        sums.append(jnp.sum(acc, axis=1, keepdims=True))
    return sums


def second_direction_kernel(
    blocks,
    got,
    coarse,
    grp,
    kap,
    resid,
    direction,
    image,
    smoothed,
    ctab,
    zmat,
    following,
    known,
    msg,
    slope_z,
):
    place = Place()
    inv_mult = [1.0 / place.mult_tile(ey) for ey in range(2)]
    part = coarse_part(place, blocks, got, coarse, grp)
    energy, curvature = gathered_scalars(got, 2)
    step = energy / curvature
    lane = lax.broadcasted_iota(jnp.int32, (1, LANES), 1)
    known[...] = jnp.where(lane == 0, energy, jnp.where(lane == 1, curvature, 0.0))
    energy_next = jnp.zeros(TILE, jnp.float32)
    cross = jnp.zeros(TILE, jnp.float32)
    for ex in range(2):
        for ey in range(2):
            kinds = [part(ex, kind, ey) for kind in range(3)]
            for a in range(8):
                value = direction[ex, a, ey] - step * (smoothed[ex, a, ey] + kinds[kind_of(a)])
                following[ex, a, ey] = value
                weighed = value * (inv_mult[ey] * place.inv_x(ex, a))
                was = image[ex, a, ey]
                energy_next = energy_next + weighed * (resid[ex, a, ey] - step * was)
                cross = cross + weighed * was
    slope_z[...] = along_z(following[...].reshape(256, LANES), zmat[2]).reshape(slope_z.shape)
    square = jnp.zeros(TILE, jnp.float32)
    for ex in range(2):
        for ey in range(2):
            values, images = own_operator(ctab, kap, following, slope_z, ex, ey)
            for a in range(8):
                square = square + values[a] * images[a]
    row = message(place, [], [total(energy_next), total(square), total(cross)])
    for i in range(msg.shape[0]):
        msg[i] = row


def pressure_kernel(got, known, direction, following, pressure):
    energy = known[:, pl.ds(0, 1)]
    curvature = known[:, pl.ds(1, 1)]
    energy_next, square, cross = gathered_scalars(got, 3)
    ratio = energy_next / energy
    step = energy / curvature
    step_next = energy_next / (square + 2.0 * ratio * cross + ratio * ratio * curvature)
    weight_old = step + step_next * ratio
    for ex in range(2):
        for a in range(8):
            for ey in range(2):
                pressure[ex, a, ey] = (
                    weight_old * direction[ex, a, ey] + step_next * following[ex, a, ey]
                )


def call(body, outs, scratch=()):
    return pl.pallas_call(
        body,
        out_shape=[jax.ShapeDtypeStruct(shape, jnp.float32) for shape in outs],
        scratch_shapes=[pltpu.VMEM(shape, jnp.float32) for shape in scratch],
        compiler_params=pltpu.CompilerParams(vmem_limit_bytes=24 * 1024 * 1024),
    )


def swap(first, second, axis):
    count = lax.axis_size(axis)
    first_pairs = [(i, i ^ 1) for i in range(count) if i ^ 1 < count]
    second_pairs = [(i, ((i + 1) ^ 1) - 1) for i in range(1, count) if ((i + 1) ^ 1) - 1 < count]
    return (
        lax.ppermute(first, axis, first_pairs),
        lax.ppermute(second, axis, second_pairs),
    )


def per_device(fields, viscosity, inv_density, elem_group, coarse_inverse):
    length = fields.shape[5]
    elems_z = length // NODES
    devices = lax.axis_size("gx") * lax.axis_size("gy")
    blocks = coarse_inverse.shape[1] // LANES
    pack_rows = -(-(8 + NCD * blocks) // 8) * 8
    tiles_np, mats_np, spread_np = constant_tables(elems_z)
    ctab, zmat, spread = jnp.asarray(tiles_np), jnp.asarray(mats_np), jnp.asarray(spread_np)
    one = fields.shape[1:]
    four = fields.shape
    xf_shape = (2, 4, 2, 8, LANES)
    faces = (64, LANES)
    ext = (4, 8, 4, 8, LANES)
    column = (2, 8, 8, LANES)
    wide = (8, 4, 8, LANES)
    rows = (devices, 1, LANES)

    def exchange_all(msg):
        return lax.all_to_all(msg, BOTH, 0, 0, tiled=True)

    summed, xf, pack, first, second = call(
        functools.partial(mass_kernel, pack_rows),
        [four, xf_shape, (pack_rows, LANES), (64 + pack_rows, LANES), (64 + pack_rows, LANES)],
    )(
        fields,
        inv_density.reshape(4, elems_z),
        elem_group.reshape(4, elems_z),
        coarse_inverse.reshape(NCD * blocks, LANES),
        ctab,
        spread,
    )
    y_got = swap(first, second, "gy")
    x_shape = (64 + 3 * pack_rows, LANES)
    first, second = call(functools.partial(turn_faces_kernel, pack_rows), [x_shape, x_shape])(
        xf, pack, *y_got
    )
    x_got = swap(first, second, "gx")
    inv_diag, kap, grp, coarse = call(
        functools.partial(setup_kernel, pack_rows, blocks),
        [ext, (16, LANES), (16, LANES), (9 * NCD * blocks, LANES)],
    )(pack, *y_got, *x_got, ctab)
    start, rhs, xf, first, second = call(
        rhs_kernel, [four, four, xf_shape, faces, faces], [four, four]
    )(summed, viscosity, *y_got, *x_got, ctab, zmat)
    y_got = swap(first, second, "gy")
    first, second = call(functools.partial(turn_faces_kernel, 0), [faces, faces])(xf, *y_got)
    x_got = swap(first, second, "gx")
    fields_new, own, first, second = call(
        advance_kernel, [four, one, column, column], [one]
    )(start, rhs, *y_got, *x_got, ctab, zmat)

    def smooth(own, first, second, extra):
        y_got = swap(first, second, "gy")
        first, second = call(turn_columns_kernel, [wide, wide])(own, *y_got)
        x_got = swap(first, second, "gx")
        return call(
            smooth_kernel, [one, one, rows], [ext, ext, (2,) + ext[1:], (8, 8, LANES)]
        )(own, *y_got, *x_got, inv_diag, kap, grp, extra, ctab, zmat)

    resid, smoothed, msg = smooth(own, first, second, jnp.zeros((1, LANES), jnp.float32))
    got = exchange_all(msg)
    direction, own, first, second, extra = call(
        functools.partial(first_direction_kernel, blocks),
        [one, one, column, column, (1, LANES)],
        [one],
    )(got, coarse, grp, kap, resid, smoothed, ctab, zmat)
    image, image_smoothed, msg = smooth(own, first, second, extra)
    got = exchange_all(msg)
    following, known, msg = call(
        functools.partial(second_direction_kernel, blocks), [one, (1, LANES), rows], [one]
    )(got, coarse, grp, kap, resid, direction, image, image_smoothed, ctab, zmat)
    got = exchange_all(msg)
    (pressure,) = call(pressure_kernel, [one])(got, known, direction, following)
    return (fields_new, pressure)


def solution(mesh):
    placed = (
        P(None, "gx", None, "gy", None, None),
        P("gx", None, "gy", None, None),
        P("gx", "gy", None),
        P("gx", "gy", None),
        P(("gx", "gy"), None),
    )
    return jax.shard_map(
        per_device,
        mesh=mesh,
        in_specs=placed,
        out_specs=(P(None, "gx", None, "gy", None, None), P("gx", None, "gy", None, None)),
        check_vma=False,
    )
```

time: 366 us -> 103 us (0.28)
  blocking collectives: 207 us -> 48.2 us
  waiting for transfers between devices: 48.8 us -> 9.76 us
  starting transfers between devices: 62.8 us -> 27 us
  matrix products: 18.2 us -> 0 us
  Pallas kernels: 0 us -> 11.9 us
  local copies, waits for them, and re-layouts: 13.9 us -> 4.69 us
  other arithmetic: 7.2 us -> 0 us
  between operations: 6.35 us -> 0.82 us
    psum x3 -> x0, blocking collectives: 124 us -> none  [total(): return lax.psum(value, ('gx', 'gy'))]
    unnamed x2 -> x0, blocking collectives: 82.6 us -> none
    all_to_all x0 -> x3, blocking collectives: none -> 48.2 us  [exchange_all(): return lax.all_to_all(msg, BOTH, 0, 0, tiled=True)]
    ppermute x28 -> x16, waiting for transfers between devices: 48.8 us -> 9.76 us  [the longest x8 9.74 us: swap(): lax.ppermute(first, axis, first_pairs)]
    ppermute x28 -> x16, starting transfers between devices: 62.8 us -> 27 us  [the longest x8 21.8 us: swap(): lax.ppermute(first, axis, first_pairs)]
    dot_general x51 -> x0, matrix products: 18.2 us -> none  [the longest x7 4.25 us: assemble(): return jnp.matmul(field, pair_table, precision=precision)]
    pallas_call x0 -> x13, Pallas kernels: none -> 11.9 us  [the longest x1 4.48 us: per_device(): call(rhs_kernel, [four, four, xf_shape, faces, faces], [four, four])]
    unnamed x45 -> x18, local copies, waits for them, and re-layouts: 9.75 us -> 4.69 us
  transfers between devices with their start and end apart: 28 -> 16, of which waited for: 18 -> 8; matrix products, arithmetic and copies ran while one was open for 0% -> 0% of each run, Pallas kernels for 0% -> 0%
where the time goes in v2:
time: 103 us; the launch traced here: 102 us
  blocking collectives  48.2 us (47%)
  starting transfers between devices  27 us (26%)
  Pallas kernels  11.9 us (12%)
  waiting for transfers between devices  9.76 us (9%)
  local copies, waits for them, and re-layouts  4.69 us (5%)
    all_to_all x3, blocking collectives, exchange_all(): return lax.all_to_all(msg, BOTH, 0, 0, tiled=True)  48.2 us
    ppermute x8, starting transfers between devices, swap(): lax.ppermute(first, axis, first_pairs)  21.8 us
    ppermute x8, waiting for transfers between devices, swap(): lax.ppermute(first, axis, first_pairs)  9.74 us
    ppermute x8, starting transfers between devices, swap(): lax.ppermute(second, axis, second_pairs)  5.24 us
    unnamed x18, local copies, waits for them, and re-layouts  4.69 us
    pallas_call x1, Pallas kernels, per_device(): call(rhs_kernel, [four, four, xf_shape, faces, faces], [four, four])  4.48 us
    pallas_call x2, Pallas kernels, smooth(): call(smooth_kernel, [one, one, rows], [ext, ext, (2,) + ext[1:], (8, 8, L...  2.74 us
  transfers between devices with their start and end apart: 16, of which 8 were waited for; matrix products, arithmetic and copies ran while one was open for 0% of the time, Pallas kernels for 0%

profile of v2, /device:TPU:0, one launch (start us, length us, event | category | flops | bytes accessed | tf_op | source)
XLA Modules:
  0.0 102.4 jit_solution(4095543362373384837)
XLA Ops:
  0.6 0.7 copy-done.5
  1.3 0.9 copy-done.1
  2.2 1.0 %copy-done.3 = f32[4,2,8,2,8,128]{5,4,3,2,1,0:T(8,128)S(1)} copy-done((f32[4,2,8,2,8,128]{5,4,3,2,1,0:T(8,128)S(1)}, f32[4,2,8,2,8,128]{5,4,3,2,1,0:T(8,128)}, u32[]{:S(2)}) %copy-start.3) | copy-done | bytes 524312
  3.3 0.7 copy-done.6
  4.0 0.7 copy-done.7
  4.6 0.7 copy-done.8
  5.3 0.8 shard_map.95
  6.7 0.7 collective-permute-start.1
  7.6 2.9 %collective-permute-start.2 = (f32[112,128]{1,0:T(8,128)S(1)}, f32[112,128]{1,0:T(8,128)S(1)}, u32[]{:S(2)}, u32[]{:S(2)}) collective-permute-start(f32[112,128]{1,0:T(8,128)S(1)} %get-tuple-element.47), channel_id=1, source_target_pairs={{0,4},{4,0},{8,12},{12,8},{16,20},{20,16},{24,28},{28,24},{1,5},{5... | collective-permute-start | bytes 172040 | tf_op jit(solution)/shard_map/ppermute | solution.py:830
  10.5 0.7 collective-permute-start.3
  11.1 1.5 %collective-permute-done.2.x_first = f32[112,128]{1,0:T(8,128)S(1)} collective-permute-done((f32[112,128]{1,0:T(8,128)S(1)}, f32[112,128]{1,0:T(8,128)S(1)}, u32[]{:S(2)}, u32[]{:S(2)}) %collective-permute-start.2) | collective-permute-done | bytes 57376 | tf_op jit(solution)/shard_map/ppermute | solution.py:830
  12.6 4.5 %shard_map.97 = (f32[4,2,8,2,8,128]{5,4,3,2,1,0:T(8,128)S(1)}, f32[4,2,8,2,8,128]{5,4,3,2,1,0:T(8,128)S(1)}, f32[2,4,2,8,128]{4,3,2,1,0:T(8,128)S(1)}, f32[64,128]{1,0:T(8,128)S(1)}, f32[64,128]{1,0:T(8,128)S(1)}) custom-call(f32[4,2,8,2,8,128]{5,4,3,2,1,0:T(8,128)S(1)} %get-tuple-element.42.summed, f32[2,8,2,8,128]{4,3,2,1,0:T(8,128)S(1)} %copy-done.4, ...), custom_call_target="tpu_custom_call" | custom-call | tf_op jit(solution)/shard_map/pallas_call | solution.py:876
  17.1 3.8 %collective-permute-start.4 = (f32[64,128]{1,0:T(8,128)S(1)}, f32[64,128]{1,0:T(8,128)S(1)}, u32[]{:S(2)}, u32[]{:S(2)}) collective-permute-start(f32[64,128]{1,0:T(8,128)S(1)} %get-tuple-element.51), channel_id=1, source_target_pairs={{0,1},{1,0},{2,3},{3,2},{4,5},{5,4},{6,7},{7,6},{8,9},{9,8},{10,11... | collective-permute-start | bytes 98312 | tf_op jit(solution)/shard_map/ppermute | solution.py:830
  20.9 0.7 collective-permute-start.5
  21.8 4.7 %collective-permute-start.6 = (f32[64,128]{1,0:T(8,128)S(1)}, f32[64,128]{1,0:T(8,128)S(1)}, u32[]{:S(2)}, u32[]{:S(2)}) collective-permute-start(f32[64,128]{1,0:T(8,128)S(1)} %get-tuple-element.54), channel_id=1, source_target_pairs={{0,4},{4,0},{8,12},{12,8},{16,20},{20,16},{24,28},{28,24},{1,5},{5... | collective-permute-start | bytes 98312 | tf_op jit(solution)/shard_map/ppermute | solution.py:830
  26.5 0.7 collective-permute-start.7
  27.2 1.2 %collective-permute-done.6.x_first = f32[64,128]{1,0:T(8,128)S(1)} collective-permute-done((f32[64,128]{1,0:T(8,128)S(1)}, f32[64,128]{1,0:T(8,128)S(1)}, u32[]{:S(2)}, u32[]{:S(2)}) %collective-permute-start.6) | collective-permute-done | bytes 32800 | tf_op jit(solution)/shard_map/ppermute | solution.py:830
  28.4 1.3 %shard_map.99 = (f32[4,2,8,2,8,128]{5,4,3,2,1,0:T(8,128)}, f32[2,8,2,8,128]{4,3,2,1,0:T(8,128)S(1)}, f32[2,8,8,128]{3,2,1,0:T(8,128)S(1)}, f32[2,8,8,128]{3,2,1,0:T(8,128)S(1)}) custom-call(f32[4,2,8,2,8,128]{5,4,3,2,1,0:T(8,128)S(1)} %get-tuple-element.49.start, f32[4,2,8,2,8,128]{5,4,3,2,1,0:T(8,128)S(1)} %get-tuple-element.50.rhs, ...), custom_call_target="tpu_custom_call" | custom-call | tf_op jit(solution)/shard_map/pallas_call | solution.py:882
  29.7 4.5 %collective-permute-start.8 = (f32[2,8,8,128]{3,2,1,0:T(8,128)S(1)}, f32[2,8,8,128]{3,2,1,0:T(8,128)S(1)}, u32[]{:S(2)}, u32[]{:S(2)}) collective-permute-start(f32[2,8,8,128]{3,2,1,0:T(8,128)S(1)} %get-tuple-element.58), channel_id=1, source_target_pairs={{0,1},{1,0},{2,3},{3,2},{4,5},{5,4},{6,7},{7,6},{8,9},{9,8},{10,11... | collective-permute-start | bytes 196616 | tf_op jit(solution)/shard_map/ppermute | solution.py:830
  34.2 0.7 collective-permute-start.9
  35.2 4.7 %collective-permute-start.10 = (f32[8,4,8,128]{3,2,1,0:T(8,128)S(1)}, f32[8,4,8,128]{3,2,1,0:T(8,128)S(1)}, u32[]{:S(2)}, u32[]{:S(2)}) collective-permute-start(f32[8,4,8,128]{3,2,1,0:T(8,128)S(1)} %get-tuple-element.60), channel_id=1, source_target_pairs={{0,4},{4,0},{8,12},{12,8},{16,20},{20,16},{24,28},{28,24},{1,5},{5... | collective-permute-start | bytes 393224 | tf_op jit(solution)/shard_map/ppermute | solution.py:830
  39.9 0.7 collective-permute-start.11
  40.8 2.0 %collective-permute-done.10.x_first = f32[8,4,8,128]{3,2,1,0:T(8,128)S(1)} collective-permute-done((f32[8,4,8,128]{3,2,1,0:T(8,128)S(1)}, f32[8,4,8,128]{3,2,1,0:T(8,128)S(1)}, u32[]{:S(2)}, u32[]{:S(2)}) %collective-permute-start.10) | collective-permute-done | bytes 131104 | tf_op jit(solution)/shard_map/ppermute | solution.py:830
  42.8 1.4 %shard_map.102 = (f32[2,8,2,8,128]{4,3,2,1,0:T(8,128)S(1)}, f32[2,8,2,8,128]{4,3,2,1,0:T(8,128)S(1)}, f32[32,1,128]{2,1,0:T(1,128)S(1)}) custom-call(f32[2,8,2,8,128]{4,3,2,1,0:T(8,128)S(1)} %get-tuple-element.57.own, f32[2,8,8,128]{3,2,1,0:T(8,128)S(1)} %collective-permute-done.8.y_first, f32[2,8,8,128]{3,2,1,0:T(8,128)S(1)} %collective-permute-done.9.y_second, ...), custom_call_target="tpu_custom_call" | custom-call | tf_op jit(solution)/shard_map/pallas_call | solution.py:890
  44.2 22.9 %all_to_all.15.got = f32[32,1,128]{2,1,0:T(1,128)S(1)} all-to-all(f32[32,1,128]{2,1,0:T(1,128)S(1)} %get-tuple-element.65), channel_id=1, replica_groups=mesh['gx'=8,'gy'=4] {'gx','gy'}, dimensions={0} | all-to-all | bytes 32768 | tf_op jit(solution)/shard_map/all_to_all | solution.py:853
  67.8 0.7 collective-permute-start.13
  69.8 0.7 collective-permute-start.15
  70.4 3.7 %collective-permute-done.14.x_first = f32[8,4,8,128]{3,2,1,0:T(8,128)S(1)} collective-permute-done((f32[8,4,8,128]{3,2,1,0:T(8,128)S(1)}, f32[8,4,8,128]{3,2,1,0:T(8,128)S(1)}, u32[]{:S(2)}, u32[]{:S(2)}) %collective-permute-start.14) | collective-permute-done | bytes 131104 | tf_op jit(solution)/shard_map/ppermute | solution.py:830
  74.2 1.4 %shard_map.105 = (f32[2,8,2,8,128]{4,3,2,1,0:T(8,128)S(1)}, f32[2,8,2,8,128]{4,3,2,1,0:T(8,128)S(1)}, f32[32,1,128]{2,1,0:T(1,128)S(1)}) custom-call(f32[2,8,2,8,128]{4,3,2,1,0:T(8,128)S(1)} %get-tuple-element.69.own, f32[2,8,8,128]{3,2,1,0:T(8,128)S(1)} %collective-permute-done.12.y_first, f32[2,8,8,128]{3,2,1,0:T(8,128)S(1)} %collective-permute-done.13.y_second, ...), custom_call_target="tpu_custom_call" | custom-call | tf_op jit(solution)/shard_map/pallas_call | solution.py:890
  75.6 16.5 %all_to_all.16.got = f32[32,1,128]{2,1,0:T(1,128)S(1)} all-to-all(f32[32,1,128]{2,1,0:T(1,128)S(1)} %get-tuple-element.75), channel_id=1, replica_groups=mesh['gx'=8,'gy'=4] {'gx','gy'}, dimensions={0} | all-to-all | bytes 32768 | tf_op jit(solution)/shard_map/all_to_all | solution.py:853
  92.7 8.8 %all_to_all.17.got = f32[32,1,128]{2,1,0:T(1,128)S(1)} all-to-all(f32[32,1,128]{2,1,0:T(1,128)S(1)} %get-tuple-element.79), channel_id=1, replica_groups=mesh['gx'=8,'gy'=4] {'gx','gy'}, dimensions={0} | all-to-all | bytes 32768 | tf_op jit(solution)/shard_map/all_to_all | solution.py:853
  101.5 0.9 shard_map.107
  (35 shorter events, 4.1 us)
Async XLA Ops:
  0.6 0.7 copy-start.5
  1.3 0.9 copy-start.1
  2.2 1.0 %copy-start.3 = (f32[4,2,8,2,8,128]{5,4,3,2,1,0:T(8,128)S(1)}, f32[4,2,8,2,8,128]{5,4,3,2,1,0:T(8,128)}, u32[]{:S(2)}) copy-start(f32[4,2,8,2,8,128]{5,4,3,2,1,0:T(8,128)} %fields.1) | copy-start | bytes 1572868
  3.3 0.7 copy-start.6
  4.0 0.7 copy-start.7
  4.6 0.7 copy-start.8
  5.3 7.3 %copy-start = (f32[3,128,128]{2,1,0:T(8,128)S(1)}, f32[3,128,128]{2,1,0:T(8,128)}, u32[]{:S(2)}) copy-start(f32[3,128,128]{2,1,0:T(8,128)} %constant.9.clone.zmat) | copy-start | bytes 589828
  5.3 7.3 %copy-start.4 = (f32[2,8,2,8,128]{4,3,2,1,0:T(8,128)S(1)}, f32[2,8,2,8,128]{4,3,2,1,0:T(8,128)}, u32[]{:S(2)}) copy-start(f32[2,8,2,8,128]{4,3,2,1,0:T(8,128)} %visc.1) | copy-start | bytes 393220
  6.1 6.5 %copy-start.2 = (f32[26,8,128]{2,1,0:T(8,128)S(1)}, f32[26,8,128]{2,1,0:T(8,128)}, u32[]{:S(2)}) copy-start(f32[26,8,128]{2,1,0:T(8,128)} %constant.8.clone.ctab) | copy-start | bytes 319492
  6.1 1.4 %collective-permute-start = (f32[80,128]{1,0:T(8,128)S(1)}, f32[80,128]{1,0:T(8,128)S(1)}, u32[]{:S(2)}, u32[]{:S(2)}) collective-permute-start(f32[80,128]{1,0:T(8,128)S(1)} %get-tuple-element.43), channel_id=1, source_target_pairs={{0,1},{1,0},{2,3},{3,2},{4,5},{5,4},{6,7},{7,6},{8,9},{9,8},{10,11... | collective-permute-start | bytes 122888 | tf_op jit(solution)/shard_map/ppermute | solution.py:830
  6.7 0.9 collective-permute-start.1
  7.6 5.1 %collective-permute-start.2 = (f32[112,128]{1,0:T(8,128)S(1)}, f32[112,128]{1,0:T(8,128)S(1)}, u32[]{:S(2)}, u32[]{:S(2)}) collective-permute-start(f32[112,128]{1,0:T(8,128)S(1)} %get-tuple-element.47), channel_id=1, source_target_pairs={{0,4},{4,0},{8,12},{12,8},{16,20},{20,16},{24,28},{28,24},{1,5},{5... | collective-permute-start | bytes 172040 | tf_op jit(solution)/shard_map/ppermute | solution.py:830
  10.5 2.2 %collective-permute-start.3 = (f32[112,128]{1,0:T(8,128)S(1)}, f32[112,128]{1,0:T(8,128)S(1)}, u32[]{:S(2)}, u32[]{:S(2)}) collective-permute-start(f32[112,128]{1,0:T(8,128)S(1)} %get-tuple-element.48), channel_id=1, source_target_pairs={{4,8},{8,4},{12,16},{16,12},{20,24},{24,20},{5,9},{9,5},{13,17},{1... | collective-permute-start | bytes 172040 | tf_op jit(solution)/shard_map/ppermute | solution.py:831
  17.1 4.6 %collective-permute-start.4 = (f32[64,128]{1,0:T(8,128)S(1)}, f32[64,128]{1,0:T(8,128)S(1)}, u32[]{:S(2)}, u32[]{:S(2)}) collective-permute-start(f32[64,128]{1,0:T(8,128)S(1)} %get-tuple-element.51), channel_id=1, source_target_pairs={{0,1},{1,0},{2,3},{3,2},{4,5},{5,4},{6,7},{7,6},{8,9},{9,8},{10,11... | collective-permute-start | bytes 98312 | tf_op jit(solution)/shard_map/ppermute | solution.py:830
  20.9 0.9 collective-permute-start.5
  21.8 6.6 %collective-permute-start.6 = (f32[64,128]{1,0:T(8,128)S(1)}, f32[64,128]{1,0:T(8,128)S(1)}, u32[]{:S(2)}, u32[]{:S(2)}) collective-permute-start(f32[64,128]{1,0:T(8,128)S(1)} %get-tuple-element.54), channel_id=1, source_target_pairs={{0,4},{4,0},{8,12},{12,8},{16,20},{20,16},{24,28},{28,24},{1,5},{5... | collective-permute-start | bytes 98312 | tf_op jit(solution)/shard_map/ppermute | solution.py:830
  26.5 1.9 %collective-permute-start.7 = (f32[64,128]{1,0:T(8,128)S(1)}, f32[64,128]{1,0:T(8,128)S(1)}, u32[]{:S(2)}, u32[]{:S(2)}) collective-permute-start(f32[64,128]{1,0:T(8,128)S(1)} %get-tuple-element.55), channel_id=1, source_target_pairs={{4,8},{8,4},{12,16},{16,12},{20,24},{24,20},{5,9},{9,5},{13,17},{1... | collective-permute-start | bytes 98312 | tf_op jit(solution)/shard_map/ppermute | solution.py:831
  29.7 5.4 %collective-permute-start.8 = (f32[2,8,8,128]{3,2,1,0:T(8,128)S(1)}, f32[2,8,8,128]{3,2,1,0:T(8,128)S(1)}, u32[]{:S(2)}, u32[]{:S(2)}) collective-permute-start(f32[2,8,8,128]{3,2,1,0:T(8,128)S(1)} %get-tuple-element.58), channel_id=1, source_target_pairs={{0,1},{1,0},{2,3},{3,2},{4,5},{5,4},{6,7},{7,6},{8,9},{9,8},{10,11... | collective-permute-start | bytes 196616 | tf_op jit(solution)/shard_map/ppermute | solution.py:830
  34.2 0.9 collective-permute-start.9
  35.2 7.7 %collective-permute-start.10 = (f32[8,4,8,128]{3,2,1,0:T(8,128)S(1)}, f32[8,4,8,128]{3,2,1,0:T(8,128)S(1)}, u32[]{:S(2)}, u32[]{:S(2)}) collective-permute-start(f32[8,4,8,128]{3,2,1,0:T(8,128)S(1)} %get-tuple-element.60), channel_id=1, source_target_pairs={{0,4},{4,0},{8,12},{12,8},{16,20},{20,16},{24,28},{28,24},{1,5},{5... | collective-permute-start | bytes 393224 | tf_op jit(solution)/shard_map/ppermute | solution.py:830
  39.9 3.0 %collective-permute-start.11 = (f32[8,4,8,128]{3,2,1,0:T(8,128)S(1)}, f32[8,4,8,128]{3,2,1,0:T(8,128)S(1)}, u32[]{:S(2)}, u32[]{:S(2)}) collective-permute-start(f32[8,4,8,128]{3,2,1,0:T(8,128)S(1)} %get-tuple-element.61), channel_id=1, source_target_pairs={{4,8},{8,4},{12,16},{16,12},{20,24},{24,20},{5,9},{9,5},{13,17},{1... | collective-permute-start | bytes 393224 | tf_op jit(solution)/shard_map/ppermute | solution.py:831
  67.8 1.3 %collective-permute-start.12 = (f32[2,8,8,128]{3,2,1,0:T(8,128)S(1)}, f32[2,8,8,128]{3,2,1,0:T(8,128)S(1)}, u32[]{:S(2)}, u32[]{:S(2)}) collective-permute-start(f32[2,8,8,128]{3,2,1,0:T(8,128)S(1)} %get-tuple-element.70), channel_id=1, source_target_pairs={{0,1},{1,0},{2,3},{3,2},{4,5},{5,4},{6,7},{7,6},{8,9},{9,8},{10,11... | collective-permute-start | bytes 196616 | tf_op jit(solution)/shard_map/ppermute | solution.py:830
  67.8 1.2 %collective-permute-start.13 = (f32[2,8,8,128]{3,2,1,0:T(8,128)S(1)}, f32[2,8,8,128]{3,2,1,0:T(8,128)S(1)}, u32[]{:S(2)}, u32[]{:S(2)}) collective-permute-start(f32[2,8,8,128]{3,2,1,0:T(8,128)S(1)} %get-tuple-element.71), channel_id=1, source_target_pairs={{1,2},{2,1},{5,6},{6,5},{9,10},{10,9},{13,14},{14,13},{17,18},{18,... | collective-permute-start | bytes 196616 | tf_op jit(solution)/shard_map/ppermute | solution.py:831
  69.1 5.0 %collective-permute-start.14 = (f32[8,4,8,128]{3,2,1,0:T(8,128)S(1)}, f32[8,4,8,128]{3,2,1,0:T(8,128)S(1)}, u32[]{:S(2)}, u32[]{:S(2)}) collective-permute-start(f32[8,4,8,128]{3,2,1,0:T(8,128)S(1)} %get-tuple-element.72), channel_id=1, source_target_pairs={{0,4},{4,0},{8,12},{12,8},{16,20},{20,16},{24,28},{28,24},{1,5},{5... | collective-permute-start | bytes 393224 | tf_op jit(solution)/shard_map/ppermute | solution.py:830
  69.8 4.4 %collective-permute-start.15 = (f32[8,4,8,128]{3,2,1,0:T(8,128)S(1)}, f32[8,4,8,128]{3,2,1,0:T(8,128)S(1)}, u32[]{:S(2)}, u32[]{:S(2)}) collective-permute-start(f32[8,4,8,128]{3,2,1,0:T(8,128)S(1)} %get-tuple-element.73), channel_id=1, source_target_pairs={{4,8},{8,4},{12,16},{16,12},{20,24},{24,20},{5,9},{9,5},{13,17},{1... | collective-permute-start | bytes 393224 | tf_op jit(solution)/shard_map/ppermute | solution.py:831

commit v3 on v2

--- a/solution.py
+++ b/solution.py
@@ -80,17 +80,13 @@
     kz = np.tile(LINE, elems_z)
     tiles = turned(DERIV) + turned(DERIV.T) + turned(SCALED)
     tiles += [WEIGHTS[:, None] * wz[None, :], LINE[:, None] + kz[None, :]]
+    tiles += [np.repeat(DERIV[7][:, None], LANES, 1), np.repeat(DERIV[0][:, None], LANES, 1)]
     eye = np.eye(elems_z)
     mats = [np.kron(eye, DERIV.T), np.kron(eye, DERIV), np.kron(eye, SCALED.T)]
-    spread = np.kron(eye, np.ones((1, 8)))
-    return (
-        np.stack(tiles).astype(np.float32),
-        np.stack(mats).astype(np.float32),
-        spread.astype(np.float32),
-    )
-
-
-T_D, T_DT, T_K, T_W, T_LINE = 0, 8, 16, 24, 25
+    return np.stack(tiles).astype(np.float32), np.stack(mats).astype(np.float32)
+
+
+T_D, T_DT, T_K, T_W, T_LINE, T_TOP, T_BOTTOM = 0, 8, 16, 24, 25, 26, 27
 
 
 class Place:
@@ -124,6 +120,33 @@
             return 0.5 if ex == 0 else jnp.where(self.next_x, 0.5, 1.0)
         return 1.0
 
+    def mult_x(self, ex, a):
+        if a == 0:
+            return 2.0 if ex == 1 else jnp.where(self.prev_x, 2.0, 1.0)
+        if a == 7:
+            return 2.0 if ex == 0 else jnp.where(self.next_x, 2.0, 1.0)
+        return 1.0
+
+    def share_x(self, ex, a):
+        if (ex, a) == (0, 0):
+            return jnp.where(self.prev_x, 0.5, 1.0)
+        if (ex, a) == (1, 7):
+            return jnp.where(self.next_x, 0.5, 1.0)
+        return 1.0
+
+    def share_y(self, ey):
+        if ey == 0:
+            return jnp.where((self.row == 0) & self.prev_y, 0.5, 1.0)
+        return jnp.where((self.row == 7) & self.next_y, 0.5, 1.0)
+
+    def inv_y(self, ey):
+        low = 0.5 if ey == 1 else jnp.where(self.prev_y, 0.5, 1.0)
+        high = 0.5 if ey == 0 else jnp.where(self.next_y, 0.5, 1.0)
+        return jnp.where(self.row == 0, low, jnp.where(self.row == 7, high, 1.0))
+
+    def inv_z(self):
+        return jnp.where(self.low_z | self.high_z, 0.5, 1.0)
+
     def join_z(self, t):
         up = pltpu.roll(t, LANES - 1, 1)
         down = pltpu.roll(t, 1, 1)
@@ -199,18 +222,58 @@
         tiles[1][0][ey] = both
 
 
-def mass_kernel(pack_rows, fields, kappa, group, coarse, ctab, spread, out, xf, pack, first, second):
+def weight_of(node):
+    edge = jnp.minimum(node, 7 - node)
+    value = jnp.where(edge == 2, float(WEIGHTS[2]), float(WEIGHTS[3]))
+    return jnp.where(
+        edge == 0, float(WEIGHTS[0]), jnp.where(edge == 1, float(WEIGHTS[1]), value)
+    )
+
+
+def mass_kernel(
+    pack_rows,
+    fields_in,
+    kappa_in,
+    group_in,
+    coarse_in,
+    out,
+    xf,
+    pack,
+    first,
+    second,
+    fields,
+    kappa,
+    group,
+    coarse,
+    sems,
+):
+    copies = [pltpu.make_async_copy(fields_in.at[ch], fields.at[ch], sems.at[ch]) for ch in range(4)]
+    copies += [
+        pltpu.make_async_copy(kappa_in, kappa, sems.at[4]),
+        pltpu.make_async_copy(group_in, group, sems.at[5]),
+        pltpu.make_async_copy(coarse_in, coarse, sems.at[6]),
+    ]
+    for copy in copies:
+        copy.start()
     place = Place()
-    spread_v = spread[...]
+    for copy in copies[4:]:
+        copy.wait()
     pack[...] = jnp.zeros(pack.shape, jnp.float32)
-    pack[pl.ds(0, 4), :] = along_z(kappa[...], spread_v)
-    pack[pl.ds(4, 4), :] = along_z(group[...].astype(jnp.float32), spread_v)
-    pack[pl.ds(8, coarse.shape[0]), :] = coarse[...]
+    elems = kappa.shape[2]
+    spread_to = lax.broadcasted_iota(jnp.int32, (elems, LANES), 1) // NODES
+    spread = (spread_to == lax.broadcasted_iota(jnp.int32, (elems, LANES), 0)).astype(jnp.float32)
+    blocks = coarse.shape[1] // LANES
+    for ex in range(2):
+        pack[pl.ds(2 * ex, 2), :] = along_z(kappa[ex], spread)
+        pack[pl.ds(4 + 2 * ex, 2), :] = along_z(group[ex].astype(jnp.float32), spread)
+    for c in range(NCD):
+        for j in range(blocks):
+            pack[pl.ds(8 + c * blocks + j, 1), :] = coarse[pl.ds(c, 1), pl.ds(j * LANES, LANES)]
     first[pl.ds(64, pack_rows), :] = pack[...]
     second[pl.ds(64, pack_rows), :] = pack[...]
-    weight = ctab[T_W]
-
-    def channel(ch, carry):
+    weight = weight_of(place.row) * weight_of(place.lane % NODES)
+    for ch in range(4):
+        copies[ch].wait()
         tiles = [
             [
                 [
@@ -230,17 +293,10 @@
             xf[0, ch, ey] = tiles[0][0][ey]
             xf[1, ch, ey] = tiles[1][7][ey]
         store_y_faces(place, out, first, second, (ch,), ch * 16)
-        return carry
-
-    lax.fori_loop(0, 4, channel, 0)
-
-
-def turn_faces_kernel(pack_rows, xf, *refs):
+
+
+def turn_faces_kernel(pack_rows, xf, pack, y_first, y_second, first, second):
     place = Place()
-    if pack_rows:
-        pack, y_first, y_second, first, second = refs
-    else:
-        y_first, y_second, first, second = refs
     for ch in range(4):
         sides = []
         for side in range(2):
@@ -253,17 +309,16 @@
             rows = pl.ds(ch * 16 + ey * 8, 8)
             first[rows, :] = place.after_x(sides[1][ey], sides[0][ey])
             second[rows, :] = place.after_x(sides[0][ey], sides[1][ey])
-    if pack_rows:
-        came = pl.ds(64, pack_rows)
-        parts = (
-            place.before_y(y_first[came, :], y_second[came, :]),
-            pack[...],
-            place.after_y(y_first[came, :], y_second[came, :]),
-        )
-        for k in range(3):
-            rows = pl.ds(64 + k * pack_rows, pack_rows)
-            first[rows, :] = parts[k]
-            second[rows, :] = parts[k]
+    came = pl.ds(64, pack_rows)
+    parts = (
+        place.before_y(y_first[came, :], y_second[came, :]),
+        pack[...],
+        place.after_y(y_first[came, :], y_second[came, :]),
+    )
+    for k in range(3):
+        rows = pl.ds(64 + k * pack_rows, pack_rows)
+        first[rows, :] = parts[k]
+        second[rows, :] = parts[k]
 
 
 def setup_kernel(
@@ -296,7 +351,7 @@
             grp[pl.ds(x * 4 + y, 1), :] = element_row(4, x + 1, y + 1)
     kappa = [
         [
-            place.join_z(jnp.broadcast_to(element_row(0, u, v), TILE)) if True else None
+            place.join_z(jnp.broadcast_to(element_row(0, u, v), TILE))
             for v in range(6)
         ]
         for u in range(6)
@@ -355,11 +410,11 @@
     x_second,
     ctab,
     zmat,
+    share,
+    first,
+    second,
     start,
     rhs,
-    xf,
-    first,
-    second,
     grad_z,
     flux_z,
 ):
@@ -423,15 +478,21 @@
         join_own(place, tiles)
         for ex in range(2):
             for a in range(8):
+                scale = place.inv_x(ex, a) * float(dt_step / WEIGHTS[a])
                 for ey in range(2):
-                    rhs[ch, ex, a, ey] = tiles[ex][a][ey]
-        for ey in range(2):
-            xf[0, ch, ey] = tiles[0][0][ey]
-            xf[1, ch, ey] = tiles[1][7][ey]
-        store_y_faces(place, rhs, first, second, (ch,), ch * 16)
+                    part = start[ch, ex, a, ey] * (place.share_y(ey) * place.share_x(ex, a))
+                    share[ch, ex, a, ey] = part + tiles[ex][a][ey] * (inv_mass[ey] * scale)
         return carry
 
     lax.fori_loop(0, 4, finish, 0)
+    for ex in range(2):
+        for a in range(8):
+            low, high = share[1, ex, a, 0], share[1, ex, a, 1]
+            rows = pl.ds((ex * 8 + a) * 8, 8)
+            first[rows, :] = place.after_y(high, low)
+            second[rows, :] = place.after_y(low, high)
+    for k, ch in enumerate((0, 2, 3)):
+        store_y_faces(place, share, first, second, (ch,), 128 + k * 16)
 
 
 def store_own(place, tiles, out, first, second):
@@ -445,49 +506,200 @@
             second[ex, a] = place.after_y(low, high)
 
 
+FACE_ROW = {0: 128, 2: 144, 3: 160}
+SIDE_ROW = {1: 128, 2: 160, 3: 176}
+
+
+def with_y(place, share, y_first, y_second, ch, ex, a):
+    low, high = share[ch, ex, a, 0], share[ch, ex, a, 1]
+    if ch == 1:
+        rows = pl.ds((ex * 8 + a) * 8, 8)
+        got_a, got_b = y_first[rows, :], y_second[rows, :]
+        return (
+            low + place.to_low(place.before_y(got_a, got_b)),
+            high + place.to_high(place.after_y(got_a, got_b)),
+        )
+    row = pl.ds(FACE_ROW[ch] + ex * 8 + a, 1)
+    got_a, got_b = y_first[row, :], y_second[row, :]
+    return (
+        low + jnp.where(place.row == 0, place.before_y(got_a, got_b), 0.0),
+        high + jnp.where(place.row == 7, place.after_y(got_a, got_b), 0.0),
+    )
+
+
+def turn_step_kernel(share, y_first, y_second, first, second):
+    place = Place()
+
+    def put(row, next_side, prev_side):
+        rows = pl.ds(row, 8)
+        first[rows, :] = place.after_x(next_side, prev_side)
+        second[rows, :] = place.after_x(prev_side, next_side)
+
+    for a in range(8):
+        prev_side = with_y(place, share, y_first, y_second, 0, 0, a)
+        next_side = with_y(place, share, y_first, y_second, 0, 1, a)
+        for ey in range(2):
+            put(a * 16 + ey * 8, next_side[ey], prev_side[ey])
+    for ch in (1, 2, 3):
+        prev_side = with_y(place, share, y_first, y_second, ch, 0, 0)
+        next_side = with_y(place, share, y_first, y_second, ch, 1, 7)
+        if ch == 1:
+            sides = []
+            for (ex, a), own in (((0, 0), prev_side), ((1, 7), next_side)):
+                rows = pl.ds((ex * 8 + a) * 8, 8)
+                got_a, got_b = y_first[rows, :], y_second[rows, :]
+                sides.append(
+                    (place.before_y(got_a, got_b),) + own + (place.after_y(got_a, got_b),)
+                )
+            prev_side, next_side = sides
+        for k, (after, before) in enumerate(zip(next_side, prev_side)):
+            put(SIDE_ROW[ch] + k * 8, after, before)
+
+
 def advance_kernel(
-    start,
-    rhs,
+    share,
     y_first,
     y_second,
     x_first,
     x_second,
+    inv_diag,
+    kap,
+    grp,
     ctab,
     zmat,
     fields_new,
-    out,
-    first,
-    second,
+    resid,
+    own,
+    msg,
     grad_z,
+    scaled,
 ):
     place = Place()
     weight = ctab[T_W]
-    inv_mass = [dt_step / (weight * place.mult_tile(ey)) for ey in range(2)]
-
-    def step(ch, carry):
+
+    def before(row):
+        rows = pl.ds(row, 8)
+        return place.before_x(x_first[rows, :], x_second[rows, :])
+
+    def after(row):
+        rows = pl.ds(row, 8)
+        return place.after_x(x_first[rows, :], x_second[rows, :])
+
+    for ch in range(4):
         for ex in range(2):
             for a in range(8):
+                tiles = list(with_y(place, share, y_first, y_second, ch, ex, a))
                 for ey in range(2):
-                    tile = got_face_sum(
-                        place, rhs[ch, ex, a, ey], ch, ex, a, ey,
-                        y_first, y_second, x_first, x_second,
-                    )
-                    scale = place.inv_x(ex, a) * float(1.0 / WEIGHTS[a])
-                    fields_new[ch, ex, a, ey] = start[ch, ex, a, ey] + tile * (
-                        inv_mass[ey] * scale
-                    )
+                    at = {0: 0, 1: 136, 2: 160, 3: 176}[ch] + ey * 8
+                    if (ex, a) == (0, 0):
+                        tiles[ey] = tiles[ey] + before(at + (112 if ch == 0 else 0))
+                    if (ex, a) == (1, 7):
+                        tiles[ey] = tiles[ey] + after(at)
+                    fields_new[ch, ex, a, ey] = tiles[ey]
+    grad_z[...] = along_z(fields_new[2].reshape(256, LANES), zmat[0]).reshape(grad_z.shape)
+    slope = [[None, None], [None, None]]
+    for ey in range(2):
+        for ex in range(2):
+            slope[ex][ey] = along_x(DERIV, [fields_new[0, ex, a, ey] for a in range(8)])
+        low = float(DERIV[7, 7]) * fields_new[0, 0, 0, ey]
+        high = float(DERIV[0, 0]) * fields_new[0, 1, 7, ey]
+        for k in range(7):
+            low = low + float(DERIV[7, k]) * before(k * 16 + ey * 8)
+            high = high + float(DERIV[0, k + 1]) * after((k + 1) * 16 + ey * 8)
+        mid = 0.5 * (slope[0][ey][7] + slope[1][ey][0])
+        slope[0][ey][7] = mid
+        slope[1][ey][0] = mid
+        own_low, own_high = slope[0][ey][0], slope[1][ey][7]
+        slope[0][ey][0] = jnp.where(place.prev_x, 0.5 * (own_low + low), own_low)
+        slope[1][ey][7] = jnp.where(place.next_x, 0.5 * (own_high + high), own_high)
+    sums = [[jnp.zeros(TILE, jnp.float32) for _ in range(2)] for _ in range(2)]
+    inv_mult = [1.0 / place.mult_tile(ey) for ey in range(2)]
+    inv_y = [place.inv_y(ey) for ey in range(2)]
+    inv_z = place.inv_z()
+    mass = [weight * place.mult_tile(ey) for ey in range(2)]
+    there_low = jnp.where(place.prev_y, 1.0, 0.0)
+    there_high = jnp.where(place.next_y, 1.0, 0.0)
+    for ex in range(2):
+        for a in range(8):
+            flow = [fields_new[1, ex, a, ey] for ey in range(2)]
+            rows = pl.ds((ex * 8 + a) * 8, 8)
+            got_a, got_b = y_first[rows, :], y_second[rows, :]
+            below = place.before_y(got_a, got_b)
+            above = place.after_y(got_a, got_b)
+            if (ex, a) == (0, 0):
+                below = below + before(128)
+                above = above + before(152)
+            if (ex, a) == (1, 7):
+                below = below + after(128)
+                above = above + after(152)
+            below = jnp.where(place.row == 7, pltpu.roll(flow[0], 7, 0), below)
+            above = jnp.where(place.row == 0, pltpu.roll(flow[1], 1, 0), above)
+            below = jnp.sum(ctab[T_TOP] * below, axis=0, keepdims=True) * there_low
+            above = jnp.sum(ctab[T_BOTTOM] * above, axis=0, keepdims=True) * there_high
+            grad_y = list(place.join_y(*[along_y(ctab, T_D, tile) for tile in flow]))
+            grad_y[0] = grad_y[0] + jnp.where(place.row == 0, below, 0.0)
+            grad_y[1] = grad_y[1] + jnp.where(place.row == 7, above, 0.0)
+            for ey in range(2):
+                div = (
+                    slope[ex][ey][a]
+                    + grad_y[ey] * inv_y[ey]
+                    + place.join_z(grad_z[ex, a, ey]) * inv_z
+                )
+                value = div * (mass[ey] * (place.mult_x(ex, a) * float(-WEIGHTS[a])))
+                resid[ex, a, ey] = value
+                scaled[ex, a, ey] = value * inv_diag[ex + 1, a, ey + 1] * float(1.0 / THETA)
+                sums[ex][ey] = sums[ex][ey] + value * (inv_mult[ey] * place.inv_x(ex, a))
+    grad_z[...] = along_z(scaled[...].reshape(256, LANES), zmat[2]).reshape(grad_z.shape)
+    tiles = [[[None, None] for _ in range(8)] for _ in range(2)]
+    for ex in range(2):
+        for ey in range(2):
+            images = own_operator(ctab, kap, scaled, grad_z, ex, ey)[1]
+            for a in range(8):
+                tiles[ex][a][ey] = place.join_z(images[a])
+    join_own(place, tiles)
+    for ex in range(2):
+        for a in range(8):
+            for ey in range(2):
+                own[ex, a, ey] = tiles[ex][a][ey]
+    row = message(place, restricted(place, sums, grp), [])
+    blank = jnp.where(place.row == 0, jnp.broadcast_to(row, TILE), 0.0)
+    zero = jnp.zeros(TILE, jnp.float32)
+
+    def clear(i, carry):
+        msg[i, pl.ds(0, 8), :] = zero
+        msg[i, pl.ds(8, 8), :] = blank
         return carry
 
-    lax.fori_loop(0, 4, step, 0)
-    grad_z[...] = along_z(fields_new[2].reshape(256, LANES), zmat[0]).reshape(grad_z.shape)
-    tiles = [[[None, None] for _ in range(8)] for _ in range(2)]
-    for ex in range(2):
-        for ey in range(2):
-            slope = along_x(DERIV, [fields_new[0, ex, a, ey] for a in range(8)])
-            for a in range(8):
-                div = slope[a] + along_y(ctab, T_D, fields_new[1, ex, a, ey]) + grad_z[ex, a, ey]
-                tiles[ex][a][ey] = place.join_z(div * (float(-WEIGHTS[a]) * weight))
-    store_own(place, tiles, out, first, second)
+    lax.fori_loop(0, msg.shape[0], clear, 0)
+    for dx, dy, there in neighbours(place):
+
+        @pl.when(there)
+        def _():
+            to = (place.ix + dx) * place.ny + place.iy + dy
+            ex, a = (0, 0) if dx < 0 else (1, 7)
+            ey, b = (0, 0) if dy < 0 else (1, 7)
+            if dy == 0:
+                msg[to, pl.ds(0, 8), :] = own[ex, a, 0]
+                msg[to, pl.ds(9, 7), :] = own[ex, a, 1, pl.ds(1, 7), :]
+            elif dx == 0:
+                for r in range(16):
+                    if r != 8:
+                        msg[to, pl.ds(r, 1), :] = own[r // 8, r % 8, ey, pl.ds(b, 1), :]
+            else:
+                msg[to, pl.ds(0, 1), :] = own[ex, a, ey, pl.ds(b, 1), :]
+
+
+def neighbours(place):
+    along = ((-1, place.prev_x), (0, None), (1, place.next_x))
+    across = ((-1, place.prev_y), (0, None), (1, place.next_y))
+    out = []
+    for dx, has_x in along:
+        for dy, has_y in across:
+            if dx == 0 and dy == 0:
+                continue
+            there = has_y if has_x is None else (has_x if has_y is None else has_x & has_y)
+            out.append((dx, dy, there))
+    return out
 
 
 def turn_columns_kernel(own, y_first, y_second, first, second):
@@ -532,6 +744,14 @@
     for c, value in enumerate(scalars):
         row = row + jnp.where(lane == after * NCD + c, value, 0.0)
     return row
+
+
+def send_to_all(msg, row):
+    def send(i, carry):
+        msg[i] = row
+        return carry
+
+    lax.fori_loop(0, msg.shape[0], send, 0, unroll=msg.shape[0] <= 64)
 
 
 def smooth_kernel(
@@ -640,17 +860,19 @@
                 )
                 scale = place.inv_x(x - 1, a)
                 sums[x - 1][ey] = sums[x - 1][ey] + value * (inv_mult[ey] * scale)
-    row = message(place, restricted(place, sums, grp), []) + extra[...]
-    for i in range(msg.shape[0]):
-        msg[i] = row
-
-
-def coarse_part(place, blocks, got, coarse, grp):
+    send_to_all(msg, message(place, restricted(place, sums, grp), []) + extra[...])
+
+
+def coarse_part(place, blocks, got, coarse, grp, at=0):
     lane = lax.broadcasted_iota(jnp.int32, (1, LANES), 1)
     values = [jnp.zeros((1, LANES), jnp.float32) for _ in range(blocks)]
     per = LANES // NCD
-    for i in range(got.shape[0]):
-        values[i // per] = jnp.where(lane // NCD == i % per, got[i], values[i // per])
+    for j in range(blocks):
+
+        def gather(i, acc, j=j):
+            return jnp.where(lane // NCD == i, got[j * per + i, pl.ds(at, 1), :], acc)
+
+        values[j] = lax.fori_loop(0, per, gather, values[j], unroll=blocks == 1)
 
     def solved(dx, dy, c):
         acc = None
@@ -710,20 +932,68 @@
 
 
 def first_direction_kernel(
-    blocks, got, coarse, grp, kap, resid, smoothed, ctab, zmat, direction, out, first, second, extra, slope_z
+    blocks,
+    got,
+    coarse,
+    grp,
+    kap,
+    inv_diag,
+    resid,
+    own,
+    ctab,
+    zmat,
+    direction,
+    out,
+    first,
+    second,
+    extra,
+    slope_z,
+    image,
 ):
     place = Place()
     inv_mult = [1.0 / place.mult_tile(ey) for ey in range(2)]
-    part = coarse_part(place, blocks, got, coarse, grp)
+    part = coarse_part(place, blocks, got, coarse, grp, 8)
+    image[...] = own[...]
+    for dx, dy, there in neighbours(place):
+
+        @pl.when(there)
+        def _():
+            frm = (place.ix + dx) * place.ny + place.iy + dy
+            ex, a = (0, 0) if dx < 0 else (1, 7)
+            ey, b = (0, 0) if dy < 0 else (1, 7)
+            edge = place.row == b
+            if dy == 0:
+                low = got[frm, pl.ds(0, 8), :]
+                high = jnp.where(
+                    place.row == 0, pltpu.roll(low, 1, 0), got[frm, pl.ds(8, 8), :]
+                )
+                image[ex, a, 0] = image[ex, a, 0] + low
+                image[ex, a, 1] = image[ex, a, 1] + high
+            elif dx == 0:
+                for r in range(16):
+                    line = got[frm, pl.ds(7 if r == 8 else r, 1), :]
+                    tile = image[r // 8, r % 8, ey]
+                    image[r // 8, r % 8, ey] = tile + jnp.where(edge, line, 0.0)
+            else:
+                line = got[frm, pl.ds(0, 1), :]
+                image[ex, a, ey] = image[ex, a, ey] + jnp.where(edge, line, 0.0)
+
     energy = jnp.zeros(TILE, jnp.float32)
     for ex in range(2):
         for ey in range(2):
             kinds = [part(ex, kind, ey) for kind in range(3)]
             for a in range(8):
-                value = smoothed[ex, a, ey] + kinds[kind_of(a)]
+                known = resid[ex, a, ey]
+                inverse = inv_diag[ex + 1, a, ey + 1]
+                defect = (known - image[ex, a, ey]) * inverse
+                value = (
+                    float((1.0 + RHO_NEXT * RHO) / THETA) * (known * inverse)
+                    + float(2.0 * RHO_NEXT / DELTA) * defect
+                    + kinds[kind_of(a)]
+                )
                 direction[ex, a, ey] = value
                 scale = place.inv_x(ex, a)
-                energy = energy + value * resid[ex, a, ey] * (inv_mult[ey] * scale)
+                energy = energy + value * known * (inv_mult[ey] * scale)
     slope_z[...] = along_z(direction[...].reshape(256, LANES), zmat[2]).reshape(slope_z.shape)
     curvature = jnp.zeros(TILE, jnp.float32)
     tiles = [[[None, None] for _ in range(8)] for _ in range(2)]
@@ -743,8 +1013,11 @@
     sums = []
     for c in range(count):
         acc = jnp.zeros((1, LANES), jnp.float32)
-        for i in range(got.shape[0]):
-            acc = acc + jnp.where(lane == ((i + 1) % per) * NCD + c, got[i], 0.0)
+
+        def gather(i, acc, c=c):
+            return acc + jnp.where(lane == ((i + 1) % per) * NCD + c, got[i], 0.0)
+
+        acc = lax.fori_loop(0, got.shape[0], gather, acc, unroll=got.shape[0] <= per)
         sums.append(jnp.sum(acc, axis=1, keepdims=True))
     return sums
 
@@ -792,9 +1065,7 @@
             values, images = own_operator(ctab, kap, following, slope_z, ex, ey)
             for a in range(8):
                 square = square + values[a] * images[a]
-    row = message(place, [], [total(energy_next), total(square), total(cross)])
-    for i in range(msg.shape[0]):
-        msg[i] = row
+    send_to_all(msg, message(place, [], [total(energy_next), total(square), total(cross)]))
 
 
 def pressure_kernel(got, known, direction, following, pressure):
@@ -813,11 +1084,15 @@
                 )
 
 
-def call(body, outs, scratch=()):
+def call(body, outs, scratch=(), **more):
     return pl.pallas_call(
         body,
         out_shape=[jax.ShapeDtypeStruct(shape, jnp.float32) for shape in outs],
-        scratch_shapes=[pltpu.VMEM(shape, jnp.float32) for shape in scratch],
+        scratch_shapes=[
+            pltpu.VMEM(shape, jnp.float32) if isinstance(shape, tuple) else shape
+            for shape in scratch
+        ],
+        **more,
         compiler_params=pltpu.CompilerParams(vmem_limit_bytes=24 * 1024 * 1024),
     )
 
@@ -826,10 +1101,8 @@
     count = lax.axis_size(axis)
     first_pairs = [(i, i ^ 1) for i in range(count) if i ^ 1 < count]
     second_pairs = [(i, ((i + 1) ^ 1) - 1) for i in range(1, count) if ((i + 1) ^ 1) - 1 < count]
-    return (
-        lax.ppermute(first, axis, first_pairs),
-        lax.ppermute(second, axis, second_pairs),
-    )
+    second_got = lax.ppermute(second, axis, second_pairs)
+    return lax.ppermute(first, axis, first_pairs), second_got
 
 
 def per_device(fields, viscosity, inv_density, elem_group, coarse_inverse):
@@ -838,33 +1111,32 @@
     devices = lax.axis_size("gx") * lax.axis_size("gy")
     blocks = coarse_inverse.shape[1] // LANES
     pack_rows = -(-(8 + NCD * blocks) // 8) * 8
-    tiles_np, mats_np, spread_np = constant_tables(elems_z)
-    ctab, zmat, spread = jnp.asarray(tiles_np), jnp.asarray(mats_np), jnp.asarray(spread_np)
+    tiles_np, mats_np = constant_tables(elems_z)
+    ctab, zmat = jnp.asarray(tiles_np), jnp.asarray(mats_np)
     one = fields.shape[1:]
     four = fields.shape
-    xf_shape = (2, 4, 2, 8, LANES)
-    faces = (64, LANES)
     ext = (4, 8, 4, 8, LANES)
     column = (2, 8, 8, LANES)
     wide = (8, 4, 8, LANES)
     rows = (devices, 1, LANES)
+    y_shape, x_shape = (64 + pack_rows, LANES), (64 + 3 * pack_rows, LANES)
 
     def exchange_all(msg):
         return lax.all_to_all(msg, BOTH, 0, 0, tiled=True)
 
     summed, xf, pack, first, second = call(
         functools.partial(mass_kernel, pack_rows),
-        [four, xf_shape, (pack_rows, LANES), (64 + pack_rows, LANES), (64 + pack_rows, LANES)],
-    )(
-        fields,
-        inv_density.reshape(4, elems_z),
-        elem_group.reshape(4, elems_z),
-        coarse_inverse.reshape(NCD * blocks, LANES),
-        ctab,
-        spread,
-    )
+        [four, (2, 4, 2, 8, LANES), (pack_rows, LANES), y_shape, y_shape],
+        [
+            four,
+            inv_density.shape,
+            pltpu.VMEM(elem_group.shape, jnp.int32),
+            coarse_inverse.shape,
+            pltpu.SemaphoreType.DMA((7,)),
+        ],
+        in_specs=[pl.BlockSpec(memory_space=pltpu.HBM)] * 4,
+    )(fields, inv_density, elem_group, coarse_inverse)
     y_got = swap(first, second, "gy")
-    x_shape = (64 + 3 * pack_rows, LANES)
     first, second = call(functools.partial(turn_faces_kernel, pack_rows), [x_shape, x_shape])(
         xf, pack, *y_got
     )
@@ -873,32 +1145,27 @@
         functools.partial(setup_kernel, pack_rows, blocks),
         [ext, (16, LANES), (16, LANES), (9 * NCD * blocks, LANES)],
     )(pack, *y_got, *x_got, ctab)
-    start, rhs, xf, first, second = call(
-        rhs_kernel, [four, four, xf_shape, faces, faces], [four, four]
+    share, first, second = call(
+        rhs_kernel, [four, (176, LANES), (176, LANES)], [four, four, four, four]
     )(summed, viscosity, *y_got, *x_got, ctab, zmat)
     y_got = swap(first, second, "gy")
-    first, second = call(functools.partial(turn_faces_kernel, 0), [faces, faces])(xf, *y_got)
+    first, second = call(turn_step_kernel, [(192, LANES), (192, LANES)])(share, *y_got)
     x_got = swap(first, second, "gx")
-    fields_new, own, first, second = call(
-        advance_kernel, [four, one, column, column], [one]
-    )(start, rhs, *y_got, *x_got, ctab, zmat)
-
-    def smooth(own, first, second, extra):
-        y_got = swap(first, second, "gy")
-        first, second = call(turn_columns_kernel, [wide, wide])(own, *y_got)
-        x_got = swap(first, second, "gx")
-        return call(
-            smooth_kernel, [one, one, rows], [ext, ext, (2,) + ext[1:], (8, 8, LANES)]
-        )(own, *y_got, *x_got, inv_diag, kap, grp, extra, ctab, zmat)
-
-    resid, smoothed, msg = smooth(own, first, second, jnp.zeros((1, LANES), jnp.float32))
+    fields_new, resid, own, msg = call(
+        advance_kernel, [four, one, one, (devices, 16, LANES)], [one, one]
+    )(share, *y_got, *x_got, inv_diag, kap, grp, ctab, zmat)
     got = exchange_all(msg)
     direction, own, first, second, extra = call(
         functools.partial(first_direction_kernel, blocks),
         [one, one, column, column, (1, LANES)],
-        [one],
-    )(got, coarse, grp, kap, resid, smoothed, ctab, zmat)
-    image, image_smoothed, msg = smooth(own, first, second, extra)
+        [one, one],
+    )(got, coarse, grp, kap, inv_diag, resid, own, ctab, zmat)
+    y_got = swap(first, second, "gy")
+    first, second = call(turn_columns_kernel, [wide, wide])(own, *y_got)
+    x_got = swap(first, second, "gx")
+    image, image_smoothed, msg = call(
+        smooth_kernel, [one, one, rows], [ext, ext, (2,) + ext[1:], (8, 8, LANES)]
+    )(own, *y_got, *x_got, inv_diag, kap, grp, extra, ctab, zmat)
     got = exchange_all(msg)
     following, known, msg = call(
         functools.partial(second_direction_kernel, blocks), [one, (1, LANES), rows], [one]

time: 103 us -> 93 us (0.903)
  starting transfers between devices: 27 us -> 16.9 us
  blocking collectives: 48.2 us -> 51.9 us
  waiting for transfers between devices: 9.76 us -> 7.66 us
  local copies, waits for them, and re-layouts: 4.69 us -> 3.09 us
    ppermute x16 -> x12, starting transfers between devices: 27 us -> 16.9 us  [the longest x6 12.9 us: swap(): return (lax.ppermute(first, axis, first_pairs), second_got)]
    all_to_all x3, blocking collectives: 48.2 us -> 51.9 us  [exchange_all(): return lax.all_to_all(msg, BOTH, 0, 0, tiled=True)]
    ppermute x16 -> x12, waiting for transfers between devices: 9.76 us -> 7.66 us  [the longest x6 7.65 us: swap(): return (lax.ppermute(first, axis, first_pairs), second_got)]
    unnamed x18 -> x14, local copies, waits for them, and re-layouts: 4.69 us -> 3.09 us
    pallas_call x8 -> x6, Pallas kernels: 9.48 us -> 9.69 us  [the longest x1 4.45 us: per_device(): call(rhs_kernel, [four, (176, LANES), (176, LANES)], [four, four, four, f...]
  transfers between devices with their start and end apart: 16 -> 12, of which waited for: 8 -> 6; matrix products, arithmetic and copies ran while one was open for 0% -> 0% of each run, Pallas kernels for 0% -> 0%
where the time goes in v3:
time: 93 us; the launch traced here: 92.6 us
  blocking collectives  51.9 us (56%)
  starting transfers between devices  16.9 us (18%)
  Pallas kernels  12.2 us (13%)
  waiting for transfers between devices  7.66 us (8%)
  local copies, waits for them, and re-layouts  3.09 us (3%)
    all_to_all x3, blocking collectives, exchange_all(): return lax.all_to_all(msg, BOTH, 0, 0, tiled=True)  51.9 us
    ppermute x6, starting transfers between devices, swap(): return (lax.ppermute(first, axis, first_pairs), second_got)  12.9 us
    ppermute x6, waiting for transfers between devices, swap(): return (lax.ppermute(first, axis, first_pairs), second_got)  7.65 us
    pallas_call x1, Pallas kernels, per_device(): call(rhs_kernel, [four, (176, LANES), (176, LANES)], [four, four, four, f...  4.45 us
    ppermute x6, starting transfers between devices, swap(): second_got = lax.ppermute(second, axis, second_pairs)  3.93 us
    unnamed x14, local copies, waits for them, and re-layouts  3.09 us
    pallas_call x1, Pallas kernels, per_device(): call(advance_kernel, [four, one, one, (devices, 16, LANES)], [one, one])  2.19 us
  transfers between devices with their start and end apart: 12, of which 6 were waited for; matrix products, arithmetic and copies ran while one was open for 0% of the time, Pallas kernels for 0%

profile of v3, /device:TPU:0, one launch (start us, length us, event | category | flops | bytes accessed | tf_op | source)
XLA Modules:
  0.0 92.6 jit_solution(3088190236727283372)
XLA Ops:
  0.6 1.0 %copy-done.2 = f32[4,2,8,2,8,128]{5,4,3,2,1,0:T(8,128)S(1)} copy-done((f32[4,2,8,2,8,128]{5,4,3,2,1,0:T(8,128)S(1)}, f32[4,2,8,2,8,128]{5,4,3,2,1,0:T(8,128)}, u32[]{:S(2)}) %copy-start.2) | copy-done | bytes 524312
  1.7 0.7 copy-done.4
  2.4 0.7 copy-done.5
  3.0 0.7 copy-done.6
  3.7 1.6 %shard_map.86 = (f32[4,2,8,2,8,128]{5,4,3,2,1,0:T(8,128)S(1)}, f32[2,4,2,8,128]{4,3,2,1,0:T(8,128)S(1)}, f32[16,128]{1,0:T(8,128)S(1)}, f32[80,128]{1,0:T(8,128)S(1)}, f32[80,128]{1,0:T(8,128)S(1)}) custom-call(f32[4,2,8,2,8,128]{5,4,3,2,1,0:T(8,128)S(1)} %copy-done.2, f32[2,2,16]{2,1,0:T(2,128)S(1)} %copy-done.4, s32[2,2,16]{2,1,0:T(2,128)S(1)} %copy-done.5, ...), custom_call_target="tpu_custom_call" | custom-call | tf_op jit(solution)/shard_map/pallas_call | solution.py:1127
  5.3 0.5 collective-permute-start
  5.8 0.7 collective-permute-start.1
  6.5 0.2 collective-permute-done.y_first
  6.7 2.9 %collective-permute-start.2 = (f32[112,128]{1,0:T(8,128)S(1)}, f32[112,128]{1,0:T(8,128)S(1)}, u32[]{:S(2)}, u32[]{:S(2)}) collective-permute-start(f32[112,128]{1,0:T(8,128)S(1)} %get-tuple-element.40), channel_id=1, source_target_pairs={{0,4},{4,0},{8,12},{12,8},{16,20},{20,16},{24,28},{28,24},{1,5},{5... | collective-permute-start | bytes 172040 | tf_op jit(solution)/shard_map/ppermute | solution.py:1105
  9.6 0.7 collective-permute-start.3
  10.3 1.5 %collective-permute-done.2.x_first = f32[112,128]{1,0:T(8,128)S(1)} collective-permute-done((f32[112,128]{1,0:T(8,128)S(1)}, f32[112,128]{1,0:T(8,128)S(1)}, u32[]{:S(2)}, u32[]{:S(2)}) %collective-permute-start.2) | collective-permute-done | bytes 57376 | tf_op jit(solution)/shard_map/ppermute | solution.py:1105
  11.8 4.4 %shard_map.88 = (f32[4,2,8,2,8,128]{5,4,3,2,1,0:T(8,128)S(1)}, f32[176,128]{1,0:T(8,128)S(1)}, f32[176,128]{1,0:T(8,128)S(1)}) custom-call(f32[4,2,8,2,8,128]{5,4,3,2,1,0:T(8,128)S(1)} %get-tuple-element.35.summed, f32[2,8,2,8,128]{4,3,2,1,0:T(8,128)S(1)} %copy-done.3, f32[80,128]{1,0:T(8,128)S(1)} %collective-permute-done.y_first, ...), custom_call_target="tpu_custom_call" | custom-call | tf_op jit(solution)/shard_map/pallas_call | solution.py:1148
  16.3 3.8 %collective-permute-start.4 = (f32[176,128]{1,0:T(8,128)S(1)}, f32[176,128]{1,0:T(8,128)S(1)}, u32[]{:S(2)}, u32[]{:S(2)}) collective-permute-start(f32[176,128]{1,0:T(8,128)S(1)} %get-tuple-element.43), channel_id=1, source_target_pairs={{0,1},{1,0},{2,3},{3,2},{4,5},{5,4},{6,7},{7,6},{8,9},{9,8},{10,11... | collective-permute-start | bytes 270344 | tf_op jit(solution)/shard_map/ppermute | solution.py:1105
  20.1 0.7 collective-permute-start.5
  20.7 0.3 collective-permute-done.4.y_first
  21.1 4.7 %collective-permute-start.6 = (f32[192,128]{1,0:T(8,128)S(1)}, f32[192,128]{1,0:T(8,128)S(1)}, u32[]{:S(2)}, u32[]{:S(2)}) collective-permute-start(f32[192,128]{1,0:T(8,128)S(1)} %get-tuple-element.45), channel_id=1, source_target_pairs={{0,4},{4,0},{8,12},{12,8},{16,20},{20,16},{24,28},{28,24},{1,5},{5... | collective-permute-start | bytes 294920 | tf_op jit(solution)/shard_map/ppermute | solution.py:1105
  25.8 0.7 collective-permute-start.7
  26.4 0.2 shard_map.90
  26.6 1.7 %collective-permute-done.6.x_first = f32[192,128]{1,0:T(8,128)S(1)} collective-permute-done((f32[192,128]{1,0:T(8,128)S(1)}, f32[192,128]{1,0:T(8,128)S(1)}, u32[]{:S(2)}, u32[]{:S(2)}) %collective-permute-start.6) | collective-permute-done | bytes 98336 | tf_op jit(solution)/shard_map/ppermute | solution.py:1105
  28.4 2.2 %shard_map.91 = (f32[4,2,8,2,8,128]{5,4,3,2,1,0:T(8,128)}, f32[2,8,2,8,128]{4,3,2,1,0:T(8,128)S(1)}, f32[2,8,2,8,128]{4,3,2,1,0:T(8,128)S(1)}, f32[32,16,128]{2,1,0:T(8,128)S(1)}) custom-call(f32[4,2,8,2,8,128]{5,4,3,2,1,0:T(8,128)S(1)} %get-tuple-element.42.share, f32[176,128]{1,0:T(8,128)S(1)} %collective-permute-done.4.y_first, ...), custom_call_target="tpu_custom_call" | custom-call | tf_op jit(solution)/shard_map/pallas_call | solution.py:1154
  30.5 26.0 %all_to_all.15.got = f32[32,16,128]{2,1,0:T(8,128)S(1)} all-to-all(f32[32,16,128]{2,1,0:T(8,128)S(1)} %get-tuple-element.51), channel_id=1, replica_groups=mesh['gx'=8,'gy'=4] {'gx','gy'}, dimensions={0} | all-to-all | bytes 524288 | tf_op jit(solution)/shard_map/all_to_all | solution.py:1125
  56.6 0.8 shard_map.92
  57.4 0.7 collective-permute-start.9
  58.1 0.6 collective-permute-done.8.y_first
  58.7 1.0 %collective-permute-start.10 = (f32[8,4,8,128]{3,2,1,0:T(8,128)S(1)}, f32[8,4,8,128]{3,2,1,0:T(8,128)S(1)}, u32[]{:S(2)}, u32[]{:S(2)}) collective-permute-start(f32[8,4,8,128]{3,2,1,0:T(8,128)S(1)} %get-tuple-element.58), channel_id=1, source_target_pairs={{0,4},{4,0},{8,12},{12,8},{16,20},{20,16},{24,28},{28,24},{1,5},{5... | collective-permute-start | bytes 393224 | tf_op jit(solution)/shard_map/ppermute | solution.py:1105
  59.7 0.7 collective-permute-start.11
  60.3 3.4 %collective-permute-done.10.x_first = f32[8,4,8,128]{3,2,1,0:T(8,128)S(1)} collective-permute-done((f32[8,4,8,128]{3,2,1,0:T(8,128)S(1)}, f32[8,4,8,128]{3,2,1,0:T(8,128)S(1)}, u32[]{:S(2)}, u32[]{:S(2)}) %collective-permute-start.10) | collective-permute-done | bytes 131104 | tf_op jit(solution)/shard_map/ppermute | solution.py:1105
  63.7 1.4 %shard_map.94 = (f32[2,8,2,8,128]{4,3,2,1,0:T(8,128)S(1)}, f32[2,8,2,8,128]{4,3,2,1,0:T(8,128)S(1)}, f32[32,1,128]{2,1,0:T(1,128)S(1)}) custom-call(f32[2,8,2,8,128]{4,3,2,1,0:T(8,128)S(1)} %get-tuple-element.55.own, f32[2,8,8,128]{3,2,1,0:T(8,128)S(1)} %collective-permute-done.8.y_first, f32[2,8,8,128]{3,2,1,0:T(8,128)S(1)} %collective-permute-done.9.y_second, ...), custom_call_target="tpu_custom_call" | custom-call | tf_op jit(solution)/shard_map/pallas_call | solution.py:1166
  65.1 17.0 %all_to_all.16.got = f32[32,1,128]{2,1,0:T(1,128)S(1)} all-to-all(f32[32,1,128]{2,1,0:T(1,128)S(1)} %get-tuple-element.61), channel_id=1, replica_groups=mesh['gx'=8,'gy'=4] {'gx','gy'}, dimensions={0} | all-to-all | bytes 32768 | tf_op jit(solution)/shard_map/all_to_all | solution.py:1125
  82.2 0.6 shard_map.95
  82.8 8.8 %all_to_all.17.got = f32[32,1,128]{2,1,0:T(1,128)S(1)} all-to-all(f32[32,1,128]{2,1,0:T(1,128)S(1)} %get-tuple-element.65), channel_id=1, replica_groups=mesh['gx'=8,'gy'=4] {'gx','gy'}, dimensions={0} | all-to-all | bytes 32768 | tf_op jit(solution)/shard_map/all_to_all | solution.py:1125
  91.7 0.9 shard_map.96
  (20 shorter events, 0.2 us)
Async XLA Ops:
  0.6 1.0 %copy-start.2 = (f32[4,2,8,2,8,128]{5,4,3,2,1,0:T(8,128)S(1)}, f32[4,2,8,2,8,128]{5,4,3,2,1,0:T(8,128)}, u32[]{:S(2)}) copy-start(f32[4,2,8,2,8,128]{5,4,3,2,1,0:T(8,128)} %fields_in.1) | copy-start | bytes 1572868
  1.7 0.7 copy-start.4
  2.4 0.7 copy-start.5
  3.0 0.7 copy-start.6
  3.7 8.1 %copy-start = (f32[3,128,128]{2,1,0:T(8,128)S(1)}, f32[3,128,128]{2,1,0:T(8,128)}, u32[]{:S(2)}) copy-start(f32[3,128,128]{2,1,0:T(8,128)} %constant.5.clone.zmat) | copy-start | bytes 589828
  3.7 8.1 %copy-start.3 = (f32[2,8,2,8,128]{4,3,2,1,0:T(8,128)S(1)}, f32[2,8,2,8,128]{4,3,2,1,0:T(8,128)}, u32[]{:S(2)}) copy-start(f32[2,8,2,8,128]{4,3,2,1,0:T(8,128)} %visc.1) | copy-start | bytes 393220
  5.3 6.5 %copy-start.1 = (f32[28,8,128]{2,1,0:T(8,128)S(1)}, f32[28,8,128]{2,1,0:T(8,128)}, u32[]{:S(2)}) copy-start(f32[28,8,128]{2,1,0:T(8,128)} %constant.4.clone.ctab) | copy-start | bytes 344068
  5.3 1.4 %collective-permute-start = (f32[80,128]{1,0:T(8,128)S(1)}, f32[80,128]{1,0:T(8,128)S(1)}, u32[]{:S(2)}, u32[]{:S(2)}) collective-permute-start(f32[80,128]{1,0:T(8,128)S(1)} %get-tuple-element.36), channel_id=1, source_target_pairs={{0,1},{1,0},{2,3},{3,2},{4,5},{5,4},{6,7},{7,6},{8,9},{9,8},{10,11... | collective-permute-start | bytes 122888 | tf_op jit(solution)/shard_map/ppermute | solution.py:1105
  5.8 0.9 collective-permute-start.1
  6.7 5.1 %collective-permute-start.2 = (f32[112,128]{1,0:T(8,128)S(1)}, f32[112,128]{1,0:T(8,128)S(1)}, u32[]{:S(2)}, u32[]{:S(2)}) collective-permute-start(f32[112,128]{1,0:T(8,128)S(1)} %get-tuple-element.40), channel_id=1, source_target_pairs={{0,4},{4,0},{8,12},{12,8},{16,20},{20,16},{24,28},{28,24},{1,5},{5... | collective-permute-start | bytes 172040 | tf_op jit(solution)/shard_map/ppermute | solution.py:1105
  9.6 2.2 %collective-permute-start.3 = (f32[112,128]{1,0:T(8,128)S(1)}, f32[112,128]{1,0:T(8,128)S(1)}, u32[]{:S(2)}, u32[]{:S(2)}) collective-permute-start(f32[112,128]{1,0:T(8,128)S(1)} %get-tuple-element.41), channel_id=1, source_target_pairs={{4,8},{8,4},{12,16},{16,12},{20,24},{24,20},{5,9},{9,5},{13,17},{1... | collective-permute-start | bytes 172040 | tf_op jit(solution)/shard_map/ppermute | solution.py:1104
  16.3 4.7 %collective-permute-start.4 = (f32[176,128]{1,0:T(8,128)S(1)}, f32[176,128]{1,0:T(8,128)S(1)}, u32[]{:S(2)}, u32[]{:S(2)}) collective-permute-start(f32[176,128]{1,0:T(8,128)S(1)} %get-tuple-element.43), channel_id=1, source_target_pairs={{0,1},{1,0},{2,3},{3,2},{4,5},{5,4},{6,7},{7,6},{8,9},{9,8},{10,11... | collective-permute-start | bytes 270344 | tf_op jit(solution)/shard_map/ppermute | solution.py:1105
  20.1 0.9 %collective-permute-start.5 = (f32[176,128]{1,0:T(8,128)S(1)}, f32[176,128]{1,0:T(8,128)S(1)}, u32[]{:S(2)}, u32[]{:S(2)}) collective-permute-start(f32[176,128]{1,0:T(8,128)S(1)} %get-tuple-element.44), channel_id=1, source_target_pairs={{1,2},{2,1},{5,6},{6,5},{9,10},{10,9},{13,14},{14,13},{17,18},{18,... | collective-permute-start | bytes 270344 | tf_op jit(solution)/shard_map/ppermute | solution.py:1104
  21.1 7.3 %collective-permute-start.6 = (f32[192,128]{1,0:T(8,128)S(1)}, f32[192,128]{1,0:T(8,128)S(1)}, u32[]{:S(2)}, u32[]{:S(2)}) collective-permute-start(f32[192,128]{1,0:T(8,128)S(1)} %get-tuple-element.45), channel_id=1, source_target_pairs={{0,4},{4,0},{8,12},{12,8},{16,20},{20,16},{24,28},{28,24},{1,5},{5... | collective-permute-start | bytes 294920 | tf_op jit(solution)/shard_map/ppermute | solution.py:1105
  25.8 2.6 %collective-permute-start.7 = (f32[192,128]{1,0:T(8,128)S(1)}, f32[192,128]{1,0:T(8,128)S(1)}, u32[]{:S(2)}, u32[]{:S(2)}) collective-permute-start(f32[192,128]{1,0:T(8,128)S(1)} %get-tuple-element.46), channel_id=1, source_target_pairs={{4,8},{8,4},{12,16},{16,12},{20,24},{24,20},{5,9},{9,5},{13,17},{1... | collective-permute-start | bytes 294920 | tf_op jit(solution)/shard_map/ppermute | solution.py:1104
  57.3 1.3 %collective-permute-start.8 = (f32[2,8,8,128]{3,2,1,0:T(8,128)S(1)}, f32[2,8,8,128]{3,2,1,0:T(8,128)S(1)}, u32[]{:S(2)}, u32[]{:S(2)}) collective-permute-start(f32[2,8,8,128]{3,2,1,0:T(8,128)S(1)} %get-tuple-element.56), channel_id=1, source_target_pairs={{0,1},{1,0},{2,3},{3,2},{4,5},{5,4},{6,7},{7,6},{8,9},{9,8},{10,11... | collective-permute-start | bytes 196616 | tf_op jit(solution)/shard_map/ppermute | solution.py:1105
  57.4 1.2 %collective-permute-start.9 = (f32[2,8,8,128]{3,2,1,0:T(8,128)S(1)}, f32[2,8,8,128]{3,2,1,0:T(8,128)S(1)}, u32[]{:S(2)}, u32[]{:S(2)}) collective-permute-start(f32[2,8,8,128]{3,2,1,0:T(8,128)S(1)} %get-tuple-element.57), channel_id=1, source_target_pairs={{1,2},{2,1},{5,6},{6,5},{9,10},{10,9},{13,14},{14,13},{17,18},{18,... | collective-permute-start | bytes 196616 | tf_op jit(solution)/shard_map/ppermute | solution.py:1104
  58.7 5.0 %collective-permute-start.10 = (f32[8,4,8,128]{3,2,1,0:T(8,128)S(1)}, f32[8,4,8,128]{3,2,1,0:T(8,128)S(1)}, u32[]{:S(2)}, u32[]{:S(2)}) collective-permute-start(f32[8,4,8,128]{3,2,1,0:T(8,128)S(1)} %get-tuple-element.58), channel_id=1, source_target_pairs={{0,4},{4,0},{8,12},{12,8},{16,20},{20,16},{24,28},{28,24},{1,5},{5... | collective-permute-start | bytes 393224 | tf_op jit(solution)/shard_map/ppermute | solution.py:1105
  59.7 4.1 %collective-permute-start.11 = (f32[8,4,8,128]{3,2,1,0:T(8,128)S(1)}, f32[8,4,8,128]{3,2,1,0:T(8,128)S(1)}, u32[]{:S(2)}, u32[]{:S(2)}) collective-permute-start(f32[8,4,8,128]{3,2,1,0:T(8,128)S(1)} %get-tuple-element.59), channel_id=1, source_target_pairs={{4,8},{8,4},{12,16},{16,12},{20,24},{24,20},{5,9},{9,5},{13,17},{1... | collective-permute-start | bytes 393224 | tf_op jit(solution)/shard_map/ppermute | solution.py:1104

commit v4 on v3

--- a/solution.py
+++ b/solution.py
@@ -80,13 +80,17 @@
     kz = np.tile(LINE, elems_z)
     tiles = turned(DERIV) + turned(DERIV.T) + turned(SCALED)
     tiles += [WEIGHTS[:, None] * wz[None, :], LINE[:, None] + kz[None, :]]
-    tiles += [np.repeat(DERIV[7][:, None], LANES, 1), np.repeat(DERIV[0][:, None], LANES, 1)]
+    for matrix in (DERIV, SCALED):
+        for node in (7, 0):
+            inner = matrix[node] * (np.arange(8) != node)
+            tiles.append(np.repeat(inner[:, None], LANES, 1))
     eye = np.eye(elems_z)
     mats = [np.kron(eye, DERIV.T), np.kron(eye, DERIV), np.kron(eye, SCALED.T)]
     return np.stack(tiles).astype(np.float32), np.stack(mats).astype(np.float32)
 
 
-T_D, T_DT, T_K, T_W, T_LINE, T_TOP, T_BOTTOM = 0, 8, 16, 24, 25, 26, 27
+T_D, T_DT, T_K, T_W, T_LINE = 0, 8, 16, 24, 25
+T_TOP, T_BOTTOM, T_KTOP, T_KBOTTOM = 26, 27, 28, 29
 
 
 class Place:
@@ -230,47 +234,11 @@
     )
 
 
-def mass_kernel(
-    pack_rows,
-    fields_in,
-    kappa_in,
-    group_in,
-    coarse_in,
-    out,
-    xf,
-    pack,
-    first,
-    second,
-    fields,
-    kappa,
-    group,
-    coarse,
-    sems,
-):
+def mass_kernel(fields_in, out, xf, first, second, fields, sems):
     copies = [pltpu.make_async_copy(fields_in.at[ch], fields.at[ch], sems.at[ch]) for ch in range(4)]
-    copies += [
-        pltpu.make_async_copy(kappa_in, kappa, sems.at[4]),
-        pltpu.make_async_copy(group_in, group, sems.at[5]),
-        pltpu.make_async_copy(coarse_in, coarse, sems.at[6]),
-    ]
     for copy in copies:
         copy.start()
     place = Place()
-    for copy in copies[4:]:
-        copy.wait()
-    pack[...] = jnp.zeros(pack.shape, jnp.float32)
-    elems = kappa.shape[2]
-    spread_to = lax.broadcasted_iota(jnp.int32, (elems, LANES), 1) // NODES
-    spread = (spread_to == lax.broadcasted_iota(jnp.int32, (elems, LANES), 0)).astype(jnp.float32)
-    blocks = coarse.shape[1] // LANES
-    for ex in range(2):
-        pack[pl.ds(2 * ex, 2), :] = along_z(kappa[ex], spread)
-        pack[pl.ds(4 + 2 * ex, 2), :] = along_z(group[ex].astype(jnp.float32), spread)
-    for c in range(NCD):
-        for j in range(blocks):
-            pack[pl.ds(8 + c * blocks + j, 1), :] = coarse[pl.ds(c, 1), pl.ds(j * LANES, LANES)]
-    first[pl.ds(64, pack_rows), :] = pack[...]
-    second[pl.ds(64, pack_rows), :] = pack[...]
     weight = weight_of(place.row) * weight_of(place.lane % NODES)
     for ch in range(4):
         copies[ch].wait()
@@ -295,8 +263,7 @@
         store_y_faces(place, out, first, second, (ch,), ch * 16)
 
 
-def turn_faces_kernel(pack_rows, xf, pack, y_first, y_second, first, second):
-    place = Place()
+def turn_faces(place, xf, y_first, y_second, first, second):
     for ch in range(4):
         sides = []
         for side in range(2):
@@ -309,14 +276,51 @@
             rows = pl.ds(ch * 16 + ey * 8, 8)
             first[rows, :] = place.after_x(sides[1][ey], sides[0][ey])
             second[rows, :] = place.after_x(sides[0][ey], sides[1][ey])
-    came = pl.ds(64, pack_rows)
+
+
+def turn_faces_kernel(xf, y_first, y_second, first, second):
+    turn_faces(Place(), xf, y_first, y_second, first, second)
+
+
+def turn_edges(place, inner_x, y_first, y_second, first, second, at, edge, inner_y):
+    sides = []
+    for side in range(2):
+        row = pl.ds(edge + side, 1)
+        got_a, got_b = y_first[row, :], y_second[row, :]
+        low = inner_x[side, 0] + jnp.where(place.row == 0, place.before_y(got_a, got_b), 0.0)
+        high = inner_x[side, 1] + jnp.where(place.row == 7, place.after_y(got_a, got_b), 0.0)
+        sides.append((low, high))
+    for ey in range(2):
+        rows = pl.ds(at + ey * 8, 8)
+        first[rows, :] = place.after_x(sides[1][ey], sides[0][ey])
+        second[rows, :] = place.after_x(sides[0][ey], sides[1][ey])
+    for k, pick in enumerate((place.before_y, place.after_y)):
+        sides = []
+        for side in range(2):
+            row = pl.ds(inner_y + 15 * side, 1)
+            sides.append(pick(y_first[row, :], y_second[row, :]))
+        row = pl.ds(edge + k, 1)
+        first[row, :] = place.after_x(sides[1], sides[0])
+        second[row, :] = place.after_x(sides[0], sides[1])
+
+
+STEP_U, STEP_V, STEP_EDGE, STEP_PACK = 64, 64, 80, 88
+
+
+def turn_step_kernel(pack_rows, xf, inner_x, pack, y_first, y_second, first, second):
+    place = Place()
+    turn_faces(place, xf, y_first, y_second, first, second)
+    first[pl.ds(STEP_EDGE, 8), :] = jnp.zeros(TILE, jnp.float32)
+    second[pl.ds(STEP_EDGE, 8), :] = jnp.zeros(TILE, jnp.float32)
+    turn_edges(place, inner_x, y_first, y_second, first, second, STEP_U, STEP_EDGE, STEP_V)
+    came = pl.ds(STEP_PACK, pack_rows)
     parts = (
         place.before_y(y_first[came, :], y_second[came, :]),
         pack[...],
         place.after_y(y_first[came, :], y_second[came, :]),
     )
     for k in range(3):
-        rows = pl.ds(64 + k * pack_rows, pack_rows)
+        rows = pl.ds(STEP_PACK + k * pack_rows, pack_rows)
         first[rows, :] = parts[k]
         second[rows, :] = parts[k]
 
@@ -325,13 +329,13 @@
     pack_rows, blocks, pack, y_first, y_second, x_first, x_second, ctab, inv_diag, kap, grp, coarse
 ):
     place = Place()
-    came = pl.ds(64, pack_rows)
+    came = pl.ds(STEP_PACK, pack_rows)
     packs = [[None] * 3 for _ in range(3)]
     packs[1][0] = place.before_y(y_first[came, :], y_second[came, :])
     packs[1][1] = pack[...]
     packs[1][2] = place.after_y(y_first[came, :], y_second[came, :])
     for k in range(3):
-        rows = pl.ds(64 + k * pack_rows, pack_rows)
+        rows = pl.ds(STEP_PACK + k * pack_rows, pack_rows)
         packs[0][k] = place.before_x(x_first[rows, :], x_second[rows, :])
         packs[2][k] = place.after_x(x_first[rows, :], x_second[rows, :])
     for dx in range(3):
@@ -351,39 +355,37 @@
             grp[pl.ds(x * 4 + y, 1), :] = element_row(4, x + 1, y + 1)
     kappa = [
         [
-            place.join_z(jnp.broadcast_to(element_row(0, u, v), TILE))
-            for v in range(6)
+            place.join_z(jnp.broadcast_to(element_row(0, u + 1, v + 1), TILE))
+            for v in range(4)
         ]
-        for u in range(6)
+        for u in range(4)
     ]
     count_z = 1.0 + jnp.where(place.low_z | place.high_z, 1.0, 0.0)
     weight = ctab[T_W]
     line = ctab[T_LINE]
 
-    def pick(values, y):
-        low = values[y] + values[y + 1]
-        high = values[y + 1] + values[y + 2]
-        return jnp.where(place.row == 0, low, jnp.where(place.row == 7, high, values[y + 1]))
-
-    for x in range(4):
+    def pick(values, ey):
+        low = values[ey] + values[ey + 1]
+        high = values[ey + 1] + values[ey + 2]
+        return jnp.where(place.row == 0, low, jnp.where(place.row == 7, high, values[ey + 1]))
+
+    for ex in range(2):
         for kind in range(3):
-            us = {0: (x, x + 1), 1: (x + 1,), 2: (x + 1, x + 2)}[kind]
+            us = {0: (ex, ex + 1), 1: (ex + 1,), 2: (ex + 1, ex + 2)}[kind]
             sums, counts = [], []
-            for v in range(6):
+            for v in range(4):
                 acc, num = None, 0.0
                 for u in us:
                     acc = kappa[u][v] if acc is None else acc + kappa[u][v]
-                    num = num + there_x[u // 2]
+                    num = num + there_x[(u + 1) // 2]
                 sums.append(acc)
-                counts.append(num * there_y[v // 2])
-            for y in range(4):
-                kappa_sum = pick(sums, y)
-                mult = pick(counts, y) * count_z
-                present = there_x[(x + 1) // 2] * there_y[(y + 1) // 2] > 0.5
+                counts.append(num * there_y[(v + 1) // 2])
+            for ey in range(2):
+                kappa_sum = pick(sums, ey)
+                mult = pick(counts, ey) * count_z
                 for a in {0: (0,), 1: range(1, 7), 2: (7,)}[kind]:
                     diag = (float(LINE[a]) + line) * kappa_sum + sigma_p * mult
-                    diag = diag * (float(WEIGHTS[a]) * weight)
-                    inv_diag[x, a, y] = jnp.where(present, 1.0 / diag, 0.0)
+                    inv_diag[ex, a, ey] = 1.0 / (diag * (float(WEIGHTS[a]) * weight))
 
 
 def got_face_sum(place, tile, ch, ex, a, ey, y_first, y_second, x_first, x_second):
@@ -401,9 +403,40 @@
     return tile
 
 
+def fill_pack(place, kappa, group, coarse, pack, facts):
+    pack[...] = jnp.zeros(pack.shape, jnp.float32)
+    facts[...] = jnp.zeros(facts.shape, jnp.float32)
+    elems = kappa.shape[2]
+    to = lax.broadcasted_iota(jnp.int32, (elems, LANES), 1)
+    element = lax.broadcasted_iota(jnp.int32, (elems, LANES), 0)
+    spread = (to // NODES == element).astype(jnp.float32)
+    blocks = coarse.shape[1] // LANES
+    for ex in range(2):
+        numbers = group[ex].astype(jnp.float32)
+        pack[pl.ds(2 * ex, 2), :] = along_z(kappa[ex], spread)
+        pack[pl.ds(4 + 2 * ex, 2), :] = along_z(numbers, spread)
+        row = jnp.zeros((1, LANES), jnp.float32)
+        for ey in range(2):
+            at = (2 * place.iy + ey) * elems
+            spot = (to == at + element).astype(jnp.float32)
+            after = (to == (at + 2 * elems) % LANES + element).astype(jnp.float32)
+            row = row + along_z(kappa[ex, pl.ds(ey, 1), :], spot)
+            row = row + along_z(numbers[ey : ey + 1], after)
+        facts[pl.ds(2 + ex, 1), :] = row
+    for c in range(NCD):
+        for j in range(blocks):
+            line = coarse[pl.ds(c, 1), pl.ds(j * LANES, LANES)]
+            pack[pl.ds(8 + c * blocks + j, 1), :] = line
+        facts[pl.ds(4 + c, 1), :] = coarse[pl.ds(c, 1), pl.ds(0, LANES)]
+
+
 def rhs_kernel(
+    pack_rows,
     summed,
     visc,
+    kappa,
+    group,
+    coarse,
     y_first,
     y_second,
     x_first,
@@ -411,6 +444,10 @@
     ctab,
     zmat,
     share,
+    xf,
+    inner_x,
+    pack,
+    facts,
     first,
     second,
     start,
@@ -485,75 +522,53 @@
         return carry
 
     lax.fori_loop(0, 4, finish, 0)
+    for ch in range(4):
+        store_y_faces(place, share, first, second, (ch,), ch * 16)
+        for ey in range(2):
+            xf[0, ch, ey] = share[ch, 0, 0, ey]
+            xf[1, ch, ey] = share[ch, 1, 7, ey]
+    first[pl.ds(STEP_EDGE, 8), :] = jnp.zeros(TILE, jnp.float32)
+    second[pl.ds(STEP_EDGE, 8), :] = jnp.zeros(TILE, jnp.float32)
+
+    def column_of(ex, ey):
+        return [share[0, ex, a, ey] for a in range(8)]
+
+    def tile_of(ex, a, ey):
+        return share[1, ex, a, ey]
+
+    store_inner(
+        place, DERIV, ctab[T_BOTTOM], ctab[T_TOP], column_of, tile_of, inner_x, first, second,
+        STEP_V, STEP_EDGE,
+    )
+    fill_pack(place, kappa, group, coarse, pack, facts)
+    first[pl.ds(STEP_PACK, pack_rows), :] = pack[...]
+    second[pl.ds(STEP_PACK, pack_rows), :] = pack[...]
+
+
+def store_inner(
+    place, matrix, bottom, top, column_of, tile_of, inner_x, first, second, at, edge
+):
+    for ey in range(2):
+        low, high = column_of(0, ey), column_of(1, ey)
+        below = float(matrix[0, 1]) * low[1]
+        above = float(matrix[7, 0]) * high[0]
+        for k in range(2, 8):
+            below = below + float(matrix[0, k]) * low[k]
+            above = above + float(matrix[7, k - 1]) * high[k - 1]
+        inner_x[0, ey] = below
+        inner_x[1, ey] = above
+    for side in range(2):
+        low = inner_x[side, 0, pl.ds(0, 1), :]
+        high = inner_x[side, 1, pl.ds(7, 1), :]
+        first[pl.ds(edge + side, 1), :] = place.after_y(high, low)
+        second[pl.ds(edge + side, 1), :] = place.after_y(low, high)
     for ex in range(2):
         for a in range(8):
-            low, high = share[1, ex, a, 0], share[1, ex, a, 1]
-            rows = pl.ds((ex * 8 + a) * 8, 8)
-            first[rows, :] = place.after_y(high, low)
-            second[rows, :] = place.after_y(low, high)
-    for k, ch in enumerate((0, 2, 3)):
-        store_y_faces(place, share, first, second, (ch,), 128 + k * 16)
-
-
-def store_own(place, tiles, out, first, second):
-    join_own(place, tiles)
-    for ex in range(2):
-        for a in range(8):
-            low, high = tiles[ex][a]
-            out[ex, a, 0] = low
-            out[ex, a, 1] = high
-            first[ex, a] = place.after_y(high, low)
-            second[ex, a] = place.after_y(low, high)
-
-
-FACE_ROW = {0: 128, 2: 144, 3: 160}
-SIDE_ROW = {1: 128, 2: 160, 3: 176}
-
-
-def with_y(place, share, y_first, y_second, ch, ex, a):
-    low, high = share[ch, ex, a, 0], share[ch, ex, a, 1]
-    if ch == 1:
-        rows = pl.ds((ex * 8 + a) * 8, 8)
-        got_a, got_b = y_first[rows, :], y_second[rows, :]
-        return (
-            low + place.to_low(place.before_y(got_a, got_b)),
-            high + place.to_high(place.after_y(got_a, got_b)),
-        )
-    row = pl.ds(FACE_ROW[ch] + ex * 8 + a, 1)
-    got_a, got_b = y_first[row, :], y_second[row, :]
-    return (
-        low + jnp.where(place.row == 0, place.before_y(got_a, got_b), 0.0),
-        high + jnp.where(place.row == 7, place.after_y(got_a, got_b), 0.0),
-    )
-
-
-def turn_step_kernel(share, y_first, y_second, first, second):
-    place = Place()
-
-    def put(row, next_side, prev_side):
-        rows = pl.ds(row, 8)
-        first[rows, :] = place.after_x(next_side, prev_side)
-        second[rows, :] = place.after_x(prev_side, next_side)
-
-    for a in range(8):
-        prev_side = with_y(place, share, y_first, y_second, 0, 0, a)
-        next_side = with_y(place, share, y_first, y_second, 0, 1, a)
-        for ey in range(2):
-            put(a * 16 + ey * 8, next_side[ey], prev_side[ey])
-    for ch in (1, 2, 3):
-        prev_side = with_y(place, share, y_first, y_second, ch, 0, 0)
-        next_side = with_y(place, share, y_first, y_second, ch, 1, 7)
-        if ch == 1:
-            sides = []
-            for (ex, a), own in (((0, 0), prev_side), ((1, 7), next_side)):
-                rows = pl.ds((ex * 8 + a) * 8, 8)
-                got_a, got_b = y_first[rows, :], y_second[rows, :]
-                sides.append(
-                    (place.before_y(got_a, got_b),) + own + (place.after_y(got_a, got_b),)
-                )
-            prev_side, next_side = sides
-        for k, (after, before) in enumerate(zip(next_side, prev_side)):
-            put(SIDE_ROW[ch] + k * 8, after, before)
+            low = jnp.sum(bottom * tile_of(ex, a, 0), axis=0, keepdims=True)
+            high = jnp.sum(top * tile_of(ex, a, 1), axis=0, keepdims=True)
+            row = pl.ds(at + ex * 8 + a, 1)
+            first[row, :] = place.after_y(high, low)
+            second[row, :] = place.after_y(low, high)
 
 
 def advance_kernel(
@@ -577,41 +592,38 @@
     place = Place()
     weight = ctab[T_W]
 
-    def before(row):
-        rows = pl.ds(row, 8)
+    def before(row, count=8):
+        rows = pl.ds(row, count)
         return place.before_x(x_first[rows, :], x_second[rows, :])
 
-    def after(row):
-        rows = pl.ds(row, 8)
+    def after(row, count=8):
+        rows = pl.ds(row, count)
         return place.after_x(x_first[rows, :], x_second[rows, :])
 
-    for ch in range(4):
+    def step(ch, carry):
         for ex in range(2):
             for a in range(8):
-                tiles = list(with_y(place, share, y_first, y_second, ch, ex, a))
                 for ey in range(2):
-                    at = {0: 0, 1: 136, 2: 160, 3: 176}[ch] + ey * 8
-                    if (ex, a) == (0, 0):
-                        tiles[ey] = tiles[ey] + before(at + (112 if ch == 0 else 0))
-                    if (ex, a) == (1, 7):
-                        tiles[ey] = tiles[ey] + after(at)
-                    fields_new[ch, ex, a, ey] = tiles[ey]
+                    fields_new[ch, ex, a, ey] = got_face_sum(
+                        place, share[ch, ex, a, ey], ch, ex, a, ey,
+                        y_first, y_second, x_first, x_second,
+                    )
+        return carry
+
+    lax.fori_loop(0, 4, step, 0)
     grad_z[...] = along_z(fields_new[2].reshape(256, LANES), zmat[0]).reshape(grad_z.shape)
     slope = [[None, None], [None, None]]
     for ey in range(2):
         for ex in range(2):
             slope[ex][ey] = along_x(DERIV, [fields_new[0, ex, a, ey] for a in range(8)])
-        low = float(DERIV[7, 7]) * fields_new[0, 0, 0, ey]
-        high = float(DERIV[0, 0]) * fields_new[0, 1, 7, ey]
-        for k in range(7):
-            low = low + float(DERIV[7, k]) * before(k * 16 + ey * 8)
-            high = high + float(DERIV[0, k + 1]) * after((k + 1) * 16 + ey * 8)
         mid = 0.5 * (slope[0][ey][7] + slope[1][ey][0])
         slope[0][ey][7] = mid
         slope[1][ey][0] = mid
-        own_low, own_high = slope[0][ey][0], slope[1][ey][7]
-        slope[0][ey][0] = jnp.where(place.prev_x, 0.5 * (own_low + low), own_low)
-        slope[1][ey][7] = jnp.where(place.next_x, 0.5 * (own_high + high), own_high)
+        low, high = slope[0][ey][0], slope[1][ey][7]
+        inner_low = low - float(DERIV[0, 0]) * fields_new[0, 0, 0, ey] + before(STEP_U + ey * 8)
+        inner_high = high - float(DERIV[7, 7]) * fields_new[0, 1, 7, ey] + after(STEP_U + ey * 8)
+        slope[0][ey][0] = jnp.where(place.prev_x, 0.5 * inner_low, low)
+        slope[1][ey][7] = jnp.where(place.next_x, 0.5 * inner_high, high)
     sums = [[jnp.zeros(TILE, jnp.float32) for _ in range(2)] for _ in range(2)]
     inv_mult = [1.0 / place.mult_tile(ey) for ey in range(2)]
     inv_y = [place.inv_y(ey) for ey in range(2)]
@@ -622,20 +634,11 @@
     for ex in range(2):
         for a in range(8):
             flow = [fields_new[1, ex, a, ey] for ey in range(2)]
-            rows = pl.ds((ex * 8 + a) * 8, 8)
-            got_a, got_b = y_first[rows, :], y_second[rows, :]
-            below = place.before_y(got_a, got_b)
-            above = place.after_y(got_a, got_b)
-            if (ex, a) == (0, 0):
-                below = below + before(128)
-                above = above + before(152)
-            if (ex, a) == (1, 7):
-                below = below + after(128)
-                above = above + after(152)
-            below = jnp.where(place.row == 7, pltpu.roll(flow[0], 7, 0), below)
-            above = jnp.where(place.row == 0, pltpu.roll(flow[1], 1, 0), above)
-            below = jnp.sum(ctab[T_TOP] * below, axis=0, keepdims=True) * there_low
-            above = jnp.sum(ctab[T_BOTTOM] * above, axis=0, keepdims=True) * there_high
+            below, above = inner_along_y(
+                place, y_first, y_second, before, after, ex, a, STEP_V, STEP_EDGE
+            )
+            below = (below - float(DERIV[0, 0]) * flow[0]) * there_low
+            above = (above - float(DERIV[7, 7]) * flow[1]) * there_high
             grad_y = list(place.join_y(*[along_y(ctab, T_D, tile) for tile in flow]))
             grad_y[0] = grad_y[0] + jnp.where(place.row == 0, below, 0.0)
             grad_y[1] = grad_y[1] + jnp.where(place.row == 7, above, 0.0)
@@ -647,7 +650,7 @@
                 )
                 value = div * (mass[ey] * (place.mult_x(ex, a) * float(-WEIGHTS[a])))
                 resid[ex, a, ey] = value
-                scaled[ex, a, ey] = value * inv_diag[ex + 1, a, ey + 1] * float(1.0 / THETA)
+                scaled[ex, a, ey] = value * inv_diag[ex, a, ey] * float(1.0 / THETA)
                 sums[ex][ey] = sums[ex][ey] + value * (inv_mult[ey] * place.inv_x(ex, a))
     grad_z[...] = along_z(scaled[...].reshape(256, LANES), zmat[2]).reshape(grad_z.shape)
     tiles = [[[None, None] for _ in range(8)] for _ in range(2)]
@@ -689,6 +692,19 @@
                 msg[to, pl.ds(0, 1), :] = own[ex, a, ey, pl.ds(b, 1), :]
 
 
+def inner_along_y(place, y_first, y_second, before, after, ex, a, at, edge):
+    row = pl.ds(at + ex * 8 + a, 1)
+    got_a, got_b = y_first[row, :], y_second[row, :]
+    below, above = place.before_y(got_a, got_b), place.after_y(got_a, got_b)
+    if (ex, a) == (0, 0):
+        below = below + before(edge, 1)
+        above = above + before(edge + 1, 1)
+    if (ex, a) == (1, 7):
+        below = below + after(edge, 1)
+        above = above + after(edge + 1, 1)
+    return below, above
+
+
 def neighbours(place):
     along = ((-1, place.prev_x), (0, None), (1, place.next_x))
     across = ((-1, place.prev_y), (0, None), (1, place.next_y))
@@ -702,24 +718,27 @@
     return out
 
 
-def turn_columns_kernel(own, y_first, y_second, first, second):
+SMOOTH_X, SMOOTH_Y, SMOOTH_EDGE, SMOOTH_ROWS = 16, 16, 32, 40
+
+
+def turn_smooth_kernel(own, inner_x, y_first, y_second, first, second):
     place = Place()
-
-    def line(a, carry):
-        for y in range(4):
-            sides = []
-            for ex in range(2):
-                if y in (1, 2):
-                    sides.append(own[ex, a, y - 1])
-                elif y == 0:
-                    sides.append(place.before_y(y_first[ex, a], y_second[ex, a]))
-                else:
-                    sides.append(place.after_y(y_first[ex, a], y_second[ex, a]))
-            first[a, y] = place.after_x(sides[1], sides[0])
-            second[a, y] = place.after_x(sides[0], sides[1])
-        return carry
-
-    lax.fori_loop(0, 8, line, 0)
+    sides = []
+    for side, (ex, a) in enumerate(((0, 0), (1, 7))):
+        row = pl.ds(15 * side, 1)
+        got_a, got_b = y_first[row, :], y_second[row, :]
+        low = own[ex, a, 0] + jnp.where(place.row == 0, place.before_y(got_a, got_b), 0.0)
+        high = own[ex, a, 1] + jnp.where(place.row == 7, place.after_y(got_a, got_b), 0.0)
+        sides.append((low, high))
+    for ey in range(2):
+        rows = pl.ds(ey * 8, 8)
+        first[rows, :] = place.after_x(sides[1][ey], sides[0][ey])
+        second[rows, :] = place.after_x(sides[0][ey], sides[1][ey])
+    first[pl.ds(SMOOTH_EDGE, 8), :] = jnp.zeros(TILE, jnp.float32)
+    second[pl.ds(SMOOTH_EDGE, 8), :] = jnp.zeros(TILE, jnp.float32)
+    turn_edges(
+        place, inner_x, y_first, y_second, first, second, SMOOTH_X, SMOOTH_EDGE, SMOOTH_Y
+    )
 
 
 def restricted(place, sums, grp):
@@ -742,6 +761,8 @@
     for c, value in enumerate(own_values):
         row = row + jnp.where(lane == spot * NCD + c, value, 0.0)
     for c, value in enumerate(scalars):
+        if value is None:
+            continue
         row = row + jnp.where(lane == after * NCD + c, value, 0.0)
     return row
 
@@ -764,103 +785,152 @@
     kap,
     grp,
     extra,
+    facts,
     ctab,
     zmat,
-    resid,
+    image,
     smoothed,
     msg,
-    ext,
     scaled,
-    local,
-    edge,
+    slope_z,
 ):
     place = Place()
     weight = ctab[T_W]
-
-    def raw(x, a, y):
-        if x in (1, 2):
-            if y in (1, 2):
-                return own[x - 1, a, y - 1]
-            if y == 0:
-                return place.before_y(y_first[x - 1, a], y_second[x - 1, a])
-            return place.after_y(y_first[x - 1, a], y_second[x - 1, a])
-        if x == 0:
-            return place.before_x(x_first[a, y], x_second[a, y])
-        return place.after_x(x_first[a, y], x_second[a, y])
-
-    def put(x, a, tiles):
-        low = place.join_y(tiles[0], tiles[1])
-        high = place.join_y(tiles[2], tiles[3])
-        for y, tile in enumerate(low + high):
-            ext[x, a, y] = tile
-            scaled[x, a, y] = tile * inv_diag[x, a, y] * float(1.0 / THETA)
-
-    joined = {}
-    for x, a, x2, a2 in ((0, 7, 1, 0), (2, 7, 3, 0)):
-        both = [raw(x, a, y) + raw(x2, a2, y) for y in range(4)]
-        put(x, a, both)
-        put(x2, a2, both)
-        joined[(x, a)] = joined[(x2, a2)] = True
-
-    for x in range(4):
-        first = 1 if (x, 0) in joined else 0
-        last = 7 if (x, 7) in joined else 8
-
-        def fill(a, carry, x=x):
-            put(x, a, [raw(x, a, y) for y in range(4)])
-            return carry
-
-        lax.fori_loop(first, last, fill, 0)
-
-    local[...] = along_z(scaled[pl.ds(1, 2)].reshape(512, LANES), zmat[2]).reshape(local.shape)
-    edge[pl.ds(0, 4)] = along_z(scaled[0, 7].reshape(32, LANES), zmat[2]).reshape(4, 8, LANES)
-    edge[pl.ds(4, 4)] = along_z(scaled[3, 0].reshape(32, LANES), zmat[2]).reshape(4, 8, LANES)
-
-    def finish_tile(tile, a, slope, x, y):
-        kappa = kap[pl.ds(x * 4 + y, 1), :]
-        stiff = slope + along_y(ctab, T_K, tile)
-        return (kappa * stiff + sigma_p * tile) * (float(WEIGHTS[a]) * weight)
-
-    def column(y, carry):
-        for x in (1, 2):
-            tiles = [scaled[x, a, y] for a in range(8)]
-            slopes = along_x(SCALED, tiles)
+    corner = float(SCALED[0, 0])
+
+    def before(row, count=8):
+        rows = pl.ds(row, count)
+        return place.before_x(x_first[rows, :], x_second[rows, :])
+
+    def after(row, count=8):
+        rows = pl.ds(row, count)
+        return place.after_x(x_first[rows, :], x_second[rows, :])
+
+    for ex in range(2):
+        for a in range(8):
+            for ey in range(2):
+                tile = got_face_sum(
+                    place, own[ex, a, ey], 0, ex, a, ey, y_first, y_second, x_first, x_second
+                )
+                image[ex, a, ey] = tile
+                scaled[ex, a, ey] = tile * inv_diag[ex, a, ey] * float(1.0 / THETA)
+    slope_z[...] = along_z(scaled[...].reshape(256, LANES), zmat[2]).reshape(slope_z.shape)
+    there_x = (jnp.where(place.prev_x, 1.0, 0.0), jnp.where(place.next_x, 1.0, 0.0))
+    there_y = (jnp.where(place.prev_y, 1.0, 0.0), jnp.where(place.next_y, 1.0, 0.0))
+
+    def kappa_of(x, y):
+        return kap[pl.ds(x * 4 + y, 1), :]
+
+    tiles = [[[None, None] for _ in range(8)] for _ in range(2)]
+    for ex in range(2):
+        for ey in range(2):
+            values = [scaled[ex, a, ey] for a in range(8)]
+            slopes = along_x(SCALED, values)
+            y_next = 0 if ey == 0 else 3
+            edge_row = place.row == (0 if ey == 0 else 7)
             for a in range(8):
-                local[x - 1, a, y] = finish_tile(tiles[a], a, slopes[a] + local[x - 1, a, y], x, y)
-        for x, a, at in ((0, 7, 0), (3, 0, 4)):
-            slope = edge[at + y]
-            for k in range(8):
-                slope = slope + float(SCALED[a, k]) * scaled[x, k, y]
-            edge[at + y] = finish_tile(scaled[x, a, y], a, slope, x, y)
-        return carry
-
-    lax.fori_loop(0, 4, column, 0)
+                value = values[a]
+                slope_y = along_y(ctab, T_K, value)
+                flat = slope_z[ex, a, ey]
+                same = slopes[a] + slope_y + flat
+                acc = kappa_of(ex + 1, ey + 1) * same + sigma_p * value
+                inner = inner_along_y(
+                    place, y_first, y_second, before, after, ex, a, SMOOTH_Y, SMOOTH_EDGE
+                )[ey]
+                turned_y = inner + corner * value
+                beyond = kappa_of(ex + 1, y_next) * (slopes[a] + turned_y + flat)
+                beyond = (beyond + sigma_p * value) * there_y[ey]
+                if (ex, a) in ((0, 0), (1, 7)):
+                    x_next = 0 if ex == 0 else 3
+                    get = before if ex == 0 else after
+                    turned_x = get(SMOOTH_X + ey * 8) + corner * value
+                    side = kappa_of(x_next, ey + 1) * (turned_x + slope_y + flat)
+                    acc = acc + (side + sigma_p * value) * there_x[ex]
+                    far = kappa_of(x_next, y_next) * (turned_x + turned_y + flat)
+                    beyond = beyond + (far + sigma_p * value) * (there_x[ex] * there_y[ey])
+                acc = acc + jnp.where(edge_row, beyond, 0.0)
+                tiles[ex][a][ey] = place.join_z(acc * (float(WEIGHTS[a]) * weight))
+    join_own(place, tiles)
     inv_mult = [1.0 / place.mult_tile(ey) for ey in range(2)]
     sums = [[jnp.zeros(TILE, jnp.float32) for _ in range(2)] for _ in range(2)]
-    for x in (1, 2):
+    square = jnp.zeros(TILE, jnp.float32)
+    for ex in range(2):
         for a in range(8):
-            if (x, a) == (1, 0):
-                tiles = [local[0, 0, y] + edge[y] for y in range(4)]
-            elif (x, a) == (2, 7):
-                tiles = [local[1, 7, y] + edge[4 + y] for y in range(4)]
-            elif (x, a) in ((1, 7), (2, 0)):
-                tiles = [local[0, 7, y] + local[1, 0, y] for y in range(4)]
-            else:
-                tiles = [local[x - 1, a, y] for y in range(4)]
-            low = tiles[1] + place.to_low(tiles[0]) + place.to_high(tiles[2])
-            high = tiles[2] + place.to_low(tiles[1]) + place.to_high(tiles[3])
-            for ey, image in enumerate((low, high)):
-                image = place.join_z(image)
-                value = ext[x, a, ey + 1]
-                update = scaled[x, a, ey + 1]
-                defect = (value - image) * inv_diag[x, a, ey + 1]
-                resid[x - 1, a, ey] = value
-                smoothed[x - 1, a, ey] = (
+            for ey in range(2):
+                value = image[ex, a, ey]
+                defect = (value - tiles[ex][a][ey]) * inv_diag[ex, a, ey]
+                update = scaled[ex, a, ey]
+                result = (
                     float(1.0 + RHO_NEXT * RHO) * update + float(2.0 * RHO_NEXT / DELTA) * defect
                 )
-                scale = place.inv_x(x - 1, a)
-                sums[x - 1][ey] = sums[x - 1][ey] + value * (inv_mult[ey] * scale)
-    send_to_all(msg, message(place, restricted(place, sums, grp), []) + extra[...])
+                smoothed[ex, a, ey] = result
+                weighed = value * (inv_mult[ey] * place.inv_x(ex, a))
+                sums[ex][ey] = sums[ex][ey] + weighed
+                square = square + weighed * result
+    own_sums = restricted(place, sums, grp)
+    if msg.shape[1] == 1:
+        send_to_all(msg, message(place, own_sums, []) + extra[...])
+        return
+    slope_z[...] = along_z(smoothed[...].reshape(256, LANES), zmat[2]).reshape(slope_z.shape)
+    energy = jnp.zeros(TILE, jnp.float32)
+    for ex in range(2):
+        for ey in range(2):
+            values, images = own_operator(ctab, kap, smoothed, slope_z, ex, ey)
+            for a in range(8):
+                energy = energy + values[a] * images[a]
+                tiles[ex][a][ey] = place.join_z(images[a])
+    join_own(place, tiles)
+    row = message(place, own_sums, [None, None, total(square), total(energy)]) + extra[...]
+    dual = restricted_around(place, tiles, inv_mult, grp)
+    out = facts[...]
+    out = out + jnp.where(place.row == 0, jnp.broadcast_to(row, TILE), 0.0)
+    out = out + jnp.where(place.row == 1, jnp.broadcast_to(dual, TILE), 0.0)
+    send_to_all(msg, out)
+
+
+def restricted_around(place, tiles, inv_mult, grp):
+    lane = lax.broadcasted_iota(jnp.int32, (1, LANES), 1)
+    weighed = [
+        [[tiles[ex][a][ey] * (inv_mult[ey] * place.inv_x(ex, a)) for ey in range(2)] for a in range(8)]
+        for ex in range(2)
+    ]
+
+    def rows_of(tile, y):
+        if y == 0:
+            return jnp.where(place.row == 0, tile[0], 0.0)
+        if y == 3:
+            return jnp.where(place.row == 7, tile[1], 0.0)
+        return tile[y - 1]
+
+    there_x = (place.prev_x, None, None, place.next_x)
+    there_y = (place.prev_y, None, None, place.next_y)
+    by_device = [
+        [[jnp.zeros(TILE, jnp.float32) for _ in range(NCD)] for _ in range(3)] for _ in range(3)
+    ]
+    for x in range(4):
+        for y in range(4):
+            if x == 0:
+                acc = rows_of(weighed[0][0], y)
+            elif x == 3:
+                acc = rows_of(weighed[1][7], y)
+            else:
+                acc = rows_of(weighed[x - 1][0], y)
+                for a in range(1, 8):
+                    acc = acc + rows_of(weighed[x - 1][a], y)
+            for there in (there_x[x], there_y[y]):
+                if there is not None:
+                    acc = jnp.where(there, acc, 0.0)
+            group = grp[pl.ds(x * 4 + y, 1), :]
+            device = by_device[(x + 1) // 2][(y + 1) // 2]
+            for c in range(NCD):
+                device[c] = device[c] + jnp.where(group == float(c), acc, 0.0)
+    row = jnp.zeros((1, LANES), jnp.float32)
+    for dx in range(3):
+        for dy in range(3):
+            at = ((place.ix + dx - 1) * place.ny + place.iy + dy - 1) * NCD
+            for c in range(NCD):
+                row = row + jnp.where(lane == at + c, total(by_device[dx][dy][c]), 0.0)
+    return row
 
 
 def coarse_part(place, blocks, got, coarse, grp, at=0):
@@ -881,6 +951,10 @@
             acc = term if acc is None else acc + term
         return jnp.sum(acc, axis=1, keepdims=True)
 
+    return prolonged(place, solved, grp)
+
+
+def prolonged(place, solved, grp):
     device = [[[solved(dx, dy, c) for c in range(NCD)] for dy in range(3)] for dx in range(3)]
     inv_z = jnp.where(place.low_z | place.high_z, 0.5, 1.0)
     rows = []
@@ -944,6 +1018,7 @@
     zmat,
     direction,
     out,
+    inner_x,
     first,
     second,
     extra,
@@ -984,7 +1059,7 @@
             kinds = [part(ex, kind, ey) for kind in range(3)]
             for a in range(8):
                 known = resid[ex, a, ey]
-                inverse = inv_diag[ex + 1, a, ey + 1]
+                inverse = inv_diag[ex, a, ey]
                 defect = (known - image[ex, a, ey]) * inverse
                 value = (
                     float((1.0 + RHO_NEXT * RHO) / THETA) * (known * inverse)
@@ -1003,7 +1078,25 @@
             for a in range(8):
                 curvature = curvature + values[a] * images[a]
                 tiles[ex][a][ey] = place.join_z(images[a])
-    store_own(place, tiles, out, first, second)
+    join_own(place, tiles)
+    for ex in range(2):
+        for a in range(8):
+            for ey in range(2):
+                out[ex, a, ey] = tiles[ex][a][ey]
+    store_y_faces(place, out, first, second, (), 0)
+    first[pl.ds(SMOOTH_EDGE, 8), :] = jnp.zeros(TILE, jnp.float32)
+    second[pl.ds(SMOOTH_EDGE, 8), :] = jnp.zeros(TILE, jnp.float32)
+
+    def tile_of(ex, a, ey):
+        return tiles[ex][a][ey] * inv_diag[ex, a, ey] * float(1.0 / THETA)
+
+    def column_of(ex, ey):
+        return [tile_of(ex, a, ey) for a in range(8)]
+
+    store_inner(
+        place, SCALED, ctab[T_KBOTTOM], ctab[T_KTOP], column_of, tile_of, inner_x, first, second,
+        SMOOTH_Y, SMOOTH_EDGE,
+    )
     extra[...] = message(place, [], [total(energy), total(curvature)])
 
 
@@ -1084,6 +1177,138 @@
                 )
 
 
+def coarse_energy(place, got, values, kappa, number):
+    lane, row = place.lane, place.row
+    for ex in range(2):
+        for gx in range(8):
+            own = jnp.zeros((1, LANES), jnp.float32)
+            group = jnp.zeros((1, LANES), jnp.float32)
+            spot = lane[0:1] // 32
+            for gy in range(4):
+                line = got[gx * 4 + gy, pl.ds(2 + ex, 1), :]
+                own = jnp.where(spot == gy, line, own)
+                group = jnp.where(spot == (gy + 1) % 4, line, group)
+            kappa[ex, pl.ds(gx, 1), :] = own
+            number[ex, pl.ds(gx, 1), :] = group
+    grid = [jnp.zeros(TILE, jnp.float32) for _ in range(2)]
+    numbers = [pltpu.roll(number[ex], 96, 1) for ex in range(2)]
+    for q in range(4):
+        for c in range(NCD):
+            mine = jnp.where(lane == row * 16 + q * 4 + c, values, 0.0)
+            mine = jnp.sum(mine, axis=1, keepdims=True)
+            for ex in range(2):
+                chosen = (lane // 32 == q) & (numbers[ex] == float(c))
+                grid[ex] = jnp.where(chosen, mine, grid[ex])
+
+    def ends_y(v):
+        low = jnp.where(lane >= 16, 0.5 * (v + pltpu.roll(v, 16, 1)), v)
+        return low, v, jnp.where(lane < 112, 0.5 * (v + pltpu.roll(v, 112, 1)), v)
+
+    def ends_z(v):
+        low = jnp.where(lane % 16 > 0, 0.5 * (v + pltpu.roll(v, 1, 1)), v)
+        return low, v, jnp.where(lane % 16 < 15, 0.5 * (v + pltpu.roll(v, 127, 1)), v)
+
+    low = jnp.where(row > 0, 0.5 * (grid[0] + pltpu.roll(grid[1], 1, 0)), grid[0])
+    mid = 0.5 * (grid[0] + grid[1])
+    high = jnp.where(row < 7, 0.5 * (grid[1] + pltpu.roll(grid[0], 7, 0)), grid[1])
+    mass = [float(WEIGHTS[0]), float(np.sum(WEIGHTS[1:7])), float(WEIGHTS[7])]
+    links = (
+        (0, 1, -float(np.sum(STIFF[0, 1:7]))),
+        (0, 2, -float(STIFF[0, 7])),
+        (1, 2, -float(np.sum(STIFF[7, 1:7]))),
+    )
+    energy = jnp.zeros(TILE, jnp.float32)
+    for ex, line in enumerate(((low, grid[0], mid), (mid, grid[1], high))):
+        nodes = [[ends_z(v) for v in ends_y(w)] for w in line]
+        stiff = jnp.zeros(TILE, jnp.float32)
+        square = jnp.zeros(TILE, jnp.float32)
+        for i in range(3):
+            for j in range(3):
+                for k, l, weight in links:
+                    factor = weight * mass[i] * mass[j]
+                    for first, second in (
+                        (nodes[k][i][j], nodes[l][i][j]),
+                        (nodes[i][k][j], nodes[i][l][j]),
+                        (nodes[i][j][k], nodes[i][j][l]),
+                    ):
+                        gap = first - second
+                        stiff = stiff + (factor * gap) * gap
+                for k in range(3):
+                    value = nodes[i][j][k]
+                    square = square + (mass[i] * mass[j] * mass[k] * value) * value
+        energy = energy + kappa[ex] * stiff + sigma_p * square
+    return total(energy)
+
+
+def finish_kernel(
+    got, grp, direction, smoothed, pressure, matrix, kappa, number
+):
+    place = Place()
+    per = LANES // NCD
+    row_lane = lax.broadcasted_iota(jnp.int32, (1, LANES), 1)
+    rest = jnp.zeros((1, LANES), jnp.float32)
+    dual = jnp.zeros((1, LANES), jnp.float32)
+    sums = [jnp.zeros((1, LANES), jnp.float32) for _ in range(4)]
+    for i in range(per):
+        line = got[i, pl.ds(0, 1), :]
+        rest = jnp.where(row_lane // NCD == i, line, rest)
+        dual = dual + got[i, pl.ds(1, 1), :]
+        for c in range(4):
+            sums[c] = sums[c] + jnp.where(row_lane == ((i + 1) % per) * NCD + c, line, 0.0)
+        matrix[pl.ds(i * NCD, NCD), :] = got[i, pl.ds(4, NCD), :]
+    energy, curvature, square, self_energy = [
+        jnp.sum(value, axis=1, keepdims=True) for value in sums
+    ]
+    values = lax.dot_general(
+        jnp.broadcast_to(rest, TILE),
+        matrix[...],
+        (((1,), (1,)), ((), ())),
+        precision=lax.Precision.HIGHEST,
+        preferred_element_type=jnp.float32,
+    )
+    line = values[0:1]
+    cross = square + jnp.sum(line * rest, axis=1, keepdims=True)
+    both = self_energy + 2.0 * jnp.sum(line * dual, axis=1, keepdims=True)
+    both = both + coarse_energy(place, got, values, kappa, number)
+    step = energy / curvature
+    energy_next = step * step * cross - energy
+    ratio = energy_next / energy
+    with_image = curvature - step * cross
+    with_itself = curvature - 2.0 * step * cross + step * step * both
+    step_next = energy_next / (
+        with_itself + 2.0 * ratio * with_image + ratio * ratio * curvature
+    )
+    old = step + step_next * (1.0 + ratio)
+    new = -step_next * step
+
+    def solved(dx, dy, c):
+        at = ((place.ix + dx - 1) * place.ny + place.iy + dy - 1) * NCD + c
+        return jnp.sum(jnp.where(row_lane == at, line, 0.0), axis=1, keepdims=True)
+
+    part = prolonged(place, masked(place, solved), grp)
+    for ex in range(2):
+        for ey in range(2):
+            kinds = [part(ex, kind, ey) for kind in range(3)]
+            for a in range(8):
+                pressure[ex, a, ey] = old * direction[ex, a, ey] + new * (
+                    smoothed[ex, a, ey] + kinds[kind_of(a)]
+                )
+
+
+def masked(place, solved):
+    there_x = (place.prev_x, None, place.next_x)
+    there_y = (place.prev_y, None, place.next_y)
+
+    def value(dx, dy, c):
+        out = solved(dx, dy, c)
+        for there in (there_x[dx], there_y[dy]):
+            if there is not None:
+                out = jnp.where(there, out, 0.0)
+        return out
+
+    return value
+
+
 def call(body, outs, scratch=(), **more):
     return pl.pallas_call(
         body,
@@ -1115,58 +1340,75 @@
     ctab, zmat = jnp.asarray(tiles_np), jnp.asarray(mats_np)
     one = fields.shape[1:]
     four = fields.shape
-    ext = (4, 8, 4, 8, LANES)
-    column = (2, 8, 8, LANES)
-    wide = (8, 4, 8, LANES)
+    faces = (64, LANES)
+    xf_shape = (2, 4, 2, 8, LANES)
+    inner_shape = (2, 2, 8, LANES)
+    y_shape, x_shape = (STEP_PACK + pack_rows, LANES), (STEP_PACK + 3 * pack_rows, LANES)
+    smooth_shape = (SMOOTH_ROWS, LANES)
     rows = (devices, 1, LANES)
-    y_shape, x_shape = (64 + pack_rows, LANES), (64 + 3 * pack_rows, LANES)
+    grid_fits = (
+        blocks == 1
+        and lax.axis_size("gx") == 8
+        and lax.axis_size("gy") * fields.shape[3] * elems_z == LANES
+    )
 
     def exchange_all(msg):
         return lax.all_to_all(msg, BOTH, 0, 0, tiled=True)
 
-    summed, xf, pack, first, second = call(
-        functools.partial(mass_kernel, pack_rows),
-        [four, (2, 4, 2, 8, LANES), (pack_rows, LANES), y_shape, y_shape],
-        [
-            four,
-            inv_density.shape,
-            pltpu.VMEM(elem_group.shape, jnp.int32),
-            coarse_inverse.shape,
-            pltpu.SemaphoreType.DMA((7,)),
-        ],
-        in_specs=[pl.BlockSpec(memory_space=pltpu.HBM)] * 4,
-    )(fields, inv_density, elem_group, coarse_inverse)
+    summed, xf, first, second = call(
+        mass_kernel,
+        [four, xf_shape, faces, faces],
+        [four, pltpu.SemaphoreType.DMA((4,))],
+        in_specs=[pl.BlockSpec(memory_space=pltpu.HBM)],
+    )(fields)
     y_got = swap(first, second, "gy")
-    first, second = call(functools.partial(turn_faces_kernel, pack_rows), [x_shape, x_shape])(
-        xf, pack, *y_got
+    first, second = call(turn_faces_kernel, [faces, faces])(xf, *y_got)
+    x_got = swap(first, second, "gx")
+    share, xf, inner_x, pack, facts, first, second = call(
+        functools.partial(rhs_kernel, pack_rows),
+        [four, xf_shape, inner_shape, (pack_rows, LANES), TILE, y_shape, y_shape],
+        [four, four, four, four],
+    )(
+        summed,
+        viscosity,
+        inv_density,
+        elem_group,
+        coarse_inverse,
+        *y_got,
+        *x_got,
+        ctab,
+        zmat,
+    )
+    y_got = swap(first, second, "gy")
+    first, second = call(functools.partial(turn_step_kernel, pack_rows), [x_shape, x_shape])(
+        xf, inner_x, pack, *y_got
     )
     x_got = swap(first, second, "gx")
     inv_diag, kap, grp, coarse = call(
         functools.partial(setup_kernel, pack_rows, blocks),
-        [ext, (16, LANES), (16, LANES), (9 * NCD * blocks, LANES)],
+        [one, (16, LANES), (16, LANES), (9 * NCD * blocks, LANES)],
     )(pack, *y_got, *x_got, ctab)
-    share, first, second = call(
-        rhs_kernel, [four, (176, LANES), (176, LANES)], [four, four, four, four]
-    )(summed, viscosity, *y_got, *x_got, ctab, zmat)
-    y_got = swap(first, second, "gy")
-    first, second = call(turn_step_kernel, [(192, LANES), (192, LANES)])(share, *y_got)
-    x_got = swap(first, second, "gx")
     fields_new, resid, own, msg = call(
         advance_kernel, [four, one, one, (devices, 16, LANES)], [one, one]
     )(share, *y_got, *x_got, inv_diag, kap, grp, ctab, zmat)
     got = exchange_all(msg)
-    direction, own, first, second, extra = call(
+    direction, own, inner_x, first, second, extra = call(
         functools.partial(first_direction_kernel, blocks),
-        [one, one, column, column, (1, LANES)],
+        [one, one, inner_shape, smooth_shape, smooth_shape, (1, LANES)],
         [one, one],
     )(got, coarse, grp, kap, inv_diag, resid, own, ctab, zmat)
     y_got = swap(first, second, "gy")
-    first, second = call(turn_columns_kernel, [wide, wide])(own, *y_got)
+    first, second = call(turn_smooth_kernel, [smooth_shape, smooth_shape])(own, inner_x, *y_got)
     x_got = swap(first, second, "gx")
     image, image_smoothed, msg = call(
-        smooth_kernel, [one, one, rows], [ext, ext, (2,) + ext[1:], (8, 8, LANES)]
-    )(own, *y_got, *x_got, inv_diag, kap, grp, extra, ctab, zmat)
+        smooth_kernel, [one, one, (devices, 8, LANES) if grid_fits else rows], [one, one]
+    )(own, *y_got, *x_got, inv_diag, kap, grp, extra, facts, ctab, zmat)
     got = exchange_all(msg)
+    if grid_fits:
+        (pressure,) = call(
+            finish_kernel, [one], [(LANES, LANES), (2,) + TILE, (2,) + TILE]
+        )(got, grp, direction, image_smoothed)
+        return (fields_new, pressure)
     following, known, msg = call(
         functools.partial(second_direction_kernel, blocks), [one, (1, LANES), rows], [one]
     )(got, coarse, grp, kap, resid, direction, image, image_smoothed, ctab, zmat)

time: 93 us -> 80.8 us (0.87)
  blocking collectives: 51.9 us -> 43.3 us
  local copies, waits for them, and re-layouts: 3.09 us -> 1.07 us
  waiting for transfers between devices: 7.66 us -> 6.03 us
    all_to_all x3 -> x2, blocking collectives: 51.9 us -> 43.3 us  [exchange_all(): return lax.all_to_all(msg, BOTH, 0, 0, tiled=True)]
    unnamed x14, local copies, waits for them, and re-layouts: 3.09 us -> 1.07 us
    ppermute x6, waiting for transfers between devices: 7.65 us -> 6.02 us  [swap(): return (lax.ppermute(first, axis, first_pairs), second_got)]
    pallas_call x10 -> x9, Pallas kernels: 10 us -> 10.3 us  [the longest x1 4.8 us: per_device(): call(functools.partial(rhs_kernel, pack_rows), [four, xf_shape, inner_sha...]
where the time goes in v4:
time: 80.8 us; the launch traced here: 80.5 us
  blocking collectives  43.3 us (54%)
  starting transfers between devices  16.7 us (21%)
  Pallas kernels  12.5 us (15%)
  waiting for transfers between devices  6.03 us (7%)
  local copies, waits for them, and re-layouts  1.07 us (1%)
  between operations  0.81 us (1%)
    all_to_all x2, blocking collectives, exchange_all(): return lax.all_to_all(msg, BOTH, 0, 0, tiled=True)  43.3 us
    ppermute x6, starting transfers between devices, swap(): return (lax.ppermute(first, axis, first_pairs), second_got)  12.8 us
    ppermute x6, waiting for transfers between devices, swap(): return (lax.ppermute(first, axis, first_pairs), second_got)  6.02 us
    pallas_call x1, Pallas kernels, per_device(): call(functools.partial(rhs_kernel, pack_rows), [four, xf_shape, inner_sha...  4.8 us
    ppermute x6, starting transfers between devices, swap(): second_got = lax.ppermute(second, axis, second_pairs)  3.92 us
    pallas_call x1, Pallas kernels, per_device(): call(advance_kernel, [four, one, one, (devices, 16, LANES)], [one, one])  2.21 us
    pallas_call x1, Pallas kernels, per_device(): call(smooth_kernel, [one, one, (devices, 8, LANES) if grid_fits else rows...  1.73 us
  transfers between devices with their start and end apart: 12, of which 6 were waited for; matrix products, arithmetic and copies ran while one was open for 0% of the time, Pallas kernels for 0%

profile of v4, /device:TPU:0, one launch (start us, length us, event | category | flops | bytes accessed | tf_op | source)
XLA Modules:
  0.0 80.5 jit_solution(5417807301480043735)
XLA Ops:
  0.6 1.0 %copy-done.2 = f32[4,2,8,2,8,128]{5,4,3,2,1,0:T(8,128)S(1)} copy-done((f32[4,2,8,2,8,128]{5,4,3,2,1,0:T(8,128)S(1)}, f32[4,2,8,2,8,128]{5,4,3,2,1,0:T(8,128)}, u32[]{:S(2)}) %copy-start.2) | copy-done | bytes 524312
  1.7 1.4 %shard_map.86 = (f32[4,2,8,2,8,128]{5,4,3,2,1,0:T(8,128)S(1)}, f32[2,4,2,8,128]{4,3,2,1,0:T(8,128)S(1)}, f32[64,128]{1,0:T(8,128)S(1)}, f32[64,128]{1,0:T(8,128)S(1)}) custom-call(f32[4,2,8,2,8,128]{5,4,3,2,1,0:T(8,128)S(1)} %copy-done.2), custom_call_target="tpu_custom_call" | custom-call | tf_op jit(solution)/shard_map/pallas_call | solution.py:1358
  3.0 0.0 copy-start.1
  3.1 0.5 collective-permute-start
  3.6 0.7 collective-permute-start.1
  4.2 0.2 collective-permute-done.y_first
  4.5 0.0 copy-start.5
  4.5 0.0 copy-start.4
  4.5 2.9 %collective-permute-start.2 = (f32[64,128]{1,0:T(8,128)S(1)}, f32[64,128]{1,0:T(8,128)S(1)}, u32[]{:S(2)}, u32[]{:S(2)}) collective-permute-start(f32[64,128]{1,0:T(8,128)S(1)} %get-tuple-element.39), channel_id=1, source_target_pairs={{0,4},{4,0},{8,12},{12,8},{16,20},{20,16},{24,28},{28,24},{1,5},{5... | collective-permute-start | bytes 98312 | tf_op jit(solution)/shard_map/ppermute | solution.py:1330
  7.4 0.7 collective-permute-start.3
  8.1 1.2 %collective-permute-done.2.x_first = f32[64,128]{1,0:T(8,128)S(1)} collective-permute-done((f32[64,128]{1,0:T(8,128)S(1)}, f32[64,128]{1,0:T(8,128)S(1)}, u32[]{:S(2)}, u32[]{:S(2)}) %collective-permute-start.2) | collective-permute-done | bytes 32800 | tf_op jit(solution)/shard_map/ppermute | solution.py:1330
  9.3 0.0 collective-permute-done.3.x_second
  9.3 4.8 %shard_map.88 = (f32[4,2,8,2,8,128]{5,4,3,2,1,0:T(8,128)S(1)}, f32[2,4,2,8,128]{4,3,2,1,0:T(8,128)S(1)}, f32[2,2,8,128]{3,2,1,0:T(8,128)S(1)}, f32[16,128]{1,0:T...) custom-call(f32[4,2,8,2,8,128]{5,4,3,2,1,0:T(8,128)S(1)} %get-tuple-element.35.summed, ...), custom_call_target="tpu_custom_call" | custom-call | tf_op jit(solution)/shard_map/pallas_call | solution.py:1367
  14.1 3.7 %collective-permute-start.4 = (f32[104,128]{1,0:T(8,128)S(1)}, f32[104,128]{1,0:T(8,128)S(1)}, u32[]{:S(2)}, u32[]{:S(2)}) collective-permute-start(f32[104,128]{1,0:T(8,128)S(1)} %get-tuple-element.42), channel_id=1, source_target_pairs={{0,1},{1,0},{2,3},{3,2},{4,5},{5,4},{6,7},{7,6},{8,9},{9,8},{10,11... | collective-permute-start | bytes 159752 | tf_op jit(solution)/shard_map/ppermute | solution.py:1330
  17.8 0.7 collective-permute-start.5
  18.5 0.2 collective-permute-done.4.y_first
  18.7 4.7 %collective-permute-start.6 = (f32[136,128]{1,0:T(8,128)S(1)}, f32[136,128]{1,0:T(8,128)S(1)}, u32[]{:S(2)}, u32[]{:S(2)}) collective-permute-start(f32[136,128]{1,0:T(8,128)S(1)} %get-tuple-element.47), channel_id=1, source_target_pairs={{0,4},{4,0},{8,12},{12,8},{16,20},{20,16},{24,28},{28,24},{1,5},{5... | collective-permute-start | bytes 208904 | tf_op jit(solution)/shard_map/ppermute | solution.py:1330
  23.4 0.7 collective-permute-start.7
  24.1 1.6 %collective-permute-done.6.x_first = f32[136,128]{1,0:T(8,128)S(1)} collective-permute-done((f32[136,128]{1,0:T(8,128)S(1)}, f32[136,128]{1,0:T(8,128)S(1)}, u32[]{:S(2)}, u32[]{:S(2)}) %collective-permute-start.6) | collective-permute-done | bytes 69664 | tf_op jit(solution)/shard_map/ppermute | solution.py:1330
  25.7 0.1 shard_map.90
  25.9 2.2 %shard_map.91 = (f32[4,2,8,2,8,128]{5,4,3,2,1,0:T(8,128)}, f32[2,8,2,8,128]{4,3,2,1,0:T(8,128)S(1)}, f32[2,8,2,8,128]{4,3,2,1,0:T(8,128)S(1)}, f32[32,16,128]{2,1,0:T(8,128)S(1)}) custom-call(f32[4,2,8,2,8,128]{5,4,3,2,1,0:T(8,128)S(1)} %get-tuple-element.41.share, f32[104,128]{1,0:T(8,128)S(1)} %collective-permute-done.4.y_first, ...), custom_call_target="tpu_custom_call" | custom-call | tf_op jit(solution)/shard_map/pallas_call | solution.py:1391
  28.1 25.6 %all_to_all.10.got = f32[32,16,128]{2,1,0:T(8,128)S(1)} all-to-all(f32[32,16,128]{2,1,0:T(8,128)S(1)} %get-tuple-element.53), channel_id=1, replica_groups=mesh['gx'=8,'gy'=4] {'gx','gy'}, dimensions={0} | all-to-all | bytes 524288 | tf_op jit(solution)/shard_map/all_to_all | solution.py:1356
  53.7 0.8 shard_map.92
  54.5 0.1 collective-permute-start.8
  54.6 0.7 collective-permute-start.9
  55.2 0.5 collective-permute-done.8.y_first
  55.8 1.0 %collective-permute-start.10 = (f32[40,128]{1,0:T(8,128)S(1)}, f32[40,128]{1,0:T(8,128)S(1)}, u32[]{:S(2)}, u32[]{:S(2)}) collective-permute-start(f32[40,128]{1,0:T(8,128)S(1)} %get-tuple-element.61), channel_id=1, source_target_pairs={{0,4},{4,0},{8,12},{12,8},{16,20},{20,16},{24,28},{28,24},{1,5},{5... | collective-permute-start | bytes 61448 | tf_op jit(solution)/shard_map/ppermute | solution.py:1330
  56.7 0.7 collective-permute-start.11
  57.4 2.2 %collective-permute-done.10.x_first = f32[40,128]{1,0:T(8,128)S(1)} collective-permute-done((f32[40,128]{1,0:T(8,128)S(1)}, f32[40,128]{1,0:T(8,128)S(1)}, u32[]{:S(2)}, u32[]{:S(2)}) %collective-permute-start.10) | collective-permute-done | bytes 20512 | tf_op jit(solution)/shard_map/ppermute | solution.py:1330
  59.6 1.7 %shard_map.94 = (f32[2,8,2,8,128]{4,3,2,1,0:T(8,128)}, f32[2,8,2,8,128]{4,3,2,1,0:T(8,128)S(1)}, f32[32,8,128]{2,1,0:T(8,128)S(1)}) custom-call(f32[2,8,2,8,128]{4,3,2,1,0:T(8,128)S(1)} %get-tuple-element.57.own, f32[40,128]{1,0:T(8,128)S(1)} %collective-permute-done.8.y_first, f32[40,128]{1,0:T(8,128)S(1)} %collective-permute-done.9.y_second, ...), custom_call_target="tpu_custom_call" | custom-call | tf_op jit(solution)/shard_map/pallas_call | solution.py:1403
  61.4 17.7 %all_to_all.11.got = f32[32,8,128]{2,1,0:T(8,128)S(1)} all-to-all(f32[32,8,128]{2,1,0:T(8,128)S(1)} %get-tuple-element.65), channel_id=1, replica_groups=mesh['gx'=8,'gy'=4] {'gx','gy'}, dimensions={0} | all-to-all | bytes 262144 | tf_op jit(solution)/shard_map/all_to_all | solution.py:1356
  79.1 1.4 %shard_map.95 = f32[2,8,2,8,128]{4,3,2,1,0:T(8,128)} custom-call(f32[32,8,128]{2,1,0:T(8,128)S(1)} %all_to_all.11.got, f32[16,128]{1,0:T(8,128)S(1)} %get-tuple-element.51.grp, f32[2,8,2,8,128]{4,3,2,1,0:T(8,128)S(1)} %get-tuple-element.66.direction, f32[2,8,2,8,128]{4,3,2,1,0:T(8,128)S(1)} %get-tuple-element.67.smoothed), custom_call_target="tpu_custom_call" | custom-call | tf_op jit(solution)/shard_map/pallas_call | solution.py:1408
  (18 shorter events, 0.1 us)
Async XLA Ops:
  0.6 1.0 %copy-start.2 = (f32[4,2,8,2,8,128]{5,4,3,2,1,0:T(8,128)S(1)}, f32[4,2,8,2,8,128]{5,4,3,2,1,0:T(8,128)}, u32[]{:S(2)}) copy-start(f32[4,2,8,2,8,128]{5,4,3,2,1,0:T(8,128)} %fields_in.1) | copy-start | bytes 1572868
  1.7 7.6 %copy-start = (f32[3,128,128]{2,1,0:T(8,128)S(1)}, f32[3,128,128]{2,1,0:T(8,128)}, u32[]{:S(2)}) copy-start(f32[3,128,128]{2,1,0:T(8,128)} %constant.5.clone.zmat) | copy-start | bytes 589828
  1.7 7.6 %copy-start.3 = (f32[2,8,2,8,128]{4,3,2,1,0:T(8,128)S(1)}, f32[2,8,2,8,128]{4,3,2,1,0:T(8,128)}, u32[]{:S(2)}) copy-start(f32[2,8,2,8,128]{4,3,2,1,0:T(8,128)} %visc.1) | copy-start | bytes 393220
  3.0 6.3 %copy-start.1 = (f32[30,8,128]{2,1,0:T(8,128)S(1)}, f32[30,8,128]{2,1,0:T(8,128)}, u32[]{:S(2)}) copy-start(f32[30,8,128]{2,1,0:T(8,128)} %constant.4.clone.ctab) | copy-start | bytes 368644
  3.1 1.4 %collective-permute-start = (f32[64,128]{1,0:T(8,128)S(1)}, f32[64,128]{1,0:T(8,128)S(1)}, u32[]{:S(2)}, u32[]{:S(2)}) collective-permute-start(f32[64,128]{1,0:T(8,128)S(1)} %get-tuple-element.36), channel_id=1, source_target_pairs={{0,1},{1,0},{2,3},{3,2},{4,5},{5,4},{6,7},{7,6},{8,9},{9,8},{10,11... | collective-permute-start | bytes 98312 | tf_op jit(solution)/shard_map/ppermute | solution.py:1330
  3.6 0.9 %collective-permute-start.1 = (f32[64,128]{1,0:T(8,128)S(1)}, f32[64,128]{1,0:T(8,128)S(1)}, u32[]{:S(2)}, u32[]{:S(2)}) collective-permute-start(f32[64,128]{1,0:T(8,128)S(1)} %get-tuple-element.37), channel_id=1, source_target_pairs={{1,2},{2,1},{5,6},{6,5},{9,10},{10,9},{13,14},{14,13},{17,18},{18,... | collective-permute-start | bytes 98312 | tf_op jit(solution)/shard_map/ppermute | solution.py:1329
  4.4 4.9 %copy-start.6 = (f32[4,128]{1,0:T(4,128)S(1)}, f32[4,128]{1,0:T(4,128)}, u32[]{:S(2)}) copy-start(f32[4,128]{1,0:T(4,128)} %coarse.1) | copy-start | bytes 6148
  4.5 4.9 %copy-start.5 = (s32[2,2,16]{2,1,0:T(2,128)S(1)}, s32[2,2,16]{2,1,0:T(2,128)}, u32[]{:S(2)}) copy-start(s32[2,2,16]{2,1,0:T(2,128)} %group.1) | copy-start | bytes 772
  4.5 4.8 %copy-start.4 = (f32[2,2,16]{2,1,0:T(2,128)S(1)}, f32[2,2,16]{2,1,0:T(2,128)}, u32[]{:S(2)}) copy-start(f32[2,2,16]{2,1,0:T(2,128)} %kappa.1) | copy-start | bytes 772
  4.5 4.8 %collective-permute-start.2 = (f32[64,128]{1,0:T(8,128)S(1)}, f32[64,128]{1,0:T(8,128)S(1)}, u32[]{:S(2)}, u32[]{:S(2)}) collective-permute-start(f32[64,128]{1,0:T(8,128)S(1)} %get-tuple-element.39), channel_id=1, source_target_pairs={{0,4},{4,0},{8,12},{12,8},{16,20},{20,16},{24,28},{28,24},{1,5},{5... | collective-permute-start | bytes 98312 | tf_op jit(solution)/shard_map/ppermute | solution.py:1330
  7.4 1.9 %collective-permute-start.3 = (f32[64,128]{1,0:T(8,128)S(1)}, f32[64,128]{1,0:T(8,128)S(1)}, u32[]{:S(2)}, u32[]{:S(2)}) collective-permute-start(f32[64,128]{1,0:T(8,128)S(1)} %get-tuple-element.40), channel_id=1, source_target_pairs={{4,8},{8,4},{12,16},{16,12},{20,24},{24,20},{5,9},{9,5},{13,17},{1... | collective-permute-start | bytes 98312 | tf_op jit(solution)/shard_map/ppermute | solution.py:1329
  14.1 4.5 %collective-permute-start.4 = (f32[104,128]{1,0:T(8,128)S(1)}, f32[104,128]{1,0:T(8,128)S(1)}, u32[]{:S(2)}, u32[]{:S(2)}) collective-permute-start(f32[104,128]{1,0:T(8,128)S(1)} %get-tuple-element.42), channel_id=1, source_target_pairs={{0,1},{1,0},{2,3},{3,2},{4,5},{5,4},{6,7},{7,6},{8,9},{9,8},{10,11... | collective-permute-start | bytes 159752 | tf_op jit(solution)/shard_map/ppermute | solution.py:1330
  17.8 0.9 %collective-permute-start.5 = (f32[104,128]{1,0:T(8,128)S(1)}, f32[104,128]{1,0:T(8,128)S(1)}, u32[]{:S(2)}, u32[]{:S(2)}) collective-permute-start(f32[104,128]{1,0:T(8,128)S(1)} %get-tuple-element.43), channel_id=1, source_target_pairs={{1,2},{2,1},{5,6},{6,5},{9,10},{10,9},{13,14},{14,13},{17,18},{18,... | collective-permute-start | bytes 159752 | tf_op jit(solution)/shard_map/ppermute | solution.py:1329
  18.7 7.0 %collective-permute-start.6 = (f32[136,128]{1,0:T(8,128)S(1)}, f32[136,128]{1,0:T(8,128)S(1)}, u32[]{:S(2)}, u32[]{:S(2)}) collective-permute-start(f32[136,128]{1,0:T(8,128)S(1)} %get-tuple-element.47), channel_id=1, source_target_pairs={{0,4},{4,0},{8,12},{12,8},{16,20},{20,16},{24,28},{28,24},{1,5},{5... | collective-permute-start | bytes 208904 | tf_op jit(solution)/shard_map/ppermute | solution.py:1330
  23.4 2.3 %collective-permute-start.7 = (f32[136,128]{1,0:T(8,128)S(1)}, f32[136,128]{1,0:T(8,128)S(1)}, u32[]{:S(2)}, u32[]{:S(2)}) collective-permute-start(f32[136,128]{1,0:T(8,128)S(1)} %get-tuple-element.48), channel_id=1, source_target_pairs={{4,8},{8,4},{12,16},{16,12},{20,24},{24,20},{5,9},{9,5},{13,17},{1... | collective-permute-start | bytes 208904 | tf_op jit(solution)/shard_map/ppermute | solution.py:1329
  54.5 1.3 %collective-permute-start.8 = (f32[40,128]{1,0:T(8,128)S(1)}, f32[40,128]{1,0:T(8,128)S(1)}, u32[]{:S(2)}, u32[]{:S(2)}) collective-permute-start(f32[40,128]{1,0:T(8,128)S(1)} %get-tuple-element.58), channel_id=1, source_target_pairs={{0,1},{1,0},{2,3},{3,2},{4,5},{5,4},{6,7},{7,6},{8,9},{9,8},{10,11... | collective-permute-start | bytes 61448 | tf_op jit(solution)/shard_map/ppermute | solution.py:1330
  54.6 1.2 %collective-permute-start.9 = (f32[40,128]{1,0:T(8,128)S(1)}, f32[40,128]{1,0:T(8,128)S(1)}, u32[]{:S(2)}, u32[]{:S(2)}) collective-permute-start(f32[40,128]{1,0:T(8,128)S(1)} %get-tuple-element.59), channel_id=1, source_target_pairs={{1,2},{2,1},{5,6},{6,5},{9,10},{10,9},{13,14},{14,13},{17,18},{18,... | collective-permute-start | bytes 61448 | tf_op jit(solution)/shard_map/ppermute | solution.py:1329
  55.8 3.8 %collective-permute-start.10 = (f32[40,128]{1,0:T(8,128)S(1)}, f32[40,128]{1,0:T(8,128)S(1)}, u32[]{:S(2)}, u32[]{:S(2)}) collective-permute-start(f32[40,128]{1,0:T(8,128)S(1)} %get-tuple-element.61), channel_id=1, source_target_pairs={{0,4},{4,0},{8,12},{12,8},{16,20},{20,16},{24,28},{28,24},{1,5},{5... | collective-permute-start | bytes 61448 | tf_op jit(solution)/shard_map/ppermute | solution.py:1330
  56.7 2.9 %collective-permute-start.11 = (f32[40,128]{1,0:T(8,128)S(1)}, f32[40,128]{1,0:T(8,128)S(1)}, u32[]{:S(2)}, u32[]{:S(2)}) collective-permute-start(f32[40,128]{1,0:T(8,128)S(1)} %get-tuple-element.62), channel_id=1, source_target_pairs={{4,8},{8,4},{12,16},{16,12},{20,24},{24,20},{5,9},{9,5},{13,17},{1... | collective-permute-start | bytes 61448 | tf_op jit(solution)/shard_map/ppermute | solution.py:1329

commit v5 on v4

--- a/solution.py
+++ b/solution.py
@@ -2,6 +2,7 @@
 
 import jax
 import jax.numpy as jnp
+import ml_dtypes
 import numpy as np
 from jax import lax
 from jax.experimental import pallas as pl
@@ -86,7 +87,13 @@
             tiles.append(np.repeat(inner[:, None], LANES, 1))
     eye = np.eye(elems_z)
     mats = [np.kron(eye, DERIV.T), np.kron(eye, DERIV), np.kron(eye, SCALED.T)]
-    return np.stack(tiles).astype(np.float32), np.stack(mats).astype(np.float32)
+    halves = []
+    for mat in mats:
+        high = mat.astype(ml_dtypes.bfloat16)
+        low = (mat - high.astype(np.float64)).astype(ml_dtypes.bfloat16)
+        both = np.concatenate([high, low], 1)
+        halves.append(np.concatenate([both, both], 0))
+    return np.stack(tiles).astype(np.float32), np.stack(halves)
 
 
 T_D, T_DT, T_K, T_W, T_LINE = 0, 8, 16, 24, 25
@@ -178,14 +185,19 @@
         return jnp.where(self.even_y, first, second)
 
 
-def along_x(matrix, tiles):
-    out = []
-    for i in range(8):
-        acc = None
-        for a in range(8):
-            term = float(matrix[i, a]) * tiles[a]
-            acc = term if acc is None else acc + term
-        out.append(acc)
+def along_x(matrix, tiles, sign):
+    even = [tiles[a] + tiles[7 - a] for a in range(4)]
+    odd = [tiles[a] - tiles[7 - a] for a in range(4)]
+    out = [None] * 8
+    for i in range(4):
+        plus, minus = None, None
+        for a in range(4):
+            p = float(0.5 * (matrix[i, a] + matrix[i, 7 - a])) * even[a]
+            m = float(0.5 * (matrix[i, a] - matrix[i, 7 - a])) * odd[a]
+            plus = p if plus is None else plus + p
+            minus = m if minus is None else minus + m
+        out[i] = plus + minus
+        out[7 - i] = minus - plus if sign < 0 else plus - minus
     return out
 
 
@@ -196,10 +208,19 @@
     return acc
 
 
-def along_z(rows, matrix):
+def exact_dot(rows, matrix):
     return jnp.dot(
         rows, matrix, precision=lax.Precision.HIGHEST, preferred_element_type=jnp.float32
     )
+
+
+def along_z(rows, matrix):
+    high = rows.astype(jnp.bfloat16)
+    low = (rows - high.astype(jnp.float32)).astype(jnp.bfloat16)
+    both = jnp.dot(
+        jnp.concatenate([high, low], axis=1), matrix, preferred_element_type=jnp.float32
+    )
+    return both[:, :LANES] + both[:, LANES:]
 
 
 def total(tile):
@@ -234,14 +255,10 @@
     )
 
 
-def mass_kernel(fields_in, out, xf, first, second, fields, sems):
-    copies = [pltpu.make_async_copy(fields_in.at[ch], fields.at[ch], sems.at[ch]) for ch in range(4)]
-    for copy in copies:
-        copy.start()
+def mass_kernel(fields, out, xf, first, second):
     place = Place()
     weight = weight_of(place.row) * weight_of(place.lane % NODES)
     for ch in range(4):
-        copies[ch].wait()
         tiles = [
             [
                 [
@@ -403,7 +420,8 @@
     return tile
 
 
-def fill_pack(place, kappa, group, coarse, pack, facts):
+def pack_kernel(kappa, group, coarse, pack, facts):
+    place = Place()
     pack[...] = jnp.zeros(pack.shape, jnp.float32)
     facts[...] = jnp.zeros(facts.shape, jnp.float32)
     elems = kappa.shape[2]
@@ -413,15 +431,15 @@
     blocks = coarse.shape[1] // LANES
     for ex in range(2):
         numbers = group[ex].astype(jnp.float32)
-        pack[pl.ds(2 * ex, 2), :] = along_z(kappa[ex], spread)
-        pack[pl.ds(4 + 2 * ex, 2), :] = along_z(numbers, spread)
+        pack[pl.ds(2 * ex, 2), :] = exact_dot(kappa[ex], spread)
+        pack[pl.ds(4 + 2 * ex, 2), :] = exact_dot(numbers, spread)
         row = jnp.zeros((1, LANES), jnp.float32)
         for ey in range(2):
             at = (2 * place.iy + ey) * elems
             spot = (to == at + element).astype(jnp.float32)
             after = (to == (at + 2 * elems) % LANES + element).astype(jnp.float32)
-            row = row + along_z(kappa[ex, pl.ds(ey, 1), :], spot)
-            row = row + along_z(numbers[ey : ey + 1], after)
+            row = row + exact_dot(kappa[ex, pl.ds(ey, 1), :], spot)
+            row = row + exact_dot(numbers[ey : ey + 1], after)
         facts[pl.ds(2 + ex, 1), :] = row
     for c in range(NCD):
         for j in range(blocks):
@@ -434,9 +452,7 @@
     pack_rows,
     summed,
     visc,
-    kappa,
-    group,
-    coarse,
+    pack,
     y_first,
     y_second,
     x_first,
@@ -446,8 +462,6 @@
     share,
     xf,
     inner_x,
-    pack,
-    facts,
     first,
     second,
     start,
@@ -478,7 +492,7 @@
         ch, ex, ey = index // 4, index // 2 % 2, index % 2
         coef = jnp.where(ch == 3, 1.0 / prandtl, 1.0)
         field = [start[ch, ex, a, ey] for a in range(8)]
-        grad_x = along_x(DERIV, field)
+        grad_x = along_x(DERIV, field, -1)
         flux_x, parts = [], []
         for a in range(8):
             grad_y = along_y(ctab, T_D, field[a])
@@ -493,7 +507,7 @@
             flux_x.append(nu * grad_x[a])
             flux_z[ch, ex, a, ey] = nu * slope
             parts.append(node * advect + along_y(ctab, T_DT, nu * grad_y))
-        back = along_x(DERIV.T, flux_x)
+        back = along_x(DERIV.T, flux_x, -1)
         for a in range(8):
             rhs[ch, ex, a, ey] = parts[a] + back[a]
         return carry
@@ -540,7 +554,6 @@
         place, DERIV, ctab[T_BOTTOM], ctab[T_TOP], column_of, tile_of, inner_x, first, second,
         STEP_V, STEP_EDGE,
     )
-    fill_pack(place, kappa, group, coarse, pack, facts)
     first[pl.ds(STEP_PACK, pack_rows), :] = pack[...]
     second[pl.ds(STEP_PACK, pack_rows), :] = pack[...]
 
@@ -615,7 +628,7 @@
     slope = [[None, None], [None, None]]
     for ey in range(2):
         for ex in range(2):
-            slope[ex][ey] = along_x(DERIV, [fields_new[0, ex, a, ey] for a in range(8)])
+            slope[ex][ey] = along_x(DERIV, [fields_new[0, ex, a, ey] for a in range(8)], -1)
         mid = 0.5 * (slope[0][ey][7] + slope[1][ey][0])
         slope[0][ey][7] = mid
         slope[1][ey][0] = mid
@@ -825,7 +838,7 @@
     for ex in range(2):
         for ey in range(2):
             values = [scaled[ex, a, ey] for a in range(8)]
-            slopes = along_x(SCALED, values)
+            slopes = along_x(SCALED, values, 1)
             y_next = 0 if ey == 0 else 3
             edge_row = place.row == (0 if ey == 0 else 7)
             for a in range(8):
@@ -996,7 +1009,7 @@
 def own_operator(ctab, kap, field, slope_z, ex, ey):
     weight = ctab[T_W]
     tiles = [field[ex, a, ey] for a in range(8)]
-    slopes = along_x(SCALED, tiles)
+    slopes = along_x(SCALED, tiles, 1)
     kappa = kap[pl.ds((ex + 1) * 4 + ey + 1, 1), :]
     out = []
     for a in range(8):
@@ -1358,22 +1371,23 @@
     summed, xf, first, second = call(
         mass_kernel,
         [four, xf_shape, faces, faces],
-        [four, pltpu.SemaphoreType.DMA((4,))],
-        in_specs=[pl.BlockSpec(memory_space=pltpu.HBM)],
     )(fields)
+    pack, facts = call(
+        pack_kernel,
+        [(pack_rows, LANES), TILE],
+        cost_estimate=pl.CostEstimate(flops=10**6, bytes_accessed=10**5, transcendentals=0),
+    )(inv_density, elem_group, coarse_inverse)
     y_got = swap(first, second, "gy")
     first, second = call(turn_faces_kernel, [faces, faces])(xf, *y_got)
     x_got = swap(first, second, "gx")
-    share, xf, inner_x, pack, facts, first, second = call(
+    share, xf, inner_x, first, second = call(
         functools.partial(rhs_kernel, pack_rows),
-        [four, xf_shape, inner_shape, (pack_rows, LANES), TILE, y_shape, y_shape],
+        [four, xf_shape, inner_shape, y_shape, y_shape],
         [four, four, four, four],
     )(
         summed,
         viscosity,
-        inv_density,
-        elem_group,
-        coarse_inverse,
+        pack,
         *y_got,
         *x_got,
         ctab,

time: 80.8 us -> 77.6 us (0.960)
  Pallas kernels: 12.5 us -> 9.51 us
    pallas_call x1, Pallas kernels: 4.8 us -> 3.28 us  [per_device(): call(functools.partial(rhs_kernel, pack_rows), [four, xf_shape, inner_sha...]
where the time goes in v5:
time: 77.6 us; the launch traced here: 77.3 us
  blocking collectives  43.4 us (56%)
  starting transfers between devices  16.8 us (22%)
  Pallas kernels  9.51 us (12%)
  waiting for transfers between devices  5.73 us (7%)
  local copies, waits for them, and re-layouts  1.12 us (1%)
  between operations  0.81 us (1%)
    all_to_all x2, blocking collectives, exchange_all(): return lax.all_to_all(msg, BOTH, 0, 0, tiled=True)  43.4 us
    ppermute x6, starting transfers between devices, swap(): return (lax.ppermute(first, axis, first_pairs), second_got)  12.9 us
    ppermute x6, waiting for transfers between devices, swap(): return (lax.ppermute(first, axis, first_pairs), second_got)  5.72 us
    ppermute x6, starting transfers between devices, swap(): second_got = lax.ppermute(second, axis, second_pairs)  3.92 us
    pallas_call x1, Pallas kernels, per_device(): call(functools.partial(rhs_kernel, pack_rows), [four, xf_shape, inner_sha...  3.28 us
    pallas_call x1, Pallas kernels, per_device(): call(advance_kernel, [four, one, one, (devices, 16, LANES)], [one, one])  1.86 us
  transfers between devices with their start and end apart: 12, of which 6 were waited for; matrix products, arithmetic and copies ran while one was open for 0% of the time, Pallas kernels for 0%

profile of v5, /device:TPU:0, one launch (start us, length us, event | category | flops | bytes accessed | tf_op | source)
XLA Modules:
  0.0 77.3 jit_solution(17096911374091850171)
XLA Ops:
  0.6 0.0 copy-start
  0.7 1.1 %copy-done.2 = f32[4,2,8,2,8,128]{5,4,3,2,1,0:T(8,128)S(1)} copy-done((f32[4,2,8,2,8,128]{5,4,3,2,1,0:T(8,128)S(1)}, f32[4,2,8,2,8,128]{5,4,3,2,1,0:T(8,128)}, u32[]{:S(2)}) %copy-start.2) | copy-done | bytes 524312
  1.7 0.4 shard_map.86
  2.2 0.0 copy-start.1
  2.2 0.5 collective-permute-start
  2.7 0.7 collective-permute-start.1
  3.4 0.2 collective-permute-done.y_first
  3.6 0.0 copy-start.4
  3.6 2.9 %collective-permute-start.2 = (f32[64,128]{1,0:T(8,128)S(1)}, f32[64,128]{1,0:T(8,128)S(1)}, u32[]{:S(2)}, u32[]{:S(2)}) collective-permute-start(f32[64,128]{1,0:T(8,128)S(1)} %get-tuple-element.40), channel_id=1, source_target_pairs={{0,4},{4,0},{8,12},{12,8},{16,20},{20,16},{24,28},{28,24},{1,5},{5... | collective-permute-start | bytes 98312 | tf_op jit(solution)/shard_map/ppermute | solution.py:1343
  6.5 0.7 collective-permute-start.3
  7.2 0.3 shard_map.87
  7.5 0.9 %collective-permute-done.2.x_first = f32[64,128]{1,0:T(8,128)S(1)} collective-permute-done((f32[64,128]{1,0:T(8,128)S(1)}, f32[64,128]{1,0:T(8,128)S(1)}, u32[]{:S(2)}, u32[]{:S(2)}) %collective-permute-start.2) | collective-permute-done | bytes 32800 | tf_op jit(solution)/shard_map/ppermute | solution.py:1343
  8.4 3.3 %shard_map.89 = (f32[4,2,8,2,8,128]{5,4,3,2,1,0:T(8,128)S(1)}, f32[2,4,2,8,128]{4,3,2,1,0:T(8,128)S(1)}, f32[2,2,8,128]{3,2,1,0:T(8,128)S(1)}, f32[104,128]{1,0:T(8,128)S(1)}, f32[104,128]{1,0:T(8,128)S(1)}) custom-call(f32[4,2,8,2,8,128]{5,4,3,2,1,0:T(8,128)S(1)} %get-tuple-element.35.summed, f32[2,8,2,8,128]{4,3,2,1,0:T(8,128)S(1)} %copy-done.3, ...), custom_call_target="tpu_custom_call" | custom-call | tf_op jit(solution)/shard_map/pallas_call | solution.py:1383
  11.7 3.7 %collective-permute-start.4 = (f32[104,128]{1,0:T(8,128)S(1)}, f32[104,128]{1,0:T(8,128)S(1)}, u32[]{:S(2)}, u32[]{:S(2)}) collective-permute-start(f32[104,128]{1,0:T(8,128)S(1)} %get-tuple-element.43), channel_id=1, source_target_pairs={{0,1},{1,0},{2,3},{3,2},{4,5},{5,4},{6,7},{7,6},{8,9},{9,8},{10,11... | collective-permute-start | bytes 159752 | tf_op jit(solution)/shard_map/ppermute | solution.py:1343
  15.4 0.7 collective-permute-start.5
  16.1 0.2 collective-permute-done.4.y_first
  16.4 4.7 %collective-permute-start.6 = (f32[136,128]{1,0:T(8,128)S(1)}, f32[136,128]{1,0:T(8,128)S(1)}, u32[]{:S(2)}, u32[]{:S(2)}) collective-permute-start(f32[136,128]{1,0:T(8,128)S(1)} %get-tuple-element.47), channel_id=1, source_target_pairs={{0,4},{4,0},{8,12},{12,8},{16,20},{20,16},{24,28},{28,24},{1,5},{5... | collective-permute-start | bytes 208904 | tf_op jit(solution)/shard_map/ppermute | solution.py:1343
  21.1 0.7 collective-permute-start.7
  21.7 1.6 %collective-permute-done.6.x_first = f32[136,128]{1,0:T(8,128)S(1)} collective-permute-done((f32[136,128]{1,0:T(8,128)S(1)}, f32[136,128]{1,0:T(8,128)S(1)}, u32[]{:S(2)}, u32[]{:S(2)}) %collective-permute-start.6) | collective-permute-done | bytes 69664 | tf_op jit(solution)/shard_map/ppermute | solution.py:1343
  23.4 0.1 shard_map.91
  23.5 1.9 %shard_map.92 = (f32[4,2,8,2,8,128]{5,4,3,2,1,0:T(8,128)}, f32[2,8,2,8,128]{4,3,2,1,0:T(8,128)S(1)}, f32[2,8,2,8,128]{4,3,2,1,0:T(8,128)S(1)}, f32[32,16,128]{2,1,0:T(8,128)S(1)}) custom-call(f32[4,2,8,2,8,128]{5,4,3,2,1,0:T(8,128)S(1)} %get-tuple-element.42.share, f32[104,128]{1,0:T(8,128)S(1)} %collective-permute-done.4.y_first, ...), custom_call_target="tpu_custom_call" | custom-call | tf_op jit(solution)/shard_map/pallas_call | solution.py:1405
  25.4 25.7 %all_to_all.10.got = f32[32,16,128]{2,1,0:T(8,128)S(1)} all-to-all(f32[32,16,128]{2,1,0:T(8,128)S(1)} %get-tuple-element.53), channel_id=1, replica_groups=mesh['gx'=8,'gy'=4] {'gx','gy'}, dimensions={0} | all-to-all | bytes 524288 | tf_op jit(solution)/shard_map/all_to_all | solution.py:1369
  51.0 0.7 shard_map.93
  51.7 0.1 collective-permute-start.8
  51.8 0.7 collective-permute-start.9
  52.5 0.5 collective-permute-done.8.y_first
  53.0 1.0 %collective-permute-start.10 = (f32[40,128]{1,0:T(8,128)S(1)}, f32[40,128]{1,0:T(8,128)S(1)}, u32[]{:S(2)}, u32[]{:S(2)}) collective-permute-start(f32[40,128]{1,0:T(8,128)S(1)} %get-tuple-element.61), channel_id=1, source_target_pairs={{0,4},{4,0},{8,12},{12,8},{16,20},{20,16},{24,28},{28,24},{1,5},{5... | collective-permute-start | bytes 61448 | tf_op jit(solution)/shard_map/ppermute | solution.py:1343
  54.0 0.7 collective-permute-start.11
  54.6 2.2 %collective-permute-done.10.x_first = f32[40,128]{1,0:T(8,128)S(1)} collective-permute-done((f32[40,128]{1,0:T(8,128)S(1)}, f32[40,128]{1,0:T(8,128)S(1)}, u32[]{:S(2)}, u32[]{:S(2)}) %collective-permute-start.10) | collective-permute-done | bytes 20512 | tf_op jit(solution)/shard_map/ppermute | solution.py:1343
  56.8 1.4 %shard_map.95 = (f32[2,8,2,8,128]{4,3,2,1,0:T(8,128)}, f32[2,8,2,8,128]{4,3,2,1,0:T(8,128)S(1)}, f32[32,8,128]{2,1,0:T(8,128)S(1)}) custom-call(f32[2,8,2,8,128]{4,3,2,1,0:T(8,128)S(1)} %get-tuple-element.57.own, f32[40,128]{1,0:T(8,128)S(1)} %collective-permute-done.8.y_first, f32[40,128]{1,0:T(8,128)S(1)} %collective-permute-done.9.y_second, ...), custom_call_target="tpu_custom_call" | custom-call | tf_op jit(solution)/shard_map/pallas_call | solution.py:1417
  58.2 17.7 %all_to_all.11.got = f32[32,8,128]{2,1,0:T(8,128)S(1)} all-to-all(f32[32,8,128]{2,1,0:T(8,128)S(1)} %get-tuple-element.65), channel_id=1, replica_groups=mesh['gx'=8,'gy'=4] {'gx','gy'}, dimensions={0} | all-to-all | bytes 262144 | tf_op jit(solution)/shard_map/all_to_all | solution.py:1369
  75.9 1.4 %shard_map.96 = f32[2,8,2,8,128]{4,3,2,1,0:T(8,128)} custom-call(f32[32,8,128]{2,1,0:T(8,128)S(1)} %all_to_all.11.got, f32[16,128]{1,0:T(8,128)S(1)} %get-tuple-element.51.grp, f32[2,8,2,8,128]{4,3,2,1,0:T(8,128)S(1)} %get-tuple-element.66.direction, f32[2,8,2,8,128]{4,3,2,1,0:T(8,128)S(1)} %get-tuple-element.67.smoothed), custom_call_target="tpu_custom_call" | custom-call | tf_op jit(solution)/shard_map/pallas_call | solution.py:1422
  (19 shorter events, 0.1 us)
Async XLA Ops:
  0.6 7.8 %copy-start = (bf16[3,256,256]{2,1,0:T(8,128)(2,1)S(1)}, bf16[3,256,256]{2,1,0:T(8,128)(2,1)}, u32[]{:S(2)}) copy-start(bf16[3,256,256]{2,1,0:T(8,128)(2,1)} %constant.5.clone.zmat) | copy-start | bytes 1179652
  0.6 1.1 %copy-start.2 = (f32[4,2,8,2,8,128]{5,4,3,2,1,0:T(8,128)S(1)}, f32[4,2,8,2,8,128]{5,4,3,2,1,0:T(8,128)}, u32[]{:S(2)}) copy-start(f32[4,2,8,2,8,128]{5,4,3,2,1,0:T(8,128)} %fields.1) | copy-start | bytes 1572868
  1.7 6.7 %copy-start.3 = (f32[2,8,2,8,128]{4,3,2,1,0:T(8,128)S(1)}, f32[2,8,2,8,128]{4,3,2,1,0:T(8,128)}, u32[]{:S(2)}) copy-start(f32[2,8,2,8,128]{4,3,2,1,0:T(8,128)} %visc.1) | copy-start | bytes 393220
  2.2 6.3 %copy-start.1 = (f32[30,8,128]{2,1,0:T(8,128)S(1)}, f32[30,8,128]{2,1,0:T(8,128)}, u32[]{:S(2)}) copy-start(f32[30,8,128]{2,1,0:T(8,128)} %constant.4.clone.ctab) | copy-start | bytes 368644
  2.2 1.4 %collective-permute-start = (f32[64,128]{1,0:T(8,128)S(1)}, f32[64,128]{1,0:T(8,128)S(1)}, u32[]{:S(2)}, u32[]{:S(2)}) collective-permute-start(f32[64,128]{1,0:T(8,128)S(1)} %get-tuple-element.37), channel_id=1, source_target_pairs={{0,1},{1,0},{2,3},{3,2},{4,5},{5,4},{6,7},{7,6},{8,9},{9,8},{10,11... | collective-permute-start | bytes 98312 | tf_op jit(solution)/shard_map/ppermute | solution.py:1343
  2.7 0.9 %collective-permute-start.1 = (f32[64,128]{1,0:T(8,128)S(1)}, f32[64,128]{1,0:T(8,128)S(1)}, u32[]{:S(2)}, u32[]{:S(2)}) collective-permute-start(f32[64,128]{1,0:T(8,128)S(1)} %get-tuple-element.38), channel_id=1, source_target_pairs={{1,2},{2,1},{5,6},{6,5},{9,10},{10,9},{13,14},{14,13},{17,18},{18,... | collective-permute-start | bytes 98312 | tf_op jit(solution)/shard_map/ppermute | solution.py:1342
  3.6 3.6 %copy-start.5 = (s32[2,2,16]{2,1,0:T(2,128)S(1)}, s32[2,2,16]{2,1,0:T(2,128)}, u32[]{:S(2)}) copy-start(s32[2,2,16]{2,1,0:T(2,128)} %group.1) | copy-start | bytes 772
  3.6 3.6 %copy-start.6 = (f32[4,128]{1,0:T(4,128)S(1)}, f32[4,128]{1,0:T(4,128)}, u32[]{:S(2)}) copy-start(f32[4,128]{1,0:T(4,128)} %coarse.1) | copy-start | bytes 6148
  3.6 3.6 %copy-start.4 = (f32[2,2,16]{2,1,0:T(2,128)S(1)}, f32[2,2,16]{2,1,0:T(2,128)}, u32[]{:S(2)}) copy-start(f32[2,2,16]{2,1,0:T(2,128)} %kappa.1) | copy-start | bytes 772
  3.6 4.8 %collective-permute-start.2 = (f32[64,128]{1,0:T(8,128)S(1)}, f32[64,128]{1,0:T(8,128)S(1)}, u32[]{:S(2)}, u32[]{:S(2)}) collective-permute-start(f32[64,128]{1,0:T(8,128)S(1)} %get-tuple-element.40), channel_id=1, source_target_pairs={{0,4},{4,0},{8,12},{12,8},{16,20},{20,16},{24,28},{28,24},{1,5},{5... | collective-permute-start | bytes 98312 | tf_op jit(solution)/shard_map/ppermute | solution.py:1343
  6.5 1.9 %collective-permute-start.3 = (f32[64,128]{1,0:T(8,128)S(1)}, f32[64,128]{1,0:T(8,128)S(1)}, u32[]{:S(2)}, u32[]{:S(2)}) collective-permute-start(f32[64,128]{1,0:T(8,128)S(1)} %get-tuple-element.41), channel_id=1, source_target_pairs={{4,8},{8,4},{12,16},{16,12},{20,24},{24,20},{5,9},{9,5},{13,17},{1... | collective-permute-start | bytes 98312 | tf_op jit(solution)/shard_map/ppermute | solution.py:1342
  11.7 4.6 %collective-permute-start.4 = (f32[104,128]{1,0:T(8,128)S(1)}, f32[104,128]{1,0:T(8,128)S(1)}, u32[]{:S(2)}, u32[]{:S(2)}) collective-permute-start(f32[104,128]{1,0:T(8,128)S(1)} %get-tuple-element.43), channel_id=1, source_target_pairs={{0,1},{1,0},{2,3},{3,2},{4,5},{5,4},{6,7},{7,6},{8,9},{9,8},{10,11... | collective-permute-start | bytes 159752 | tf_op jit(solution)/shard_map/ppermute | solution.py:1343
  15.4 0.9 %collective-permute-start.5 = (f32[104,128]{1,0:T(8,128)S(1)}, f32[104,128]{1,0:T(8,128)S(1)}, u32[]{:S(2)}, u32[]{:S(2)}) collective-permute-start(f32[104,128]{1,0:T(8,128)S(1)} %get-tuple-element.44), channel_id=1, source_target_pairs={{1,2},{2,1},{5,6},{6,5},{9,10},{10,9},{13,14},{14,13},{17,18},{18,... | collective-permute-start | bytes 159752 | tf_op jit(solution)/shard_map/ppermute | solution.py:1342
  16.4 7.0 %collective-permute-start.6 = (f32[136,128]{1,0:T(8,128)S(1)}, f32[136,128]{1,0:T(8,128)S(1)}, u32[]{:S(2)}, u32[]{:S(2)}) collective-permute-start(f32[136,128]{1,0:T(8,128)S(1)} %get-tuple-element.47), channel_id=1, source_target_pairs={{0,4},{4,0},{8,12},{12,8},{16,20},{20,16},{24,28},{28,24},{1,5},{5... | collective-permute-start | bytes 208904 | tf_op jit(solution)/shard_map/ppermute | solution.py:1343
  21.1 2.3 %collective-permute-start.7 = (f32[136,128]{1,0:T(8,128)S(1)}, f32[136,128]{1,0:T(8,128)S(1)}, u32[]{:S(2)}, u32[]{:S(2)}) collective-permute-start(f32[136,128]{1,0:T(8,128)S(1)} %get-tuple-element.48), channel_id=1, source_target_pairs={{4,8},{8,4},{12,16},{16,12},{20,24},{24,20},{5,9},{9,5},{13,17},{1... | collective-permute-start | bytes 208904 | tf_op jit(solution)/shard_map/ppermute | solution.py:1342
  51.7 1.3 %collective-permute-start.8 = (f32[40,128]{1,0:T(8,128)S(1)}, f32[40,128]{1,0:T(8,128)S(1)}, u32[]{:S(2)}, u32[]{:S(2)}) collective-permute-start(f32[40,128]{1,0:T(8,128)S(1)} %get-tuple-element.58), channel_id=1, source_target_pairs={{0,1},{1,0},{2,3},{3,2},{4,5},{5,4},{6,7},{7,6},{8,9},{9,8},{10,11... | collective-permute-start | bytes 61448 | tf_op jit(solution)/shard_map/ppermute | solution.py:1343
  51.8 1.2 %collective-permute-start.9 = (f32[40,128]{1,0:T(8,128)S(1)}, f32[40,128]{1,0:T(8,128)S(1)}, u32[]{:S(2)}, u32[]{:S(2)}) collective-permute-start(f32[40,128]{1,0:T(8,128)S(1)} %get-tuple-element.59), channel_id=1, source_target_pairs={{1,2},{2,1},{5,6},{6,5},{9,10},{10,9},{13,14},{14,13},{17,18},{18,... | collective-permute-start | bytes 61448 | tf_op jit(solution)/shard_map/ppermute | solution.py:1342
  53.0 3.8 %collective-permute-start.10 = (f32[40,128]{1,0:T(8,128)S(1)}, f32[40,128]{1,0:T(8,128)S(1)}, u32[]{:S(2)}, u32[]{:S(2)}) collective-permute-start(f32[40,128]{1,0:T(8,128)S(1)} %get-tuple-element.61), channel_id=1, source_target_pairs={{0,4},{4,0},{8,12},{12,8},{16,20},{20,16},{24,28},{28,24},{1,5},{5... | collective-permute-start | bytes 61448 | tf_op jit(solution)/shard_map/ppermute | solution.py:1343
  54.0 2.9 %collective-permute-start.11 = (f32[40,128]{1,0:T(8,128)S(1)}, f32[40,128]{1,0:T(8,128)S(1)}, u32[]{:S(2)}, u32[]{:S(2)}) collective-permute-start(f32[40,128]{1,0:T(8,128)S(1)} %get-tuple-element.62), channel_id=1, source_target_pairs={{4,8},{8,4},{12,16},{16,12},{20,24},{24,20},{5,9},{9,5},{13,17},{1... | collective-permute-start | bytes 61448 | tf_op jit(solution)/shard_map/ppermute | solution.py:1342

commit v6 on v5

--- a/solution.py
+++ b/solution.py
@@ -405,19 +405,23 @@
                     inv_diag[ex, a, ey] = 1.0 / (diag * (float(WEIGHTS[a]) * weight))
 
 
-def got_face_sum(place, tile, ch, ex, a, ey, y_first, y_second, x_first, x_second):
+OUTER = ((0, 0), (1, 7))
+
+
+def got_y_sum(place, tile, ch, ex, a, ey, y_first, y_second):
     row = pl.ds(ch * 16 + ex * 8 + a, 1)
     got_a, got_b = y_first[row, :], y_second[row, :]
     if ey == 0:
         tile = tile + jnp.where(place.row == 0, place.before_y(got_a, got_b), 0.0)
     else:
         tile = tile + jnp.where(place.row == 7, place.after_y(got_a, got_b), 0.0)
-    rows = pl.ds(pl.multiple_of(ch * 16 + ey * 8, 8), 8)
-    if ex == 0 and a == 0:
-        tile = tile + place.before_x(x_first[rows, :], x_second[rows, :])
-    if ex == 1 and a == 7:
-        tile = tile + place.after_x(x_first[rows, :], x_second[rows, :])
     return tile
+
+
+def got_x_sum(place, tile, ch, ex, ey, x_first, x_second):
+    rows = pl.ds(ch * 16 + ey * 8, 8)
+    pick = place.before_x if ex == 0 else place.after_x
+    return tile + pick(x_first[rows, :], x_second[rows, :])
 
 
 def pack_kernel(kappa, group, coarse, pack, facts):
@@ -448,13 +452,63 @@
         facts[pl.ds(4 + c, 1), :] = coarse[pl.ds(c, 1), pl.ds(0, LANES)]
 
 
+def prepare_kernel(
+    summed, visc, y_first, y_second, ctab, zmat, start, part, grad_z, flux_z
+):
+    place = Place()
+    weight = ctab[T_W]
+    inv_mass = [1.0 / (weight * place.mult_tile(ey)) for ey in range(2)]
+
+    def begin(ch, carry):
+        for ex in range(2):
+            for a in range(8):
+                for ey in range(2):
+                    tile = got_y_sum(
+                        place, summed[ch, ex, a, ey], ch, ex, a, ey, y_first, y_second
+                    )
+                    scale = place.inv_x(ex, a) * float(1.0 / WEIGHTS[a])
+                    start[ch, ex, a, ey] = tile * (inv_mass[ey] * scale)
+        return carry
+
+    lax.fori_loop(0, 4, begin, 0)
+    grad_z[...] = along_z(start[...].reshape(1024, LANES), zmat[0]).reshape(grad_z.shape)
+
+    def column(index, carry):
+        ch, ey = index // 2, index % 2
+        coef = jnp.where(ch == 3, 1.0 / prandtl, 1.0)
+        for ex in range(2):
+            for a in range(8):
+                if (ex, a) in OUTER:
+                    continue
+                parts = across(
+                    ctab, weight, a, coef, start[ch, ex, a, ey], grad_z[ch, ex, a, ey],
+                    start[1, ex, a, ey], start[2, ex, a, ey], visc[ex, a, ey],
+                )
+                part[ch, ex, a, ey], flux_z[ch, ex, a, ey] = parts
+        return carry
+
+    lax.fori_loop(0, 8, column, 0)
+    for ch in range(4):
+        for ex in range(2):
+            inner = pl.ds(1 - ex, 7)
+            back = along_z(flux_z[ch, ex, inner].reshape(112, LANES), zmat[1])
+            part[ch, ex, inner] = part[ch, ex, inner] + back.reshape(7, 2, 8, LANES)
+
+
+def across(ctab, weight, a, coef, value, grad_z, flow_y, flow_z, visc):
+    node = float(WEIGHTS[a]) * weight
+    grad_y = along_y(ctab, T_D, value)
+    nu = visc * node * coef
+    part = node * (flow_y * grad_y + flow_z * grad_z) + along_y(ctab, T_DT, nu * grad_y)
+    return part, nu * grad_z
+
+
 def rhs_kernel(
     pack_rows,
-    summed,
+    begun,
+    given,
     visc,
     pack,
-    y_first,
-    y_second,
     x_first,
     x_second,
     ctab,
@@ -464,62 +518,64 @@
     inner_x,
     first,
     second,
-    start,
     rhs,
-    grad_z,
-    flux_z,
+    edge,
+    edge_z,
+    edge_part,
 ):
     place = Place()
     weight = ctab[T_W]
     inv_mass = [1.0 / (weight * place.mult_tile(ey)) for ey in range(2)]
-
-    def begin(ch, carry):
+    for ch in range(4):
+        for side, (ex, a) in enumerate(OUTER):
+            scale = place.inv_x(ex, a) * float(1.0 / WEIGHTS[a])
+            for ey in range(2):
+                zero = jnp.zeros(TILE, jnp.float32)
+                came = got_x_sum(place, zero, ch, ex, ey, x_first, x_second)
+                edge[ch, side, ey] = begun[ch, ex, a, ey] + came * (inv_mass[ey] * scale)
+    edge_z[...] = along_z(edge[...].reshape(128, LANES), zmat[0]).reshape(edge.shape)
+    for ch in range(4):
+        coef = 1.0 / prandtl if ch == 3 else 1.0
+        for side, (ex, a) in enumerate(OUTER):
+            for ey in range(2):
+                parts = across(
+                    ctab, weight, a, coef, edge[ch, side, ey], edge_z[ch, side, ey],
+                    edge[1, side, ey], edge[2, side, ey], visc[ex, a, ey],
+                )
+                edge_part[ch, side, ey], edge_z[ch, side, ey] = parts
+    edge_part[...] = edge_part[...] + along_z(
+        edge_z[...].reshape(128, LANES), zmat[1]
+    ).reshape(edge.shape)
+
+    def value_of(ch, ex, a, ey):
+        if (ex, a) in OUTER:
+            return edge[ch, ex, ey]
+        return begun[ch, ex, a, ey]
+
+    def column(index, carry):
+        ch, ey = index // 2, index % 2
+        coef = jnp.where(ch == 3, 1.0 / prandtl, 1.0)
         for ex in range(2):
+            field = [value_of(ch, ex, a, ey) for a in range(8)]
+            grad_x = along_x(DERIV, field, -1)
+            flux_x, parts = [], []
             for a in range(8):
-                for ey in range(2):
-                    tile = got_face_sum(
-                        place, summed[ch, ex, a, ey], ch, ex, a, ey,
-                        y_first, y_second, x_first, x_second,
-                    )
-                    scale = place.inv_x(ex, a) * float(1.0 / WEIGHTS[a])
-                    start[ch, ex, a, ey] = tile * (inv_mass[ey] * scale)
+                node = float(WEIGHTS[a]) * weight
+                flux_x.append(visc[ex, a, ey] * node * coef * grad_x[a])
+                known = edge_part[ch, ex, ey] if (ex, a) in OUTER else given[ch, ex, a, ey]
+                parts.append(known + node * (value_of(0, ex, a, ey) * grad_x[a]))
+            back = along_x(DERIV.T, flux_x, -1)
+            for a in range(8):
+                rhs[ch, ex, a, ey] = parts[a] + back[a]
         return carry
 
-    lax.fori_loop(0, 4, begin, 0)
-    grad_z[...] = along_z(start[...].reshape(1024, LANES), zmat[0]).reshape(grad_z.shape)
-
-    def column(index, carry):
-        ch, ex, ey = index // 4, index // 2 % 2, index % 2
-        coef = jnp.where(ch == 3, 1.0 / prandtl, 1.0)
-        field = [start[ch, ex, a, ey] for a in range(8)]
-        grad_x = along_x(DERIV, field, -1)
-        flux_x, parts = [], []
-        for a in range(8):
-            grad_y = along_y(ctab, T_D, field[a])
-            slope = grad_z[ch, ex, a, ey]
-            node = float(WEIGHTS[a]) * weight
-            advect = (
-                start[0, ex, a, ey] * grad_x[a]
-                + start[1, ex, a, ey] * grad_y
-                + start[2, ex, a, ey] * slope
-            )
-            nu = visc[ex, a, ey] * node * coef
-            flux_x.append(nu * grad_x[a])
-            flux_z[ch, ex, a, ey] = nu * slope
-            parts.append(node * advect + along_y(ctab, T_DT, nu * grad_y))
-        back = along_x(DERIV.T, flux_x, -1)
-        for a in range(8):
-            rhs[ch, ex, a, ey] = parts[a] + back[a]
-        return carry
-
-    lax.fori_loop(0, 16, column, 0)
-    grad_z[...] = along_z(flux_z[...].reshape(1024, LANES), zmat[1]).reshape(grad_z.shape)
+    lax.fori_loop(0, 8, column, 0)
 
     def finish(ch, carry):
         tiles = [
             [
                 [
-                    place.join_z(-(rhs[ch, ex, a, ey] + grad_z[ch, ex, a, ey]))
+                    place.join_z(-rhs[ch, ex, a, ey])
                     for ey in range(2)
                 ]
                 for a in range(8)
@@ -531,7 +587,8 @@
             for a in range(8):
                 scale = place.inv_x(ex, a) * float(dt_step / WEIGHTS[a])
                 for ey in range(2):
-                    part = start[ch, ex, a, ey] * (place.share_y(ey) * place.share_x(ex, a))
+                    value = value_of(ch, ex, a, ey)
+                    part = value * (place.share_y(ey) * place.share_x(ex, a))
                     share[ch, ex, a, ey] = part + tiles[ex][a][ey] * (inv_mass[ey] * scale)
         return carry
 
@@ -584,8 +641,46 @@
             second[row, :] = place.after_y(low, high)
 
 
+def cross_flow(place, ctab, flow, slopes, rows, inv_y, inv_z):
+    below, above = rows
+    below = (below - float(DERIV[0, 0]) * flow[0]) * jnp.where(place.prev_y, 1.0, 0.0)
+    above = (above - float(DERIV[7, 7]) * flow[1]) * jnp.where(place.next_y, 1.0, 0.0)
+    grad_y = list(place.join_y(*[along_y(ctab, T_D, tile) for tile in flow]))
+    grad_y[0] = grad_y[0] + jnp.where(place.row == 0, below, 0.0)
+    grad_y[1] = grad_y[1] + jnp.where(place.row == 7, above, 0.0)
+    return [grad_y[ey] * inv_y[ey] + place.join_z(slopes[ey]) * inv_z for ey in range(2)]
+
+
+def approach_kernel(share, y_first, y_second, ctab, zmat, fields_new, part, grad_z):
+    place = Place()
+
+    def step(ch, carry):
+        for ex in range(2):
+            for a in range(8):
+                for ey in range(2):
+                    fields_new[ch, ex, a, ey] = got_y_sum(
+                        place, share[ch, ex, a, ey], ch, ex, a, ey, y_first, y_second
+                    )
+        return carry
+
+    lax.fori_loop(0, 4, step, 0)
+    grad_z[...] = along_z(fields_new[2].reshape(256, LANES), zmat[0]).reshape(grad_z.shape)
+    inv_y = [place.inv_y(ey) for ey in range(2)]
+    inv_z = place.inv_z()
+    for ex in range(2):
+        for a in range(8):
+            if (ex, a) in OUTER:
+                continue
+            flow = [fields_new[1, ex, a, ey] for ey in range(2)]
+            rows = inner_along_y(place, y_first, y_second, None, None, ex, a, STEP_V, STEP_EDGE)
+            slopes = [grad_z[ex, a, ey] for ey in range(2)]
+            both = cross_flow(place, ctab, flow, slopes, rows, inv_y, inv_z)
+            part[ex, a, 0], part[ex, a, 1] = both
+
+
 def advance_kernel(
-    share,
+    begun,
+    given,
     y_first,
     y_second,
     x_first,
@@ -601,6 +696,8 @@
     msg,
     grad_z,
     scaled,
+    edge,
+    part,
 ):
     place = Place()
     weight = ctab[T_W]
@@ -613,18 +710,25 @@
         rows = pl.ds(row, count)
         return place.after_x(x_first[rows, :], x_second[rows, :])
 
-    def step(ch, carry):
-        for ex in range(2):
-            for a in range(8):
-                for ey in range(2):
-                    fields_new[ch, ex, a, ey] = got_face_sum(
-                        place, share[ch, ex, a, ey], ch, ex, a, ey,
-                        y_first, y_second, x_first, x_second,
-                    )
-        return carry
-
-    lax.fori_loop(0, 4, step, 0)
-    grad_z[...] = along_z(fields_new[2].reshape(256, LANES), zmat[0]).reshape(grad_z.shape)
+    fields_new[...] = begun[...]
+    part[...] = given[...]
+    for ch in range(4):
+        for ex, a in OUTER:
+            for ey in range(2):
+                fields_new[ch, ex, a, ey] = got_x_sum(
+                    place, begun[ch, ex, a, ey], ch, ex, ey, x_first, x_second
+                )
+    for side, (ex, a) in enumerate(OUTER):
+        edge[side] = fields_new[2, ex, a]
+    edge[...] = along_z(edge[...].reshape(32, LANES), zmat[0]).reshape(edge.shape)
+    inv_y = [place.inv_y(ey) for ey in range(2)]
+    inv_z = place.inv_z()
+    for side, (ex, a) in enumerate(OUTER):
+        flow = [fields_new[1, ex, a, ey] for ey in range(2)]
+        rows = inner_along_y(place, y_first, y_second, before, after, ex, a, STEP_V, STEP_EDGE)
+        slopes = [edge[side, ey] for ey in range(2)]
+        both = cross_flow(place, ctab, flow, slopes, rows, inv_y, inv_z)
+        part[ex, a, 0], part[ex, a, 1] = both
     slope = [[None, None], [None, None]]
     for ey in range(2):
         for ex in range(2):
@@ -639,28 +743,11 @@
         slope[1][ey][7] = jnp.where(place.next_x, 0.5 * inner_high, high)
     sums = [[jnp.zeros(TILE, jnp.float32) for _ in range(2)] for _ in range(2)]
     inv_mult = [1.0 / place.mult_tile(ey) for ey in range(2)]
-    inv_y = [place.inv_y(ey) for ey in range(2)]
-    inv_z = place.inv_z()
     mass = [weight * place.mult_tile(ey) for ey in range(2)]
-    there_low = jnp.where(place.prev_y, 1.0, 0.0)
-    there_high = jnp.where(place.next_y, 1.0, 0.0)
     for ex in range(2):
         for a in range(8):
-            flow = [fields_new[1, ex, a, ey] for ey in range(2)]
-            below, above = inner_along_y(
-                place, y_first, y_second, before, after, ex, a, STEP_V, STEP_EDGE
-            )
-            below = (below - float(DERIV[0, 0]) * flow[0]) * there_low
-            above = (above - float(DERIV[7, 7]) * flow[1]) * there_high
-            grad_y = list(place.join_y(*[along_y(ctab, T_D, tile) for tile in flow]))
-            grad_y[0] = grad_y[0] + jnp.where(place.row == 0, below, 0.0)
-            grad_y[1] = grad_y[1] + jnp.where(place.row == 7, above, 0.0)
             for ey in range(2):
-                div = (
-                    slope[ex][ey][a]
-                    + grad_y[ey] * inv_y[ey]
-                    + place.join_z(grad_z[ex, a, ey]) * inv_z
-                )
+                div = slope[ex][ey][a] + part[ex, a, ey]
                 value = div * (mass[ey] * (place.mult_x(ex, a) * float(-WEIGHTS[a])))
                 resid[ex, a, ey] = value
                 scaled[ex, a, ey] = value * inv_diag[ex, a, ey] * float(1.0 / THETA)
@@ -709,6 +796,8 @@
     row = pl.ds(at + ex * 8 + a, 1)
     got_a, got_b = y_first[row, :], y_second[row, :]
     below, above = place.before_y(got_a, got_b), place.after_y(got_a, got_b)
+    if before is None:
+        return below, above
     if (ex, a) == (0, 0):
         below = below + before(edge, 1)
         above = above + before(edge + 1, 1)
@@ -788,8 +877,48 @@
     lax.fori_loop(0, msg.shape[0], send, 0, unroll=msg.shape[0] <= 64)
 
 
+def cross_image(place, ctab, kap, value, flat, inner, ex, ey):
+    slope_y = along_y(ctab, T_K, value)
+    turned_y = inner + float(SCALED[0, 0]) * value
+    own = kap[pl.ds((ex + 1) * 4 + ey + 1, 1), :] * (slope_y + flat) + sigma_p * value
+    beyond = kap[pl.ds((ex + 1) * 4 + 3 * ey, 1), :] * (turned_y + flat) + sigma_p * value
+    return own + jnp.where(beyond_y(place, ey), beyond, 0.0), slope_y, turned_y
+
+
+def beyond_y(place, ey):
+    if ey == 0:
+        return (place.row == 0) & place.prev_y
+    return (place.row == 7) & place.next_y
+
+
+def ready_kernel(
+    own, y_first, y_second, inv_diag, kap, ctab, zmat, image, scaled, part, slope_z
+):
+    place = Place()
+    for ex in range(2):
+        for a in range(8):
+            for ey in range(2):
+                tile = got_y_sum(place, own[ex, a, ey], 0, ex, a, ey, y_first, y_second)
+                image[ex, a, ey] = tile
+                scaled[ex, a, ey] = tile * inv_diag[ex, a, ey] * float(1.0 / THETA)
+    slope_z[...] = along_z(scaled[...].reshape(256, LANES), zmat[2]).reshape(slope_z.shape)
+    for ex in range(2):
+        for a in range(8):
+            if (ex, a) in OUTER:
+                continue
+            rows = inner_along_y(
+                place, y_first, y_second, None, None, ex, a, SMOOTH_Y, SMOOTH_EDGE
+            )
+            for ey in range(2):
+                part[ex, a, ey] = cross_image(
+                    place, ctab, kap, scaled[ex, a, ey], slope_z[ex, a, ey], rows[ey], ex, ey
+                )[0]
+
+
 def smooth_kernel(
-    own,
+    begun,
+    begun_scaled,
+    given,
     y_first,
     y_second,
     x_first,
@@ -806,6 +935,7 @@
     msg,
     scaled,
     slope_z,
+    edge,
 ):
     place = Place()
     weight = ctab[T_W]
@@ -819,49 +949,46 @@
         rows = pl.ds(row, count)
         return place.after_x(x_first[rows, :], x_second[rows, :])
 
-    for ex in range(2):
-        for a in range(8):
-            for ey in range(2):
-                tile = got_face_sum(
-                    place, own[ex, a, ey], 0, ex, a, ey, y_first, y_second, x_first, x_second
-                )
-                image[ex, a, ey] = tile
-                scaled[ex, a, ey] = tile * inv_diag[ex, a, ey] * float(1.0 / THETA)
-    slope_z[...] = along_z(scaled[...].reshape(256, LANES), zmat[2]).reshape(slope_z.shape)
-    there_x = (jnp.where(place.prev_x, 1.0, 0.0), jnp.where(place.next_x, 1.0, 0.0))
-    there_y = (jnp.where(place.prev_y, 1.0, 0.0), jnp.where(place.next_y, 1.0, 0.0))
-
-    def kappa_of(x, y):
-        return kap[pl.ds(x * 4 + y, 1), :]
-
+    image[...] = begun[...]
+    scaled[...] = begun_scaled[...]
+    for side, (ex, a) in enumerate(OUTER):
+        for ey in range(2):
+            tile = got_x_sum(place, begun[ex, a, ey], 0, ex, ey, x_first, x_second)
+            image[ex, a, ey] = tile
+            scaled[ex, a, ey] = tile * inv_diag[ex, a, ey] * float(1.0 / THETA)
+            edge[side, ey] = scaled[ex, a, ey]
+    edge[...] = along_z(edge[...].reshape(32, LANES), zmat[2]).reshape(edge.shape)
+    there_x = (place.prev_x, place.next_x)
+    zero = jnp.zeros(TILE, jnp.float32)
     tiles = [[[None, None] for _ in range(8)] for _ in range(2)]
     for ex in range(2):
+        a_out = OUTER[ex][1]
+        rows = inner_along_y(
+            place, y_first, y_second, before, after, ex, a_out, SMOOTH_Y, SMOOTH_EDGE
+        )
         for ey in range(2):
             values = [scaled[ex, a, ey] for a in range(8)]
             slopes = along_x(SCALED, values, 1)
-            y_next = 0 if ey == 0 else 3
-            edge_row = place.row == (0 if ey == 0 else 7)
+            far_row = beyond_y(place, ey)
+            beside = kap[pl.ds((ex + 1) * 4 + 3 * ey, 1), :]
+            kappa = kap[pl.ds((ex + 1) * 4 + ey + 1, 1), :] + jnp.where(far_row, beside, 0.0)
             for a in range(8):
-                value = values[a]
-                slope_y = along_y(ctab, T_K, value)
-                flat = slope_z[ex, a, ey]
-                same = slopes[a] + slope_y + flat
-                acc = kappa_of(ex + 1, ey + 1) * same + sigma_p * value
-                inner = inner_along_y(
-                    place, y_first, y_second, before, after, ex, a, SMOOTH_Y, SMOOTH_EDGE
-                )[ey]
-                turned_y = inner + corner * value
-                beyond = kappa_of(ex + 1, y_next) * (slopes[a] + turned_y + flat)
-                beyond = (beyond + sigma_p * value) * there_y[ey]
-                if (ex, a) in ((0, 0), (1, 7)):
-                    x_next = 0 if ex == 0 else 3
+                if a != a_out:
+                    acc = given[ex, a, ey]
+                else:
+                    value, flat = values[a], edge[ex, ey]
+                    acc, slope_y, turned_y = cross_image(
+                        place, ctab, kap, value, flat, rows[ey], ex, ey
+                    )
+                    x_next = 3 * ex
                     get = before if ex == 0 else after
                     turned_x = get(SMOOTH_X + ey * 8) + corner * value
-                    side = kappa_of(x_next, ey + 1) * (turned_x + slope_y + flat)
-                    acc = acc + (side + sigma_p * value) * there_x[ex]
-                    far = kappa_of(x_next, y_next) * (turned_x + turned_y + flat)
-                    beyond = beyond + (far + sigma_p * value) * (there_x[ex] * there_y[ey])
-                acc = acc + jnp.where(edge_row, beyond, 0.0)
+                    side = kap[pl.ds(x_next * 4 + ey + 1, 1), :] * (turned_x + slope_y + flat)
+                    far = kap[pl.ds(x_next * 4 + 3 * ey, 1), :] * (turned_x + turned_y + flat)
+                    side = side + sigma_p * value
+                    side = side + jnp.where(far_row, far + sigma_p * value, zero)
+                    acc = acc + jnp.where(there_x[ex], side, zero)
+                acc = acc + kappa * slopes[a]
                 tiles[ex][a][ey] = place.join_z(acc * (float(WEIGHTS[a]) * weight))
     join_own(place, tiles)
     inv_mult = [1.0 / place.mult_tile(ey) for ey in range(2)]
@@ -1368,6 +1495,7 @@
     def exchange_all(msg):
         return lax.all_to_all(msg, BOTH, 0, 0, tiled=True)
 
+    beside = pl.CostEstimate(flops=10**7, bytes_accessed=10**6, transcendentals=0)
     summed, xf, first, second = call(
         mass_kernel,
         [four, xf_shape, faces, faces],
@@ -1375,24 +1503,20 @@
     pack, facts = call(
         pack_kernel,
         [(pack_rows, LANES), TILE],
-        cost_estimate=pl.CostEstimate(flops=10**6, bytes_accessed=10**5, transcendentals=0),
+        cost_estimate=beside,
     )(inv_density, elem_group, coarse_inverse)
     y_got = swap(first, second, "gy")
     first, second = call(turn_faces_kernel, [faces, faces])(xf, *y_got)
     x_got = swap(first, second, "gx")
+    begun, given = call(prepare_kernel, [four, four], [four, four], cost_estimate=beside)(
+        summed, viscosity, *y_got, ctab, zmat
+    )
+    edge_shape = (4, 2, 2, 8, LANES)
     share, xf, inner_x, first, second = call(
         functools.partial(rhs_kernel, pack_rows),
         [four, xf_shape, inner_shape, y_shape, y_shape],
-        [four, four, four, four],
-    )(
-        summed,
-        viscosity,
-        pack,
-        *y_got,
-        *x_got,
-        ctab,
-        zmat,
-    )
+        [four, edge_shape, edge_shape, edge_shape],
+    )(begun, given, viscosity, pack, *x_got, ctab, zmat)
     y_got = swap(first, second, "gy")
     first, second = call(functools.partial(turn_step_kernel, pack_rows), [x_shape, x_shape])(
         xf, inner_x, pack, *y_got
@@ -1402,9 +1526,15 @@
         functools.partial(setup_kernel, pack_rows, blocks),
         [one, (16, LANES), (16, LANES), (9 * NCD * blocks, LANES)],
     )(pack, *y_got, *x_got, ctab)
+    begun, given = call(approach_kernel, [four, one], [one], cost_estimate=beside)(
+        share, *y_got, ctab, zmat
+    )
+    side_shape = (2, 2, 8, LANES)
     fields_new, resid, own, msg = call(
-        advance_kernel, [four, one, one, (devices, 16, LANES)], [one, one]
-    )(share, *y_got, *x_got, inv_diag, kap, grp, ctab, zmat)
+        advance_kernel,
+        [four, one, one, (devices, 16, LANES)],
+        [one, one, side_shape, one],
+    )(begun, given, *y_got, *x_got, inv_diag, kap, grp, ctab, zmat)
     got = exchange_all(msg)
     direction, own, inner_x, first, second, extra = call(
         functools.partial(first_direction_kernel, blocks),
@@ -1414,9 +1544,16 @@
     y_got = swap(first, second, "gy")
     first, second = call(turn_smooth_kernel, [smooth_shape, smooth_shape])(own, inner_x, *y_got)
     x_got = swap(first, second, "gx")
+    begun, begun_scaled, given = call(
+        ready_kernel, [one, one, one], [one], cost_estimate=beside
+    )(own, *y_got, inv_diag, kap, ctab, zmat)
     image, image_smoothed, msg = call(
-        smooth_kernel, [one, one, (devices, 8, LANES) if grid_fits else rows], [one, one]
-    )(own, *y_got, *x_got, inv_diag, kap, grp, extra, facts, ctab, zmat)
+        smooth_kernel,
+        [one, one, (devices, 8, LANES) if grid_fits else rows],
+        [one, one, side_shape],
+    )(
+        begun, begun_scaled, given, *y_got, *x_got, inv_diag, kap, grp, extra, facts, ctab, zmat
+    )
     got = exchange_all(msg)
     if grid_fits:
         (pressure,) = call(

time: 77.6 us -> 75.4 us (0.972)
  waiting for transfers between devices: 5.73 us -> 4.13 us
  blocking collectives: 43.4 us -> 42.4 us
    pallas_call x2 -> x5, Pallas kernels: 2.13 us -> 4.4 us  [the longest x1 1.9 us: per_device(): call(prepare_kernel, [four, four], [four, four], cost_estimate=beside)]
    pallas_call x1, Pallas kernels: 3.28 us -> 1.51 us  [per_device(): call(functools.partial(rhs_kernel, pack_rows), [four, xf_shape, inner_sha...]
    ppermute x6, waiting for transfers between devices: 5.72 us -> 4.12 us  [swap(): return (lax.ppermute(first, axis, first_pairs), second_got)]
    all_to_all x2, blocking collectives: 43.4 us -> 42.4 us  [exchange_all(): return lax.all_to_all(msg, BOTH, 0, 0, tiled=True)]
  transfers between devices with their start and end apart: 12 -> 12, of which waited for: 6 -> 5; matrix products, arithmetic and copies ran while one was open for 0% -> 0% of each run, Pallas kernels for 0% -> 4%
where the time goes in v6:
time: 75.4 us; the launch traced here: 75.1 us
  blocking collectives  42.4 us (56%)
  starting transfers between devices  16.7 us (22%)
  Pallas kernels  9.87 us (13%)
  waiting for transfers between devices  4.13 us (5%)
  local copies, waits for them, and re-layouts  1.12 us (1%)
  between operations  0.84 us (1%)
    all_to_all x2, blocking collectives, exchange_all(): return lax.all_to_all(msg, BOTH, 0, 0, tiled=True)  42.4 us
    ppermute x6, starting transfers between devices, swap(): return (lax.ppermute(first, axis, first_pairs), second_got)  12.8 us
    ppermute x6, waiting for transfers between devices, swap(): return (lax.ppermute(first, axis, first_pairs), second_got)  4.12 us
    ppermute x6, starting transfers between devices, swap(): second_got = lax.ppermute(second, axis, second_pairs)  3.92 us
    pallas_call x1, Pallas kernels, per_device(): call(prepare_kernel, [four, four], [four, four], cost_estimate=beside)  1.9 us
    pallas_call x1, Pallas kernels, per_device(): call(advance_kernel, [four, one, one, (devices, 16, LANES)], [one, one, s...  1.57 us
    pallas_call x1, Pallas kernels, per_device(): call(functools.partial(rhs_kernel, pack_rows), [four, xf_shape, inner_sha...  1.51 us
  transfers between devices with their start and end apart: 12, of which 5 were waited for; matrix products, arithmetic and copies ran while one was open for 0% of the time, Pallas kernels for 4%

profile of v6, /device:TPU:0, one launch (start us, length us, event | category | flops | bytes accessed | tf_op | source)
XLA Modules:
  0.0 75.1 jit_solution(17371420953495604478)
XLA Ops:
  0.7 1.1 %copy-done.3 = f32[4,2,8,2,8,128]{5,4,3,2,1,0:T(8,128)S(1)} copy-done((f32[4,2,8,2,8,128]{5,4,3,2,1,0:T(8,128)S(1)}, f32[4,2,8,2,8,128]{5,4,3,2,1,0:T(8,128)}, u32[]{:S(2)}) %copy-start.3) | copy-done | bytes 524312
  1.7 0.4 shard_map.86
  2.2 0.0 copy-start.1
  2.2 0.5 collective-permute-start
  2.7 0.7 collective-permute-start.1
  3.4 0.2 collective-permute-done.y_first
  3.6 2.9 %collective-permute-start.2 = (f32[64,128]{1,0:T(8,128)S(1)}, f32[64,128]{1,0:T(8,128)S(1)}, u32[]{:S(2)}, u32[]{:S(2)}) collective-permute-start(f32[64,128]{1,0:T(8,128)S(1)} %get-tuple-element.49), channel_id=1, source_target_pairs={{0,4},{4,0},{8,12},{12,8},{16,20},{20,16},{24,28},{28,24},{1,5},{5... | collective-permute-start | bytes 98312 | tf_op jit(solution)/shard_map/ppermute | solution.py:1470
  6.5 0.7 collective-permute-start.3
  7.2 0.3 shard_map.88
  7.5 1.9 %shard_map.87 = (f32[4,2,8,2,8,128]{5,4,3,2,1,0:T(8,128)S(1)}, f32[4,2,8,2,8,128]{5,4,3,2,1,0:T(8,128)S(1)}) custom-call(f32[4,2,8,2,8,128]{5,4,3,2,1,0:T(8,128)S(1)} %get-tuple-element.42.summed, f32[2,8,2,8,128]{4,3,2,1,0:T(8,128)S(1)} %copy-done.2, f32[64,128]{1,0:T(8,128)S(1)} %collective-permute-done.y_first, ...), custom_call_target="tpu_custom_call" | custom-call | flops 10000000 | bytes 1000000 | tf_op jit(solution)/shard_map/pallas_call | solution.py:1511
  9.4 1.5 %shard_map.90 = (f32[4,2,8,2,8,128]{5,4,3,2,1,0:T(8,128)S(1)}, f32[2,4,2,8,128]{4,3,2,1,0:T(8,128)S(1)}, f32[2,2,8,128]{3,2,1,0:T(8,128)S(1)}, f32[104,128]{1,0:T(8,128)S(1)}, f32[104,128]{1,0:T(8,128)S(1)}) custom-call(f32[4,2,8,2,8,128]{5,4,3,2,1,0:T(8,128)S(1)} %get-tuple-element.45.begun, f32[4,2,8,2,8,128]{5,4,3,2,1,0:T(8,128)S(1)} %get-tuple-element.46.given, ...), custom_call_target="tpu_custom_call" | custom-call | tf_op jit(solution)/shard_map/pallas_call | solution.py:1515
  10.9 4.3 %collective-permute-start.4 = (f32[104,128]{1,0:T(8,128)S(1)}, f32[104,128]{1,0:T(8,128)S(1)}, u32[]{:S(2)}, u32[]{:S(2)}) collective-permute-start(f32[104,128]{1,0:T(8,128)S(1)} %get-tuple-element.52), channel_id=1, source_target_pairs={{0,1},{1,0},{2,3},{3,2},{4,5},{5,4},{6,7},{7,6},{8,9},{9,8},{10,11... | collective-permute-start | bytes 159752 | tf_op jit(solution)/shard_map/ppermute | solution.py:1470
  15.2 0.7 collective-permute-start.5
  15.9 0.2 collective-permute-done.4.y_first
  16.2 4.1 %collective-permute-start.6 = (f32[136,128]{1,0:T(8,128)S(1)}, f32[136,128]{1,0:T(8,128)S(1)}, u32[]{:S(2)}, u32[]{:S(2)}) collective-permute-start(f32[136,128]{1,0:T(8,128)S(1)} %get-tuple-element.58), channel_id=1, source_target_pairs={{0,4},{4,0},{8,12},{12,8},{16,20},{20,16},{24,28},{28,24},{1,5},{5... | collective-permute-start | bytes 208904 | tf_op jit(solution)/shard_map/ppermute | solution.py:1470
  20.2 0.7 collective-permute-start.7
  20.9 0.4 shard_map.91
  21.3 1.2 %collective-permute-done.6.x_first = f32[136,128]{1,0:T(8,128)S(1)} collective-permute-done((f32[136,128]{1,0:T(8,128)S(1)}, f32[136,128]{1,0:T(8,128)S(1)}, u32[]{:S(2)}, u32[]{:S(2)}) %collective-permute-start.6) | collective-permute-done | bytes 69664 | tf_op jit(solution)/shard_map/ppermute | solution.py:1470
  22.5 0.1 shard_map.93
  22.7 1.6 %shard_map.94 = (f32[4,2,8,2,8,128]{5,4,3,2,1,0:T(8,128)}, f32[2,8,2,8,128]{4,3,2,1,0:T(8,128)S(1)}, f32[2,8,2,8,128]{4,3,2,1,0:T(8,128)S(1)}, f32[32,16,128]{2,1,0:T(8,128)S(1)}) custom-call(f32[4,2,8,2,8,128]{5,4,3,2,1,0:T(8,128)S(1)} %get-tuple-element.54.begun, f32[2,8,2,8,128]{4,3,2,1,0:T(8,128)S(1)} %get-tuple-element.55.given, ...), custom_call_target="tpu_custom_call" | custom-call | tf_op jit(solution)/shard_map/pallas_call | solution.py:1533
  24.2 24.7 %all_to_all.10.got = f32[32,16,128]{2,1,0:T(8,128)S(1)} all-to-all(f32[32,16,128]{2,1,0:T(8,128)S(1)} %get-tuple-element.64), channel_id=1, replica_groups=mesh['gx'=8,'gy'=4] {'gx','gy'}, dimensions={0} | all-to-all | bytes 524288 | tf_op jit(solution)/shard_map/all_to_all | solution.py:1496
  48.9 0.7 shard_map.95
  49.6 0.1 collective-permute-start.8
  49.7 0.7 collective-permute-start.9
  50.4 0.5 collective-permute-done.8.y_first
  50.9 1.0 %collective-permute-start.10 = (f32[40,128]{1,0:T(8,128)S(1)}, f32[40,128]{1,0:T(8,128)S(1)}, u32[]{:S(2)}, u32[]{:S(2)}) collective-permute-start(f32[40,128]{1,0:T(8,128)S(1)} %get-tuple-element.75), channel_id=1, source_target_pairs={{0,4},{4,0},{8,12},{12,8},{16,20},{20,16},{24,28},{28,24},{1,5},{5... | collective-permute-start | bytes 61448 | tf_op jit(solution)/shard_map/ppermute | solution.py:1470
  51.9 0.7 collective-permute-start.11
  52.5 0.2 shard_map.96
  52.8 2.0 %collective-permute-done.10.x_first = f32[40,128]{1,0:T(8,128)S(1)} collective-permute-done((f32[40,128]{1,0:T(8,128)S(1)}, f32[40,128]{1,0:T(8,128)S(1)}, u32[]{:S(2)}, u32[]{:S(2)}) %collective-permute-start.10) | collective-permute-done | bytes 20512 | tf_op jit(solution)/shard_map/ppermute | solution.py:1470
  54.8 1.2 %shard_map.98 = (f32[2,8,2,8,128]{4,3,2,1,0:T(8,128)}, f32[2,8,2,8,128]{4,3,2,1,0:T(8,128)S(1)}, f32[32,8,128]{2,1,0:T(8,128)S(1)}) custom-call(f32[2,8,2,8,128]{4,3,2,1,0:T(8,128)S(1)} %get-tuple-element.71.begun, f32[2,8,2,8,128]{4,3,2,1,0:T(8,128)S(1)} %get-tuple-element.72.begun_scaled, f32[2,8,2,8,128]{4,3,2,1,0:T(8,128)S(1)} %get-tuple-element.73.given, ...), custom_call_target="tpu_custom_call" | custom-call | tf_op jit(solution)/shard_map/pallas_call | solution.py:1550
  56.0 17.7 %all_to_all.11.got = f32[32,8,128]{2,1,0:T(8,128)S(1)} all-to-all(f32[32,8,128]{2,1,0:T(8,128)S(1)} %get-tuple-element.79), channel_id=1, replica_groups=mesh['gx'=8,'gy'=4] {'gx','gy'}, dimensions={0} | all-to-all | bytes 262144 | tf_op jit(solution)/shard_map/all_to_all | solution.py:1496
  73.7 1.4 %shard_map.99 = f32[2,8,2,8,128]{4,3,2,1,0:T(8,128)} custom-call(f32[32,8,128]{2,1,0:T(8,128)S(1)} %all_to_all.11.got, f32[16,128]{1,0:T(8,128)S(1)} %get-tuple-element.62.grp, f32[2,8,2,8,128]{4,3,2,1,0:T(8,128)S(1)} %get-tuple-element.80.direction, f32[2,8,2,8,128]{4,3,2,1,0:T(8,128)S(1)} %get-tuple-element.81.smoothed), custom_call_target="tpu_custom_call" | custom-call | tf_op jit(solution)/shard_map/pallas_call | solution.py:1559
  (22 shorter events, 0.1 us)
Async XLA Ops:
  0.6 6.9 %copy-start = (bf16[3,256,256]{2,1,0:T(8,128)(2,1)S(1)}, bf16[3,256,256]{2,1,0:T(8,128)(2,1)}, u32[]{:S(2)}) copy-start(bf16[3,256,256]{2,1,0:T(8,128)(2,1)} %constant.5.clone.zmat) | copy-start | bytes 1179652
  0.6 1.1 %copy-start.3 = (f32[4,2,8,2,8,128]{5,4,3,2,1,0:T(8,128)S(1)}, f32[4,2,8,2,8,128]{5,4,3,2,1,0:T(8,128)}, u32[]{:S(2)}) copy-start(f32[4,2,8,2,8,128]{5,4,3,2,1,0:T(8,128)} %fields.1) | copy-start | bytes 1572868
  1.7 5.8 %copy-start.2 = (f32[2,8,2,8,128]{4,3,2,1,0:T(8,128)S(1)}, f32[2,8,2,8,128]{4,3,2,1,0:T(8,128)}, u32[]{:S(2)}) copy-start(f32[2,8,2,8,128]{4,3,2,1,0:T(8,128)} %visc.3) | copy-start | bytes 393220
  2.2 5.3 %copy-start.1 = (f32[30,8,128]{2,1,0:T(8,128)S(1)}, f32[30,8,128]{2,1,0:T(8,128)}, u32[]{:S(2)}) copy-start(f32[30,8,128]{2,1,0:T(8,128)} %constant.4.clone.ctab) | copy-start | bytes 368644
  2.2 1.4 %collective-permute-start = (f32[64,128]{1,0:T(8,128)S(1)}, f32[64,128]{1,0:T(8,128)S(1)}, u32[]{:S(2)}, u32[]{:S(2)}) collective-permute-start(f32[64,128]{1,0:T(8,128)S(1)} %get-tuple-element.43), channel_id=1, source_target_pairs={{0,1},{1,0},{2,3},{3,2},{4,5},{5,4},{6,7},{7,6},{8,9},{9,8},{10,11... | collective-permute-start | bytes 98312 | tf_op jit(solution)/shard_map/ppermute | solution.py:1470
  2.7 0.9 %collective-permute-start.1 = (f32[64,128]{1,0:T(8,128)S(1)}, f32[64,128]{1,0:T(8,128)S(1)}, u32[]{:S(2)}, u32[]{:S(2)}) collective-permute-start(f32[64,128]{1,0:T(8,128)S(1)} %get-tuple-element.44), channel_id=1, source_target_pairs={{1,2},{2,1},{5,6},{6,5},{9,10},{10,9},{13,14},{14,13},{17,18},{18,... | collective-permute-start | bytes 98312 | tf_op jit(solution)/shard_map/ppermute | solution.py:1469
  3.6 3.6 %copy-start.5 = (s32[2,2,16]{2,1,0:T(2,128)S(1)}, s32[2,2,16]{2,1,0:T(2,128)}, u32[]{:S(2)}) copy-start(s32[2,2,16]{2,1,0:T(2,128)} %group.1) | copy-start | bytes 772
  3.6 3.6 %copy-start.6 = (f32[4,128]{1,0:T(4,128)S(1)}, f32[4,128]{1,0:T(4,128)}, u32[]{:S(2)}) copy-start(f32[4,128]{1,0:T(4,128)} %coarse.1) | copy-start | bytes 6148
  3.6 3.6 %copy-start.4 = (f32[2,2,16]{2,1,0:T(2,128)S(1)}, f32[2,2,16]{2,1,0:T(2,128)}, u32[]{:S(2)}) copy-start(f32[2,2,16]{2,1,0:T(2,128)} %kappa.1) | copy-start | bytes 772
  3.6 5.8 %collective-permute-start.2 = (f32[64,128]{1,0:T(8,128)S(1)}, f32[64,128]{1,0:T(8,128)S(1)}, u32[]{:S(2)}, u32[]{:S(2)}) collective-permute-start(f32[64,128]{1,0:T(8,128)S(1)} %get-tuple-element.49), channel_id=1, source_target_pairs={{0,4},{4,0},{8,12},{12,8},{16,20},{20,16},{24,28},{28,24},{1,5},{5... | collective-permute-start | bytes 98312 | tf_op jit(solution)/shard_map/ppermute | solution.py:1470
  6.5 2.9 %collective-permute-start.3 = (f32[64,128]{1,0:T(8,128)S(1)}, f32[64,128]{1,0:T(8,128)S(1)}, u32[]{:S(2)}, u32[]{:S(2)}) collective-permute-start(f32[64,128]{1,0:T(8,128)S(1)} %get-tuple-element.50), channel_id=1, source_target_pairs={{4,8},{8,4},{12,16},{16,12},{20,24},{24,20},{5,9},{9,5},{13,17},{1... | collective-permute-start | bytes 98312 | tf_op jit(solution)/shard_map/ppermute | solution.py:1469
  10.9 5.2 %collective-permute-start.4 = (f32[104,128]{1,0:T(8,128)S(1)}, f32[104,128]{1,0:T(8,128)S(1)}, u32[]{:S(2)}, u32[]{:S(2)}) collective-permute-start(f32[104,128]{1,0:T(8,128)S(1)} %get-tuple-element.52), channel_id=1, source_target_pairs={{0,1},{1,0},{2,3},{3,2},{4,5},{5,4},{6,7},{7,6},{8,9},{9,8},{10,11... | collective-permute-start | bytes 159752 | tf_op jit(solution)/shard_map/ppermute | solution.py:1470
  15.2 0.9 %collective-permute-start.5 = (f32[104,128]{1,0:T(8,128)S(1)}, f32[104,128]{1,0:T(8,128)S(1)}, u32[]{:S(2)}, u32[]{:S(2)}) collective-permute-start(f32[104,128]{1,0:T(8,128)S(1)} %get-tuple-element.53), channel_id=1, source_target_pairs={{1,2},{2,1},{5,6},{6,5},{9,10},{10,9},{13,14},{14,13},{17,18},{18,... | collective-permute-start | bytes 159752 | tf_op jit(solution)/shard_map/ppermute | solution.py:1469
  16.2 6.4 %collective-permute-start.6 = (f32[136,128]{1,0:T(8,128)S(1)}, f32[136,128]{1,0:T(8,128)S(1)}, u32[]{:S(2)}, u32[]{:S(2)}) collective-permute-start(f32[136,128]{1,0:T(8,128)S(1)} %get-tuple-element.58), channel_id=1, source_target_pairs={{0,4},{4,0},{8,12},{12,8},{16,20},{20,16},{24,28},{28,24},{1,5},{5... | collective-permute-start | bytes 208904 | tf_op jit(solution)/shard_map/ppermute | solution.py:1470
  20.2 2.3 %collective-permute-start.7 = (f32[136,128]{1,0:T(8,128)S(1)}, f32[136,128]{1,0:T(8,128)S(1)}, u32[]{:S(2)}, u32[]{:S(2)}) collective-permute-start(f32[136,128]{1,0:T(8,128)S(1)} %get-tuple-element.59), channel_id=1, source_target_pairs={{4,8},{8,4},{12,16},{16,12},{20,24},{24,20},{5,9},{9,5},{13,17},{1... | collective-permute-start | bytes 208904 | tf_op jit(solution)/shard_map/ppermute | solution.py:1469
  49.6 1.3 %collective-permute-start.8 = (f32[40,128]{1,0:T(8,128)S(1)}, f32[40,128]{1,0:T(8,128)S(1)}, u32[]{:S(2)}, u32[]{:S(2)}) collective-permute-start(f32[40,128]{1,0:T(8,128)S(1)} %get-tuple-element.69), channel_id=1, source_target_pairs={{0,1},{1,0},{2,3},{3,2},{4,5},{5,4},{6,7},{7,6},{8,9},{9,8},{10,11... | collective-permute-start | bytes 61448 | tf_op jit(solution)/shard_map/ppermute | solution.py:1470
  49.7 1.2 %collective-permute-start.9 = (f32[40,128]{1,0:T(8,128)S(1)}, f32[40,128]{1,0:T(8,128)S(1)}, u32[]{:S(2)}, u32[]{:S(2)}) collective-permute-start(f32[40,128]{1,0:T(8,128)S(1)} %get-tuple-element.70), channel_id=1, source_target_pairs={{1,2},{2,1},{5,6},{6,5},{9,10},{10,9},{13,14},{14,13},{17,18},{18,... | collective-permute-start | bytes 61448 | tf_op jit(solution)/shard_map/ppermute | solution.py:1469
  50.9 3.8 %collective-permute-start.10 = (f32[40,128]{1,0:T(8,128)S(1)}, f32[40,128]{1,0:T(8,128)S(1)}, u32[]{:S(2)}, u32[]{:S(2)}) collective-permute-start(f32[40,128]{1,0:T(8,128)S(1)} %get-tuple-element.75), channel_id=1, source_target_pairs={{0,4},{4,0},{8,12},{12,8},{16,20},{20,16},{24,28},{28,24},{1,5},{5... | collective-permute-start | bytes 61448 | tf_op jit(solution)/shard_map/ppermute | solution.py:1470
  51.9 2.9 %collective-permute-start.11 = (f32[40,128]{1,0:T(8,128)S(1)}, f32[40,128]{1,0:T(8,128)S(1)}, u32[]{:S(2)}, u32[]{:S(2)}) collective-permute-start(f32[40,128]{1,0:T(8,128)S(1)} %get-tuple-element.76), channel_id=1, source_target_pairs={{4,8},{8,4},{12,16},{16,12},{20,24},{24,20},{5,9},{9,5},{13,17},{1... | collective-permute-start | bytes 61448 | tf_op jit(solution)/shard_map/ppermute | solution.py:1469

commit v7 on v6

--- a/solution.py
+++ b/solution.py
@@ -295,8 +295,10 @@
             second[rows, :] = place.after_x(sides[0][ey], sides[1][ey])
 
 
-def turn_faces_kernel(xf, y_first, y_second, first, second):
+def turn_faces_kernel(pack_rows, xf, pack, y_first, y_second, first, second):
     turn_faces(Place(), xf, y_first, y_second, first, second)
+    first[pl.ds(64, pack_rows), :] = pack[...]
+    second[pl.ds(64, pack_rows), :] = pack[...]
 
 
 def turn_edges(place, inner_x, y_first, y_second, first, second, at, edge, inner_y):
@@ -324,47 +326,58 @@
 STEP_U, STEP_V, STEP_EDGE, STEP_PACK = 64, 64, 80, 88
 
 
-def turn_step_kernel(pack_rows, xf, inner_x, pack, y_first, y_second, first, second):
+def turn_step_kernel(xf, inner_x, y_first, y_second, first, second):
     place = Place()
     turn_faces(place, xf, y_first, y_second, first, second)
     first[pl.ds(STEP_EDGE, 8), :] = jnp.zeros(TILE, jnp.float32)
     second[pl.ds(STEP_EDGE, 8), :] = jnp.zeros(TILE, jnp.float32)
     turn_edges(place, inner_x, y_first, y_second, first, second, STEP_U, STEP_EDGE, STEP_V)
-    came = pl.ds(STEP_PACK, pack_rows)
-    parts = (
-        place.before_y(y_first[came, :], y_second[came, :]),
-        pack[...],
-        place.after_y(y_first[came, :], y_second[came, :]),
-    )
-    for k in range(3):
-        rows = pl.ds(STEP_PACK + k * pack_rows, pack_rows)
-        first[rows, :] = parts[k]
-        second[rows, :] = parts[k]
 
 
 def setup_kernel(
-    pack_rows, blocks, pack, y_first, y_second, x_first, x_second, ctab, inv_diag, kap, grp, coarse
+    pack_rows,
+    blocks,
+    pack,
+    x_first,
+    x_second,
+    y_first,
+    y_second,
+    ctab,
+    inv_diag,
+    kap,
+    grp,
+    coarse,
+    compact,
+    spread,
 ):
     place = Place()
-    came = pl.ds(STEP_PACK, pack_rows)
+    beside = pl.ds(64, pack_rows)
     packs = [[None] * 3 for _ in range(3)]
-    packs[1][0] = place.before_y(y_first[came, :], y_second[came, :])
+    packs[0][1] = place.before_x(x_first[beside, :], x_second[beside, :])
     packs[1][1] = pack[...]
-    packs[1][2] = place.after_y(y_first[came, :], y_second[came, :])
-    for k in range(3):
-        rows = pl.ds(STEP_PACK + k * pack_rows, pack_rows)
-        packs[0][k] = place.before_x(x_first[rows, :], x_second[rows, :])
-        packs[2][k] = place.after_x(x_first[rows, :], x_second[rows, :])
+    packs[2][1] = place.after_x(x_first[beside, :], x_second[beside, :])
+    for dx in range(3):
+        rows = pl.ds(STEP_PACK + dx * pack_rows, pack_rows)
+        packs[dx][0] = place.before_y(y_first[rows, :], y_second[rows, :])
+        packs[dx][2] = place.after_y(y_first[rows, :], y_second[rows, :])
+    compact[...] = jnp.zeros(compact.shape, jnp.float32)
     for dx in range(3):
         for dy in range(3):
             at = (dx * 3 + dy) * NCD * blocks
-            coarse[pl.ds(at, NCD * blocks), :] = packs[dx][dy][8 : 8 + NCD * blocks]
+            coarse[pl.ds(at, NCD * blocks), :] = packs[dx][dy][1 : 1 + NCD * blocks]
+            compact[pl.ds(dx * 3 + dy, 1), :] = packs[dx][dy][0:1]
+    elems = LANES // NODES
+    lane = lax.broadcasted_iota(jnp.int32, (LANES, LANES), 1)
+    source = lax.broadcasted_iota(jnp.int32, (LANES, LANES), 0)
+    for k in range(8):
+        spot = (source == k * elems + lane // NODES).astype(jnp.float32)
+        spread[k] = exact_dot(compact[...], spot)
     there_x = [jnp.where(place.prev_x, 1.0, 0.0), 1.0, jnp.where(place.next_x, 1.0, 0.0)]
     there_y = [jnp.where(place.prev_y, 1.0, 0.0), 1.0, jnp.where(place.next_y, 1.0, 0.0)]
 
     def element_row(base, u, v):
-        row = base + (u % 2) * 2 + v % 2
-        return packs[u // 2][v // 2][row : row + 1]
+        device = (u // 2) * 3 + v // 2
+        return spread[base + (u % 2) * 2 + v % 2, pl.ds(device, 1), :]
 
     for x in range(4):
         for y in range(4):
@@ -431,29 +444,32 @@
     elems = kappa.shape[2]
     to = lax.broadcasted_iota(jnp.int32, (elems, LANES), 1)
     element = lax.broadcasted_iota(jnp.int32, (elems, LANES), 0)
-    spread = (to // NODES == element).astype(jnp.float32)
     blocks = coarse.shape[1] // LANES
+    packed = jnp.zeros((1, LANES), jnp.float32)
     for ex in range(2):
         numbers = group[ex].astype(jnp.float32)
-        pack[pl.ds(2 * ex, 2), :] = exact_dot(kappa[ex], spread)
-        pack[pl.ds(4 + 2 * ex, 2), :] = exact_dot(numbers, spread)
         row = jnp.zeros((1, LANES), jnp.float32)
         for ey in range(2):
+            mine, number = kappa[ex, pl.ds(ey, 1), :], numbers[ey : ey + 1]
+            at = (2 * ex + ey) * elems
+            packed = packed + exact_dot(mine, (to == at + element).astype(jnp.float32))
+            at = at + 4 * elems
+            packed = packed + exact_dot(number, (to == at + element).astype(jnp.float32))
             at = (2 * place.iy + ey) * elems
-            spot = (to == at + element).astype(jnp.float32)
-            after = (to == (at + 2 * elems) % LANES + element).astype(jnp.float32)
-            row = row + exact_dot(kappa[ex, pl.ds(ey, 1), :], spot)
-            row = row + exact_dot(numbers[ey : ey + 1], after)
+            row = row + exact_dot(mine, (to == at + element).astype(jnp.float32))
+            at = (at + 2 * elems) % LANES
+            row = row + exact_dot(number, (to == at + element).astype(jnp.float32))
         facts[pl.ds(2 + ex, 1), :] = row
+    pack[pl.ds(0, 1), :] = packed
     for c in range(NCD):
         for j in range(blocks):
             line = coarse[pl.ds(c, 1), pl.ds(j * LANES, LANES)]
-            pack[pl.ds(8 + c * blocks + j, 1), :] = line
+            pack[pl.ds(1 + c * blocks + j, 1), :] = line
         facts[pl.ds(4 + c, 1), :] = coarse[pl.ds(c, 1), pl.ds(0, LANES)]
 
 
 def prepare_kernel(
-    summed, visc, y_first, y_second, ctab, zmat, start, part, grad_z, flux_z
+    summed, visc, y_first, y_second, ctab, zmat, start, part, slope, answer, grad_z, flux_z
 ):
     place = Place()
     weight = ctab[T_W]
@@ -477,16 +493,33 @@
         ch, ey = index // 2, index % 2
         coef = jnp.where(ch == 3, 1.0 / prandtl, 1.0)
         for ex in range(2):
+            grad_x = along_x(DERIV, [start[ch, ex, a, ey] for a in range(8)], -1)
+            flux_x = [
+                visc[ex, a, ey] * (float(WEIGHTS[a]) * weight) * coef * grad_x[a]
+                for a in range(8)
+            ]
+            back = along_x(DERIV.T, flux_x, -1)
             for a in range(8):
                 if (ex, a) in OUTER:
+                    slope[ch, ex, ey] = grad_x[a]
+                    part[ch, ex, a, ey] = back[a]
                     continue
-                parts = across(
+                rest, flux_z[ch, ex, a, ey] = across(
                     ctab, weight, a, coef, start[ch, ex, a, ey], grad_z[ch, ex, a, ey],
                     start[1, ex, a, ey], start[2, ex, a, ey], visc[ex, a, ey],
                 )
-                part[ch, ex, a, ey], flux_z[ch, ex, a, ey] = parts
+                flow = float(WEIGHTS[a]) * weight * start[0, ex, a, ey]
+                part[ch, ex, a, ey] = rest + flow * grad_x[a] + back[a]
         return carry
 
+    for ex, outer in OUTER:
+        for ey in range(2):
+            flux_x = [
+                visc[ex, a, ey] * (float(WEIGHTS[a] * DERIV[a, outer]) * weight) for a in range(8)
+            ]
+            back = along_x(DERIV.T, flux_x, -1)
+            for a in range(8):
+                answer[ex, a, ey] = back[a]
     lax.fori_loop(0, 8, column, 0)
     for ch in range(4):
         for ex in range(2):
@@ -507,6 +540,8 @@
     pack_rows,
     begun,
     given,
+    slope,
+    answer,
     visc,
     pack,
     x_first,
@@ -518,10 +553,10 @@
     inner_x,
     first,
     second,
-    rhs,
     edge,
     edge_z,
     edge_part,
+    came,
 ):
     place = Place()
     weight = ctab[T_W]
@@ -531,8 +566,10 @@
             scale = place.inv_x(ex, a) * float(1.0 / WEIGHTS[a])
             for ey in range(2):
                 zero = jnp.zeros(TILE, jnp.float32)
-                came = got_x_sum(place, zero, ch, ex, ey, x_first, x_second)
-                edge[ch, side, ey] = begun[ch, ex, a, ey] + came * (inv_mass[ey] * scale)
+                extra = got_x_sum(place, zero, ch, ex, ey, x_first, x_second)
+                extra = extra * (inv_mass[ey] * scale)
+                came[ch, side, ey] = extra
+                edge[ch, side, ey] = begun[ch, ex, a, ey] + extra
     edge_z[...] = along_z(edge[...].reshape(128, LANES), zmat[0]).reshape(edge.shape)
     for ch in range(4):
         coef = 1.0 / prandtl if ch == 3 else 1.0
@@ -547,39 +584,22 @@
         edge_z[...].reshape(128, LANES), zmat[1]
     ).reshape(edge.shape)
 
-    def value_of(ch, ex, a, ey):
-        if (ex, a) in OUTER:
-            return edge[ch, ex, ey]
-        return begun[ch, ex, a, ey]
-
-    def column(index, carry):
-        ch, ey = index // 2, index % 2
+    def side_of(ch, ex, a, ey):
+        outer = OUTER[ex][1]
         coef = jnp.where(ch == 3, 1.0 / prandtl, 1.0)
-        for ex in range(2):
-            field = [value_of(ch, ex, a, ey) for a in range(8)]
-            grad_x = along_x(DERIV, field, -1)
-            flux_x, parts = [], []
-            for a in range(8):
-                node = float(WEIGHTS[a]) * weight
-                flux_x.append(visc[ex, a, ey] * node * coef * grad_x[a])
-                known = edge_part[ch, ex, ey] if (ex, a) in OUTER else given[ch, ex, a, ey]
-                parts.append(known + node * (value_of(0, ex, a, ey) * grad_x[a]))
-            back = along_x(DERIV.T, flux_x, -1)
-            for a in range(8):
-                rhs[ch, ex, a, ey] = parts[a] + back[a]
-        return carry
-
-    lax.fori_loop(0, 8, column, 0)
+        extra = came[ch, ex, ey]
+        node = float(WEIGHTS[a]) * weight
+        turn = float(DERIV[a, outer])
+        if a == outer:
+            known = given[ch, ex, a, ey] + edge_part[ch, ex, ey]
+            known = known + node * edge[0, ex, ey] * (slope[ch, ex, ey] + turn * extra)
+            return known + extra * (coef * answer[ex, a, ey])
+        flow = float(WEIGHTS[a] * turn) * weight * begun[0, ex, a, ey]
+        return given[ch, ex, a, ey] + extra * (coef * answer[ex, a, ey] + flow)
 
     def finish(ch, carry):
         tiles = [
-            [
-                [
-                    place.join_z(-rhs[ch, ex, a, ey])
-                    for ey in range(2)
-                ]
-                for a in range(8)
-            ]
+            [[place.join_z(-side_of(ch, ex, a, ey)) for ey in range(2)] for a in range(8)]
             for ex in range(2)
         ]
         join_own(place, tiles)
@@ -587,7 +607,7 @@
             for a in range(8):
                 scale = place.inv_x(ex, a) * float(dt_step / WEIGHTS[a])
                 for ey in range(2):
-                    value = value_of(ch, ex, a, ey)
+                    value = edge[ch, ex, ey] if (ex, a) in OUTER else begun[ch, ex, a, ey]
                     part = value * (place.share_y(ey) * place.share_x(ex, a))
                     share[ch, ex, a, ey] = part + tiles[ex][a][ey] * (inv_mass[ey] * scale)
         return carry
@@ -611,8 +631,16 @@
         place, DERIV, ctab[T_BOTTOM], ctab[T_TOP], column_of, tile_of, inner_x, first, second,
         STEP_V, STEP_EDGE,
     )
-    first[pl.ds(STEP_PACK, pack_rows), :] = pack[...]
-    second[pl.ds(STEP_PACK, pack_rows), :] = pack[...]
+    beside = pl.ds(64, pack_rows)
+    parts = (
+        place.before_x(x_first[beside, :], x_second[beside, :]),
+        pack[...],
+        place.after_x(x_first[beside, :], x_second[beside, :]),
+    )
+    for k in range(3):
+        rows = pl.ds(STEP_PACK + k * pack_rows, pack_rows)
+        first[rows, :] = parts[k]
+        second[rows, :] = parts[k]
 
 
 def store_inner(
@@ -678,6 +706,17 @@
             part[ex, a, 0], part[ex, a, 1] = both
 
 
+def emit_kernel(begun, x_first, x_second, fields_new):
+    place = Place()
+    fields_new[...] = begun[...]
+    for ch in range(4):
+        for ex, a in OUTER:
+            for ey in range(2):
+                fields_new[ch, ex, a, ey] = got_x_sum(
+                    place, begun[ch, ex, a, ey], ch, ex, ey, x_first, x_second
+                )
+
+
 def advance_kernel(
     begun,
     given,
@@ -690,7 +729,6 @@
     grp,
     ctab,
     zmat,
-    fields_new,
     resid,
     own,
     msg,
@@ -698,6 +736,7 @@
     scaled,
     edge,
     part,
+    outer,
 ):
     place = Place()
     weight = ctab[T_W]
@@ -710,21 +749,18 @@
         rows = pl.ds(row, count)
         return place.after_x(x_first[rows, :], x_second[rows, :])
 
-    fields_new[...] = begun[...]
     part[...] = given[...]
-    for ch in range(4):
-        for ex, a in OUTER:
+    for ch in range(3):
+        for side, (ex, a) in enumerate(OUTER):
             for ey in range(2):
-                fields_new[ch, ex, a, ey] = got_x_sum(
+                outer[ch, side, ey] = got_x_sum(
                     place, begun[ch, ex, a, ey], ch, ex, ey, x_first, x_second
                 )
-    for side, (ex, a) in enumerate(OUTER):
-        edge[side] = fields_new[2, ex, a]
-    edge[...] = along_z(edge[...].reshape(32, LANES), zmat[0]).reshape(edge.shape)
+    edge[...] = along_z(outer[2].reshape(32, LANES), zmat[0]).reshape(edge.shape)
     inv_y = [place.inv_y(ey) for ey in range(2)]
     inv_z = place.inv_z()
     for side, (ex, a) in enumerate(OUTER):
-        flow = [fields_new[1, ex, a, ey] for ey in range(2)]
+        flow = [outer[1, side, ey] for ey in range(2)]
         rows = inner_along_y(place, y_first, y_second, before, after, ex, a, STEP_V, STEP_EDGE)
         slopes = [edge[side, ey] for ey in range(2)]
         both = cross_flow(place, ctab, flow, slopes, rows, inv_y, inv_z)
@@ -732,13 +768,16 @@
     slope = [[None, None], [None, None]]
     for ey in range(2):
         for ex in range(2):
-            slope[ex][ey] = along_x(DERIV, [fields_new[0, ex, a, ey] for a in range(8)], -1)
+            line = [
+                outer[0, ex, ey] if (ex, a) in OUTER else begun[0, ex, a, ey] for a in range(8)
+            ]
+            slope[ex][ey] = along_x(DERIV, line, -1)
         mid = 0.5 * (slope[0][ey][7] + slope[1][ey][0])
         slope[0][ey][7] = mid
         slope[1][ey][0] = mid
         low, high = slope[0][ey][0], slope[1][ey][7]
-        inner_low = low - float(DERIV[0, 0]) * fields_new[0, 0, 0, ey] + before(STEP_U + ey * 8)
-        inner_high = high - float(DERIV[7, 7]) * fields_new[0, 1, 7, ey] + after(STEP_U + ey * 8)
+        inner_low = low - float(DERIV[0, 0]) * outer[0, 0, ey] + before(STEP_U + ey * 8)
+        inner_high = high - float(DERIV[7, 7]) * outer[0, 1, ey] + after(STEP_U + ey * 8)
         slope[0][ey][0] = jnp.where(place.prev_x, 0.5 * inner_low, low)
         slope[1][ey][7] = jnp.where(place.next_x, 0.5 * inner_high, high)
     sums = [[jnp.zeros(TILE, jnp.float32) for _ in range(2)] for _ in range(2)]
@@ -1475,7 +1514,7 @@
     elems_z = length // NODES
     devices = lax.axis_size("gx") * lax.axis_size("gy")
     blocks = coarse_inverse.shape[1] // LANES
-    pack_rows = -(-(8 + NCD * blocks) // 8) * 8
+    pack_rows = -(-(1 + NCD * blocks) // 8) * 8
     tiles_np, mats_np = constant_tables(elems_z)
     ctab, zmat = jnp.asarray(tiles_np), jnp.asarray(mats_np)
     one = fields.shape[1:]
@@ -1483,7 +1522,8 @@
     faces = (64, LANES)
     xf_shape = (2, 4, 2, 8, LANES)
     inner_shape = (2, 2, 8, LANES)
-    y_shape, x_shape = (STEP_PACK + pack_rows, LANES), (STEP_PACK + 3 * pack_rows, LANES)
+    y_shape, x_shape = (STEP_PACK + 3 * pack_rows, LANES), (STEP_PACK, LANES)
+    turned = (64 + pack_rows, LANES)
     smooth_shape = (SMOOTH_ROWS, LANES)
     rows = (devices, 1, LANES)
     grid_fits = (
@@ -1506,34 +1546,37 @@
         cost_estimate=beside,
     )(inv_density, elem_group, coarse_inverse)
     y_got = swap(first, second, "gy")
-    first, second = call(turn_faces_kernel, [faces, faces])(xf, *y_got)
-    x_got = swap(first, second, "gx")
-    begun, given = call(prepare_kernel, [four, four], [four, four], cost_estimate=beside)(
-        summed, viscosity, *y_got, ctab, zmat
-    )
+    first, second = call(functools.partial(turn_faces_kernel, pack_rows), [turned, turned])(
+        xf, pack, *y_got
+    )
+    side_got = x_got = swap(first, second, "gx")
     edge_shape = (4, 2, 2, 8, LANES)
+    begun, given, slope, answer = call(
+        prepare_kernel, [four, four, edge_shape, one], [four, four], cost_estimate=beside
+    )(summed, viscosity, *y_got, ctab, zmat)
     share, xf, inner_x, first, second = call(
         functools.partial(rhs_kernel, pack_rows),
         [four, xf_shape, inner_shape, y_shape, y_shape],
-        [four, edge_shape, edge_shape, edge_shape],
-    )(begun, given, viscosity, pack, *x_got, ctab, zmat)
+        [edge_shape, edge_shape, edge_shape, edge_shape],
+    )(begun, given, slope, answer, viscosity, pack, *x_got, ctab, zmat)
     y_got = swap(first, second, "gy")
-    first, second = call(functools.partial(turn_step_kernel, pack_rows), [x_shape, x_shape])(
-        xf, inner_x, pack, *y_got
-    )
+    first, second = call(turn_step_kernel, [x_shape, x_shape])(xf, inner_x, *y_got)
     x_got = swap(first, second, "gx")
     inv_diag, kap, grp, coarse = call(
         functools.partial(setup_kernel, pack_rows, blocks),
         [one, (16, LANES), (16, LANES), (9 * NCD * blocks, LANES)],
-    )(pack, *y_got, *x_got, ctab)
+        [(16, LANES), (8, 16, LANES)],
+        cost_estimate=beside,
+    )(pack, *side_got, *y_got, ctab)
     begun, given = call(approach_kernel, [four, one], [one], cost_estimate=beside)(
         share, *y_got, ctab, zmat
     )
     side_shape = (2, 2, 8, LANES)
-    fields_new, resid, own, msg = call(
+    (fields_new,) = call(emit_kernel, [four], cost_estimate=beside)(begun, *x_got)
+    resid, own, msg = call(
         advance_kernel,
-        [four, one, one, (devices, 16, LANES)],
-        [one, one, side_shape, one],
+        [one, one, (devices, 16, LANES)],
+        [one, one, side_shape, one, (3,) + side_shape],
     )(begun, given, *y_got, *x_got, inv_diag, kap, grp, ctab, zmat)
     got = exchange_all(msg)
     direction, own, inner_x, first, second, extra = call(

time: 75.4 us -> 74.2 us (0.984)
  blocking collectives: 42.4 us -> 24.7 us
  starting transfers between devices: 16.7 us -> 24.8 us
  waiting for transfers between devices: 4.13 us -> 10.5 us
  local copies, waits for them, and re-layouts: 1.12 us -> 2.46 us
    all_to_all x2 -> x1, blocking collectives: 42.4 us -> 24.7 us  [exchange_all(): return lax.all_to_all(msg, BOTH, 0, 0, tiled=True)]
    all_to_all x0 -> x1, starting transfers between devices: none -> 9.67 us  [exchange_all(): return lax.all_to_all(msg, BOTH, 0, 0, tiled=True)]
    all_to_all x0 -> x1, waiting for transfers between devices: none -> 7.39 us  [exchange_all(): return lax.all_to_all(msg, BOTH, 0, 0, tiled=True)]
    ppermute x6, starting transfers between devices: 12.8 us -> 11.2 us  [swap(): return (lax.ppermute(first, axis, first_pairs), second_got)]
    unnamed x14, local copies, waits for them, and re-layouts: 1.12 us -> 2.46 us
    ppermute x6, waiting for transfers between devices: 4.12 us -> 3.1 us  [swap(): return (lax.ppermute(first, axis, first_pairs), second_got)]
    pallas_call x4 -> x5, Pallas kernels: 3.53 us -> 3.99 us  [the longest x1 2.33 us: per_device(): call(prepare_kernel, [four, four, edge_shape, one], [four, four], cost_es...]
  transfers between devices with their start and end apart: 12 -> 13, of which waited for: 5 -> 5; matrix products, arithmetic and copies ran while one was open for 0% -> 0% of each run, Pallas kernels for 4% -> 6%
where the time goes in v7:
time: 74.2 us; the launch traced here: 73.8 us
  starting transfers between devices  24.8 us (33%)
  blocking collectives  24.7 us (33%)
  Pallas kernels  10.5 us (14%)
  waiting for transfers between devices  10.5 us (14%)
  local copies, waits for them, and re-layouts  2.46 us (3%)
  between operations  0.86 us (1%)
    all_to_all x1, blocking collectives, exchange_all(): return lax.all_to_all(msg, BOTH, 0, 0, tiled=True)  24.7 us
    ppermute x6, starting transfers between devices, swap(): return (lax.ppermute(first, axis, first_pairs), second_got)  11.2 us
    all_to_all x1, starting transfers between devices, exchange_all(): return lax.all_to_all(msg, BOTH, 0, 0, tiled=True)  9.67 us
    all_to_all x1, waiting for transfers between devices, exchange_all(): return lax.all_to_all(msg, BOTH, 0, 0, tiled=True)  7.39 us
    ppermute x6, starting transfers between devices, swap(): second_got = lax.ppermute(second, axis, second_pairs)  3.92 us
    ppermute x6, waiting for transfers between devices, swap(): return (lax.ppermute(first, axis, first_pairs), second_got)  3.1 us
    unnamed x14, local copies, waits for them, and re-layouts  2.46 us
    pallas_call x1, Pallas kernels, per_device(): call(prepare_kernel, [four, four, edge_shape, one], [four, four], cost_es...  2.33 us
  transfers between devices with their start and end apart: 13, of which 5 were waited for; matrix products, arithmetic and copies ran while one was open for 0% of the time, Pallas kernels for 6%

profile of v7, /device:TPU:0, one launch (start us, length us, event | category | flops | bytes accessed | tf_op | source)
XLA Modules:
  0.0 73.8 jit_solution(10822765467811999249)
XLA Ops:
  0.7 1.1 %copy-done.2 = f32[4,2,8,2,8,128]{5,4,3,2,1,0:T(8,128)S(1)} copy-done((f32[4,2,8,2,8,128]{5,4,3,2,1,0:T(8,128)S(1)}, f32[4,2,8,2,8,128]{5,4,3,2,1,0:T(8,128)}, u32[]{:S(2)}) %copy-start.2) | copy-done | bytes 524312
  1.7 0.4 shard_map.86
  2.2 0.5 collective-permute-start
  2.7 0.7 collective-permute-start.1
  3.4 0.7 copy-done.5
  4.1 0.7 copy-done.6
  4.8 0.4 shard_map.88
  5.2 2.6 %collective-permute-start.2 = (f32[72,128]{1,0:T(8,128)S(1)}, f32[72,128]{1,0:T(8,128)S(1)}, u32[]{:S(2)}, u32[]{:S(2)}) collective-permute-start(f32[72,128]{1,0:T(8,128)S(1)} %get-tuple-element.52), channel_id=1, source_target_pairs={{0,4},{4,0},{8,12},{12,8},{16,20},{20,16},{24,28},{28,24},{1,5},{5... | collective-permute-start | bytes 110600 | tf_op jit(solution)/shard_map/ppermute | solution.py:1509
  7.8 0.7 collective-permute-start.3
  8.5 2.3 %shard_map.87 = (f32[4,2,8,2,8,128]{5,4,3,2,1,0:T(8,128)S(1)}, f32[4,2,8,2,8,128]{5,4,3,2,1,0:T(8,128)S(1)}, f32[4,2,2,8,128]{4,3,2,1,0:T(8,128)S(1)}, f32[2,8,2,8,128]{4,3,2,1,0:T(8,128)S(1)}) custom-call(f32[4,2,8,2,8,128]{5,4,3,2,1,0:T(8,128)S(1)} %get-tuple-element.43.summed, f32[2,8,2,8,128]{4,3,2,1,0:T(8,128)S(1)} %copy-done.3, ...), custom_call_target="tpu_custom_call" | custom-call | flops 10000000 | bytes 1000000 | tf_op jit(solution)/shard_map/pallas_call | solution.py:1554
  10.8 1.0 %shard_map.90 = (f32[4,2,8,2,8,128]{5,4,3,2,1,0:T(8,128)S(1)}, f32[2,4,2,8,128]{4,3,2,1,0:T(8,128)S(1)}, f32[2,2,8,128]{3,2,1,0:T(8,128)S(1)}, f32[112,128]{1,0:T(8,128)S(1)}, f32[112,128]{1,0:T(8,128)S(1)}) custom-call(f32[4,2,8,2,8,128]{5,4,3,2,1,0:T(8,128)S(1)} %get-tuple-element.46.begun, f32[4,2,8,2,8,128]{5,4,3,2,1,0:T(8,128)S(1)} %get-tuple-element.47.given, ...), custom_call_target="tpu_custom_call" | custom-call | tf_op jit(solution)/shard_map/pallas_call | solution.py:1557
  11.9 3.0 %collective-permute-start.4 = (f32[112,128]{1,0:T(8,128)S(1)}, f32[112,128]{1,0:T(8,128)S(1)}, u32[]{:S(2)}, u32[]{:S(2)}) collective-permute-start(f32[112,128]{1,0:T(8,128)S(1)} %get-tuple-element.55), channel_id=1, source_target_pairs={{0,1},{1,0},{2,3},{3,2},{4,5},{5,4},{6,7},{7,6},{8,9},{9,8},{10,11... | collective-permute-start | bytes 172040 | tf_op jit(solution)/shard_map/ppermute | solution.py:1509
  14.9 0.7 collective-permute-start.5
  15.8 4.1 %collective-permute-start.6 = (f32[88,128]{1,0:T(8,128)S(1)}, f32[88,128]{1,0:T(8,128)S(1)}, u32[]{:S(2)}, u32[]{:S(2)}) collective-permute-start(f32[88,128]{1,0:T(8,128)S(1)} %get-tuple-element.60), channel_id=1, source_target_pairs={{0,4},{4,0},{8,12},{12,8},{16,20},{20,16},{24,28},{28,24},{1,5},{5... | collective-permute-start | bytes 135176 | tf_op jit(solution)/shard_map/ppermute | solution.py:1509
  19.9 0.7 collective-permute-start.7
  20.6 0.5 shard_map.94
  21.0 0.5 shard_map.91
  21.5 0.4 collective-permute-done.6.x_first
  21.9 0.8 %shard_map.95 = (f32[2,8,2,8,128]{4,3,2,1,0:T(8,128)S(1)}, f32[2,8,2,8,128]{4,3,2,1,0:T(8,128)S(1)}, f32[32,16,128]{2,1,0:T(8,128)S(1)}) custom-call(f32[4,2,8,2,8,128]{5,4,3,2,1,0:T(8,128)S(1)} %get-tuple-element.57.begun, f32[2,8,2,8,128]{4,3,2,1,0:T(8,128)S(1)} %get-tuple-element.62.given, f32[112,128]{1,0:T(8,128)S(1)} %collective-permute-done.4.y_first, ...), custom_call_target="tpu_custom_call" | custom-call | tf_op jit(solution)/shard_map/pallas_call | solution.py:1576
  22.7 24.7 %all_to_all.10.got = f32[32,16,128]{2,1,0:T(8,128)S(1)} all-to-all(f32[32,16,128]{2,1,0:T(8,128)S(1)} %get-tuple-element.66), channel_id=1, replica_groups=mesh['gx'=8,'gy'=4] {'gx','gy'}, dimensions={0} | all-to-all | bytes 524288 | tf_op jit(solution)/shard_map/all_to_all | solution.py:1536
  47.4 0.7 shard_map.96
  48.1 0.7 collective-permute-start.9
  48.8 0.5 collective-permute-done.8.y_first
  49.3 1.0 %collective-permute-start.10 = (f32[40,128]{1,0:T(8,128)S(1)}, f32[40,128]{1,0:T(8,128)S(1)}, u32[]{:S(2)}, u32[]{:S(2)}) collective-permute-start(f32[40,128]{1,0:T(8,128)S(1)} %get-tuple-element.77), channel_id=1, source_target_pairs={{0,4},{4,0},{8,12},{12,8},{16,20},{20,16},{24,28},{28,24},{1,5},{5... | collective-permute-start | bytes 61448 | tf_op jit(solution)/shard_map/ppermute | solution.py:1509
  50.3 0.7 collective-permute-start.11
  51.0 0.2 shard_map.97
  51.2 2.0 %collective-permute-done.10.x_first = f32[40,128]{1,0:T(8,128)S(1)} collective-permute-done((f32[40,128]{1,0:T(8,128)S(1)}, f32[40,128]{1,0:T(8,128)S(1)}, u32[]{:S(2)}, u32[]{:S(2)}) %collective-permute-start.10) | collective-permute-done | bytes 20512 | tf_op jit(solution)/shard_map/ppermute | solution.py:1509
  53.2 1.3 %shard_map.99 = (f32[2,8,2,8,128]{4,3,2,1,0:T(8,128)}, f32[2,8,2,8,128]{4,3,2,1,0:T(8,128)S(1)}, f32[32,8,128]{2,1,0:T(8,128)}) custom-call(f32[2,8,2,8,128]{4,3,2,1,0:T(8,128)S(1)} %get-tuple-element.73.begun, f32[2,8,2,8,128]{4,3,2,1,0:T(8,128)S(1)} %get-tuple-element.74.begun_scaled, f32[2,8,2,8,128]{4,3,2,1,0:T(8,128)S(1)} %get-tuple-element.75.given, ...), custom_call_target="tpu_custom_call" | custom-call | tf_op jit(solution)/shard_map/pallas_call | solution.py:1593
  54.5 9.7 %all-to-all-start.1 = ((f32[32,8,128]{2,1,0:T(8,128)}), f32[32,8,128]{2,1,0:T(8,128)S(1)}, u32[]{:S(2)}, u32[]{:S(2)}) async-start(f32[32,8,128]{2,1,0:T(8,128)} %get-tuple-element.81), calls=%async_computation.1 | async-start | bytes 262144 | tf_op jit(solution)/shard_map/all_to_all | solution.py:1536
  64.2 0.8 %shard_map.93 = f32[4,2,8,2,8,128]{5,4,3,2,1,0:T(8,128)} custom-call(f32[4,2,8,2,8,128]{5,4,3,2,1,0:T(8,128)S(1)} %get-tuple-element.57.begun, f32[88,128]{1,0:T(8,128)S(1)} %collective-permute-done.6.x_first, f32[88,128]{1,0:T(8,128)S(1)} %collective-permute-done.7.x_second), custom_call_target="tpu_custom_call" | custom-call | flops 10000000 | bytes 1000000 | tf_op jit(solution)/shard_map/pallas_call | solution.py:1575
  65.0 7.4 %all-to-all-done.1.got = f32[32,8,128]{2,1,0:T(8,128)S(1)} async-done(((f32[32,8,128]{2,1,0:T(8,128)}), f32[32,8,128]{2,1,0:T(8,128)S(1)}, u32[]{:S(2)}, u32[]{:S(2)}) %all-to-all-start.1) | async-done | bytes 131104 | tf_op jit(solution)/shard_map/all_to_all | solution.py:1536
  72.4 1.4 %shard_map.100 = f32[2,8,2,8,128]{4,3,2,1,0:T(8,128)} custom-call(f32[32,8,128]{2,1,0:T(8,128)S(1)} %all-to-all-done.1.got, f32[16,128]{1,0:T(8,128)S(1)} %get-tuple-element.65.grp, f32[2,8,2,8,128]{4,3,2,1,0:T(8,128)S(1)} %get-tuple-element.82.direction, f32[2,8,2,8,128]{4,3,2,1,0:T(8,128)S(1)} %get-tuple-element.83.smoothed), custom_call_target="tpu_custom_call" | custom-call | tf_op jit(solution)/shard_map/pallas_call | solution.py:1602
  (24 shorter events, 0.4 us)
Async XLA Ops:
  0.6 7.8 %copy-start = (bf16[3,256,256]{2,1,0:T(8,128)(2,1)S(1)}, bf16[3,256,256]{2,1,0:T(8,128)(2,1)}, u32[]{:S(2)}) copy-start(bf16[3,256,256]{2,1,0:T(8,128)(2,1)} %constant.5.clone.zmat) | copy-start | bytes 1179652
  0.6 1.1 %copy-start.2 = (f32[4,2,8,2,8,128]{5,4,3,2,1,0:T(8,128)S(1)}, f32[4,2,8,2,8,128]{5,4,3,2,1,0:T(8,128)}, u32[]{:S(2)}) copy-start(f32[4,2,8,2,8,128]{5,4,3,2,1,0:T(8,128)} %fields.1) | copy-start | bytes 1572868
  1.7 1.6 %copy-start.4 = (f32[2,2,16]{2,1,0:T(2,128)S(1)}, f32[2,2,16]{2,1,0:T(2,128)}, u32[]{:S(2)}) copy-start(f32[2,2,16]{2,1,0:T(2,128)} %kappa.1) | copy-start | bytes 772
  1.7 6.7 %copy-start.3 = (f32[2,8,2,8,128]{4,3,2,1,0:T(8,128)S(1)}, f32[2,8,2,8,128]{4,3,2,1,0:T(8,128)}, u32[]{:S(2)}) copy-start(f32[2,8,2,8,128]{4,3,2,1,0:T(8,128)} %visc.3) | copy-start | bytes 393220
  2.2 6.3 %copy-start.1 = (f32[30,8,128]{2,1,0:T(8,128)S(1)}, f32[30,8,128]{2,1,0:T(8,128)}, u32[]{:S(2)}) copy-start(f32[30,8,128]{2,1,0:T(8,128)} %constant.4.clone.ctab) | copy-start | bytes 368644
  2.2 2.9 %collective-permute-start = (f32[64,128]{1,0:T(8,128)S(1)}, f32[64,128]{1,0:T(8,128)S(1)}, u32[]{:S(2)}, u32[]{:S(2)}) collective-permute-start(f32[64,128]{1,0:T(8,128)S(1)} %get-tuple-element.44), channel_id=1, source_target_pairs={{0,1},{1,0},{2,3},{3,2},{4,5},{5,4},{6,7},{7,6},{8,9},{9,8},{10,11... | collective-permute-start | bytes 98312 | tf_op jit(solution)/shard_map/ppermute | solution.py:1509
  2.7 2.4 %collective-permute-start.1 = (f32[64,128]{1,0:T(8,128)S(1)}, f32[64,128]{1,0:T(8,128)S(1)}, u32[]{:S(2)}, u32[]{:S(2)}) collective-permute-start(f32[64,128]{1,0:T(8,128)S(1)} %get-tuple-element.45), channel_id=1, source_target_pairs={{1,2},{2,1},{5,6},{6,5},{9,10},{10,9},{13,14},{14,13},{17,18},{18,... | collective-permute-start | bytes 98312 | tf_op jit(solution)/shard_map/ppermute | solution.py:1508
  3.4 0.7 copy-start.5
  4.1 0.7 copy-start.6
  5.2 5.6 %collective-permute-start.2 = (f32[72,128]{1,0:T(8,128)S(1)}, f32[72,128]{1,0:T(8,128)S(1)}, u32[]{:S(2)}, u32[]{:S(2)}) collective-permute-start(f32[72,128]{1,0:T(8,128)S(1)} %get-tuple-element.52), channel_id=1, source_target_pairs={{0,4},{4,0},{8,12},{12,8},{16,20},{20,16},{24,28},{28,24},{1,5},{5... | collective-permute-start | bytes 110600 | tf_op jit(solution)/shard_map/ppermute | solution.py:1509
  7.8 3.0 %collective-permute-start.3 = (f32[72,128]{1,0:T(8,128)S(1)}, f32[72,128]{1,0:T(8,128)S(1)}, u32[]{:S(2)}, u32[]{:S(2)}) collective-permute-start(f32[72,128]{1,0:T(8,128)S(1)} %get-tuple-element.53), channel_id=1, source_target_pairs={{4,8},{8,4},{12,16},{16,12},{20,24},{24,20},{5,9},{9,5},{13,17},{1... | collective-permute-start | bytes 110600 | tf_op jit(solution)/shard_map/ppermute | solution.py:1508
  11.9 3.9 %collective-permute-start.4 = (f32[112,128]{1,0:T(8,128)S(1)}, f32[112,128]{1,0:T(8,128)S(1)}, u32[]{:S(2)}, u32[]{:S(2)}) collective-permute-start(f32[112,128]{1,0:T(8,128)S(1)} %get-tuple-element.55), channel_id=1, source_target_pairs={{0,1},{1,0},{2,3},{3,2},{4,5},{5,4},{6,7},{7,6},{8,9},{9,8},{10,11... | collective-permute-start | bytes 172040 | tf_op jit(solution)/shard_map/ppermute | solution.py:1509
  14.9 0.9 %collective-permute-start.5 = (f32[112,128]{1,0:T(8,128)S(1)}, f32[112,128]{1,0:T(8,128)S(1)}, u32[]{:S(2)}, u32[]{:S(2)}) collective-permute-start(f32[112,128]{1,0:T(8,128)S(1)} %get-tuple-element.56), channel_id=1, source_target_pairs={{1,2},{2,1},{5,6},{6,5},{9,10},{10,9},{13,14},{14,13},{17,18},{18,... | collective-permute-start | bytes 172040 | tf_op jit(solution)/shard_map/ppermute | solution.py:1508
  15.8 6.1 %collective-permute-start.6 = (f32[88,128]{1,0:T(8,128)S(1)}, f32[88,128]{1,0:T(8,128)S(1)}, u32[]{:S(2)}, u32[]{:S(2)}) collective-permute-start(f32[88,128]{1,0:T(8,128)S(1)} %get-tuple-element.60), channel_id=1, source_target_pairs={{0,4},{4,0},{8,12},{12,8},{16,20},{20,16},{24,28},{28,24},{1,5},{5... | collective-permute-start | bytes 135176 | tf_op jit(solution)/shard_map/ppermute | solution.py:1509
  19.9 2.0 %collective-permute-start.7 = (f32[88,128]{1,0:T(8,128)S(1)}, f32[88,128]{1,0:T(8,128)S(1)}, u32[]{:S(2)}, u32[]{:S(2)}) collective-permute-start(f32[88,128]{1,0:T(8,128)S(1)} %get-tuple-element.61), channel_id=1, source_target_pairs={{4,8},{8,4},{12,16},{16,12},{20,24},{24,20},{5,9},{9,5},{13,17},{1... | collective-permute-start | bytes 135176 | tf_op jit(solution)/shard_map/ppermute | solution.py:1508
  48.0 1.3 %collective-permute-start.8 = (f32[40,128]{1,0:T(8,128)S(1)}, f32[40,128]{1,0:T(8,128)S(1)}, u32[]{:S(2)}, u32[]{:S(2)}) collective-permute-start(f32[40,128]{1,0:T(8,128)S(1)} %get-tuple-element.71), channel_id=1, source_target_pairs={{0,1},{1,0},{2,3},{3,2},{4,5},{5,4},{6,7},{7,6},{8,9},{9,8},{10,11... | collective-permute-start | bytes 61448 | tf_op jit(solution)/shard_map/ppermute | solution.py:1509
  48.1 1.2 %collective-permute-start.9 = (f32[40,128]{1,0:T(8,128)S(1)}, f32[40,128]{1,0:T(8,128)S(1)}, u32[]{:S(2)}, u32[]{:S(2)}) collective-permute-start(f32[40,128]{1,0:T(8,128)S(1)} %get-tuple-element.72), channel_id=1, source_target_pairs={{1,2},{2,1},{5,6},{6,5},{9,10},{10,9},{13,14},{14,13},{17,18},{18,... | collective-permute-start | bytes 61448 | tf_op jit(solution)/shard_map/ppermute | solution.py:1508
  49.3 3.8 %collective-permute-start.10 = (f32[40,128]{1,0:T(8,128)S(1)}, f32[40,128]{1,0:T(8,128)S(1)}, u32[]{:S(2)}, u32[]{:S(2)}) collective-permute-start(f32[40,128]{1,0:T(8,128)S(1)} %get-tuple-element.77), channel_id=1, source_target_pairs={{0,4},{4,0},{8,12},{12,8},{16,20},{20,16},{24,28},{28,24},{1,5},{5... | collective-permute-start | bytes 61448 | tf_op jit(solution)/shard_map/ppermute | solution.py:1509
  50.3 2.9 %collective-permute-start.11 = (f32[40,128]{1,0:T(8,128)S(1)}, f32[40,128]{1,0:T(8,128)S(1)}, u32[]{:S(2)}, u32[]{:S(2)}) collective-permute-start(f32[40,128]{1,0:T(8,128)S(1)} %get-tuple-element.78), channel_id=1, source_target_pairs={{4,8},{8,4},{12,16},{16,12},{20,24},{24,20},{5,9},{9,5},{13,17},{1... | collective-permute-start | bytes 61448 | tf_op jit(solution)/shard_map/ppermute | solution.py:1508
  54.5 17.9 %all-to-all-start.1 = ((f32[32,8,128]{2,1,0:T(8,128)}), f32[32,8,128]{2,1,0:T(8,128)S(1)}, u32[]{:S(2)}, u32[]{:S(2)}) async-start(f32[32,8,128]{2,1,0:T(8,128)} %get-tuple-element.81), calls=%async_computation.1 | async-start | bytes 262144 | tf_op jit(solution)/shard_map/all_to_all | solution.py:1536

commit v8 on v7

--- a/solution.py
+++ b/solution.py
@@ -323,14 +323,12 @@
         second[row, :] = place.after_x(sides[0], sides[1])
 
 
-STEP_U, STEP_V, STEP_EDGE, STEP_PACK = 64, 64, 80, 88
+STEP_U, STEP_V, STEP_EDGE, STEP_PACK = 64, 64, 80, 82
 
 
 def turn_step_kernel(xf, inner_x, y_first, y_second, first, second):
     place = Place()
     turn_faces(place, xf, y_first, y_second, first, second)
-    first[pl.ds(STEP_EDGE, 8), :] = jnp.zeros(TILE, jnp.float32)
-    second[pl.ds(STEP_EDGE, 8), :] = jnp.zeros(TILE, jnp.float32)
     turn_edges(place, inner_x, y_first, y_second, first, second, STEP_U, STEP_EDGE, STEP_V)
 
 
@@ -439,8 +437,8 @@
 
 def pack_kernel(kappa, group, coarse, pack, facts):
     place = Place()
-    pack[...] = jnp.zeros(pack.shape, jnp.float32)
     facts[...] = jnp.zeros(facts.shape, jnp.float32)
+    grid = jnp.zeros((1, LANES), jnp.float32)
     elems = kappa.shape[2]
     to = lax.broadcasted_iota(jnp.int32, (elems, LANES), 1)
     element = lax.broadcasted_iota(jnp.int32, (elems, LANES), 0)
@@ -448,24 +446,23 @@
     packed = jnp.zeros((1, LANES), jnp.float32)
     for ex in range(2):
         numbers = group[ex].astype(jnp.float32)
-        row = jnp.zeros((1, LANES), jnp.float32)
         for ey in range(2):
             mine, number = kappa[ex, pl.ds(ey, 1), :], numbers[ey : ey + 1]
             at = (2 * ex + ey) * elems
             packed = packed + exact_dot(mine, (to == at + element).astype(jnp.float32))
             at = at + 4 * elems
             packed = packed + exact_dot(number, (to == at + element).astype(jnp.float32))
-            at = (2 * place.iy + ey) * elems
-            row = row + exact_dot(mine, (to == at + element).astype(jnp.float32))
+            at = ((2 * place.iy + ey) * elems + 4 * ex * elems) % LANES
+            grid = grid + exact_dot(mine, (to == at + element).astype(jnp.float32))
             at = (at + 2 * elems) % LANES
-            row = row + exact_dot(number, (to == at + element).astype(jnp.float32))
-        facts[pl.ds(2 + ex, 1), :] = row
+            grid = grid + exact_dot(number, (to == at + element).astype(jnp.float32))
     pack[pl.ds(0, 1), :] = packed
     for c in range(NCD):
         for j in range(blocks):
             line = coarse[pl.ds(c, 1), pl.ds(j * LANES, LANES)]
             pack[pl.ds(1 + c * blocks + j, 1), :] = line
-        facts[pl.ds(4 + c, 1), :] = coarse[pl.ds(c, 1), pl.ds(0, LANES)]
+        facts[:, pl.ds((2 + c) * LANES, LANES)] = coarse[pl.ds(c, 1), pl.ds(0, LANES)]
+    facts[:, pl.ds(LANES, LANES)] = grid
 
 
 def prepare_kernel(
@@ -618,8 +615,6 @@
         for ey in range(2):
             xf[0, ch, ey] = share[ch, 0, 0, ey]
             xf[1, ch, ey] = share[ch, 1, 7, ey]
-    first[pl.ds(STEP_EDGE, 8), :] = jnp.zeros(TILE, jnp.float32)
-    second[pl.ds(STEP_EDGE, 8), :] = jnp.zeros(TILE, jnp.float32)
 
     def column_of(ex, ey):
         return [share[0, ex, a, ey] for a in range(8)]
@@ -706,8 +701,9 @@
             part[ex, a, 0], part[ex, a, 1] = both
 
 
-def emit_kernel(begun, x_first, x_second, fields_new):
+def emit_kernel(begun, x_first, x_second, extra, fields_new, passed):
     place = Place()
+    passed[...] = extra[...]
     fields_new[...] = begun[...]
     for ch in range(4):
         for ex, a in OUTER:
@@ -859,7 +855,7 @@
     return out
 
 
-SMOOTH_X, SMOOTH_Y, SMOOTH_EDGE, SMOOTH_ROWS = 16, 16, 32, 40
+SMOOTH_X, SMOOTH_Y, SMOOTH_EDGE, SMOOTH_ROWS = 16, 16, 32, 34
 
 
 def turn_smooth_kernel(own, inner_x, y_first, y_second, first, second):
@@ -875,8 +871,6 @@
         rows = pl.ds(ey * 8, 8)
         first[rows, :] = place.after_x(sides[1][ey], sides[0][ey])
         second[rows, :] = place.after_x(sides[0][ey], sides[1][ey])
-    first[pl.ds(SMOOTH_EDGE, 8), :] = jnp.zeros(TILE, jnp.float32)
-    second[pl.ds(SMOOTH_EDGE, 8), :] = jnp.zeros(TILE, jnp.float32)
     turn_edges(
         place, inner_x, y_first, y_second, first, second, SMOOTH_X, SMOOTH_EDGE, SMOOTH_Y
     )
@@ -894,10 +888,15 @@
     return values
 
 
-def message(place, own_values, scalars):
+AWAY = 16
+BEYOND = 18
+
+
+def message(place, own_values, scalars, away=0, beyond=1):
     lane = lax.broadcasted_iota(jnp.int32, (1, LANES), 1)
     spot = (place.ix * place.ny + place.iy) % (LANES // NCD)
-    after = (spot + 1) % (LANES // NCD)
+    after = (spot + beyond) % (LANES // NCD)
+    spot = (spot + away) % (LANES // NCD)
     row = jnp.zeros((1, LANES), jnp.float32)
     for c, value in enumerate(own_values):
         row = row + jnp.where(lane == spot * NCD + c, value, 0.0)
@@ -1047,8 +1046,9 @@
                 sums[ex][ey] = sums[ex][ey] + weighed
                 square = square + weighed * result
     own_sums = restricted(place, sums, grp)
-    if msg.shape[1] == 1:
-        send_to_all(msg, message(place, own_sums, []) + extra[...])
+    if msg.shape[2] == LANES:
+        sums = [extra[:, pl.ds(k, 1)] for k in range(2)]
+        send_to_all(msg, message(place, own_sums, sums))
         return
     slope_z[...] = along_z(smoothed[...].reshape(256, LANES), zmat[2]).reshape(slope_z.shape)
     energy = jnp.zeros(TILE, jnp.float32)
@@ -1059,12 +1059,10 @@
                 energy = energy + values[a] * images[a]
                 tiles[ex][a][ey] = place.join_z(images[a])
     join_own(place, tiles)
-    row = message(place, own_sums, [None, None, total(square), total(energy)]) + extra[...]
-    dual = restricted_around(place, tiles, inv_mult, grp)
-    out = facts[...]
-    out = out + jnp.where(place.row == 0, jnp.broadcast_to(row, TILE), 0.0)
-    out = out + jnp.where(place.row == 1, jnp.broadcast_to(dual, TILE), 0.0)
-    send_to_all(msg, out)
+    sums = [extra[:, pl.ds(k, 1)] for k in range(2)] + [total(square), total(energy)]
+    row = message(place, own_sums, sums, AWAY, BEYOND)
+    row = row + restricted_around(place, tiles, inv_mult, grp)
+    send_to_all(msg, jnp.concatenate([row, facts[:, LANES:]], axis=1))
 
 
 def restricted_around(place, tiles, inv_mult, grp):
@@ -1263,8 +1261,6 @@
             for ey in range(2):
                 out[ex, a, ey] = tiles[ex][a][ey]
     store_y_faces(place, out, first, second, (), 0)
-    first[pl.ds(SMOOTH_EDGE, 8), :] = jnp.zeros(TILE, jnp.float32)
-    second[pl.ds(SMOOTH_EDGE, 8), :] = jnp.zeros(TILE, jnp.float32)
 
     def tile_of(ex, a, ey):
         return tiles[ex][a][ey] * inv_diag[ex, a, ey] * float(1.0 / THETA)
@@ -1276,7 +1272,8 @@
         place, SCALED, ctab[T_KBOTTOM], ctab[T_KTOP], column_of, tile_of, inner_x, first, second,
         SMOOTH_Y, SMOOTH_EDGE,
     )
-    extra[...] = message(place, [], [total(energy), total(curvature)])
+    lane = lax.broadcasted_iota(jnp.int32, (1, LANES), 1)
+    extra[...] = jnp.where(lane == 0, total(energy), total(curvature))
 
 
 def gathered_scalars(got, count):
@@ -1364,13 +1361,14 @@
             group = jnp.zeros((1, LANES), jnp.float32)
             spot = lane[0:1] // 32
             for gy in range(4):
-                line = got[gx * 4 + gy, pl.ds(2 + ex, 1), :]
-                own = jnp.where(spot == gy, line, own)
-                group = jnp.where(spot == (gy + 1) % 4, line, group)
+                line = got[gx * 4 + gy, :, pl.ds(LANES, LANES)]
+                own = jnp.where(spot == (gy + 2 * ex) % 4, line, own)
+                group = jnp.where(spot == (gy + 1 + 2 * ex) % 4, line, group)
             kappa[ex, pl.ds(gx, 1), :] = own
             number[ex, pl.ds(gx, 1), :] = group
     grid = [jnp.zeros(TILE, jnp.float32) for _ in range(2)]
-    numbers = [pltpu.roll(number[ex], 96, 1) for ex in range(2)]
+    numbers = [pltpu.roll(number[0], 96, 1), pltpu.roll(number[1], 32, 1)]
+    kappa = [kappa[0], pltpu.roll(kappa[1], 64, 1)]
     for q in range(4):
         for c in range(NCD):
             mine = jnp.where(lane == row * 16 + q * 4 + c, values, 0.0)
@@ -1429,12 +1427,16 @@
     dual = jnp.zeros((1, LANES), jnp.float32)
     sums = [jnp.zeros((1, LANES), jnp.float32) for _ in range(4)]
     for i in range(per):
-        line = got[i, pl.ds(0, 1), :]
-        rest = jnp.where(row_lane // NCD == i, line, rest)
-        dual = dual + got[i, pl.ds(1, 1), :]
+        line = got[i, :, pl.ds(0, LANES)]
+        mine = row_lane // NCD == (i + AWAY) % per
+        known = row_lane // NCD == (i + BEYOND) % per
+        rest = jnp.where(mine, line, rest)
+        dual = dual + jnp.where(mine | known, 0.0, line)
         for c in range(4):
-            sums[c] = sums[c] + jnp.where(row_lane == ((i + 1) % per) * NCD + c, line, 0.0)
-        matrix[pl.ds(i * NCD, NCD), :] = got[i, pl.ds(4, NCD), :]
+            sums[c] = sums[c] + jnp.where(row_lane == ((i + BEYOND) % per) * NCD + c, line, 0.0)
+            block = got[i, :, pl.ds((2 + c) * LANES, LANES)]
+            matrix[pl.ds(i * NCD + c, 1), :] = block
+    rest = pltpu.roll(rest, (per - AWAY) * NCD, 1)
     energy, curvature, square, self_energy = [
         jnp.sum(value, axis=1, keepdims=True) for value in sums
     ]
@@ -1514,7 +1516,7 @@
     elems_z = length // NODES
     devices = lax.axis_size("gx") * lax.axis_size("gy")
     blocks = coarse_inverse.shape[1] // LANES
-    pack_rows = -(-(1 + NCD * blocks) // 8) * 8
+    pack_rows = 1 + NCD * blocks
     tiles_np, mats_np = constant_tables(elems_z)
     ctab, zmat = jnp.asarray(tiles_np), jnp.asarray(mats_np)
     one = fields.shape[1:]
@@ -1542,7 +1544,7 @@
     )(fields)
     pack, facts = call(
         pack_kernel,
-        [(pack_rows, LANES), TILE],
+        [(pack_rows, LANES), (1, 6 * LANES)],
         cost_estimate=beside,
     )(inv_density, elem_group, coarse_inverse)
     y_got = swap(first, second, "gy")
@@ -1572,7 +1574,8 @@
         share, *y_got, ctab, zmat
     )
     side_shape = (2, 2, 8, LANES)
-    (fields_new,) = call(emit_kernel, [four], cost_estimate=beside)(begun, *x_got)
+    fields_got = x_got
+    fields_begun = begun
     resid, own, msg = call(
         advance_kernel,
         [one, one, (devices, 16, LANES)],
@@ -1587,12 +1590,15 @@
     y_got = swap(first, second, "gy")
     first, second = call(turn_smooth_kernel, [smooth_shape, smooth_shape])(own, inner_x, *y_got)
     x_got = swap(first, second, "gx")
+    fields_new, extra = call(emit_kernel, [four, (1, LANES)], cost_estimate=beside)(
+        fields_begun, *fields_got, extra
+    )
     begun, begun_scaled, given = call(
         ready_kernel, [one, one, one], [one], cost_estimate=beside
     )(own, *y_got, inv_diag, kap, ctab, zmat)
     image, image_smoothed, msg = call(
         smooth_kernel,
-        [one, one, (devices, 8, LANES) if grid_fits else rows],
+        [one, one, (devices, 1, 6 * LANES) if grid_fits else rows],
         [one, one, side_shape],
     )(
         begun, begun_scaled, given, *y_got, *x_got, inv_diag, kap, grp, extra, facts, ctab, zmat

time: 74.2 us -> 73.5 us (level)
  blocking collectives: 24.7 us -> 41.9 us
  starting transfers between devices: 24.8 us -> 15.2 us
  waiting for transfers between devices: 10.5 us -> 2.29 us
    all_to_all x1 -> x2, blocking collectives: 24.7 us -> 41.9 us  [exchange_all(): return lax.all_to_all(msg, BOTH, 0, 0, tiled=True)]
    all_to_all x1 -> x0, starting transfers between devices: 9.67 us -> none  [exchange_all(): return lax.all_to_all(msg, BOTH, 0, 0, tiled=True)]
    all_to_all x1 -> x0, waiting for transfers between devices: 7.39 us -> none  [exchange_all(): return lax.all_to_all(msg, BOTH, 0, 0, tiled=True)]
    ppermute x6, waiting for transfers between devices: 3.1 us -> 2.27 us  [swap(): return (lax.ppermute(first, axis, first_pairs), second_got)]
  transfers between devices with their start and end apart: 13 -> 12, of which waited for: 5 -> 4; matrix products, arithmetic and copies ran while one was open for 0% -> 0% of each run, Pallas kernels for 6% -> 7%
where the time goes in v8:
time: 73.5 us; the launch traced here: 73.1 us
  blocking collectives  41.9 us (57%)
  starting transfers between devices  15.2 us (21%)
  Pallas kernels  10.5 us (14%)
  local copies, waits for them, and re-layouts  2.46 us (3%)
  waiting for transfers between devices  2.29 us (3%)
  between operations  0.84 us (1%)
    all_to_all x2, blocking collectives, exchange_all(): return lax.all_to_all(msg, BOTH, 0, 0, tiled=True)  41.9 us
    ppermute x6, starting transfers between devices, swap(): return (lax.ppermute(first, axis, first_pairs), second_got)  11.2 us
    ppermute x6, starting transfers between devices, swap(): second_got = lax.ppermute(second, axis, second_pairs)  3.92 us
    unnamed x14, local copies, waits for them, and re-layouts  2.46 us
    pallas_call x1, Pallas kernels, per_device(): call(prepare_kernel, [four, four, edge_shape, one], [four, four], cost_es...  2.33 us
    ppermute x6, waiting for transfers between devices, swap(): return (lax.ppermute(first, axis, first_pairs), second_got)  2.27 us
    pallas_call x1, Pallas kernels, per_device(): call(finish_kernel, [one], [(LANES, LANES), (2,) + TILE, (2,) + TILE])  1.49 us
  transfers between devices with their start and end apart: 12, of which 4 were waited for; matrix products, arithmetic and copies ran while one was open for 0% of the time, Pallas kernels for 7%

profile of v8, /device:TPU:0, one launch (start us, length us, event | category | flops | bytes accessed | tf_op | source)
XLA Modules:
  0.0 73.1 jit_solution(3256821496044709029)
XLA Ops:
  0.7 1.1 %copy-done.2 = f32[4,2,8,2,8,128]{5,4,3,2,1,0:T(8,128)S(1)} copy-done((f32[4,2,8,2,8,128]{5,4,3,2,1,0:T(8,128)S(1)}, f32[4,2,8,2,8,128]{5,4,3,2,1,0:T(8,128)}, u32[]{:S(2)}) %copy-start.2) | copy-done | bytes 524312
  1.7 0.4 shard_map.86
  2.2 0.5 collective-permute-start
  2.7 0.7 collective-permute-start.1
  3.4 0.7 copy-done.5
  4.1 0.7 copy-done.6
  4.8 0.4 shard_map.88
  5.2 2.6 %collective-permute-start.2 = (f32[69,128]{1,0:T(8,128)S(1)}, f32[69,128]{1,0:T(8,128)S(1)}, u32[]{:S(2)}, u32[]{:S(2)}) collective-permute-start(f32[69,128]{1,0:T(8,128)S(1)} %get-tuple-element.54), channel_id=1, source_target_pairs={{0,4},{4,0},{8,12},{12,8},{16,20},{20,16},{24,28},{28,24},{1,5},{5... | collective-permute-start | bytes 105992 | tf_op jit(solution)/shard_map/ppermute | solution.py:1511
  7.8 0.7 collective-permute-start.3
  8.5 2.3 %shard_map.87 = (f32[4,2,8,2,8,128]{5,4,3,2,1,0:T(8,128)S(1)}, f32[4,2,8,2,8,128]{5,4,3,2,1,0:T(8,128)S(1)}, f32[4,2,2,8,128]{4,3,2,1,0:T(8,128)S(1)}, f32[2,8,2,8,128]{4,3,2,1,0:T(8,128)S(1)}) custom-call(f32[4,2,8,2,8,128]{5,4,3,2,1,0:T(8,128)S(1)} %get-tuple-element.45.summed, f32[2,8,2,8,128]{4,3,2,1,0:T(8,128)S(1)} %copy-done.3, ...), custom_call_target="tpu_custom_call" | custom-call | flops 10000000 | bytes 1000000 | tf_op jit(solution)/shard_map/pallas_call | solution.py:1556
  10.8 1.0 %shard_map.90 = (f32[4,2,8,2,8,128]{5,4,3,2,1,0:T(8,128)S(1)}, f32[2,4,2,8,128]{4,3,2,1,0:T(8,128)S(1)}, f32[2,2,8,128]{3,2,1,0:T(8,128)S(1)}, f32[97,128]{1,0:T(8,128)S(1)}, f32[97,128]{1,0:T(8,128)S(1)}) custom-call(f32[4,2,8,2,8,128]{5,4,3,2,1,0:T(8,128)S(1)} %get-tuple-element.48.begun, f32[4,2,8,2,8,128]{5,4,3,2,1,0:T(8,128)S(1)} %get-tuple-element.49.given, ...), custom_call_target="tpu_custom_call" | custom-call | tf_op jit(solution)/shard_map/pallas_call | solution.py:1559
  11.9 3.0 %collective-permute-start.4 = (f32[97,128]{1,0:T(8,128)S(1)}, f32[97,128]{1,0:T(8,128)S(1)}, u32[]{:S(2)}, u32[]{:S(2)}) collective-permute-start(f32[97,128]{1,0:T(8,128)S(1)} %get-tuple-element.57), channel_id=1, source_target_pairs={{0,1},{1,0},{2,3},{3,2},{4,5},{5,4},{6,7},{7,6},{8,9},{9,8},{10,11... | collective-permute-start | bytes 149000 | tf_op jit(solution)/shard_map/ppermute | solution.py:1511
  14.9 0.7 collective-permute-start.5
  15.6 0.2 collective-permute-done.4.y_first
  15.8 4.1 %collective-permute-start.6 = (f32[82,128]{1,0:T(8,128)S(1)}, f32[82,128]{1,0:T(8,128)S(1)}, u32[]{:S(2)}, u32[]{:S(2)}) collective-permute-start(f32[82,128]{1,0:T(8,128)S(1)} %get-tuple-element.62), channel_id=1, source_target_pairs={{0,4},{4,0},{8,12},{12,8},{16,20},{20,16},{24,28},{28,24},{1,5},{5... | collective-permute-start | bytes 125960 | tf_op jit(solution)/shard_map/ppermute | solution.py:1511
  19.9 0.7 collective-permute-start.7
  20.5 0.5 shard_map.93
  21.0 0.5 shard_map.91
  21.5 0.4 collective-permute-done.6.x_first
  21.9 0.8 %shard_map.94 = (f32[2,8,2,8,128]{4,3,2,1,0:T(8,128)S(1)}, f32[2,8,2,8,128]{4,3,2,1,0:T(8,128)S(1)}, f32[32,16,128]{2,1,0:T(8,128)S(1)}) custom-call(f32[4,2,8,2,8,128]{5,4,3,2,1,0:T(8,128)S(1)} %get-tuple-element.59.begun, f32[2,8,2,8,128]{4,3,2,1,0:T(8,128)S(1)} %get-tuple-element.64.given, f32[97,128]{1,0:T(8,128)S(1)} %collective-permute-done.4.y_first, ...), custom_call_target="tpu_custom_call" | custom-call | tf_op jit(solution)/shard_map/pallas_call | solution.py:1579
  22.7 24.6 %all_to_all.10.got = f32[32,16,128]{2,1,0:T(8,128)S(1)} all-to-all(f32[32,16,128]{2,1,0:T(8,128)S(1)} %get-tuple-element.68), channel_id=1, replica_groups=mesh['gx'=8,'gy'=4] {'gx','gy'}, dimensions={0} | all-to-all | bytes 524288 | tf_op jit(solution)/shard_map/all_to_all | solution.py:1538
  47.3 0.7 shard_map.95
  48.1 0.7 collective-permute-start.9
  48.7 0.5 collective-permute-done.8.y_first
  49.3 1.0 %collective-permute-start.10 = (f32[34,128]{1,0:T(8,128)S(1)}, f32[34,128]{1,0:T(8,128)S(1)}, u32[]{:S(2)}, u32[]{:S(2)}) collective-permute-start(f32[34,128]{1,0:T(8,128)S(1)} %get-tuple-element.81), channel_id=1, source_target_pairs={{0,4},{4,0},{8,12},{12,8},{16,20},{20,16},{24,28},{28,24},{1,5},{5... | collective-permute-start | bytes 52232 | tf_op jit(solution)/shard_map/ppermute | solution.py:1511
  50.2 0.7 collective-permute-start.11
  50.9 0.8 %shard_map.96 = (f32[4,2,8,2,8,128]{5,4,3,2,1,0:T(8,128)}, f32[1,128]{1,0:T(1,128)S(1)}) custom-call(f32[4,2,8,2,8,128]{5,4,3,2,1,0:T(8,128)S(1)} %get-tuple-element.59.begun, f32[82,128]{1,0:T(8,128)S(1)} %collective-permute-done.6.x_first, f32[82,128]{1,0:T(8,128)S(1)} %collective-permute-done.7.x_second, f32[1,128]{1,0:T(1,128)S(1)} %get-tuple-element.72.extra), custom_call_target="tpu_custom_call" | custom-call | flops 10000000 | bytes 1000000 | tf_op jit(solution)/shard_map/pallas_call | solution.py:1593
  51.7 0.2 shard_map.97
  52.0 1.1 %collective-permute-done.10.x_first = f32[34,128]{1,0:T(8,128)S(1)} collective-permute-done((f32[34,128]{1,0:T(8,128)S(1)}, f32[34,128]{1,0:T(8,128)S(1)}, u32[]{:S(2)}, u32[]{:S(2)}) %collective-permute-start.10) | collective-permute-done | bytes 17440 | tf_op jit(solution)/shard_map/ppermute | solution.py:1511
  53.1 1.2 %shard_map.99 = (f32[2,8,2,8,128]{4,3,2,1,0:T(8,128)}, f32[2,8,2,8,128]{4,3,2,1,0:T(8,128)S(1)}, f32[32,1,768]{2,1,0:T(1,128)S(1)}) custom-call(f32[2,8,2,8,128]{4,3,2,1,0:T(8,128)S(1)} %get-tuple-element.77.begun, f32[2,8,2,8,128]{4,3,2,1,0:T(8,128)S(1)} %get-tuple-element.78.begun_scaled, f32[2,8,2,8,128]{4,3,2,1,0:T(8,128)S(1)} %get-tuple-element.79.given, ...), custom_call_target="tpu_custom_call" | custom-call | tf_op jit(solution)/shard_map/pallas_call | solution.py:1599
  54.4 17.3 %all_to_all.11.got = f32[32,1,768]{2,1,0:T(1,128)S(1)} all-to-all(f32[32,1,768]{2,1,0:T(1,128)S(1)} %get-tuple-element.85), channel_id=1, replica_groups=mesh['gx'=8,'gy'=4] {'gx','gy'}, dimensions={0} | all-to-all | bytes 196608 | tf_op jit(solution)/shard_map/all_to_all | solution.py:1538
  71.6 1.5 %shard_map.100 = f32[2,8,2,8,128]{4,3,2,1,0:T(8,128)} custom-call(f32[32,1,768]{2,1,0:T(1,128)S(1)} %all_to_all.11.got, f32[16,128]{1,0:T(8,128)S(1)} %get-tuple-element.67.grp, f32[2,8,2,8,128]{4,3,2,1,0:T(8,128)S(1)} %get-tuple-element.86.direction, f32[2,8,2,8,128]{4,3,2,1,0:T(8,128)S(1)} %get-tuple-element.87.smoothed), custom_call_target="tpu_custom_call" | custom-call | tf_op jit(solution)/shard_map/pallas_call | solution.py:1608
  (23 shorter events, 0.2 us)
Async XLA Ops:
  0.6 7.8 %copy-start = (bf16[3,256,256]{2,1,0:T(8,128)(2,1)S(1)}, bf16[3,256,256]{2,1,0:T(8,128)(2,1)}, u32[]{:S(2)}) copy-start(bf16[3,256,256]{2,1,0:T(8,128)(2,1)} %constant.5.clone.zmat) | copy-start | bytes 1179652
  0.6 1.1 %copy-start.2 = (f32[4,2,8,2,8,128]{5,4,3,2,1,0:T(8,128)S(1)}, f32[4,2,8,2,8,128]{5,4,3,2,1,0:T(8,128)}, u32[]{:S(2)}) copy-start(f32[4,2,8,2,8,128]{5,4,3,2,1,0:T(8,128)} %fields.1) | copy-start | bytes 1572868
  1.7 1.6 %copy-start.4 = (f32[2,2,16]{2,1,0:T(2,128)S(1)}, f32[2,2,16]{2,1,0:T(2,128)}, u32[]{:S(2)}) copy-start(f32[2,2,16]{2,1,0:T(2,128)} %kappa.1) | copy-start | bytes 772
  1.7 6.7 %copy-start.3 = (f32[2,8,2,8,128]{4,3,2,1,0:T(8,128)S(1)}, f32[2,8,2,8,128]{4,3,2,1,0:T(8,128)}, u32[]{:S(2)}) copy-start(f32[2,8,2,8,128]{4,3,2,1,0:T(8,128)} %visc.3) | copy-start | bytes 393220
  2.2 6.3 %copy-start.1 = (f32[30,8,128]{2,1,0:T(8,128)S(1)}, f32[30,8,128]{2,1,0:T(8,128)}, u32[]{:S(2)}) copy-start(f32[30,8,128]{2,1,0:T(8,128)} %constant.4.clone.ctab) | copy-start | bytes 368644
  2.2 3.0 %collective-permute-start = (f32[64,128]{1,0:T(8,128)S(1)}, f32[64,128]{1,0:T(8,128)S(1)}, u32[]{:S(2)}, u32[]{:S(2)}) collective-permute-start(f32[64,128]{1,0:T(8,128)S(1)} %get-tuple-element.46), channel_id=1, source_target_pairs={{0,1},{1,0},{2,3},{3,2},{4,5},{5,4},{6,7},{7,6},{8,9},{9,8},{10,11... | collective-permute-start | bytes 98312 | tf_op jit(solution)/shard_map/ppermute | solution.py:1511
  2.7 2.4 %collective-permute-start.1 = (f32[64,128]{1,0:T(8,128)S(1)}, f32[64,128]{1,0:T(8,128)S(1)}, u32[]{:S(2)}, u32[]{:S(2)}) collective-permute-start(f32[64,128]{1,0:T(8,128)S(1)} %get-tuple-element.47), channel_id=1, source_target_pairs={{1,2},{2,1},{5,6},{6,5},{9,10},{10,9},{13,14},{14,13},{17,18},{18,... | collective-permute-start | bytes 98312 | tf_op jit(solution)/shard_map/ppermute | solution.py:1510
  3.4 0.7 copy-start.5
  4.1 0.7 copy-start.6
  5.2 5.6 %collective-permute-start.2 = (f32[69,128]{1,0:T(8,128)S(1)}, f32[69,128]{1,0:T(8,128)S(1)}, u32[]{:S(2)}, u32[]{:S(2)}) collective-permute-start(f32[69,128]{1,0:T(8,128)S(1)} %get-tuple-element.54), channel_id=1, source_target_pairs={{0,4},{4,0},{8,12},{12,8},{16,20},{20,16},{24,28},{28,24},{1,5},{5... | collective-permute-start | bytes 105992 | tf_op jit(solution)/shard_map/ppermute | solution.py:1511
  7.8 3.0 %collective-permute-start.3 = (f32[69,128]{1,0:T(8,128)S(1)}, f32[69,128]{1,0:T(8,128)S(1)}, u32[]{:S(2)}, u32[]{:S(2)}) collective-permute-start(f32[69,128]{1,0:T(8,128)S(1)} %get-tuple-element.55), channel_id=1, source_target_pairs={{4,8},{8,4},{12,16},{16,12},{20,24},{24,20},{5,9},{9,5},{13,17},{1... | collective-permute-start | bytes 105992 | tf_op jit(solution)/shard_map/ppermute | solution.py:1510
  11.9 3.9 %collective-permute-start.4 = (f32[97,128]{1,0:T(8,128)S(1)}, f32[97,128]{1,0:T(8,128)S(1)}, u32[]{:S(2)}, u32[]{:S(2)}) collective-permute-start(f32[97,128]{1,0:T(8,128)S(1)} %get-tuple-element.57), channel_id=1, source_target_pairs={{0,1},{1,0},{2,3},{3,2},{4,5},{5,4},{6,7},{7,6},{8,9},{9,8},{10,11... | collective-permute-start | bytes 149000 | tf_op jit(solution)/shard_map/ppermute | solution.py:1511
  14.9 0.9 %collective-permute-start.5 = (f32[97,128]{1,0:T(8,128)S(1)}, f32[97,128]{1,0:T(8,128)S(1)}, u32[]{:S(2)}, u32[]{:S(2)}) collective-permute-start(f32[97,128]{1,0:T(8,128)S(1)} %get-tuple-element.58), channel_id=1, source_target_pairs={{1,2},{2,1},{5,6},{6,5},{9,10},{10,9},{13,14},{14,13},{17,18},{18,... | collective-permute-start | bytes 149000 | tf_op jit(solution)/shard_map/ppermute | solution.py:1510
  15.8 6.1 %collective-permute-start.6 = (f32[82,128]{1,0:T(8,128)S(1)}, f32[82,128]{1,0:T(8,128)S(1)}, u32[]{:S(2)}, u32[]{:S(2)}) collective-permute-start(f32[82,128]{1,0:T(8,128)S(1)} %get-tuple-element.62), channel_id=1, source_target_pairs={{0,4},{4,0},{8,12},{12,8},{16,20},{20,16},{24,28},{28,24},{1,5},{5... | collective-permute-start | bytes 125960 | tf_op jit(solution)/shard_map/ppermute | solution.py:1511
  19.9 2.0 %collective-permute-start.7 = (f32[82,128]{1,0:T(8,128)S(1)}, f32[82,128]{1,0:T(8,128)S(1)}, u32[]{:S(2)}, u32[]{:S(2)}) collective-permute-start(f32[82,128]{1,0:T(8,128)S(1)} %get-tuple-element.63), channel_id=1, source_target_pairs={{4,8},{8,4},{12,16},{16,12},{20,24},{24,20},{5,9},{9,5},{13,17},{1... | collective-permute-start | bytes 125960 | tf_op jit(solution)/shard_map/ppermute | solution.py:1510
  48.0 1.3 %collective-permute-start.8 = (f32[34,128]{1,0:T(8,128)S(1)}, f32[34,128]{1,0:T(8,128)S(1)}, u32[]{:S(2)}, u32[]{:S(2)}) collective-permute-start(f32[34,128]{1,0:T(8,128)S(1)} %get-tuple-element.75), channel_id=1, source_target_pairs={{0,1},{1,0},{2,3},{3,2},{4,5},{5,4},{6,7},{7,6},{8,9},{9,8},{10,11... | collective-permute-start | bytes 52232 | tf_op jit(solution)/shard_map/ppermute | solution.py:1511
  48.1 1.2 %collective-permute-start.9 = (f32[34,128]{1,0:T(8,128)S(1)}, f32[34,128]{1,0:T(8,128)S(1)}, u32[]{:S(2)}, u32[]{:S(2)}) collective-permute-start(f32[34,128]{1,0:T(8,128)S(1)} %get-tuple-element.76), channel_id=1, source_target_pairs={{1,2},{2,1},{5,6},{6,5},{9,10},{10,9},{13,14},{14,13},{17,18},{18,... | collective-permute-start | bytes 52232 | tf_op jit(solution)/shard_map/ppermute | solution.py:1510
  49.3 3.8 %collective-permute-start.10 = (f32[34,128]{1,0:T(8,128)S(1)}, f32[34,128]{1,0:T(8,128)S(1)}, u32[]{:S(2)}, u32[]{:S(2)}) collective-permute-start(f32[34,128]{1,0:T(8,128)S(1)} %get-tuple-element.81), channel_id=1, source_target_pairs={{0,4},{4,0},{8,12},{12,8},{16,20},{20,16},{24,28},{28,24},{1,5},{5... | collective-permute-start | bytes 52232 | tf_op jit(solution)/shard_map/ppermute | solution.py:1511
  50.2 2.9 %collective-permute-start.11 = (f32[34,128]{1,0:T(8,128)S(1)}, f32[34,128]{1,0:T(8,128)S(1)}, u32[]{:S(2)}, u32[]{:S(2)}) collective-permute-start(f32[34,128]{1,0:T(8,128)S(1)} %get-tuple-element.82), channel_id=1, source_target_pairs={{4,8},{8,4},{12,16},{16,12},{20,24},{24,20},{5,9},{9,5},{13,17},{1... | collective-permute-start | bytes 52232 | tf_op jit(solution)/shard_map/ppermute | solution.py:1510

commit v9 on v8

--- a/solution.py
+++ b/solution.py
@@ -173,10 +173,10 @@
         return below + self.to_high(above), above + self.to_low(below)
 
     def before_x(self, first, second):
+        return jnp.where(self.even_x, first, second)
+
+    def after_x(self, first, second):
         return jnp.where(self.even_x, second, first)
-
-    def after_x(self, first, second):
-        return jnp.where(self.even_x, first, second)
 
     def before_y(self, first, second):
         return jnp.where(self.even_y, second, first)
@@ -1507,8 +1507,10 @@
     count = lax.axis_size(axis)
     first_pairs = [(i, i ^ 1) for i in range(count) if i ^ 1 < count]
     second_pairs = [(i, ((i + 1) ^ 1) - 1) for i in range(1, count) if ((i + 1) ^ 1) - 1 < count]
-    second_got = lax.ppermute(second, axis, second_pairs)
-    return lax.ppermute(first, axis, first_pairs), second_got
+    if axis in ('gx',):
+        first_pairs, second_pairs = second_pairs, first_pairs
+    first_got = lax.ppermute(first, axis, first_pairs)
+    return first_got, lax.ppermute(second, axis, second_pairs)
 
 
 def per_device(fields, viscosity, inv_density, elem_group, coarse_inverse):

time: 73.5 us -> 72.2 us (0.982)
  blocking collectives: 41.9 us -> 34.9 us
  starting transfers between devices: 15.2 us -> 20.7 us
    all_to_all x2, blocking collectives: 41.9 us -> 34.9 us  [exchange_all(): return lax.all_to_all(msg, BOTH, 0, 0, tiled=True)]
    ppermute x12, starting transfers between devices: 15.2 us -> 20.7 us  [the longest x6 15.4 us: swap(): return (first_got, lax.ppermute(second, axis, second_pairs))]
where the time goes in v9:
time: 72.2 us; the launch traced here: 71.9 us
  blocking collectives  34.9 us (48%)
  starting transfers between devices  20.7 us (29%)
  Pallas kernels  10.5 us (15%)
  waiting for transfers between devices  2.47 us (3%)
  local copies, waits for them, and re-layouts  2.46 us (3%)
  between operations  0.84 us (1%)
    all_to_all x2, blocking collectives, exchange_all(): return lax.all_to_all(msg, BOTH, 0, 0, tiled=True)  34.9 us
    ppermute x6, starting transfers between devices, swap(): return (first_got, lax.ppermute(second, axis, second_pairs))  15.4 us
    ppermute x6, starting transfers between devices, swap(): first_got = lax.ppermute(first, axis, first_pairs)  5.33 us
    unnamed x14, local copies, waits for them, and re-layouts  2.46 us
    pallas_call x1, Pallas kernels, per_device(): call(prepare_kernel, [four, four, edge_shape, one], [four, four], cost_es...  2.32 us
    ppermute x6, waiting for transfers between devices, swap(): return (first_got, lax.ppermute(second, axis, second_pairs))  1.73 us
    pallas_call x1, Pallas kernels, per_device(): call(finish_kernel, [one], [(LANES, LANES), (2,) + TILE, (2,) + TILE])  1.49 us
  transfers between devices with their start and end apart: 12, of which 4 were waited for; matrix products, arithmetic and copies ran while one was open for 0% of the time, Pallas kernels for 7%

profile of v9, /device:TPU:0, one launch (start us, length us, event | category | flops | bytes accessed | tf_op | source)
XLA Modules:
  0.0 71.9 jit_solution(3058022572899650666)
XLA Ops:
  0.7 1.1 %copy-done.2 = f32[4,2,8,2,8,128]{5,4,3,2,1,0:T(8,128)S(1)} copy-done((f32[4,2,8,2,8,128]{5,4,3,2,1,0:T(8,128)S(1)}, f32[4,2,8,2,8,128]{5,4,3,2,1,0:T(8,128)}, u32[]{:S(2)}) %copy-start.2) | copy-done | bytes 524312
  1.7 0.4 shard_map.86
  2.2 0.5 collective-permute-start
  2.7 0.7 collective-permute-start.1
  3.4 0.7 copy-done.5
  4.1 0.7 copy-done.6
  4.8 0.4 shard_map.88
  5.2 0.7 collective-permute-start.2
  5.9 5.4 %collective-permute-start.3 = (f32[69,128]{1,0:T(8,128)S(1)}, f32[69,128]{1,0:T(8,128)S(1)}, u32[]{:S(2)}, u32[]{:S(2)}) collective-permute-start(f32[69,128]{1,0:T(8,128)S(1)} %get-tuple-element.55), channel_id=1, source_target_pairs={{0,4},{4,0},{8,12},{12,8},{16,20},{20,16},{24,28},{28,24},{1,5},{5... | collective-permute-start | bytes 105992 | tf_op jit(solution)/shard_map/ppermute | solution.py:1513
  11.3 2.3 %shard_map.87 = (f32[4,2,8,2,8,128]{5,4,3,2,1,0:T(8,128)S(1)}, f32[4,2,8,2,8,128]{5,4,3,2,1,0:T(8,128)S(1)}, f32[4,2,2,8,128]{4,3,2,1,0:T(8,128)S(1)}, f32[2,8,2,8,128]{4,3,2,1,0:T(8,128)S(1)}) custom-call(f32[4,2,8,2,8,128]{5,4,3,2,1,0:T(8,128)S(1)} %get-tuple-element.45.summed, f32[2,8,2,8,128]{4,3,2,1,0:T(8,128)S(1)} %copy-done.3, ...), custom_call_target="tpu_custom_call" | custom-call | flops 10000000 | bytes 1000000 | tf_op jit(solution)/shard_map/pallas_call | solution.py:1558
  13.6 1.0 %shard_map.90 = (f32[4,2,8,2,8,128]{5,4,3,2,1,0:T(8,128)S(1)}, f32[2,4,2,8,128]{4,3,2,1,0:T(8,128)S(1)}, f32[2,2,8,128]{3,2,1,0:T(8,128)S(1)}, f32[97,128]{1,0:T(8,128)S(1)}, f32[97,128]{1,0:T(8,128)S(1)}) custom-call(f32[4,2,8,2,8,128]{5,4,3,2,1,0:T(8,128)S(1)} %get-tuple-element.48.begun, f32[4,2,8,2,8,128]{5,4,3,2,1,0:T(8,128)S(1)} %get-tuple-element.49.given, ...), custom_call_target="tpu_custom_call" | custom-call | tf_op jit(solution)/shard_map/pallas_call | solution.py:1561
  14.7 2.7 %collective-permute-start.4 = (f32[97,128]{1,0:T(8,128)S(1)}, f32[97,128]{1,0:T(8,128)S(1)}, u32[]{:S(2)}, u32[]{:S(2)}) collective-permute-start(f32[97,128]{1,0:T(8,128)S(1)} %get-tuple-element.57), channel_id=1, source_target_pairs={{0,1},{1,0},{2,3},{3,2},{4,5},{5,4},{6,7},{7,6},{8,9},{9,8},{10,11... | collective-permute-start | bytes 149000 | tf_op jit(solution)/shard_map/ppermute | solution.py:1512
  17.4 0.7 collective-permute-start.5
  18.1 0.2 collective-permute-done.4.y_first
  18.3 0.7 collective-permute-start.6
  19.0 4.3 %collective-permute-start.7 = (f32[82,128]{1,0:T(8,128)S(1)}, f32[82,128]{1,0:T(8,128)S(1)}, u32[]{:S(2)}, u32[]{:S(2)}) collective-permute-start(f32[82,128]{1,0:T(8,128)S(1)} %get-tuple-element.63), channel_id=1, source_target_pairs={{0,4},{4,0},{8,12},{12,8},{16,20},{20,16},{24,28},{28,24},{1,5},{5... | collective-permute-start | bytes 125960 | tf_op jit(solution)/shard_map/ppermute | solution.py:1513
  23.3 0.5 shard_map.93
  23.8 0.5 shard_map.91
  24.3 1.0 %collective-permute-done.7.x_second = f32[82,128]{1,0:T(8,128)S(1)} collective-permute-done((f32[82,128]{1,0:T(8,128)S(1)}, f32[82,128]{1,0:T(8,128)S(1)}, u32[]{:S(2)}, u32[]{:S(2)}) %collective-permute-start.7) | collective-permute-done | bytes 42016 | tf_op jit(solution)/shard_map/ppermute | solution.py:1513
  25.4 0.8 %shard_map.94 = (f32[2,8,2,8,128]{4,3,2,1,0:T(8,128)S(1)}, f32[2,8,2,8,128]{4,3,2,1,0:T(8,128)S(1)}, f32[32,16,128]{2,1,0:T(8,128)S(1)}) custom-call(f32[4,2,8,2,8,128]{5,4,3,2,1,0:T(8,128)S(1)} %get-tuple-element.59.begun, f32[2,8,2,8,128]{4,3,2,1,0:T(8,128)S(1)} %get-tuple-element.64.given, f32[97,128]{1,0:T(8,128)S(1)} %collective-permute-done.4.y_first, ...), custom_call_target="tpu_custom_call" | custom-call | tf_op jit(solution)/shard_map/pallas_call | solution.py:1581
  26.1 20.4 %all_to_all.10.got = f32[32,16,128]{2,1,0:T(8,128)S(1)} all-to-all(f32[32,16,128]{2,1,0:T(8,128)S(1)} %get-tuple-element.68), channel_id=1, replica_groups=mesh['gx'=8,'gy'=4] {'gx','gy'}, dimensions={0} | all-to-all | bytes 524288 | tf_op jit(solution)/shard_map/all_to_all | solution.py:1540
  46.6 0.7 shard_map.95
  47.3 0.7 collective-permute-start.9
  48.0 0.5 collective-permute-done.8.y_first
  48.5 0.7 collective-permute-start.10
  49.2 3.7 %collective-permute-start.11 = (f32[34,128]{1,0:T(8,128)S(1)}, f32[34,128]{1,0:T(8,128)S(1)}, u32[]{:S(2)}, u32[]{:S(2)}) collective-permute-start(f32[34,128]{1,0:T(8,128)S(1)} %get-tuple-element.82), channel_id=1, source_target_pairs={{0,4},{4,0},{8,12},{12,8},{16,20},{20,16},{24,28},{28,24},{1,5},{5... | collective-permute-start | bytes 52232 | tf_op jit(solution)/shard_map/ppermute | solution.py:1513
  52.9 0.8 %shard_map.96 = (f32[4,2,8,2,8,128]{5,4,3,2,1,0:T(8,128)}, f32[1,128]{1,0:T(1,128)S(1)}) custom-call(f32[4,2,8,2,8,128]{5,4,3,2,1,0:T(8,128)S(1)} %get-tuple-element.59.begun, f32[82,128]{1,0:T(8,128)S(1)} %collective-permute-done.6.x_first, f32[82,128]{1,0:T(8,128)S(1)} %collective-permute-done.7.x_second, f32[1,128]{1,0:T(1,128)S(1)} %get-tuple-element.72.extra), custom_call_target="tpu_custom_call" | custom-call | flops 10000000 | bytes 1000000 | tf_op jit(solution)/shard_map/pallas_call | solution.py:1595
  53.7 0.2 shard_map.97
  54.0 0.7 collective-permute-done.11.x_second
  54.7 1.2 %shard_map.99 = (f32[2,8,2,8,128]{4,3,2,1,0:T(8,128)}, f32[2,8,2,8,128]{4,3,2,1,0:T(8,128)S(1)}, f32[32,1,768]{2,1,0:T(1,128)S(1)}) custom-call(f32[2,8,2,8,128]{4,3,2,1,0:T(8,128)S(1)} %get-tuple-element.77.begun, f32[2,8,2,8,128]{4,3,2,1,0:T(8,128)S(1)} %get-tuple-element.78.begun_scaled, f32[2,8,2,8,128]{4,3,2,1,0:T(8,128)S(1)} %get-tuple-element.79.given, ...), custom_call_target="tpu_custom_call" | custom-call | tf_op jit(solution)/shard_map/pallas_call | solution.py:1601
  55.9 14.5 %all_to_all.11.got = f32[32,1,768]{2,1,0:T(1,128)S(1)} all-to-all(f32[32,1,768]{2,1,0:T(1,128)S(1)} %get-tuple-element.85), channel_id=1, replica_groups=mesh['gx'=8,'gy'=4] {'gx','gy'}, dimensions={0} | all-to-all | bytes 196608 | tf_op jit(solution)/shard_map/all_to_all | solution.py:1540
  70.4 1.5 %shard_map.100 = f32[2,8,2,8,128]{4,3,2,1,0:T(8,128)} custom-call(f32[32,1,768]{2,1,0:T(1,128)S(1)} %all_to_all.11.got, f32[16,128]{1,0:T(8,128)S(1)} %get-tuple-element.67.grp, f32[2,8,2,8,128]{4,3,2,1,0:T(8,128)S(1)} %get-tuple-element.86.direction, f32[2,8,2,8,128]{4,3,2,1,0:T(8,128)S(1)} %get-tuple-element.87.smoothed), custom_call_target="tpu_custom_call" | custom-call | tf_op jit(solution)/shard_map/pallas_call | solution.py:1610
  (23 shorter events, 0.2 us)
Async XLA Ops:
  0.6 10.6 %copy-start = (bf16[3,256,256]{2,1,0:T(8,128)(2,1)S(1)}, bf16[3,256,256]{2,1,0:T(8,128)(2,1)}, u32[]{:S(2)}) copy-start(bf16[3,256,256]{2,1,0:T(8,128)(2,1)} %constant.5.clone.zmat) | copy-start | bytes 1179652
  0.6 1.1 %copy-start.2 = (f32[4,2,8,2,8,128]{5,4,3,2,1,0:T(8,128)S(1)}, f32[4,2,8,2,8,128]{5,4,3,2,1,0:T(8,128)}, u32[]{:S(2)}) copy-start(f32[4,2,8,2,8,128]{5,4,3,2,1,0:T(8,128)} %fields.1) | copy-start | bytes 1572868
  1.7 1.6 %copy-start.4 = (f32[2,2,16]{2,1,0:T(2,128)S(1)}, f32[2,2,16]{2,1,0:T(2,128)}, u32[]{:S(2)}) copy-start(f32[2,2,16]{2,1,0:T(2,128)} %kappa.1) | copy-start | bytes 772
  1.7 9.5 %copy-start.3 = (f32[2,8,2,8,128]{4,3,2,1,0:T(8,128)S(1)}, f32[2,8,2,8,128]{4,3,2,1,0:T(8,128)}, u32[]{:S(2)}) copy-start(f32[2,8,2,8,128]{4,3,2,1,0:T(8,128)} %visc.3) | copy-start | bytes 393220
  2.2 9.1 %copy-start.1 = (f32[30,8,128]{2,1,0:T(8,128)S(1)}, f32[30,8,128]{2,1,0:T(8,128)}, u32[]{:S(2)}) copy-start(f32[30,8,128]{2,1,0:T(8,128)} %constant.4.clone.ctab) | copy-start | bytes 368644
  2.2 3.0 %collective-permute-start = (f32[64,128]{1,0:T(8,128)S(1)}, f32[64,128]{1,0:T(8,128)S(1)}, u32[]{:S(2)}, u32[]{:S(2)}) collective-permute-start(f32[64,128]{1,0:T(8,128)S(1)} %get-tuple-element.46), channel_id=1, source_target_pairs={{0,1},{1,0},{2,3},{3,2},{4,5},{5,4},{6,7},{7,6},{8,9},{9,8},{10,11... | collective-permute-start | bytes 98312 | tf_op jit(solution)/shard_map/ppermute | solution.py:1512
  2.7 2.4 %collective-permute-start.1 = (f32[64,128]{1,0:T(8,128)S(1)}, f32[64,128]{1,0:T(8,128)S(1)}, u32[]{:S(2)}, u32[]{:S(2)}) collective-permute-start(f32[64,128]{1,0:T(8,128)S(1)} %get-tuple-element.47), channel_id=1, source_target_pairs={{1,2},{2,1},{5,6},{6,5},{9,10},{10,9},{13,14},{14,13},{17,18},{18,... | collective-permute-start | bytes 98312 | tf_op jit(solution)/shard_map/ppermute | solution.py:1513
  3.4 0.7 copy-start.5
  4.1 0.7 copy-start.6
  5.2 8.4 %collective-permute-start.2 = (f32[69,128]{1,0:T(8,128)S(1)}, f32[69,128]{1,0:T(8,128)S(1)}, u32[]{:S(2)}, u32[]{:S(2)}) collective-permute-start(f32[69,128]{1,0:T(8,128)S(1)} %get-tuple-element.54), channel_id=1, source_target_pairs={{4,8},{8,4},{12,16},{16,12},{20,24},{24,20},{5,9},{9,5},{13,17},{1... | collective-permute-start | bytes 105992 | tf_op jit(solution)/shard_map/ppermute | solution.py:1512
  5.9 7.7 %collective-permute-start.3 = (f32[69,128]{1,0:T(8,128)S(1)}, f32[69,128]{1,0:T(8,128)S(1)}, u32[]{:S(2)}, u32[]{:S(2)}) collective-permute-start(f32[69,128]{1,0:T(8,128)S(1)} %get-tuple-element.55), channel_id=1, source_target_pairs={{0,4},{4,0},{8,12},{12,8},{16,20},{20,16},{24,28},{28,24},{1,5},{5... | collective-permute-start | bytes 105992 | tf_op jit(solution)/shard_map/ppermute | solution.py:1513
  14.7 3.6 %collective-permute-start.4 = (f32[97,128]{1,0:T(8,128)S(1)}, f32[97,128]{1,0:T(8,128)S(1)}, u32[]{:S(2)}, u32[]{:S(2)}) collective-permute-start(f32[97,128]{1,0:T(8,128)S(1)} %get-tuple-element.57), channel_id=1, source_target_pairs={{0,1},{1,0},{2,3},{3,2},{4,5},{5,4},{6,7},{7,6},{8,9},{9,8},{10,11... | collective-permute-start | bytes 149000 | tf_op jit(solution)/shard_map/ppermute | solution.py:1512
  17.4 0.9 %collective-permute-start.5 = (f32[97,128]{1,0:T(8,128)S(1)}, f32[97,128]{1,0:T(8,128)S(1)}, u32[]{:S(2)}, u32[]{:S(2)}) collective-permute-start(f32[97,128]{1,0:T(8,128)S(1)} %get-tuple-element.58), channel_id=1, source_target_pairs={{1,2},{2,1},{5,6},{6,5},{9,10},{10,9},{13,14},{14,13},{17,18},{18,... | collective-permute-start | bytes 149000 | tf_op jit(solution)/shard_map/ppermute | solution.py:1513
  18.3 6.0 %collective-permute-start.6 = (f32[82,128]{1,0:T(8,128)S(1)}, f32[82,128]{1,0:T(8,128)S(1)}, u32[]{:S(2)}, u32[]{:S(2)}) collective-permute-start(f32[82,128]{1,0:T(8,128)S(1)} %get-tuple-element.62), channel_id=1, source_target_pairs={{4,8},{8,4},{12,16},{16,12},{20,24},{24,20},{5,9},{9,5},{13,17},{1... | collective-permute-start | bytes 125960 | tf_op jit(solution)/shard_map/ppermute | solution.py:1512
  19.0 6.4 %collective-permute-start.7 = (f32[82,128]{1,0:T(8,128)S(1)}, f32[82,128]{1,0:T(8,128)S(1)}, u32[]{:S(2)}, u32[]{:S(2)}) collective-permute-start(f32[82,128]{1,0:T(8,128)S(1)} %get-tuple-element.63), channel_id=1, source_target_pairs={{0,4},{4,0},{8,12},{12,8},{16,20},{20,16},{24,28},{28,24},{1,5},{5... | collective-permute-start | bytes 125960 | tf_op jit(solution)/shard_map/ppermute | solution.py:1513
  47.2 1.3 %collective-permute-start.8 = (f32[34,128]{1,0:T(8,128)S(1)}, f32[34,128]{1,0:T(8,128)S(1)}, u32[]{:S(2)}, u32[]{:S(2)}) collective-permute-start(f32[34,128]{1,0:T(8,128)S(1)} %get-tuple-element.75), channel_id=1, source_target_pairs={{0,1},{1,0},{2,3},{3,2},{4,5},{5,4},{6,7},{7,6},{8,9},{9,8},{10,11... | collective-permute-start | bytes 52232 | tf_op jit(solution)/shard_map/ppermute | solution.py:1512
  47.3 1.2 %collective-permute-start.9 = (f32[34,128]{1,0:T(8,128)S(1)}, f32[34,128]{1,0:T(8,128)S(1)}, u32[]{:S(2)}, u32[]{:S(2)}) collective-permute-start(f32[34,128]{1,0:T(8,128)S(1)} %get-tuple-element.76), channel_id=1, source_target_pairs={{1,2},{2,1},{5,6},{6,5},{9,10},{10,9},{13,14},{14,13},{17,18},{18,... | collective-permute-start | bytes 52232 | tf_op jit(solution)/shard_map/ppermute | solution.py:1513
  48.5 5.4 %collective-permute-start.10 = (f32[34,128]{1,0:T(8,128)S(1)}, f32[34,128]{1,0:T(8,128)S(1)}, u32[]{:S(2)}, u32[]{:S(2)}) collective-permute-start(f32[34,128]{1,0:T(8,128)S(1)} %get-tuple-element.81), channel_id=1, source_target_pairs={{4,8},{8,4},{12,16},{16,12},{20,24},{24,20},{5,9},{9,5},{13,17},{1... | collective-permute-start | bytes 52232 | tf_op jit(solution)/shard_map/ppermute | solution.py:1512
  49.2 5.5 %collective-permute-start.11 = (f32[34,128]{1,0:T(8,128)S(1)}, f32[34,128]{1,0:T(8,128)S(1)}, u32[]{:S(2)}, u32[]{:S(2)}) collective-permute-start(f32[34,128]{1,0:T(8,128)S(1)} %get-tuple-element.82), channel_id=1, source_target_pairs={{0,4},{4,0},{8,12},{12,8},{16,20},{20,16},{24,28},{28,24},{1,5},{5... | collective-permute-start | bytes 52232 | tf_op jit(solution)/shard_map/ppermute | solution.py:1513

commit v10 on v9

--- a/solution.py
+++ b/solution.py
@@ -801,30 +801,32 @@
                 own[ex, a, ey] = tiles[ex][a][ey]
     row = message(place, restricted(place, sums, grp), [])
     blank = jnp.where(place.row == 0, jnp.broadcast_to(row, TILE), 0.0)
-    zero = jnp.zeros(TILE, jnp.float32)
 
     def clear(i, carry):
-        msg[i, pl.ds(0, 8), :] = zero
-        msg[i, pl.ds(8, 8), :] = blank
+        msg[i] = blank
         return carry
 
-    lax.fori_loop(0, msg.shape[0], clear, 0)
-    for dx, dy, there in neighbours(place):
+    lax.fori_loop(0, msg.shape[0], clear, 0, unroll=msg.shape[0] <= 64)
+    across = Pairing(place)
+    for side, (ex, a) in enumerate(OUTER):
+        there, ix = across.beside(side)
 
         @pl.when(there)
         def _():
-            to = (place.ix + dx) * place.ny + place.iy + dy
-            ex, a = (0, 0) if dx < 0 else (1, 7)
-            ey, b = (0, 0) if dy < 0 else (1, 7)
-            if dy == 0:
-                msg[to, pl.ds(0, 8), :] = own[ex, a, 0]
-                msg[to, pl.ds(9, 7), :] = own[ex, a, 1, pl.ds(1, 7), :]
-            elif dx == 0:
-                for r in range(16):
-                    if r != 8:
-                        msg[to, pl.ds(r, 1), :] = own[r // 8, r % 8, ey, pl.ds(b, 1), :]
-            else:
-                msg[to, pl.ds(0, 1), :] = own[ex, a, ey, pl.ds(b, 1), :]
+            msg[ix * place.ny + place.iy] = own[ex, a, 0]
+            msg[ix * place.ny + across.twin, pl.ds(1, 7), :] = own[ex, a, 1, pl.ds(1, 7), :]
+
+        @pl.when(there & across.has_far)
+        def _():
+            msg[ix * place.ny + across.far, pl.ds(1, 1), :] = across.far_row(own, ex, a)
+
+    @pl.when(across.has_far)
+    def _():
+        for a in range(8):
+            msg[place.ix * place.ny + across.far, pl.ds(a, 1), :] = across.far_row(own, 0, a)
+            if a > 0:
+                to = place.ix * place.ny + across.beyond
+                msg[to, pl.ds(a, 1), :] = across.far_row(own, 1, a)
 
 
 def inner_along_y(place, y_first, y_second, before, after, ex, a, at, edge):
@@ -842,17 +844,56 @@
     return below, above
 
 
-def neighbours(place):
-    along = ((-1, place.prev_x), (0, None), (1, place.next_x))
-    across = ((-1, place.prev_y), (0, None), (1, place.next_y))
-    out = []
-    for dx, has_x in along:
-        for dy, has_y in across:
-            if dx == 0 and dy == 0:
-                continue
-            there = has_y if has_x is None else (has_x if has_y is None else has_x & has_y)
-            out.append((dx, dy, there))
-    return out
+class Pairing:
+    def __init__(self, place):
+        self.place = place
+        even = place.even_y
+        self.even = even
+        self.twin = jnp.where(even, place.iy + 1, place.iy - 1)
+        self.far = jnp.where(even, place.iy - 1, place.iy + 1)
+        self.has_far = jnp.where(even, place.iy - 1, place.ny - 2 - place.iy) >= 0
+        self.beyond = jnp.where(even, place.iy - 2, place.iy + 2)
+        self.twin_far = jnp.where(even, place.iy + 2, place.iy - 2)
+        self.twin_has_far = jnp.where(even, place.ny - 3 - place.iy, place.iy - 2) >= 0
+
+    def beside(self, side):
+        place = self.place
+        if side == 0:
+            return place.prev_x, place.ix - 1
+        return place.next_x, place.ix + 1
+
+    def far_row(self, field, ex, a):
+        low = field[ex, a, 0, pl.ds(0, 1), :]
+        return jnp.where(self.even, low, field[ex, a, 1, pl.ds(7, 1), :])
+
+    def twin_row(self, field, ex, a):
+        low = field[ex, a, 0, pl.ds(0, 1), :]
+        return jnp.where(self.even, field[ex, a, 1, pl.ds(7, 1), :], low)
+
+
+RELAY_FACE, RELAY_EDGE, RELAY_ROWS = 24, 40, 42
+
+
+def relay_kernel(got, own, out):
+    place = Place()
+    across = Pairing(place)
+    out[...] = jnp.zeros(out.shape, jnp.float32)
+    for side in range(2):
+        there, ix = across.beside(side)
+
+        @pl.when(there)
+        def _():
+            out[pl.ds(side * 8, 8), :] = got[ix * place.ny + across.twin]
+            corner = got[ix * place.ny + place.iy, pl.ds(0, 1), :]
+            out[pl.ds(RELAY_EDGE + side, 1), :] = corner
+
+    @pl.when(across.twin_has_far)
+    def _():
+        out[pl.ds(16, 8), :] = got[place.ix * place.ny + across.twin_far]
+
+    for ex in range(2):
+        for a in range(8):
+            out[pl.ds(RELAY_FACE + ex * 8 + a, 1), :] = across.twin_row(own, ex, a)
 
 
 SMOOTH_X, SMOOTH_Y, SMOOTH_EDGE, SMOOTH_ROWS = 16, 16, 32, 34
@@ -1110,16 +1151,19 @@
     return row
 
 
-def coarse_part(place, blocks, got, coarse, grp, at=0):
+def coarse_part(place, blocks, got, coarse, grp, others=()):
     lane = lax.broadcasted_iota(jnp.int32, (1, LANES), 1)
     values = [jnp.zeros((1, LANES), jnp.float32) for _ in range(blocks)]
     per = LANES // NCD
     for j in range(blocks):
 
         def gather(i, acc, j=j):
-            return jnp.where(lane // NCD == i, got[j * per + i, pl.ds(at, 1), :], acc)
+            return jnp.where(lane // NCD == i, got[j * per + i, pl.ds(0, 1), :], acc)
 
         values[j] = lax.fori_loop(0, per, gather, values[j], unroll=blocks == 1)
+        for there, device, row in others:
+            spot = (lane // NCD == device % per) & (device // per == j) & there
+            values[j] = jnp.where(spot, row, values[j])
 
     def solved(dx, dy, c):
         acc = None
@@ -1185,6 +1229,7 @@
 def first_direction_kernel(
     blocks,
     got,
+    relayed,
     coarse,
     grp,
     kap,
@@ -1204,31 +1249,60 @@
 ):
     place = Place()
     inv_mult = [1.0 / place.mult_tile(ey) for ey in range(2)]
-    part = coarse_part(place, blocks, got, coarse, grp, 8)
+    across = Pairing(place)
+    others = []
+    for side in range(2):
+        there, ix = across.beside(side)
+        others.append((there, ix * place.ny + place.iy, relayed[pl.ds(side * 8, 1), :]))
+    others.append(
+        (across.has_far, place.ix * place.ny + across.far, relayed[pl.ds(16, 1), :])
+    )
+    part = coarse_part(place, blocks, got, coarse, grp, others)
     image[...] = own[...]
-    for dx, dy, there in neighbours(place):
+    far_edge = jnp.where(across.even, 0, 7)
+
+    def add_row(ex, a, row, edge, low):
+        extra = jnp.where(place.row == edge, row, 0.0)
+        image[ex, a, 0] = image[ex, a, 0] + jnp.where(low, extra, 0.0)
+        image[ex, a, 1] = image[ex, a, 1] + jnp.where(low, 0.0, extra)
+
+    for ex in range(2):
+        for a in range(8):
+            row = relayed[pl.ds(RELAY_FACE + ex * 8 + a, 1), :]
+            add_row(ex, a, row, 7 - far_edge, ~across.even)
+
+    @pl.when(across.has_far)
+    def _():
+        for a in range(8):
+            row = got[place.ix * place.ny + across.far, pl.ds(a, 1), :]
+            add_row(0, a, row, far_edge, across.even)
+            if a == 7:
+                add_row(1, 0, row, far_edge, across.even)
+            if a > 0:
+                add_row(1, a, relayed[pl.ds(16 + a, 1), :], far_edge, across.even)
+
+    for side, (ex, a) in enumerate(OUTER):
+        there, ix = across.beside(side)
 
         @pl.when(there)
         def _():
-            frm = (place.ix + dx) * place.ny + place.iy + dy
-            ex, a = (0, 0) if dx < 0 else (1, 7)
-            ey, b = (0, 0) if dy < 0 else (1, 7)
-            edge = place.row == b
-            if dy == 0:
-                low = got[frm, pl.ds(0, 8), :]
-                high = jnp.where(
-                    place.row == 0, pltpu.roll(low, 1, 0), got[frm, pl.ds(8, 8), :]
-                )
-                image[ex, a, 0] = image[ex, a, 0] + low
-                image[ex, a, 1] = image[ex, a, 1] + high
-            elif dx == 0:
-                for r in range(16):
-                    line = got[frm, pl.ds(7 if r == 8 else r, 1), :]
-                    tile = image[r // 8, r % 8, ey]
-                    image[r // 8, r % 8, ey] = tile + jnp.where(edge, line, 0.0)
-            else:
-                line = got[frm, pl.ds(0, 1), :]
-                image[ex, a, ey] = image[ex, a, ey] + jnp.where(edge, line, 0.0)
+            low = got[ix * place.ny + place.iy]
+            high = jnp.where(
+                place.row == 0, pltpu.roll(low, 1, 0), relayed[pl.ds(side * 8, 8), :]
+            )
+            image[ex, a, 0] = image[ex, a, 0] + low
+            image[ex, a, 1] = image[ex, a, 1] + high
+            corner = jnp.where(
+                across.even,
+                relayed[pl.ds(RELAY_EDGE + side, 1), :],
+                got[ix * place.ny + across.twin, pl.ds(7, 1), :],
+            )
+            add_row(ex, a, corner, 7 - far_edge, ~across.even)
+
+        @pl.when(there & across.has_far)
+        def _():
+            corner = got[ix * place.ny + across.far, pl.ds(1, 1), :]
+            add_row(ex, a, corner, far_edge, across.even)
 
     energy = jnp.zeros(TILE, jnp.float32)
     for ex in range(2):
@@ -1580,15 +1654,19 @@
     fields_begun = begun
     resid, own, msg = call(
         advance_kernel,
-        [one, one, (devices, 16, LANES)],
+        [one, one, (devices, 8, LANES)],
         [one, one, side_shape, one, (3,) + side_shape],
     )(begun, given, *y_got, *x_got, inv_diag, kap, grp, ctab, zmat)
     got = exchange_all(msg)
+    (relayed,) = call(relay_kernel, [(RELAY_ROWS, LANES)])(got, own)
+    relayed = lax.ppermute(
+        relayed, "gy", [(i, i ^ 1) for i in range(lax.axis_size("gy")) if i ^ 1 < lax.axis_size("gy")]
+    )
     direction, own, inner_x, first, second, extra = call(
         functools.partial(first_direction_kernel, blocks),
         [one, one, inner_shape, smooth_shape, smooth_shape, (1, LANES)],
         [one, one],
-    )(got, coarse, grp, kap, inv_diag, resid, own, ctab, zmat)
+    )(got, relayed, coarse, grp, kap, inv_diag, resid, own, ctab, zmat)
     y_got = swap(first, second, "gy")
     first, second = call(turn_smooth_kernel, [smooth_shape, smooth_shape])(own, inner_x, *y_got)
     x_got = swap(first, second, "gx")

time: 72.2 us -> 70.7 us (0.979)
  blocking collectives: 34.9 us -> 32.6 us
  waiting for transfers between devices: 2.47 us -> 3.24 us
    all_to_all x2, blocking collectives: 34.9 us -> 32.6 us  [exchange_all(): return lax.all_to_all(msg, BOTH, 0, 0, tiled=True)]
    ppermute x0 -> x1, waiting for transfers between devices: none -> 0.98 us  [per_device(): lax.ppermute(relayed, 'gy', [(i, i ^ 1) for i in range(lax.axis_size('gy'...]
  transfers between devices with their start and end apart: 12 -> 13, of which waited for: 4 -> 5; matrix products, arithmetic and copies ran while one was open for 0% -> 0% of each run, Pallas kernels for 7% -> 7%
where the time goes in v10:
time: 70.7 us; the launch traced here: 70.4 us
  blocking collectives  32.6 us (46%)
  starting transfers between devices  20.9 us (30%)
  Pallas kernels  10.3 us (15%)
  waiting for transfers between devices  3.24 us (5%)
  local copies, waits for them, and re-layouts  2.46 us (3%)
  between operations  0.84 us (1%)
    all_to_all x2, blocking collectives, exchange_all(): return lax.all_to_all(msg, BOTH, 0, 0, tiled=True)  32.6 us
    ppermute x6, starting transfers between devices, swap(): return (first_got, lax.ppermute(second, axis, second_pairs))  15.1 us
    ppermute x6, starting transfers between devices, swap(): first_got = lax.ppermute(first, axis, first_pairs)  5.55 us
    unnamed x14, local copies, waits for them, and re-layouts  2.46 us
    pallas_call x1, Pallas kernels, per_device(): call(prepare_kernel, [four, four, edge_shape, one], [four, four], cost_es...  2.32 us
    ppermute x6, waiting for transfers between devices, swap(): return (first_got, lax.ppermute(second, axis, second_pairs))  1.73 us
    pallas_call x1, Pallas kernels, per_device(): call(finish_kernel, [one], [(LANES, LANES), (2,) + TILE, (2,) + TILE])  1.49 us
  transfers between devices with their start and end apart: 13, of which 5 were waited for; matrix products, arithmetic and copies ran while one was open for 0% of the time, Pallas kernels for 7%

profile of v10, /device:TPU:0, one launch (start us, length us, event | category | flops | bytes accessed | tf_op | source)
XLA Modules:
  0.0 70.4 jit_solution(14224411043930705944)
XLA Ops:
  0.7 1.1 %copy-done.2 = f32[4,2,8,2,8,128]{5,4,3,2,1,0:T(8,128)S(1)} copy-done((f32[4,2,8,2,8,128]{5,4,3,2,1,0:T(8,128)S(1)}, f32[4,2,8,2,8,128]{5,4,3,2,1,0:T(8,128)}, u32[]{:S(2)}) %copy-start.2) | copy-done | bytes 524312
  1.7 0.4 shard_map.86
  2.2 0.5 collective-permute-start
  2.7 0.7 collective-permute-start.1
  3.4 0.7 copy-done.5
  4.1 0.7 copy-done.6
  4.8 0.4 shard_map.88
  5.2 0.7 collective-permute-start.2
  5.9 5.4 %collective-permute-start.3 = (f32[69,128]{1,0:T(8,128)S(1)}, f32[69,128]{1,0:T(8,128)S(1)}, u32[]{:S(2)}, u32[]{:S(2)}) collective-permute-start(f32[69,128]{1,0:T(8,128)S(1)} %get-tuple-element.55), channel_id=1, source_target_pairs={{0,4},{4,0},{8,12},{12,8},{16,20},{20,16},{24,28},{28,24},{1,5},{5... | collective-permute-start | bytes 105992 | tf_op jit(solution)/shard_map/ppermute | solution.py:1587
  11.3 2.3 %shard_map.87 = (f32[4,2,8,2,8,128]{5,4,3,2,1,0:T(8,128)S(1)}, f32[4,2,8,2,8,128]{5,4,3,2,1,0:T(8,128)S(1)}, f32[4,2,2,8,128]{4,3,2,1,0:T(8,128)S(1)}, f32[2,8,2,8,128]{4,3,2,1,0:T(8,128)S(1)}) custom-call(f32[4,2,8,2,8,128]{5,4,3,2,1,0:T(8,128)S(1)} %get-tuple-element.45.summed, f32[2,8,2,8,128]{4,3,2,1,0:T(8,128)S(1)} %copy-done.3, ...), custom_call_target="tpu_custom_call" | custom-call | flops 10000000 | bytes 1000000 | tf_op jit(solution)/shard_map/pallas_call | solution.py:1632
  13.6 1.0 %shard_map.90 = (f32[4,2,8,2,8,128]{5,4,3,2,1,0:T(8,128)S(1)}, f32[2,4,2,8,128]{4,3,2,1,0:T(8,128)S(1)}, f32[2,2,8,128]{3,2,1,0:T(8,128)S(1)}, f32[97,128]{1,0:T(8,128)S(1)}, f32[97,128]{1,0:T(8,128)S(1)}) custom-call(f32[4,2,8,2,8,128]{5,4,3,2,1,0:T(8,128)S(1)} %get-tuple-element.48.begun, f32[4,2,8,2,8,128]{5,4,3,2,1,0:T(8,128)S(1)} %get-tuple-element.49.given, ...), custom_call_target="tpu_custom_call" | custom-call | tf_op jit(solution)/shard_map/pallas_call | solution.py:1635
  14.7 2.7 %collective-permute-start.4 = (f32[97,128]{1,0:T(8,128)S(1)}, f32[97,128]{1,0:T(8,128)S(1)}, u32[]{:S(2)}, u32[]{:S(2)}) collective-permute-start(f32[97,128]{1,0:T(8,128)S(1)} %get-tuple-element.57), channel_id=1, source_target_pairs={{0,1},{1,0},{2,3},{3,2},{4,5},{5,4},{6,7},{7,6},{8,9},{9,8},{10,11... | collective-permute-start | bytes 149000 | tf_op jit(solution)/shard_map/ppermute | solution.py:1586
  17.4 0.7 collective-permute-start.5
  18.3 0.7 collective-permute-start.6
  19.0 4.3 %collective-permute-start.7 = (f32[82,128]{1,0:T(8,128)S(1)}, f32[82,128]{1,0:T(8,128)S(1)}, u32[]{:S(2)}, u32[]{:S(2)}) collective-permute-start(f32[82,128]{1,0:T(8,128)S(1)} %get-tuple-element.63), channel_id=1, source_target_pairs={{0,4},{4,0},{8,12},{12,8},{16,20},{20,16},{24,28},{28,24},{1,5},{5... | collective-permute-start | bytes 125960 | tf_op jit(solution)/shard_map/ppermute | solution.py:1587
  23.3 0.5 shard_map.93
  23.8 0.5 shard_map.91
  24.3 1.0 %collective-permute-done.7.x_second = f32[82,128]{1,0:T(8,128)S(1)} collective-permute-done((f32[82,128]{1,0:T(8,128)S(1)}, f32[82,128]{1,0:T(8,128)S(1)}, u32[]{:S(2)}, u32[]{:S(2)}) %collective-permute-start.7) | collective-permute-done | bytes 42016 | tf_op jit(solution)/shard_map/ppermute | solution.py:1587
  25.4 0.6 shard_map.94
  25.9 18.1 %all_to_all.10.got = f32[32,8,128]{2,1,0:T(8,128)S(1)} all-to-all(f32[32,8,128]{2,1,0:T(8,128)S(1)} %get-tuple-element.68), channel_id=1, replica_groups=mesh['gx'=8,'gy'=4] {'gx','gy'}, dimensions={0} | all-to-all | bytes 262144 | tf_op jit(solution)/shard_map/all_to_all | solution.py:1614
  44.3 1.0 %collective-permute-done.8.relayed = f32[42,128]{1,0:T(8,128)S(1)} collective-permute-done((f32[42,128]{1,0:T(8,128)S(1)}, f32[42,128]{1,0:T(8,128)S(1)}, u32[]{:S(2)}, u32[]{:S(2)}) %collective-permute-start.8) | collective-permute-done | bytes 21536 | tf_op jit(solution)/shard_map/ppermute | solution.py:1662
  45.3 0.7 shard_map.96
  46.0 0.3 collective-permute-start.9
  46.2 0.7 collective-permute-start.10
  46.9 0.3 collective-permute-done.9.y_first
  47.2 0.7 collective-permute-start.11
  47.9 3.4 %collective-permute-start.12 = (f32[34,128]{1,0:T(8,128)S(1)}, f32[34,128]{1,0:T(8,128)S(1)}, u32[]{:S(2)}, u32[]{:S(2)}) collective-permute-start(f32[34,128]{1,0:T(8,128)S(1)} %get-tuple-element.82), channel_id=1, source_target_pairs={{0,4},{4,0},{8,12},{12,8},{16,20},{20,16},{24,28},{28,24},{1,5},{5... | collective-permute-start | bytes 52232 | tf_op jit(solution)/shard_map/ppermute | solution.py:1587
  51.3 0.8 %shard_map.97 = (f32[4,2,8,2,8,128]{5,4,3,2,1,0:T(8,128)}, f32[1,128]{1,0:T(1,128)S(1)}) custom-call(f32[4,2,8,2,8,128]{5,4,3,2,1,0:T(8,128)S(1)} %get-tuple-element.59.begun, f32[82,128]{1,0:T(8,128)S(1)} %collective-permute-done.6.x_first, f32[82,128]{1,0:T(8,128)S(1)} %collective-permute-done.7.x_second, f32[1,128]{1,0:T(1,128)S(1)} %get-tuple-element.72.extra), custom_call_target="tpu_custom_call" | custom-call | flops 10000000 | bytes 1000000 | tf_op jit(solution)/shard_map/pallas_call | solution.py:1673
  52.4 0.7 collective-permute-done.12.x_second
  53.1 1.2 %shard_map.100 = (f32[2,8,2,8,128]{4,3,2,1,0:T(8,128)}, f32[2,8,2,8,128]{4,3,2,1,0:T(8,128)S(1)}, f32[32,1,768]{2,1,0:T(1,128)S(1)}) custom-call(f32[2,8,2,8,128]{4,3,2,1,0:T(8,128)S(1)} %get-tuple-element.77.begun, f32[2,8,2,8,128]{4,3,2,1,0:T(8,128)S(1)} %get-tuple-element.78.begun_scaled, f32[2,8,2,8,128]{4,3,2,1,0:T(8,128)S(1)} %get-tuple-element.79.given, ...), custom_call_target="tpu_custom_call" | custom-call | tf_op jit(solution)/shard_map/pallas_call | solution.py:1679
  54.3 14.5 %all_to_all.11.got = f32[32,1,768]{2,1,0:T(1,128)S(1)} all-to-all(f32[32,1,768]{2,1,0:T(1,128)S(1)} %get-tuple-element.85), channel_id=1, replica_groups=mesh['gx'=8,'gy'=4] {'gx','gy'}, dimensions={0} | all-to-all | bytes 196608 | tf_op jit(solution)/shard_map/all_to_all | solution.py:1614
  68.9 1.5 %shard_map.101 = f32[2,8,2,8,128]{4,3,2,1,0:T(8,128)} custom-call(f32[32,1,768]{2,1,0:T(1,128)S(1)} %all_to_all.11.got, f32[16,128]{1,0:T(8,128)S(1)} %get-tuple-element.67.grp, f32[2,8,2,8,128]{4,3,2,1,0:T(8,128)S(1)} %get-tuple-element.86.direction, f32[2,8,2,8,128]{4,3,2,1,0:T(8,128)S(1)} %get-tuple-element.87.smoothed), custom_call_target="tpu_custom_call" | custom-call | tf_op jit(solution)/shard_map/pallas_call | solution.py:1688
  (26 shorter events, 0.9 us)
Async XLA Ops:
  0.6 10.6 %copy-start = (bf16[3,256,256]{2,1,0:T(8,128)(2,1)S(1)}, bf16[3,256,256]{2,1,0:T(8,128)(2,1)}, u32[]{:S(2)}) copy-start(bf16[3,256,256]{2,1,0:T(8,128)(2,1)} %constant.5.clone.zmat) | copy-start | bytes 1179652
  0.6 1.1 %copy-start.2 = (f32[4,2,8,2,8,128]{5,4,3,2,1,0:T(8,128)S(1)}, f32[4,2,8,2,8,128]{5,4,3,2,1,0:T(8,128)}, u32[]{:S(2)}) copy-start(f32[4,2,8,2,8,128]{5,4,3,2,1,0:T(8,128)} %fields.1) | copy-start | bytes 1572868
  1.7 1.6 %copy-start.4 = (f32[2,2,16]{2,1,0:T(2,128)S(1)}, f32[2,2,16]{2,1,0:T(2,128)}, u32[]{:S(2)}) copy-start(f32[2,2,16]{2,1,0:T(2,128)} %kappa.1) | copy-start | bytes 772
  1.7 9.5 %copy-start.3 = (f32[2,8,2,8,128]{4,3,2,1,0:T(8,128)S(1)}, f32[2,8,2,8,128]{4,3,2,1,0:T(8,128)}, u32[]{:S(2)}) copy-start(f32[2,8,2,8,128]{4,3,2,1,0:T(8,128)} %visc.3) | copy-start | bytes 393220
  2.2 9.1 %copy-start.1 = (f32[30,8,128]{2,1,0:T(8,128)S(1)}, f32[30,8,128]{2,1,0:T(8,128)}, u32[]{:S(2)}) copy-start(f32[30,8,128]{2,1,0:T(8,128)} %constant.4.clone.ctab) | copy-start | bytes 368644
  2.2 3.0 %collective-permute-start = (f32[64,128]{1,0:T(8,128)S(1)}, f32[64,128]{1,0:T(8,128)S(1)}, u32[]{:S(2)}, u32[]{:S(2)}) collective-permute-start(f32[64,128]{1,0:T(8,128)S(1)} %get-tuple-element.46), channel_id=1, source_target_pairs={{0,1},{1,0},{2,3},{3,2},{4,5},{5,4},{6,7},{7,6},{8,9},{9,8},{10,11... | collective-permute-start | bytes 98312 | tf_op jit(solution)/shard_map/ppermute | solution.py:1586
  2.7 2.4 %collective-permute-start.1 = (f32[64,128]{1,0:T(8,128)S(1)}, f32[64,128]{1,0:T(8,128)S(1)}, u32[]{:S(2)}, u32[]{:S(2)}) collective-permute-start(f32[64,128]{1,0:T(8,128)S(1)} %get-tuple-element.47), channel_id=1, source_target_pairs={{1,2},{2,1},{5,6},{6,5},{9,10},{10,9},{13,14},{14,13},{17,18},{18,... | collective-permute-start | bytes 98312 | tf_op jit(solution)/shard_map/ppermute | solution.py:1587
  3.4 0.7 copy-start.5
  4.1 0.7 copy-start.6
  5.2 8.4 %collective-permute-start.2 = (f32[69,128]{1,0:T(8,128)S(1)}, f32[69,128]{1,0:T(8,128)S(1)}, u32[]{:S(2)}, u32[]{:S(2)}) collective-permute-start(f32[69,128]{1,0:T(8,128)S(1)} %get-tuple-element.54), channel_id=1, source_target_pairs={{4,8},{8,4},{12,16},{16,12},{20,24},{24,20},{5,9},{9,5},{13,17},{1... | collective-permute-start | bytes 105992 | tf_op jit(solution)/shard_map/ppermute | solution.py:1586
  5.9 7.7 %collective-permute-start.3 = (f32[69,128]{1,0:T(8,128)S(1)}, f32[69,128]{1,0:T(8,128)S(1)}, u32[]{:S(2)}, u32[]{:S(2)}) collective-permute-start(f32[69,128]{1,0:T(8,128)S(1)} %get-tuple-element.55), channel_id=1, source_target_pairs={{0,4},{4,0},{8,12},{12,8},{16,20},{20,16},{24,28},{28,24},{1,5},{5... | collective-permute-start | bytes 105992 | tf_op jit(solution)/shard_map/ppermute | solution.py:1587
  14.7 3.6 %collective-permute-start.4 = (f32[97,128]{1,0:T(8,128)S(1)}, f32[97,128]{1,0:T(8,128)S(1)}, u32[]{:S(2)}, u32[]{:S(2)}) collective-permute-start(f32[97,128]{1,0:T(8,128)S(1)} %get-tuple-element.57), channel_id=1, source_target_pairs={{0,1},{1,0},{2,3},{3,2},{4,5},{5,4},{6,7},{7,6},{8,9},{9,8},{10,11... | collective-permute-start | bytes 149000 | tf_op jit(solution)/shard_map/ppermute | solution.py:1586
  17.4 0.9 %collective-permute-start.5 = (f32[97,128]{1,0:T(8,128)S(1)}, f32[97,128]{1,0:T(8,128)S(1)}, u32[]{:S(2)}, u32[]{:S(2)}) collective-permute-start(f32[97,128]{1,0:T(8,128)S(1)} %get-tuple-element.58), channel_id=1, source_target_pairs={{1,2},{2,1},{5,6},{6,5},{9,10},{10,9},{13,14},{14,13},{17,18},{18,... | collective-permute-start | bytes 149000 | tf_op jit(solution)/shard_map/ppermute | solution.py:1587
  18.3 6.0 %collective-permute-start.6 = (f32[82,128]{1,0:T(8,128)S(1)}, f32[82,128]{1,0:T(8,128)S(1)}, u32[]{:S(2)}, u32[]{:S(2)}) collective-permute-start(f32[82,128]{1,0:T(8,128)S(1)} %get-tuple-element.62), channel_id=1, source_target_pairs={{4,8},{8,4},{12,16},{16,12},{20,24},{24,20},{5,9},{9,5},{13,17},{1... | collective-permute-start | bytes 125960 | tf_op jit(solution)/shard_map/ppermute | solution.py:1586
  19.0 6.4 %collective-permute-start.7 = (f32[82,128]{1,0:T(8,128)S(1)}, f32[82,128]{1,0:T(8,128)S(1)}, u32[]{:S(2)}, u32[]{:S(2)}) collective-permute-start(f32[82,128]{1,0:T(8,128)S(1)} %get-tuple-element.63), channel_id=1, source_target_pairs={{0,4},{4,0},{8,12},{12,8},{16,20},{20,16},{24,28},{28,24},{1,5},{5... | collective-permute-start | bytes 125960 | tf_op jit(solution)/shard_map/ppermute | solution.py:1587
  44.0 1.3 %collective-permute-start.8 = (f32[42,128]{1,0:T(8,128)S(1)}, f32[42,128]{1,0:T(8,128)S(1)}, u32[]{:S(2)}, u32[]{:S(2)}) collective-permute-start(f32[42,128]{1,0:T(8,128)S(1)} %shard_map.95), channel_id=1, source_target_pairs={{0,1},{1,0},{2,3},{3,2},{4,5},{5,4},{6,7},{7,6},{8,9},{9,8},{10,11... | collective-permute-start | bytes 64520 | tf_op jit(solution)/shard_map/ppermute | solution.py:1662
  46.0 1.3 %collective-permute-start.9 = (f32[34,128]{1,0:T(8,128)S(1)}, f32[34,128]{1,0:T(8,128)S(1)}, u32[]{:S(2)}, u32[]{:S(2)}) collective-permute-start(f32[34,128]{1,0:T(8,128)S(1)} %get-tuple-element.75), channel_id=1, source_target_pairs={{0,1},{1,0},{2,3},{3,2},{4,5},{5,4},{6,7},{7,6},{8,9},{9,8},{10,11... | collective-permute-start | bytes 52232 | tf_op jit(solution)/shard_map/ppermute | solution.py:1586
  46.2 1.0 %collective-permute-start.10 = (f32[34,128]{1,0:T(8,128)S(1)}, f32[34,128]{1,0:T(8,128)S(1)}, u32[]{:S(2)}, u32[]{:S(2)}) collective-permute-start(f32[34,128]{1,0:T(8,128)S(1)} %get-tuple-element.76), channel_id=1, source_target_pairs={{1,2},{2,1},{5,6},{6,5},{9,10},{10,9},{13,14},{14,13},{17,18},{18,... | collective-permute-start | bytes 52232 | tf_op jit(solution)/shard_map/ppermute | solution.py:1587
  47.2 5.2 %collective-permute-start.11 = (f32[34,128]{1,0:T(8,128)S(1)}, f32[34,128]{1,0:T(8,128)S(1)}, u32[]{:S(2)}, u32[]{:S(2)}) collective-permute-start(f32[34,128]{1,0:T(8,128)S(1)} %get-tuple-element.81), channel_id=1, source_target_pairs={{4,8},{8,4},{12,16},{16,12},{20,24},{24,20},{5,9},{9,5},{13,17},{1... | collective-permute-start | bytes 52232 | tf_op jit(solution)/shard_map/ppermute | solution.py:1586
  47.9 5.2 %collective-permute-start.12 = (f32[34,128]{1,0:T(8,128)S(1)}, f32[34,128]{1,0:T(8,128)S(1)}, u32[]{:S(2)}, u32[]{:S(2)}) collective-permute-start(f32[34,128]{1,0:T(8,128)S(1)} %get-tuple-element.82), channel_id=1, source_target_pairs={{0,4},{4,0},{8,12},{12,8},{16,20},{20,16},{24,28},{28,24},{1,5},{5... | collective-permute-start | bytes 52232 | tf_op jit(solution)/shard_map/ppermute | solution.py:1587

commit v11 on v10

--- a/solution.py
+++ b/solution.py
@@ -173,15 +173,21 @@
         return below + self.to_high(above), above + self.to_low(below)
 
     def before_x(self, first, second):
-        return jnp.where(self.even_x, first, second)
+        return jnp.where(self.prev_x, jnp.where(self.even_x, first, second), 0.0)
 
     def after_x(self, first, second):
+        return jnp.where(self.next_x, jnp.where(self.even_x, second, first), 0.0)
+
+    def send_x(self, first, second):
         return jnp.where(self.even_x, second, first)
 
     def before_y(self, first, second):
-        return jnp.where(self.even_y, second, first)
+        return jnp.where(self.prev_y, jnp.where(self.even_y, second, first), 0.0)
 
     def after_y(self, first, second):
+        return jnp.where(self.next_y, jnp.where(self.even_y, first, second), 0.0)
+
+    def send_y(self, first, second):
         return jnp.where(self.even_y, first, second)
 
 
@@ -233,8 +239,8 @@
             low = field[lead + (ex, a, 0, pl.ds(0, 1), slice(None))]
             high = field[lead + (ex, a, 1, pl.ds(7, 1), slice(None))]
             row = at + ex * 8 + a
-            first_out[pl.ds(row, 1), :] = place.after_y(high, low)
-            second_out[pl.ds(row, 1), :] = place.after_y(low, high)
+            first_out[pl.ds(row, 1), :] = place.send_y(high, low)
+            second_out[pl.ds(row, 1), :] = place.send_y(low, high)
 
 
 def join_own(place, tiles):
@@ -291,8 +297,8 @@
             sides.append((low, high))
         for ey in range(2):
             rows = pl.ds(ch * 16 + ey * 8, 8)
-            first[rows, :] = place.after_x(sides[1][ey], sides[0][ey])
-            second[rows, :] = place.after_x(sides[0][ey], sides[1][ey])
+            first[rows, :] = place.send_x(sides[1][ey], sides[0][ey])
+            second[rows, :] = place.send_x(sides[0][ey], sides[1][ey])
 
 
 def turn_faces_kernel(pack_rows, xf, pack, y_first, y_second, first, second):
@@ -311,16 +317,16 @@
         sides.append((low, high))
     for ey in range(2):
         rows = pl.ds(at + ey * 8, 8)
-        first[rows, :] = place.after_x(sides[1][ey], sides[0][ey])
-        second[rows, :] = place.after_x(sides[0][ey], sides[1][ey])
+        first[rows, :] = place.send_x(sides[1][ey], sides[0][ey])
+        second[rows, :] = place.send_x(sides[0][ey], sides[1][ey])
     for k, pick in enumerate((place.before_y, place.after_y)):
         sides = []
         for side in range(2):
             row = pl.ds(inner_y + 15 * side, 1)
             sides.append(pick(y_first[row, :], y_second[row, :]))
         row = pl.ds(edge + k, 1)
-        first[row, :] = place.after_x(sides[1], sides[0])
-        second[row, :] = place.after_x(sides[0], sides[1])
+        first[row, :] = place.send_x(sides[1], sides[0])
+        second[row, :] = place.send_x(sides[0], sides[1])
 
 
 STEP_U, STEP_V, STEP_EDGE, STEP_PACK = 64, 64, 80, 82
@@ -653,15 +659,15 @@
     for side in range(2):
         low = inner_x[side, 0, pl.ds(0, 1), :]
         high = inner_x[side, 1, pl.ds(7, 1), :]
-        first[pl.ds(edge + side, 1), :] = place.after_y(high, low)
-        second[pl.ds(edge + side, 1), :] = place.after_y(low, high)
+        first[pl.ds(edge + side, 1), :] = place.send_y(high, low)
+        second[pl.ds(edge + side, 1), :] = place.send_y(low, high)
     for ex in range(2):
         for a in range(8):
             low = jnp.sum(bottom * tile_of(ex, a, 0), axis=0, keepdims=True)
             high = jnp.sum(top * tile_of(ex, a, 1), axis=0, keepdims=True)
             row = pl.ds(at + ex * 8 + a, 1)
-            first[row, :] = place.after_y(high, low)
-            second[row, :] = place.after_y(low, high)
+            first[row, :] = place.send_y(high, low)
+            second[row, :] = place.send_y(low, high)
 
 
 def cross_flow(place, ctab, flow, slopes, rows, inv_y, inv_z):
@@ -910,8 +916,8 @@
         sides.append((low, high))
     for ey in range(2):
         rows = pl.ds(ey * 8, 8)
-        first[rows, :] = place.after_x(sides[1][ey], sides[0][ey])
-        second[rows, :] = place.after_x(sides[0][ey], sides[1][ey])
+        first[rows, :] = place.send_x(sides[1][ey], sides[0][ey])
+        second[rows, :] = place.send_x(sides[0][ey], sides[1][ey])
     turn_edges(
         place, inner_x, y_first, y_second, first, second, SMOOTH_X, SMOOTH_EDGE, SMOOTH_Y
     )
@@ -1514,13 +1520,7 @@
     energy, curvature, square, self_energy = [
         jnp.sum(value, axis=1, keepdims=True) for value in sums
     ]
-    values = lax.dot_general(
-        jnp.broadcast_to(rest, TILE),
-        matrix[...],
-        (((1,), (1,)), ((), ())),
-        precision=lax.Precision.HIGHEST,
-        preferred_element_type=jnp.float32,
-    )
+    values = exact_dot(jnp.broadcast_to(rest, TILE), matrix[...])
     line = values[0:1]
     cross = square + jnp.sum(line * rest, axis=1, keepdims=True)
     both = self_energy + 2.0 * jnp.sum(line * dual, axis=1, keepdims=True)
@@ -1579,9 +1579,9 @@
 
 def swap(first, second, axis):
     count = lax.axis_size(axis)
-    first_pairs = [(i, i ^ 1) for i in range(count) if i ^ 1 < count]
-    second_pairs = [(i, ((i + 1) ^ 1) - 1) for i in range(1, count) if ((i + 1) ^ 1) - 1 < count]
-    if axis in ('gx',):
+    first_pairs = [(i, i ^ 1) for i in range(count)]
+    second_pairs = [(i, (((i + 1) ^ 1) - 1) % count) for i in range(count)]
+    if axis == "gx":
         first_pairs, second_pairs = second_pairs, first_pairs
     first_got = lax.ppermute(first, axis, first_pairs)
     return first_got, lax.ppermute(second, axis, second_pairs)

time: 70.7 us -> 65.2 us (0.922)
  waiting for transfers between devices: 3.24 us -> 14.5 us
  blocking collectives: 32.6 us -> 21.7 us
  starting transfers between devices: 20.9 us -> 15.3 us
    all_to_all x2, blocking collectives: 32.6 us -> 21.7 us  [exchange_all(): return lax.all_to_all(msg, BOTH, 0, 0, tiled=True)]
    ppermute x6, starting transfers between devices: 15.1 us -> 5.29 us  [swap(): return (first_got, lax.ppermute(second, axis, second_pairs))]
    ppermute x6, waiting for transfers between devices: 0.54 us -> 7.08 us  [swap(): first_got = lax.ppermute(first, axis, first_pairs)]
    ppermute x6, waiting for transfers between devices: 1.73 us -> 6.42 us  [swap(): return (first_got, lax.ppermute(second, axis, second_pairs))]
    ppermute x6, starting transfers between devices: 5.55 us -> 9.69 us  [swap(): first_got = lax.ppermute(first, axis, first_pairs)]
  transfers between devices with their start and end apart: 13 -> 13, of which waited for: 5 -> 8; matrix products, arithmetic and copies ran while one was open for 0% -> 0% of each run, Pallas kernels for 7% -> 7%
where the time goes in v11:
time: 65.2 us; the launch traced here: 65 us
  blocking collectives  21.7 us (33%)
  starting transfers between devices  15.3 us (23%)
  waiting for transfers between devices  14.5 us (22%)
  Pallas kernels  10.3 us (16%)
  local copies, waits for them, and re-layouts  2.47 us (4%)
  between operations  0.77 us (1%)
    all_to_all x2, blocking collectives, exchange_all(): return lax.all_to_all(msg, BOTH, 0, 0, tiled=True)  21.7 us
    ppermute x6, starting transfers between devices, swap(): first_got = lax.ppermute(first, axis, first_pairs)  9.69 us
    ppermute x6, waiting for transfers between devices, swap(): first_got = lax.ppermute(first, axis, first_pairs)  7.08 us
    ppermute x6, waiting for transfers between devices, swap(): return (first_got, lax.ppermute(second, axis, second_pairs))  6.42 us
    ppermute x6, starting transfers between devices, swap(): return (first_got, lax.ppermute(second, axis, second_pairs))  5.29 us
    unnamed x14, local copies, waits for them, and re-layouts  2.47 us
    pallas_call x1, Pallas kernels, per_device(): call(prepare_kernel, [four, four, edge_shape, one], [four, four], cost_es...  2.34 us
    pallas_call x1, Pallas kernels, per_device(): call(finish_kernel, [one], [(LANES, LANES), (2,) + TILE, (2,) + TILE])  1.46 us
  transfers between devices with their start and end apart: 13, of which 8 were waited for; matrix products, arithmetic and copies ran while one was open for 0% of the time, Pallas kernels for 7%

profile of v11, /device:TPU:0, one launch (start us, length us, event | category | flops | bytes accessed | tf_op | source)
XLA Modules:
  0.0 65.0 jit_solution(9458339997001581395)
XLA Ops:
  0.7 1.1 %copy-done.2 = f32[4,2,8,2,8,128]{5,4,3,2,1,0:T(8,128)S(1)} copy-done((f32[4,2,8,2,8,128]{5,4,3,2,1,0:T(8,128)S(1)}, f32[4,2,8,2,8,128]{5,4,3,2,1,0:T(8,128)}, u32[]{:S(2)}) %copy-start.2) | copy-done | bytes 524312
  1.7 0.4 shard_map.86
  2.2 0.5 collective-permute-start
  2.7 2.6 %collective-permute-start.1 = (f32[64,128]{1,0:T(8,128)S(1)}, f32[64,128]{1,0:T(8,128)S(1)}, u32[]{:S(2)}, u32[]{:S(2)}) collective-permute-start(f32[64,128]{1,0:T(8,128)S(1)} %get-tuple-element.47), channel_id=1, source_target_pairs={{0,3},{1,2},{2,1},{3,0},{4,7},{5,6},{6,5},{7,4},{8,11},{9,10},{10,... | collective-permute-start | bytes 98312 | tf_op jit(solution)/shard_map/ppermute | solution.py:1587
  5.4 0.7 %copy-done.5 = s32[2,2,16]{2,1,0:T(2,128)S(1)} copy-done((s32[2,2,16]{2,1,0:T(2,128)S(1)}, s32[2,2,16]{2,1,0:T(2,128)}, u32[]{:S(2)}) %copy-start.5) | copy-done | bytes 280
  6.0 0.7 %copy-done.6 = f32[4,128]{1,0:T(4,128)S(1)} copy-done((f32[4,128]{1,0:T(4,128)S(1)}, f32[4,128]{1,0:T(4,128)}, u32[]{:S(2)}) %copy-start.6) | copy-done | bytes 2072
  6.7 0.4 shard_map.88
  7.2 4.6 %collective-permute-start.2 = (f32[69,128]{1,0:T(8,128)S(1)}, f32[69,128]{1,0:T(8,128)S(1)}, u32[]{:S(2)}, u32[]{:S(2)}) collective-permute-start(f32[69,128]{1,0:T(8,128)S(1)} %get-tuple-element.54), channel_id=1, source_target_pairs={{0,28},{4,8},{8,4},{12,16},{16,12},{20,24},{24,20},{28,0},{1,29},{... | collective-permute-start | bytes 105992 | tf_op jit(solution)/shard_map/ppermute | solution.py:1586
  11.8 2.3 %shard_map.87 = (f32[4,2,8,2,8,128]{5,4,3,2,1,0:T(8,128)S(1)}, f32[4,2,8,2,8,128]{5,4,3,2,1,0:T(8,128)S(1)}, f32[4,2,2,8,128]{4,3,2,1,0:T(8,128)S(1)}, f32[2,8,2,8,128]{4,3,2,1,0:T(8,128)S(1)}) custom-call(f32[4,2,8,2,8,128]{5,4,3,2,1,0:T(8,128)S(1)} %get-tuple-element.45.summed, f32[2,8,2,8,128]{4,3,2,1,0:T(8,128)S(1)} %copy-done.3, ...), custom_call_target="tpu_custom_call" | custom-call | flops 10000000 | bytes 1000000 | tf_op jit(solution)/shard_map/pallas_call | solution.py:1632
  14.2 1.6 %collective-permute-done.3.x_second = f32[69,128]{1,0:T(8,128)S(1)} collective-permute-done((f32[69,128]{1,0:T(8,128)S(1)}, f32[69,128]{1,0:T(8,128)S(1)}, u32[]{:S(2)}, u32[]{:S(2)}) %collective-permute-start.3) | collective-permute-done | bytes 35360 | tf_op jit(solution)/shard_map/ppermute | solution.py:1587
  15.7 1.0 %shard_map.90 = (f32[4,2,8,2,8,128]{5,4,3,2,1,0:T(8,128)S(1)}, f32[2,4,2,8,128]{4,3,2,1,0:T(8,128)S(1)}, f32[2,2,8,128]{3,2,1,0:T(8,128)S(1)}, f32[97,128]{1,0:T(8,128)S(1)}, f32[97,128]{1,0:T(8,128)S(1)}) custom-call(f32[4,2,8,2,8,128]{5,4,3,2,1,0:T(8,128)S(1)} %get-tuple-element.48.begun, f32[4,2,8,2,8,128]{5,4,3,2,1,0:T(8,128)S(1)} %get-tuple-element.49.given, ...), custom_call_target="tpu_custom_call" | custom-call | tf_op jit(solution)/shard_map/pallas_call | solution.py:1635
  16.9 1.6 %collective-permute-start.5 = (f32[97,128]{1,0:T(8,128)S(1)}, f32[97,128]{1,0:T(8,128)S(1)}, u32[]{:S(2)}, u32[]{:S(2)}) collective-permute-start(f32[97,128]{1,0:T(8,128)S(1)} %get-tuple-element.58), channel_id=1, source_target_pairs={{0,3},{1,2},{2,1},{3,0},{4,7},{5,6},{6,5},{7,4},{8,11},{9,10},{10,... | collective-permute-start | bytes 149000 | tf_op jit(solution)/shard_map/ppermute | solution.py:1587
  18.5 2.0 %collective-permute-done.5.y_second = f32[97,128]{1,0:T(8,128)S(1)} collective-permute-done((f32[97,128]{1,0:T(8,128)S(1)}, f32[97,128]{1,0:T(8,128)S(1)}, u32[]{:S(2)}, u32[]{:S(2)}) %collective-permute-start.5) | collective-permute-done | bytes 49696 | tf_op jit(solution)/shard_map/ppermute | solution.py:1587
  20.5 2.8 %collective-permute-start.6 = (f32[82,128]{1,0:T(8,128)S(1)}, f32[82,128]{1,0:T(8,128)S(1)}, u32[]{:S(2)}, u32[]{:S(2)}) collective-permute-start(f32[82,128]{1,0:T(8,128)S(1)} %get-tuple-element.62), channel_id=1, source_target_pairs={{0,28},{4,8},{8,4},{12,16},{16,12},{20,24},{24,20},{28,0},{1,29},{... | collective-permute-start | bytes 125960 | tf_op jit(solution)/shard_map/ppermute | solution.py:1586
  23.3 0.5 shard_map.93
  23.8 0.5 shard_map.91
  24.3 3.1 %collective-permute-done.6.x_first = f32[82,128]{1,0:T(8,128)S(1)} collective-permute-done((f32[82,128]{1,0:T(8,128)S(1)}, f32[82,128]{1,0:T(8,128)S(1)}, u32[]{:S(2)}, u32[]{:S(2)}) %collective-permute-start.6) | collective-permute-done | bytes 42016 | tf_op jit(solution)/shard_map/ppermute | solution.py:1586
  27.4 0.6 collective-permute-done.7.x_second
  28.0 0.6 shard_map.94
  28.5 11.7 %all_to_all.10.got = f32[32,8,128]{2,1,0:T(8,128)S(1)} all-to-all(f32[32,8,128]{2,1,0:T(8,128)S(1)} %get-tuple-element.68), channel_id=1, replica_groups=mesh['gx'=8,'gy'=4] {'gx','gy'}, dimensions={0} | all-to-all | bytes 262144 | tf_op jit(solution)/shard_map/all_to_all | solution.py:1614
  40.5 1.0 %collective-permute-done.8.relayed = f32[42,128]{1,0:T(8,128)S(1)} collective-permute-done((f32[42,128]{1,0:T(8,128)S(1)}, f32[42,128]{1,0:T(8,128)S(1)}, u32[]{:S(2)}, u32[]{:S(2)}) %collective-permute-start.8) | collective-permute-done | bytes 21536 | tf_op jit(solution)/shard_map/ppermute | solution.py:1662
  41.5 0.7 %shard_map.96 = (f32[2,8,2,8,128]{4,3,2,1,0:T(8,128)S(1)}, f32[2,8,2,8,128]{4,3,2,1,0:T(8,128)S(1)}, f32[2,2,8,128]{3,2,1,0:T(8,128)S(1)}, f32[34,128]{1,0:T(8,1...) custom-call(f32[32,8,128]{2,1,0:T(8,128)S(1)} %all_to_all.10.got, f32[42,128]{1,0:T(8,128)S(1)} %collective-permute-done.8.relayed, ...), custom_call_target="tpu_custom_call" | custom-call | tf_op jit(solution)/shard_map/pallas_call | solution.py:1665
  42.5 0.3 collective-permute-start.10
  42.8 0.6 collective-permute-done.9.y_first
  43.4 2.2 %collective-permute-done.10.y_second = f32[34,128]{1,0:T(8,128)S(1)} collective-permute-done((f32[34,128]{1,0:T(8,128)S(1)}, f32[34,128]{1,0:T(8,128)S(1)}, u32[]{:S(2)}, u32[]{:S(2)}) %collective-permute-start.10) | collective-permute-done | bytes 17440 | tf_op jit(solution)/shard_map/ppermute | solution.py:1587
  45.7 1.4 %collective-permute-start.11 = (f32[34,128]{1,0:T(8,128)S(1)}, f32[34,128]{1,0:T(8,128)S(1)}, u32[]{:S(2)}, u32[]{:S(2)}) collective-permute-start(f32[34,128]{1,0:T(8,128)S(1)} %get-tuple-element.81), channel_id=1, source_target_pairs={{0,28},{4,8},{8,4},{12,16},{16,12},{20,24},{24,20},{28,0},{1,29},{... | collective-permute-start | bytes 52232 | tf_op jit(solution)/shard_map/ppermute | solution.py:1586
  47.1 0.7 %collective-permute-start.12 = (f32[34,128]{1,0:T(8,128)S(1)}, f32[34,128]{1,0:T(8,128)S(1)}, u32[]{:S(2)}, u32[]{:S(2)}) collective-permute-start(f32[34,128]{1,0:T(8,128)S(1)} %get-tuple-element.82), channel_id=1, source_target_pairs={{0,4},{4,0},{8,12},{12,8},{16,20},{20,16},{24,28},{28,24},{1,5},{5... | collective-permute-start | bytes 52232 | tf_op jit(solution)/shard_map/ppermute | solution.py:1587
  47.8 0.8 %shard_map.97 = (f32[4,2,8,2,8,128]{5,4,3,2,1,0:T(8,128)}, f32[1,128]{1,0:T(1,128)S(1)}) custom-call(f32[4,2,8,2,8,128]{5,4,3,2,1,0:T(8,128)S(1)} %get-tuple-element.59.begun, f32[82,128]{1,0:T(8,128)S(1)} %collective-permute-done.6.x_first, f32[82,128]{1,0:T(8,128)S(1)} %collective-permute-done.7.x_second, f32[1,128]{1,0:T(1,128)S(1)} %get-tuple-element.72.extra), custom_call_target="tpu_custom_call" | custom-call | flops 10000000 | bytes 1000000 | tf_op jit(solution)/shard_map/pallas_call | solution.py:1673
  48.9 3.3 %collective-permute-done.11.x_first = f32[34,128]{1,0:T(8,128)S(1)} collective-permute-done((f32[34,128]{1,0:T(8,128)S(1)}, f32[34,128]{1,0:T(8,128)S(1)}, u32[]{:S(2)}, u32[]{:S(2)}) %collective-permute-start.11) | collective-permute-done | bytes 17440 | tf_op jit(solution)/shard_map/ppermute | solution.py:1586
  52.2 1.3 %shard_map.100 = (f32[2,8,2,8,128]{4,3,2,1,0:T(8,128)}, f32[2,8,2,8,128]{4,3,2,1,0:T(8,128)S(1)}, f32[32,1,768]{2,1,0:T(1,128)S(1)}) custom-call(f32[2,8,2,8,128]{4,3,2,1,0:T(8,128)S(1)} %get-tuple-element.77.begun, f32[2,8,2,8,128]{4,3,2,1,0:T(8,128)S(1)} %get-tuple-element.78.begun_scaled, f32[2,8,2,8,128]{4,3,2,1,0:T(8,128)S(1)} %get-tuple-element.79.given, ...), custom_call_target="tpu_custom_call" | custom-call | tf_op jit(solution)/shard_map/pallas_call | solution.py:1679
  53.5 10.0 %all_to_all.11.got = f32[32,1,768]{2,1,0:T(1,128)S(1)} all-to-all(f32[32,1,768]{2,1,0:T(1,128)S(1)} %get-tuple-element.85), channel_id=1, replica_groups=mesh['gx'=8,'gy'=4] {'gx','gy'}, dimensions={0} | all-to-all | bytes 196608 | tf_op jit(solution)/shard_map/all_to_all | solution.py:1614
  63.5 1.5 %shard_map.101 = f32[2,8,2,8,128]{4,3,2,1,0:T(8,128)} custom-call(f32[32,1,768]{2,1,0:T(1,128)S(1)} %all_to_all.11.got, f32[16,128]{1,0:T(8,128)S(1)} %get-tuple-element.67.grp, f32[2,8,2,8,128]{4,3,2,1,0:T(8,128)S(1)} %get-tuple-element.86.direction, f32[2,8,2,8,128]{4,3,2,1,0:T(8,128)S(1)} %get-tuple-element.87.smoothed), custom_call_target="tpu_custom_call" | custom-call | tf_op jit(solution)/shard_map/pallas_call | solution.py:1688
  (26 shorter events, 1.0 us)
Async XLA Ops:
  0.6 11.2 %copy-start = (bf16[3,256,256]{2,1,0:T(8,128)(2,1)S(1)}, bf16[3,256,256]{2,1,0:T(8,128)(2,1)}, u32[]{:S(2)}) copy-start(bf16[3,256,256]{2,1,0:T(8,128)(2,1)} %constant.5.clone.zmat) | copy-start | bytes 1179652
  0.6 1.1 %copy-start.2 = (f32[4,2,8,2,8,128]{5,4,3,2,1,0:T(8,128)S(1)}, f32[4,2,8,2,8,128]{5,4,3,2,1,0:T(8,128)}, u32[]{:S(2)}) copy-start(f32[4,2,8,2,8,128]{5,4,3,2,1,0:T(8,128)} %fields.1) | copy-start | bytes 1572868
  1.7 3.6 %copy-start.4 = (f32[2,2,16]{2,1,0:T(2,128)S(1)}, f32[2,2,16]{2,1,0:T(2,128)}, u32[]{:S(2)}) copy-start(f32[2,2,16]{2,1,0:T(2,128)} %kappa.1) | copy-start | bytes 772
  1.7 10.0 %copy-start.3 = (f32[2,8,2,8,128]{4,3,2,1,0:T(8,128)S(1)}, f32[2,8,2,8,128]{4,3,2,1,0:T(8,128)}, u32[]{:S(2)}) copy-start(f32[2,8,2,8,128]{4,3,2,1,0:T(8,128)} %visc.3) | copy-start | bytes 393220
  2.2 9.6 %copy-start.1 = (f32[30,8,128]{2,1,0:T(8,128)S(1)}, f32[30,8,128]{2,1,0:T(8,128)}, u32[]{:S(2)}) copy-start(f32[30,8,128]{2,1,0:T(8,128)} %constant.4.clone.ctab) | copy-start | bytes 368644
  2.2 4.9 %collective-permute-start = (f32[64,128]{1,0:T(8,128)S(1)}, f32[64,128]{1,0:T(8,128)S(1)}, u32[]{:S(2)}, u32[]{:S(2)}) collective-permute-start(f32[64,128]{1,0:T(8,128)S(1)} %get-tuple-element.46), channel_id=1, source_target_pairs={{0,1},{1,0},{2,3},{3,2},{4,5},{5,4},{6,7},{7,6},{8,9},{9,8},{10,11... | collective-permute-start | bytes 98312 | tf_op jit(solution)/shard_map/ppermute | solution.py:1586
  2.7 4.4 %collective-permute-start.1 = (f32[64,128]{1,0:T(8,128)S(1)}, f32[64,128]{1,0:T(8,128)S(1)}, u32[]{:S(2)}, u32[]{:S(2)}) collective-permute-start(f32[64,128]{1,0:T(8,128)S(1)} %get-tuple-element.47), channel_id=1, source_target_pairs={{0,3},{1,2},{2,1},{3,0},{4,7},{5,6},{6,5},{7,4},{8,11},{9,10},{10,... | collective-permute-start | bytes 98312 | tf_op jit(solution)/shard_map/ppermute | solution.py:1587
  5.4 0.7 %copy-start.5 = (s32[2,2,16]{2,1,0:T(2,128)S(1)}, s32[2,2,16]{2,1,0:T(2,128)}, u32[]{:S(2)}) copy-start(s32[2,2,16]{2,1,0:T(2,128)} %group.1) | copy-start | bytes 772
  6.0 0.7 %copy-start.6 = (f32[4,128]{1,0:T(4,128)S(1)}, f32[4,128]{1,0:T(4,128)}, u32[]{:S(2)}) copy-start(f32[4,128]{1,0:T(4,128)} %coarse.1) | copy-start | bytes 6148
  7.2 7.0 %collective-permute-start.2 = (f32[69,128]{1,0:T(8,128)S(1)}, f32[69,128]{1,0:T(8,128)S(1)}, u32[]{:S(2)}, u32[]{:S(2)}) collective-permute-start(f32[69,128]{1,0:T(8,128)S(1)} %get-tuple-element.54), channel_id=1, source_target_pairs={{0,28},{4,8},{8,4},{12,16},{16,12},{20,24},{24,20},{28,0},{1,29},{... | collective-permute-start | bytes 105992 | tf_op jit(solution)/shard_map/ppermute | solution.py:1586
  11.8 4.0 %collective-permute-start.3 = (f32[69,128]{1,0:T(8,128)S(1)}, f32[69,128]{1,0:T(8,128)S(1)}, u32[]{:S(2)}, u32[]{:S(2)}) collective-permute-start(f32[69,128]{1,0:T(8,128)S(1)} %get-tuple-element.55), channel_id=1, source_target_pairs={{0,4},{4,0},{8,12},{12,8},{16,20},{20,16},{24,28},{28,24},{1,5},{5... | collective-permute-start | bytes 105992 | tf_op jit(solution)/shard_map/ppermute | solution.py:1587
  16.8 1.7 %collective-permute-start.4 = (f32[97,128]{1,0:T(8,128)S(1)}, f32[97,128]{1,0:T(8,128)S(1)}, u32[]{:S(2)}, u32[]{:S(2)}) collective-permute-start(f32[97,128]{1,0:T(8,128)S(1)} %get-tuple-element.57), channel_id=1, source_target_pairs={{0,1},{1,0},{2,3},{3,2},{4,5},{5,4},{6,7},{7,6},{8,9},{9,8},{10,11... | collective-permute-start | bytes 149000 | tf_op jit(solution)/shard_map/ppermute | solution.py:1586
  16.9 3.6 %collective-permute-start.5 = (f32[97,128]{1,0:T(8,128)S(1)}, f32[97,128]{1,0:T(8,128)S(1)}, u32[]{:S(2)}, u32[]{:S(2)}) collective-permute-start(f32[97,128]{1,0:T(8,128)S(1)} %get-tuple-element.58), channel_id=1, source_target_pairs={{0,3},{1,2},{2,1},{3,0},{4,7},{5,6},{6,5},{7,4},{8,11},{9,10},{10,... | collective-permute-start | bytes 149000 | tf_op jit(solution)/shard_map/ppermute | solution.py:1587
  20.5 6.9 %collective-permute-start.6 = (f32[82,128]{1,0:T(8,128)S(1)}, f32[82,128]{1,0:T(8,128)S(1)}, u32[]{:S(2)}, u32[]{:S(2)}) collective-permute-start(f32[82,128]{1,0:T(8,128)S(1)} %get-tuple-element.62), channel_id=1, source_target_pairs={{0,28},{4,8},{8,4},{12,16},{16,12},{20,24},{24,20},{28,0},{1,29},{... | collective-permute-start | bytes 125960 | tf_op jit(solution)/shard_map/ppermute | solution.py:1586
  23.3 4.7 %collective-permute-start.7 = (f32[82,128]{1,0:T(8,128)S(1)}, f32[82,128]{1,0:T(8,128)S(1)}, u32[]{:S(2)}, u32[]{:S(2)}) collective-permute-start(f32[82,128]{1,0:T(8,128)S(1)} %get-tuple-element.63), channel_id=1, source_target_pairs={{0,4},{4,0},{8,12},{12,8},{16,20},{20,16},{24,28},{28,24},{1,5},{5... | collective-permute-start | bytes 125960 | tf_op jit(solution)/shard_map/ppermute | solution.py:1587
  40.2 1.3 %collective-permute-start.8 = (f32[42,128]{1,0:T(8,128)S(1)}, f32[42,128]{1,0:T(8,128)S(1)}, u32[]{:S(2)}, u32[]{:S(2)}) collective-permute-start(f32[42,128]{1,0:T(8,128)S(1)} %shard_map.95), channel_id=1, source_target_pairs={{0,1},{1,0},{2,3},{3,2},{4,5},{5,4},{6,7},{7,6},{8,9},{9,8},{10,11... | collective-permute-start | bytes 64520 | tf_op jit(solution)/shard_map/ppermute | solution.py:1662
  42.2 1.3 %collective-permute-start.9 = (f32[34,128]{1,0:T(8,128)S(1)}, f32[34,128]{1,0:T(8,128)S(1)}, u32[]{:S(2)}, u32[]{:S(2)}) collective-permute-start(f32[34,128]{1,0:T(8,128)S(1)} %get-tuple-element.75), channel_id=1, source_target_pairs={{0,1},{1,0},{2,3},{3,2},{4,5},{5,4},{6,7},{7,6},{8,9},{9,8},{10,11... | collective-permute-start | bytes 52232 | tf_op jit(solution)/shard_map/ppermute | solution.py:1586
  42.5 3.2 %collective-permute-start.10 = (f32[34,128]{1,0:T(8,128)S(1)}, f32[34,128]{1,0:T(8,128)S(1)}, u32[]{:S(2)}, u32[]{:S(2)}) collective-permute-start(f32[34,128]{1,0:T(8,128)S(1)} %get-tuple-element.76), channel_id=1, source_target_pairs={{0,3},{1,2},{2,1},{3,0},{4,7},{5,6},{6,5},{7,4},{8,11},{9,10},{10,... | collective-permute-start | bytes 52232 | tf_op jit(solution)/shard_map/ppermute | solution.py:1587
  45.7 6.5 %collective-permute-start.11 = (f32[34,128]{1,0:T(8,128)S(1)}, f32[34,128]{1,0:T(8,128)S(1)}, u32[]{:S(2)}, u32[]{:S(2)}) collective-permute-start(f32[34,128]{1,0:T(8,128)S(1)} %get-tuple-element.81), channel_id=1, source_target_pairs={{0,28},{4,8},{8,4},{12,16},{16,12},{20,24},{24,20},{28,0},{1,29},{... | collective-permute-start | bytes 52232 | tf_op jit(solution)/shard_map/ppermute | solution.py:1586
  47.1 5.1 %collective-permute-start.12 = (f32[34,128]{1,0:T(8,128)S(1)}, f32[34,128]{1,0:T(8,128)S(1)}, u32[]{:S(2)}, u32[]{:S(2)}) collective-permute-start(f32[34,128]{1,0:T(8,128)S(1)} %get-tuple-element.82), channel_id=1, source_target_pairs={{0,4},{4,0},{8,12},{12,8},{16,20},{20,16},{24,28},{28,24},{1,5},{5... | collective-permute-start | bytes 52232 | tf_op jit(solution)/shard_map/ppermute | solution.py:1587

commit v12 on v11

--- a/solution.py
+++ b/solution.py
@@ -1578,13 +1578,25 @@
 
 
 def swap(first, second, axis):
-    count = lax.axis_size(axis)
-    first_pairs = [(i, i ^ 1) for i in range(count)]
-    second_pairs = [(i, (((i + 1) ^ 1) - 1) % count) for i in range(count)]
+    along, across = lax.axis_size("gx"), lax.axis_size("gy")
+
+    def number(ix, iy):
+        return ix * across + iy
+
+    pairs = ([], [])
+    for ix in range(along):
+        for iy in range(across):
+            at, count = (ix, along) if axis == "gx" else (iy, across)
+            for k, to in enumerate((at ^ 1, ((at + 1) ^ 1) - 1)):
+                if 0 <= to < count:
+                    there = (to, iy) if axis == "gx" else (ix, to)
+                else:
+                    there = (ix, iy ^ 1) if axis == "gx" else (ix, across - 1 - iy)
+                pairs[k].append((number(ix, iy), number(*there)))
     if axis == "gx":
-        first_pairs, second_pairs = second_pairs, first_pairs
-    first_got = lax.ppermute(first, axis, first_pairs)
-    return first_got, lax.ppermute(second, axis, second_pairs)
+        pairs = pairs[::-1]
+    first_got = lax.ppermute(first, BOTH, pairs[0])
+    return first_got, lax.ppermute(second, BOTH, pairs[1])
 
 
 def per_device(fields, viscosity, inv_density, elem_group, coarse_inverse):

time: 65.2 us -> 60 us (0.920)
  waiting for transfers between devices: 14.5 us -> 7.81 us
  blocking collectives: 21.7 us -> 24.2 us
  starting transfers between devices: 15.3 us -> 14.2 us
    ppermute x12, waiting for transfers between devices: 13.5 us -> 6.82 us  [the longest x6 6.19 us: swap(): return (first_got, lax.ppermute(second, BOTH, pairs[1]))]
    all_to_all x2, blocking collectives: 21.7 us -> 24.2 us  [exchange_all(): return lax.all_to_all(msg, BOTH, 0, 0, tiled=True)]
    ppermute x12, starting transfers between devices: 15 us -> 13.9 us  [the longest x6 12 us: swap(): return (first_got, lax.ppermute(second, BOTH, pairs[1]))]
  transfers between devices with their start and end apart: 13 -> 13, of which waited for: 8 -> 6; matrix products, arithmetic and copies ran while one was open for 0% -> 0% of each run, Pallas kernels for 7% -> 8%
where the time goes in v12:
time: 60 us; the launch traced here: 59.8 us
  blocking collectives  24.2 us (40%)
  starting transfers between devices  14.2 us (24%)
  Pallas kernels  10.3 us (17%)
  waiting for transfers between devices  7.81 us (13%)
  local copies, waits for them, and re-layouts  2.47 us (4%)
  between operations  0.78 us (1%)
    all_to_all x2, blocking collectives, exchange_all(): return lax.all_to_all(msg, BOTH, 0, 0, tiled=True)  24.2 us
    ppermute x6, starting transfers between devices, swap(): return (first_got, lax.ppermute(second, BOTH, pairs[1]))  12 us
    ppermute x6, waiting for transfers between devices, swap(): return (first_got, lax.ppermute(second, BOTH, pairs[1]))  6.19 us
    unnamed x14, local copies, waits for them, and re-layouts  2.47 us
    pallas_call x1, Pallas kernels, per_device(): call(prepare_kernel, [four, four, edge_shape, one], [four, four], cost_es...  2.34 us
    ppermute x6, starting transfers between devices, swap(): first_got = lax.ppermute(first, BOTH, pairs[0])  1.87 us
    pallas_call x1, Pallas kernels, per_device(): call(finish_kernel, [one], [(LANES, LANES), (2,) + TILE, (2,) + TILE])  1.46 us
    pallas_call x1, Pallas kernels, per_device(): call(smooth_kernel, [one, one, (devices, 1, 6 * LANES) if grid_fits else...  1.27 us
  transfers between devices with their start and end apart: 13, of which 6 were waited for; matrix products, arithmetic and copies ran while one was open for 0% of the time, Pallas kernels for 8%

profile of v12, /device:TPU:0, one launch (start us, length us, event | category | flops | bytes accessed | tf_op | source)
XLA Modules:
  0.0 59.8 jit_solution(6695744610897098776)
XLA Ops:
  0.7 1.1 %copy-done.2 = f32[4,2,8,2,8,128]{5,4,3,2,1,0:T(8,128)S(1)} copy-done((f32[4,2,8,2,8,128]{5,4,3,2,1,0:T(8,128)S(1)}, f32[4,2,8,2,8,128]{5,4,3,2,1,0:T(8,128)}, u32[]{:S(2)}) %copy-start.2) | copy-done | bytes 524312
  1.7 0.4 shard_map.86
  2.2 0.5 collective-permute-start
  2.7 2.6 %collective-permute-start.1 = (f32[64,128]{1,0:T(8,128)S(1)}, f32[64,128]{1,0:T(8,128)S(1)}, u32[]{:S(2)}, u32[]{:S(2)}) collective-permute-start(f32[64,128]{1,0:T(8,128)S(1)} %get-tuple-element.47), channel_id=1, source_target_pairs={{0,3},{1,2},{2,1},{3,0},{4,7},{5,6},{6,5},{7,4},{8,11},{9,10},{10,... | collective-permute-start | bytes 98312 | tf_op jit(solution)/shard_map/ppermute | solution.py:1599
  5.4 0.7 %copy-done.5 = s32[2,2,16]{2,1,0:T(2,128)S(1)} copy-done((s32[2,2,16]{2,1,0:T(2,128)S(1)}, s32[2,2,16]{2,1,0:T(2,128)}, u32[]{:S(2)}) %copy-start.5) | copy-done | bytes 280
  6.0 0.7 %copy-done.6 = f32[4,128]{1,0:T(4,128)S(1)} copy-done((f32[4,128]{1,0:T(4,128)S(1)}, f32[4,128]{1,0:T(4,128)}, u32[]{:S(2)}) %copy-start.6) | copy-done | bytes 2072
  6.7 0.4 shard_map.88
  7.3 3.0 %collective-permute-start.3 = (f32[69,128]{1,0:T(8,128)S(1)}, f32[69,128]{1,0:T(8,128)S(1)}, u32[]{:S(2)}, u32[]{:S(2)}) collective-permute-start(f32[69,128]{1,0:T(8,128)S(1)} %get-tuple-element.55), channel_id=1, source_target_pairs={{0,4},{1,5},{2,6},{3,7},{4,0},{5,1},{6,2},{7,3},{8,12},{9,13},{10,... | collective-permute-start | bytes 105992 | tf_op jit(solution)/shard_map/ppermute | solution.py:1599
  10.3 2.3 %shard_map.87 = (f32[4,2,8,2,8,128]{5,4,3,2,1,0:T(8,128)S(1)}, f32[4,2,8,2,8,128]{5,4,3,2,1,0:T(8,128)S(1)}, f32[4,2,2,8,128]{4,3,2,1,0:T(8,128)S(1)}, f32[2,8,2,8,128]{4,3,2,1,0:T(8,128)S(1)}) custom-call(f32[4,2,8,2,8,128]{5,4,3,2,1,0:T(8,128)S(1)} %get-tuple-element.45.summed, f32[2,8,2,8,128]{4,3,2,1,0:T(8,128)S(1)} %copy-done.3, ...), custom_call_target="tpu_custom_call" | custom-call | flops 10000000 | bytes 1000000 | tf_op jit(solution)/shard_map/pallas_call | solution.py:1644
  12.7 1.0 %shard_map.90 = (f32[4,2,8,2,8,128]{5,4,3,2,1,0:T(8,128)S(1)}, f32[2,4,2,8,128]{4,3,2,1,0:T(8,128)S(1)}, f32[2,2,8,128]{3,2,1,0:T(8,128)S(1)}, f32[97,128]{1,0:T(8,128)S(1)}, f32[97,128]{1,0:T(8,128)S(1)}) custom-call(f32[4,2,8,2,8,128]{5,4,3,2,1,0:T(8,128)S(1)} %get-tuple-element.48.begun, f32[4,2,8,2,8,128]{5,4,3,2,1,0:T(8,128)S(1)} %get-tuple-element.49.given, ...), custom_call_target="tpu_custom_call" | custom-call | tf_op jit(solution)/shard_map/pallas_call | solution.py:1647
  13.8 1.6 %collective-permute-start.5 = (f32[97,128]{1,0:T(8,128)S(1)}, f32[97,128]{1,0:T(8,128)S(1)}, u32[]{:S(2)}, u32[]{:S(2)}) collective-permute-start(f32[97,128]{1,0:T(8,128)S(1)} %get-tuple-element.58), channel_id=1, source_target_pairs={{0,3},{1,2},{2,1},{3,0},{4,7},{5,6},{6,5},{7,4},{8,11},{9,10},{10,... | collective-permute-start | bytes 149000 | tf_op jit(solution)/shard_map/ppermute | solution.py:1599
  15.4 2.0 %collective-permute-done.5.y_second = f32[97,128]{1,0:T(8,128)S(1)} collective-permute-done((f32[97,128]{1,0:T(8,128)S(1)}, f32[97,128]{1,0:T(8,128)S(1)}, u32[]{:S(2)}, u32[]{:S(2)}) %collective-permute-start.5) | collective-permute-done | bytes 49696 | tf_op jit(solution)/shard_map/ppermute | solution.py:1599
  17.4 0.5 collective-permute-start.6
  18.0 2.7 %collective-permute-start.7 = (f32[82,128]{1,0:T(8,128)S(1)}, f32[82,128]{1,0:T(8,128)S(1)}, u32[]{:S(2)}, u32[]{:S(2)}) collective-permute-start(f32[82,128]{1,0:T(8,128)S(1)} %get-tuple-element.63), channel_id=1, source_target_pairs={{0,4},{1,5},{2,6},{3,7},{4,0},{5,1},{6,2},{7,3},{8,12},{9,13},{10,... | collective-permute-start | bytes 125960 | tf_op jit(solution)/shard_map/ppermute | solution.py:1599
  20.6 0.5 shard_map.93
  21.1 0.5 shard_map.91
  21.6 1.0 %collective-permute-done.7.x_second = f32[82,128]{1,0:T(8,128)S(1)} collective-permute-done((f32[82,128]{1,0:T(8,128)S(1)}, f32[82,128]{1,0:T(8,128)S(1)}, u32[]{:S(2)}, u32[]{:S(2)}) %collective-permute-start.7) | collective-permute-done | bytes 42016 | tf_op jit(solution)/shard_map/ppermute | solution.py:1599
  22.7 0.6 shard_map.94
  23.2 13.8 %all_to_all.10.got = f32[32,8,128]{2,1,0:T(8,128)S(1)} all-to-all(f32[32,8,128]{2,1,0:T(8,128)S(1)} %get-tuple-element.68), channel_id=1, replica_groups=mesh['gx'=8,'gy'=4] {'gx','gy'}, dimensions={0} | all-to-all | bytes 262144 | tf_op jit(solution)/shard_map/all_to_all | solution.py:1626
  37.3 1.0 %collective-permute-done.8.relayed = f32[42,128]{1,0:T(8,128)S(1)} collective-permute-done((f32[42,128]{1,0:T(8,128)S(1)}, f32[42,128]{1,0:T(8,128)S(1)}, u32[]{:S(2)}, u32[]{:S(2)}) %collective-permute-start.8) | collective-permute-done | bytes 21536 | tf_op jit(solution)/shard_map/ppermute | solution.py:1674
  38.3 0.7 %shard_map.96 = (f32[2,8,2,8,128]{4,3,2,1,0:T(8,128)S(1)}, f32[2,8,2,8,128]{4,3,2,1,0:T(8,128)S(1)}, f32[2,2,8,128]{3,2,1,0:T(8,128)S(1)}, f32[34,128]{1,0:T(8,1...) custom-call(f32[32,8,128]{2,1,0:T(8,128)S(1)} %all_to_all.10.got, f32[42,128]{1,0:T(8,128)S(1)} %collective-permute-done.8.relayed, ...), custom_call_target="tpu_custom_call" | custom-call | tf_op jit(solution)/shard_map/pallas_call | solution.py:1677
  38.9 0.3 collective-permute-start.9
  39.2 0.3 collective-permute-start.10
  39.6 0.6 %collective-permute-done.9.y_first = f32[34,128]{1,0:T(8,128)S(1)} collective-permute-done((f32[34,128]{1,0:T(8,128)S(1)}, f32[34,128]{1,0:T(8,128)S(1)}, u32[]{:S(2)}, u32[]{:S(2)}) %collective-permute-start.9) | collective-permute-done | bytes 17440 | tf_op jit(solution)/shard_map/ppermute | solution.py:1598
  40.2 2.2 %collective-permute-done.10.y_second = f32[34,128]{1,0:T(8,128)S(1)} collective-permute-done((f32[34,128]{1,0:T(8,128)S(1)}, f32[34,128]{1,0:T(8,128)S(1)}, u32[]{:S(2)}, u32[]{:S(2)}) %collective-permute-start.10) | collective-permute-done | bytes 17440 | tf_op jit(solution)/shard_map/ppermute | solution.py:1599
  42.5 0.3 collective-permute-start.11
  42.8 1.8 %collective-permute-start.12 = (f32[34,128]{1,0:T(8,128)S(1)}, f32[34,128]{1,0:T(8,128)S(1)}, u32[]{:S(2)}, u32[]{:S(2)}) collective-permute-start(f32[34,128]{1,0:T(8,128)S(1)} %get-tuple-element.82), channel_id=1, source_target_pairs={{0,4},{1,5},{2,6},{3,7},{4,0},{5,1},{6,2},{7,3},{8,12},{9,13},{10,... | collective-permute-start | bytes 52232 | tf_op jit(solution)/shard_map/ppermute | solution.py:1599
  44.6 0.8 %shard_map.97 = (f32[4,2,8,2,8,128]{5,4,3,2,1,0:T(8,128)}, f32[1,128]{1,0:T(1,128)S(1)}) custom-call(f32[4,2,8,2,8,128]{5,4,3,2,1,0:T(8,128)S(1)} %get-tuple-element.59.begun, f32[82,128]{1,0:T(8,128)S(1)} %collective-permute-done.6.x_first, f32[82,128]{1,0:T(8,128)S(1)} %collective-permute-done.7.x_second, f32[1,128]{1,0:T(1,128)S(1)} %get-tuple-element.72.extra), custom_call_target="tpu_custom_call" | custom-call | flops 10000000 | bytes 1000000 | tf_op jit(solution)/shard_map/pallas_call | solution.py:1685
  45.7 0.9 %collective-permute-done.12.x_second = f32[34,128]{1,0:T(8,128)S(1)} collective-permute-done((f32[34,128]{1,0:T(8,128)S(1)}, f32[34,128]{1,0:T(8,128)S(1)}, u32[]{:S(2)}, u32[]{:S(2)}) %collective-permute-start.12) | collective-permute-done | bytes 17440 | tf_op jit(solution)/shard_map/ppermute | solution.py:1599
  46.6 1.3 %shard_map.100 = (f32[2,8,2,8,128]{4,3,2,1,0:T(8,128)}, f32[2,8,2,8,128]{4,3,2,1,0:T(8,128)S(1)}, f32[32,1,768]{2,1,0:T(1,128)S(1)}) custom-call(f32[2,8,2,8,128]{4,3,2,1,0:T(8,128)S(1)} %get-tuple-element.77.begun, f32[2,8,2,8,128]{4,3,2,1,0:T(8,128)S(1)} %get-tuple-element.78.begun_scaled, f32[2,8,2,8,128]{4,3,2,1,0:T(8,128)S(1)} %get-tuple-element.79.given, ...), custom_call_target="tpu_custom_call" | custom-call | tf_op jit(solution)/shard_map/pallas_call | solution.py:1691
  47.9 10.4 %all_to_all.11.got = f32[32,1,768]{2,1,0:T(1,128)S(1)} all-to-all(f32[32,1,768]{2,1,0:T(1,128)S(1)} %get-tuple-element.85), channel_id=1, replica_groups=mesh['gx'=8,'gy'=4] {'gx','gy'}, dimensions={0} | all-to-all | bytes 196608 | tf_op jit(solution)/shard_map/all_to_all | solution.py:1626
  58.3 1.5 %shard_map.101 = f32[2,8,2,8,128]{4,3,2,1,0:T(8,128)} custom-call(f32[32,1,768]{2,1,0:T(1,128)S(1)} %all_to_all.11.got, f32[16,128]{1,0:T(8,128)S(1)} %get-tuple-element.67.grp, f32[2,8,2,8,128]{4,3,2,1,0:T(8,128)S(1)} %get-tuple-element.86.direction, f32[2,8,2,8,128]{4,3,2,1,0:T(8,128)S(1)} %get-tuple-element.87.smoothed), custom_call_target="tpu_custom_call" | custom-call | tf_op jit(solution)/shard_map/pallas_call | solution.py:1700
  (26 shorter events, 0.9 us)
Async XLA Ops:
  0.6 9.7 %copy-start = (bf16[3,256,256]{2,1,0:T(8,128)(2,1)S(1)}, bf16[3,256,256]{2,1,0:T(8,128)(2,1)}, u32[]{:S(2)}) copy-start(bf16[3,256,256]{2,1,0:T(8,128)(2,1)} %constant.5.clone.zmat) | copy-start | bytes 1179652
  0.6 1.1 %copy-start.2 = (f32[4,2,8,2,8,128]{5,4,3,2,1,0:T(8,128)S(1)}, f32[4,2,8,2,8,128]{5,4,3,2,1,0:T(8,128)}, u32[]{:S(2)}) copy-start(f32[4,2,8,2,8,128]{5,4,3,2,1,0:T(8,128)} %fields.1) | copy-start | bytes 1572868
  1.7 3.6 %copy-start.4 = (f32[2,2,16]{2,1,0:T(2,128)S(1)}, f32[2,2,16]{2,1,0:T(2,128)}, u32[]{:S(2)}) copy-start(f32[2,2,16]{2,1,0:T(2,128)} %kappa.1) | copy-start | bytes 772
  1.7 8.6 %copy-start.3 = (f32[2,8,2,8,128]{4,3,2,1,0:T(8,128)S(1)}, f32[2,8,2,8,128]{4,3,2,1,0:T(8,128)}, u32[]{:S(2)}) copy-start(f32[2,8,2,8,128]{4,3,2,1,0:T(8,128)} %visc.3) | copy-start | bytes 393220
  2.2 8.1 %copy-start.1 = (f32[30,8,128]{2,1,0:T(8,128)S(1)}, f32[30,8,128]{2,1,0:T(8,128)}, u32[]{:S(2)}) copy-start(f32[30,8,128]{2,1,0:T(8,128)} %constant.4.clone.ctab) | copy-start | bytes 368644
  2.2 4.9 %collective-permute-start = (f32[64,128]{1,0:T(8,128)S(1)}, f32[64,128]{1,0:T(8,128)S(1)}, u32[]{:S(2)}, u32[]{:S(2)}) collective-permute-start(f32[64,128]{1,0:T(8,128)S(1)} %get-tuple-element.46), channel_id=1, source_target_pairs={{0,1},{1,0},{2,3},{3,2},{4,5},{5,4},{6,7},{7,6},{8,9},{9,8},{10,11... | collective-permute-start | bytes 98312 | tf_op jit(solution)/shard_map/ppermute | solution.py:1598
  2.7 4.4 %collective-permute-start.1 = (f32[64,128]{1,0:T(8,128)S(1)}, f32[64,128]{1,0:T(8,128)S(1)}, u32[]{:S(2)}, u32[]{:S(2)}) collective-permute-start(f32[64,128]{1,0:T(8,128)S(1)} %get-tuple-element.47), channel_id=1, source_target_pairs={{0,3},{1,2},{2,1},{3,0},{4,7},{5,6},{6,5},{7,4},{8,11},{9,10},{10,... | collective-permute-start | bytes 98312 | tf_op jit(solution)/shard_map/ppermute | solution.py:1599
  5.4 0.7 %copy-start.5 = (s32[2,2,16]{2,1,0:T(2,128)S(1)}, s32[2,2,16]{2,1,0:T(2,128)}, u32[]{:S(2)}) copy-start(s32[2,2,16]{2,1,0:T(2,128)} %group.1) | copy-start | bytes 772
  6.0 0.7 %copy-start.6 = (f32[4,128]{1,0:T(4,128)S(1)}, f32[4,128]{1,0:T(4,128)}, u32[]{:S(2)}) copy-start(f32[4,128]{1,0:T(4,128)} %coarse.1) | copy-start | bytes 6148
  7.2 5.5 %collective-permute-start.2 = (f32[69,128]{1,0:T(8,128)S(1)}, f32[69,128]{1,0:T(8,128)S(1)}, u32[]{:S(2)}, u32[]{:S(2)}) collective-permute-start(f32[69,128]{1,0:T(8,128)S(1)} %get-tuple-element.54), channel_id=1, source_target_pairs={{0,1},{1,0},{2,3},{3,2},{4,8},{5,9},{6,10},{7,11},{8,4},{9,5},{10,... | collective-permute-start | bytes 105992 | tf_op jit(solution)/shard_map/ppermute | solution.py:1598
  7.3 5.3 %collective-permute-start.3 = (f32[69,128]{1,0:T(8,128)S(1)}, f32[69,128]{1,0:T(8,128)S(1)}, u32[]{:S(2)}, u32[]{:S(2)}) collective-permute-start(f32[69,128]{1,0:T(8,128)S(1)} %get-tuple-element.55), channel_id=1, source_target_pairs={{0,4},{1,5},{2,6},{3,7},{4,0},{5,1},{6,2},{7,3},{8,12},{9,13},{10,... | collective-permute-start | bytes 105992 | tf_op jit(solution)/shard_map/ppermute | solution.py:1599
  13.7 1.7 %collective-permute-start.4 = (f32[97,128]{1,0:T(8,128)S(1)}, f32[97,128]{1,0:T(8,128)S(1)}, u32[]{:S(2)}, u32[]{:S(2)}) collective-permute-start(f32[97,128]{1,0:T(8,128)S(1)} %get-tuple-element.57), channel_id=1, source_target_pairs={{0,1},{1,0},{2,3},{3,2},{4,5},{5,4},{6,7},{7,6},{8,9},{9,8},{10,11... | collective-permute-start | bytes 149000 | tf_op jit(solution)/shard_map/ppermute | solution.py:1598
  13.8 3.6 %collective-permute-start.5 = (f32[97,128]{1,0:T(8,128)S(1)}, f32[97,128]{1,0:T(8,128)S(1)}, u32[]{:S(2)}, u32[]{:S(2)}) collective-permute-start(f32[97,128]{1,0:T(8,128)S(1)} %get-tuple-element.58), channel_id=1, source_target_pairs={{0,3},{1,2},{2,1},{3,0},{4,7},{5,6},{6,5},{7,4},{8,11},{9,10},{10,... | collective-permute-start | bytes 149000 | tf_op jit(solution)/shard_map/ppermute | solution.py:1599
  17.4 4.2 %collective-permute-start.6 = (f32[82,128]{1,0:T(8,128)S(1)}, f32[82,128]{1,0:T(8,128)S(1)}, u32[]{:S(2)}, u32[]{:S(2)}) collective-permute-start(f32[82,128]{1,0:T(8,128)S(1)} %get-tuple-element.62), channel_id=1, source_target_pairs={{0,1},{1,0},{2,3},{3,2},{4,8},{5,9},{6,10},{7,11},{8,4},{9,5},{10,... | collective-permute-start | bytes 125960 | tf_op jit(solution)/shard_map/ppermute | solution.py:1598
  18.0 4.7 %collective-permute-start.7 = (f32[82,128]{1,0:T(8,128)S(1)}, f32[82,128]{1,0:T(8,128)S(1)}, u32[]{:S(2)}, u32[]{:S(2)}) collective-permute-start(f32[82,128]{1,0:T(8,128)S(1)} %get-tuple-element.63), channel_id=1, source_target_pairs={{0,4},{1,5},{2,6},{3,7},{4,0},{5,1},{6,2},{7,3},{8,12},{9,13},{10,... | collective-permute-start | bytes 125960 | tf_op jit(solution)/shard_map/ppermute | solution.py:1599
  37.0 1.3 %collective-permute-start.8 = (f32[42,128]{1,0:T(8,128)S(1)}, f32[42,128]{1,0:T(8,128)S(1)}, u32[]{:S(2)}, u32[]{:S(2)}) collective-permute-start(f32[42,128]{1,0:T(8,128)S(1)} %shard_map.95), channel_id=1, source_target_pairs={{0,1},{1,0},{2,3},{3,2},{4,5},{5,4},{6,7},{7,6},{8,9},{9,8},{10,11... | collective-permute-start | bytes 64520 | tf_op jit(solution)/shard_map/ppermute | solution.py:1674
  38.9 1.3 %collective-permute-start.9 = (f32[34,128]{1,0:T(8,128)S(1)}, f32[34,128]{1,0:T(8,128)S(1)}, u32[]{:S(2)}, u32[]{:S(2)}) collective-permute-start(f32[34,128]{1,0:T(8,128)S(1)} %get-tuple-element.75), channel_id=1, source_target_pairs={{0,1},{1,0},{2,3},{3,2},{4,5},{5,4},{6,7},{7,6},{8,9},{9,8},{10,11... | collective-permute-start | bytes 52232 | tf_op jit(solution)/shard_map/ppermute | solution.py:1598
  39.2 3.2 %collective-permute-start.10 = (f32[34,128]{1,0:T(8,128)S(1)}, f32[34,128]{1,0:T(8,128)S(1)}, u32[]{:S(2)}, u32[]{:S(2)}) collective-permute-start(f32[34,128]{1,0:T(8,128)S(1)} %get-tuple-element.76), channel_id=1, source_target_pairs={{0,3},{1,2},{2,1},{3,0},{4,7},{5,6},{6,5},{7,4},{8,11},{9,10},{10,... | collective-permute-start | bytes 52232 | tf_op jit(solution)/shard_map/ppermute | solution.py:1599
  42.5 3.2 %collective-permute-start.11 = (f32[34,128]{1,0:T(8,128)S(1)}, f32[34,128]{1,0:T(8,128)S(1)}, u32[]{:S(2)}, u32[]{:S(2)}) collective-permute-start(f32[34,128]{1,0:T(8,128)S(1)} %get-tuple-element.81), channel_id=1, source_target_pairs={{0,1},{1,0},{2,3},{3,2},{4,8},{5,9},{6,10},{7,11},{8,4},{9,5},{10,... | collective-permute-start | bytes 52232 | tf_op jit(solution)/shard_map/ppermute | solution.py:1598
  42.8 3.8 %collective-permute-start.12 = (f32[34,128]{1,0:T(8,128)S(1)}, f32[34,128]{1,0:T(8,128)S(1)}, u32[]{:S(2)}, u32[]{:S(2)}) collective-permute-start(f32[34,128]{1,0:T(8,128)S(1)} %get-tuple-element.82), channel_id=1, source_target_pairs={{0,4},{1,5},{2,6},{3,7},{4,0},{5,1},{6,2},{7,3},{8,12},{9,13},{10,... | collective-permute-start | bytes 52232 | tf_op jit(solution)/shard_map/ppermute | solution.py:1599

commit v13 on v12

--- a/solution.py
+++ b/solution.py
@@ -182,13 +182,13 @@
         return jnp.where(self.even_x, second, first)
 
     def before_y(self, first, second):
-        return jnp.where(self.prev_y, jnp.where(self.even_y, second, first), 0.0)
+        return jnp.where(self.prev_y, jnp.where(self.even_y, first, second), 0.0)
 
     def after_y(self, first, second):
-        return jnp.where(self.next_y, jnp.where(self.even_y, first, second), 0.0)
+        return jnp.where(self.next_y, jnp.where(self.even_y, second, first), 0.0)
 
     def send_y(self, first, second):
-        return jnp.where(self.even_y, first, second)
+        return jnp.where(self.even_y, second, first)
 
 
 def along_x(matrix, tiles, sign):
@@ -261,7 +261,26 @@
     )
 
 
-def mass_kernel(fields, out, xf, first, second):
+def faces_kernel(fields, first, second, edges):
+    place = Place()
+    weight = weight_of(place.row) * weight_of(place.lane % NODES) * float(WEIGHTS[0])
+    for ch in range(4):
+        for ex in range(2):
+            for a in range(8):
+                edges[0, ch, ex, pl.ds(a, 1), :] = fields[ch, ex, a, 0, pl.ds(0, 1), :]
+                edges[1, ch, ex, pl.ds(a, 1), :] = fields[ch, ex, a, 1, pl.ds(7, 1), :]
+    for ch in range(4):
+        sides = [
+            place.join_y(*[place.join_z(edges[side, ch, ex] * weight) for ex in range(2)])
+            for side in range(2)
+        ]
+        for ex in range(2):
+            rows = pl.ds(ch * 16 + ex * 8, 8)
+            first[rows, :] = place.send_y(sides[1][ex], sides[0][ex])
+            second[rows, :] = place.send_y(sides[0][ex], sides[1][ex])
+
+
+def mass_kernel(fields, out, xf):
     place = Place()
     weight = weight_of(place.row) * weight_of(place.lane % NODES)
     for ch in range(4):
@@ -283,7 +302,6 @@
         for ey in range(2):
             xf[0, ch, ey] = tiles[0][0][ey]
             xf[1, ch, ey] = tiles[1][7][ey]
-        store_y_faces(place, out, first, second, (ch,), ch * 16)
 
 
 def turn_faces(place, xf, y_first, y_second, first, second):
@@ -374,7 +392,8 @@
     lane = lax.broadcasted_iota(jnp.int32, (LANES, LANES), 1)
     source = lax.broadcasted_iota(jnp.int32, (LANES, LANES), 0)
     for k in range(8):
-        spot = (source == k * elems + lane // NODES).astype(jnp.float32)
+        at = (k % 4 // 2) * 4 * elems + (k // 4) * 2 * elems + (k % 2) * elems
+        spot = (source == at + lane // NODES).astype(jnp.float32)
         spread[k] = exact_dot(compact[...], spot)
     there_x = [jnp.where(place.prev_x, 1.0, 0.0), 1.0, jnp.where(place.next_x, 1.0, 0.0)]
     there_y = [jnp.where(place.prev_y, 1.0, 0.0), 1.0, jnp.where(place.next_y, 1.0, 0.0)]
@@ -441,34 +460,13 @@
     return tile + pick(x_first[rows, :], x_second[rows, :])
 
 
-def pack_kernel(kappa, group, coarse, pack, facts):
+def facts_kernel(pack, facts):
     place = Place()
-    facts[...] = jnp.zeros(facts.shape, jnp.float32)
-    grid = jnp.zeros((1, LANES), jnp.float32)
-    elems = kappa.shape[2]
-    to = lax.broadcasted_iota(jnp.int32, (elems, LANES), 1)
-    element = lax.broadcasted_iota(jnp.int32, (elems, LANES), 0)
-    blocks = coarse.shape[1] // LANES
-    packed = jnp.zeros((1, LANES), jnp.float32)
-    for ex in range(2):
-        numbers = group[ex].astype(jnp.float32)
-        for ey in range(2):
-            mine, number = kappa[ex, pl.ds(ey, 1), :], numbers[ey : ey + 1]
-            at = (2 * ex + ey) * elems
-            packed = packed + exact_dot(mine, (to == at + element).astype(jnp.float32))
-            at = at + 4 * elems
-            packed = packed + exact_dot(number, (to == at + element).astype(jnp.float32))
-            at = ((2 * place.iy + ey) * elems + 4 * ex * elems) % LANES
-            grid = grid + exact_dot(mine, (to == at + element).astype(jnp.float32))
-            at = (at + 2 * elems) % LANES
-            grid = grid + exact_dot(number, (to == at + element).astype(jnp.float32))
-    pack[pl.ds(0, 1), :] = packed
+    grid = pltpu.roll(pack[pl.ds(0, 1), :], (place.iy % 4) * (LANES // 4), 1)
+    facts[:, pl.ds(0, LANES)] = jnp.zeros((1, LANES), jnp.float32)
+    facts[:, pl.ds(LANES, LANES)] = grid
     for c in range(NCD):
-        for j in range(blocks):
-            line = coarse[pl.ds(c, 1), pl.ds(j * LANES, LANES)]
-            pack[pl.ds(1 + c * blocks + j, 1), :] = line
-        facts[:, pl.ds((2 + c) * LANES, LANES)] = coarse[pl.ds(c, 1), pl.ds(0, LANES)]
-    facts[:, pl.ds(LANES, LANES)] = grid
+        facts[:, pl.ds((2 + c) * LANES, LANES)] = pack[pl.ds(1 + c, 1), :]
 
 
 def prepare_kernel(
@@ -1593,8 +1591,7 @@
                 else:
                     there = (ix, iy ^ 1) if axis == "gx" else (ix, across - 1 - iy)
                 pairs[k].append((number(ix, iy), number(*there)))
-    if axis == "gx":
-        pairs = pairs[::-1]
+    pairs = pairs[::-1]
     first_got = lax.ppermute(first, BOTH, pairs[0])
     return first_got, lax.ppermute(second, BOTH, pairs[1])
 
@@ -1626,15 +1623,12 @@
         return lax.all_to_all(msg, BOTH, 0, 0, tiled=True)
 
     beside = pl.CostEstimate(flops=10**7, bytes_accessed=10**6, transcendentals=0)
-    summed, xf, first, second = call(
-        mass_kernel,
-        [four, xf_shape, faces, faces],
-    )(fields)
-    pack, facts = call(
-        pack_kernel,
-        [(pack_rows, LANES), (1, 6 * LANES)],
-        cost_estimate=beside,
-    )(inv_density, elem_group, coarse_inverse)
+    first, second = call(faces_kernel, [faces, faces], [xf_shape])(fields)
+    numbers = elem_group.astype(jnp.float32)
+    row = jnp.stack([inv_density, numbers], 1).reshape(1, LANES)
+    pack = jnp.concatenate([row, coarse_inverse.reshape(NCD * blocks, LANES)], 0)
+    (facts,) = call(facts_kernel, [(1, 6 * LANES)], cost_estimate=beside)(pack)
+    summed, xf = call(mass_kernel, [four, xf_shape], cost_estimate=beside)(fields)
     y_got = swap(first, second, "gy")
     first, second = call(functools.partial(turn_faces_kernel, pack_rows), [turned, turned])(
         xf, pack, *y_got

time: 60 us -> 59.4 us (0.990)
  local copies, waits for them, and re-layouts: 2.47 us -> 1.16 us
  starting transfers between devices: 14.2 us -> 15 us
  waiting for transfers between devices: 7.81 us -> 8.6 us
  blocking collectives: 24.2 us -> 23.5 us
    ppermute x6, waiting for transfers between devices: 0.64 us -> 5.14 us  [swap(): first_got = lax.ppermute(first, BOTH, pairs[0])]
    ppermute x6, waiting for transfers between devices: 6.19 us -> 2.49 us  [swap(): return (first_got, lax.ppermute(second, BOTH, pairs[1]))]
    ppermute x6, starting transfers between devices: 1.87 us -> 4.71 us  [swap(): first_got = lax.ppermute(first, BOTH, pairs[0])]
    ppermute x6, starting transfers between devices: 12 us -> 10.1 us  [swap(): return (first_got, lax.ppermute(second, BOTH, pairs[1]))]
    unnamed x14 -> x16, local copies, waits for them, and re-layouts: 2.47 us -> 1.07 us
    all_to_all x2, blocking collectives: 24.2 us -> 23.5 us  [exchange_all(): return lax.all_to_all(msg, BOTH, 0, 0, tiled=True)]
  transfers between devices with their start and end apart: 13 -> 13, of which waited for: 6 -> 7; matrix products, arithmetic and copies ran while one was open for 0% -> 0% of each run, Pallas kernels for 8% -> 8%
where the time goes in v13:
time: 59.4 us; the launch traced here: 59.2 us
  blocking collectives  23.5 us (40%)
  starting transfers between devices  15 us (25%)
  Pallas kernels  10 us (17%)
  waiting for transfers between devices  8.6 us (14%)
  local copies, waits for them, and re-layouts  1.16 us (2%)
  between operations  0.82 us (1%)
    all_to_all x2, blocking collectives, exchange_all(): return lax.all_to_all(msg, BOTH, 0, 0, tiled=True)  23.5 us
    ppermute x6, starting transfers between devices, swap(): return (first_got, lax.ppermute(second, BOTH, pairs[1]))  10.1 us
    ppermute x6, waiting for transfers between devices, swap(): first_got = lax.ppermute(first, BOTH, pairs[0])  5.14 us
    ppermute x6, starting transfers between devices, swap(): first_got = lax.ppermute(first, BOTH, pairs[0])  4.71 us
    ppermute x6, waiting for transfers between devices, swap(): return (first_got, lax.ppermute(second, BOTH, pairs[1]))  2.49 us
    pallas_call x1, Pallas kernels, per_device(): call(prepare_kernel, [four, four, edge_shape, one], [four, four], cost_es...  2.33 us
    pallas_call x1, Pallas kernels, per_device(): call(finish_kernel, [one], [(LANES, LANES), (2,) + TILE, (2,) + TILE])  1.46 us
    pallas_call x1, Pallas kernels, per_device(): call(smooth_kernel, [one, one, (devices, 1, 6 * LANES) if grid_fits else...  1.28 us
  transfers between devices with their start and end apart: 13, of which 7 were waited for; matrix products, arithmetic and copies ran while one was open for 0% of the time, Pallas kernels for 8%

profile of v13, /device:TPU:0, one launch (start us, length us, event | category | flops | bytes accessed | tf_op | source)
XLA Modules:
  0.0 59.2 jit_solution(4659468529543122324)
XLA Ops:
  0.6 1.0 %copy-done.2 = f32[4,2,8,2,8,128]{5,4,3,2,1,0:T(8,128)S(1)} copy-done((f32[4,2,8,2,8,128]{5,4,3,2,1,0:T(8,128)S(1)}, f32[4,2,8,2,8,128]{5,4,3,2,1,0:T(8,128)}, u32[]{:S(2)}) %copy-start.2) | copy-done | bytes 524312
  1.9 2.5 %collective-permute-start = (f32[64,128]{1,0:T(8,128)S(1)}, f32[64,128]{1,0:T(8,128)S(1)}, u32[]{:S(2)}, u32[]{:S(2)}) collective-permute-start(f32[64,128]{1,0:T(8,128)S(1)} %get-tuple-element.44), channel_id=1, source_target_pairs={{0,3},{1,2},{2,1},{3,0},{4,7},{5,6},{6,5},{7,4},{8,11},{9,10},{10,... | collective-permute-start | bytes 98312 | tf_op jit(solution)/shard_map/ppermute | solution.py:1595
  4.3 0.7 %collective-permute-start.1 = (f32[64,128]{1,0:T(8,128)S(1)}, f32[64,128]{1,0:T(8,128)S(1)}, u32[]{:S(2)}, u32[]{:S(2)}) collective-permute-start(f32[64,128]{1,0:T(8,128)S(1)} %get-tuple-element.45), channel_id=1, source_target_pairs={{0,1},{1,0},{2,3},{3,2},{4,5},{5,4},{6,7},{7,6},{8,9},{9,8},{10,11... | collective-permute-start | bytes 98312 | tf_op jit(solution)/shard_map/ppermute | solution.py:1596
  5.2 0.3 shard_map.86
  5.5 0.6 collective-permute-done.y_first
  6.1 0.6 collective-permute-start.2
  6.7 3.4 %collective-permute-start.3 = (f32[69,128]{1,0:T(8,128)S(1)}, f32[69,128]{1,0:T(8,128)S(1)}, u32[]{:S(2)}, u32[]{:S(2)}) collective-permute-start(f32[69,128]{1,0:T(8,128)S(1)} %get-tuple-element.52), channel_id=1, source_target_pairs={{0,4},{1,5},{2,6},{3,7},{4,0},{5,1},{6,2},{7,3},{8,12},{9,13},{10,... | collective-permute-start | bytes 105992 | tf_op jit(solution)/shard_map/ppermute | solution.py:1596
  10.1 2.3 %shard_map.88 = (f32[4,2,8,2,8,128]{5,4,3,2,1,0:T(8,128)S(1)}, f32[4,2,8,2,8,128]{5,4,3,2,1,0:T(8,128)S(1)}, f32[4,2,2,8,128]{4,3,2,1,0:T(8,128)S(1)}, f32[2,8,2,8,128]{4,3,2,1,0:T(8,128)S(1)}) custom-call(f32[4,2,8,2,8,128]{5,4,3,2,1,0:T(8,128)S(1)} %get-tuple-element.43.summed, f32[2,8,2,8,128]{4,3,2,1,0:T(8,128)S(1)} %copy-done.4, ...), custom_call_target="tpu_custom_call" | custom-call | flops 10000000 | bytes 1000000 | tf_op jit(solution)/shard_map/pallas_call | solution.py:1638
  12.5 1.0 %shard_map.90 = (f32[4,2,8,2,8,128]{5,4,3,2,1,0:T(8,128)S(1)}, f32[2,4,2,8,128]{4,3,2,1,0:T(8,128)S(1)}, f32[2,2,8,128]{3,2,1,0:T(8,128)S(1)}, f32[97,128]{1,0:T(8,128)S(1)}, f32[97,128]{1,0:T(8,128)S(1)}) custom-call(f32[4,2,8,2,8,128]{5,4,3,2,1,0:T(8,128)S(1)} %get-tuple-element.46.begun, f32[4,2,8,2,8,128]{5,4,3,2,1,0:T(8,128)S(1)} %get-tuple-element.47.given, ...), custom_call_target="tpu_custom_call" | custom-call | tf_op jit(solution)/shard_map/pallas_call | solution.py:1641
  13.5 0.8 %collective-permute-start.4 = (f32[97,128]{1,0:T(8,128)S(1)}, f32[97,128]{1,0:T(8,128)S(1)}, u32[]{:S(2)}, u32[]{:S(2)}) collective-permute-start(f32[97,128]{1,0:T(8,128)S(1)} %get-tuple-element.54), channel_id=1, source_target_pairs={{0,3},{1,2},{2,1},{3,0},{4,7},{5,6},{6,5},{7,4},{8,11},{9,10},{10,... | collective-permute-start | bytes 149000 | tf_op jit(solution)/shard_map/ppermute | solution.py:1595
  14.4 1.0 %collective-permute-start.5 = (f32[97,128]{1,0:T(8,128)S(1)}, f32[97,128]{1,0:T(8,128)S(1)}, u32[]{:S(2)}, u32[]{:S(2)}) collective-permute-start(f32[97,128]{1,0:T(8,128)S(1)} %get-tuple-element.55), channel_id=1, source_target_pairs={{0,1},{1,0},{2,3},{3,2},{4,5},{5,4},{6,7},{7,6},{8,9},{9,8},{10,11... | collective-permute-start | bytes 149000 | tf_op jit(solution)/shard_map/ppermute | solution.py:1596
  15.3 2.3 %collective-permute-done.4.y_first = f32[97,128]{1,0:T(8,128)S(1)} collective-permute-done((f32[97,128]{1,0:T(8,128)S(1)}, f32[97,128]{1,0:T(8,128)S(1)}, u32[]{:S(2)}, u32[]{:S(2)}) %collective-permute-start.4) | collective-permute-done | bytes 49696 | tf_op jit(solution)/shard_map/ppermute | solution.py:1595
  17.8 2.9 %collective-permute-start.7 = (f32[82,128]{1,0:T(8,128)S(1)}, f32[82,128]{1,0:T(8,128)S(1)}, u32[]{:S(2)}, u32[]{:S(2)}) collective-permute-start(f32[82,128]{1,0:T(8,128)S(1)} %get-tuple-element.60), channel_id=1, source_target_pairs={{0,4},{1,5},{2,6},{3,7},{4,0},{5,1},{6,2},{7,3},{8,12},{9,13},{10,... | collective-permute-start | bytes 125960 | tf_op jit(solution)/shard_map/ppermute | solution.py:1596
  20.8 0.5 shard_map.93
  21.2 0.5 shard_map.91
  21.8 1.0 %collective-permute-done.7.x_second = f32[82,128]{1,0:T(8,128)S(1)} collective-permute-done((f32[82,128]{1,0:T(8,128)S(1)}, f32[82,128]{1,0:T(8,128)S(1)}, u32[]{:S(2)}, u32[]{:S(2)}) %collective-permute-start.7) | collective-permute-done | bytes 42016 | tf_op jit(solution)/shard_map/ppermute | solution.py:1596
  22.8 0.6 shard_map.94
  23.3 13.0 %all_to_all.10.got = f32[32,8,128]{2,1,0:T(8,128)S(1)} all-to-all(f32[32,8,128]{2,1,0:T(8,128)S(1)} %get-tuple-element.65), channel_id=1, replica_groups=mesh['gx'=8,'gy'=4] {'gx','gy'}, dimensions={0} | all-to-all | bytes 262144 | tf_op jit(solution)/shard_map/all_to_all | solution.py:1623
  36.4 0.3 collective-permute-start.8
  36.7 1.0 %collective-permute-done.8.relayed = f32[42,128]{1,0:T(8,128)S(1)} collective-permute-done((f32[42,128]{1,0:T(8,128)S(1)}, f32[42,128]{1,0:T(8,128)S(1)}, u32[]{:S(2)}, u32[]{:S(2)}) %collective-permute-start.8) | collective-permute-done | bytes 21536 | tf_op jit(solution)/shard_map/ppermute | solution.py:1668
  37.7 0.7 %shard_map.96 = (f32[2,8,2,8,128]{4,3,2,1,0:T(8,128)S(1)}, f32[2,8,2,8,128]{4,3,2,1,0:T(8,128)S(1)}, f32[2,2,8,128]{3,2,1,0:T(8,128)S(1)}, f32[34,128]{1,0:T(8,1...) custom-call(f32[32,8,128]{2,1,0:T(8,128)S(1)} %all_to_all.10.got, f32[42,128]{1,0:T(8,128)S(1)} %collective-permute-done.8.relayed, ...), custom_call_target="tpu_custom_call" | custom-call | tf_op jit(solution)/shard_map/pallas_call | solution.py:1671
  38.3 0.3 collective-permute-start.10
  38.6 0.3 collective-permute-start.9
  39.0 0.6 %collective-permute-done.10.y_second = f32[34,128]{1,0:T(8,128)S(1)} collective-permute-done((f32[34,128]{1,0:T(8,128)S(1)}, f32[34,128]{1,0:T(8,128)S(1)}, u32[]{:S(2)}, u32[]{:S(2)}) %collective-permute-start.10) | collective-permute-done | bytes 17440 | tf_op jit(solution)/shard_map/ppermute | solution.py:1596
  39.6 2.2 %collective-permute-done.9.y_first = f32[34,128]{1,0:T(8,128)S(1)} collective-permute-done((f32[34,128]{1,0:T(8,128)S(1)}, f32[34,128]{1,0:T(8,128)S(1)}, u32[]{:S(2)}, u32[]{:S(2)}) %collective-permute-start.9) | collective-permute-done | bytes 17440 | tf_op jit(solution)/shard_map/ppermute | solution.py:1595
  41.9 0.3 collective-permute-start.11
  42.2 1.8 %collective-permute-start.12 = (f32[34,128]{1,0:T(8,128)S(1)}, f32[34,128]{1,0:T(8,128)S(1)}, u32[]{:S(2)}, u32[]{:S(2)}) collective-permute-start(f32[34,128]{1,0:T(8,128)S(1)} %get-tuple-element.79), channel_id=1, source_target_pairs={{0,4},{1,5},{2,6},{3,7},{4,0},{5,1},{6,2},{7,3},{8,12},{9,13},{10,... | collective-permute-start | bytes 52232 | tf_op jit(solution)/shard_map/ppermute | solution.py:1596
  44.1 0.8 %shard_map.97 = (f32[4,2,8,2,8,128]{5,4,3,2,1,0:T(8,128)}, f32[1,128]{1,0:T(1,128)S(1)}) custom-call(f32[4,2,8,2,8,128]{5,4,3,2,1,0:T(8,128)S(1)} %get-tuple-element.56.begun, f32[82,128]{1,0:T(8,128)S(1)} %collective-permute-done.6.x_first, f32[82,128]{1,0:T(8,128)S(1)} %collective-permute-done.7.x_second, f32[1,128]{1,0:T(1,128)S(1)} %get-tuple-element.69.extra), custom_call_target="tpu_custom_call" | custom-call | flops 10000000 | bytes 1000000 | tf_op jit(solution)/shard_map/pallas_call | solution.py:1679
  45.2 0.8 %collective-permute-done.12.x_second = f32[34,128]{1,0:T(8,128)S(1)} collective-permute-done((f32[34,128]{1,0:T(8,128)S(1)}, f32[34,128]{1,0:T(8,128)S(1)}, u32[]{:S(2)}, u32[]{:S(2)}) %collective-permute-start.12) | collective-permute-done | bytes 17440 | tf_op jit(solution)/shard_map/ppermute | solution.py:1596
  46.0 1.3 %shard_map.101 = (f32[2,8,2,8,128]{4,3,2,1,0:T(8,128)}, f32[2,8,2,8,128]{4,3,2,1,0:T(8,128)S(1)}, f32[32,1,768]{2,1,0:T(1,128)S(1)}) custom-call(f32[2,8,2,8,128]{4,3,2,1,0:T(8,128)S(1)} %get-tuple-element.74.begun, f32[2,8,2,8,128]{4,3,2,1,0:T(8,128)S(1)} %get-tuple-element.75.begun_scaled, f32[2,8,2,8,128]{4,3,2,1,0:T(8,128)S(1)} %get-tuple-element.76.given, ...), custom_call_target="tpu_custom_call" | custom-call | tf_op jit(solution)/shard_map/pallas_call | solution.py:1685
  47.3 10.4 %all_to_all.11.got = f32[32,1,768]{2,1,0:T(1,128)S(1)} all-to-all(f32[32,1,768]{2,1,0:T(1,128)S(1)} %get-tuple-element.81), channel_id=1, replica_groups=mesh['gx'=8,'gy'=4] {'gx','gy'}, dimensions={0} | all-to-all | bytes 196608 | tf_op jit(solution)/shard_map/all_to_all | solution.py:1623
  57.7 1.5 %shard_map.102 = f32[2,8,2,8,128]{4,3,2,1,0:T(8,128)} custom-call(f32[32,1,768]{2,1,0:T(1,128)S(1)} %all_to_all.11.got, f32[16,128]{1,0:T(8,128)S(1)} %get-tuple-element.64.grp, f32[2,8,2,8,128]{4,3,2,1,0:T(8,128)S(1)} %get-tuple-element.82.direction, f32[2,8,2,8,128]{4,3,2,1,0:T(8,128)S(1)} %get-tuple-element.83.smoothed), custom_call_target="tpu_custom_call" | custom-call | tf_op jit(solution)/shard_map/pallas_call | solution.py:1694
  (34 shorter events, 0.9 us)
Async XLA Ops:
  0.6 1.0 %copy-start.2 = (f32[4,2,8,2,8,128]{5,4,3,2,1,0:T(8,128)S(1)}, f32[4,2,8,2,8,128]{5,4,3,2,1,0:T(8,128)}, u32[]{:S(2)}) copy-start(f32[4,2,8,2,8,128]{5,4,3,2,1,0:T(8,128)} %fields.3) | copy-start | bytes 1572868
  1.7 3.3 %copy-start.5 = (s32[2,2,16]{2,1,0:T(2,128)S(1)}, s32[2,2,16]{2,1,0:T(2,128)}, u32[]{:S(2)}) copy-start(s32[2,2,16]{2,1,0:T(2,128)} %param.10) | copy-start | bytes 772
  1.7 3.3 %copy-start.7 = (f32[2,2,16]{2,1,0:T(2,128)S(1)}, f32[2,2,16]{2,1,0:T(2,128)}, u32[]{:S(2)}) copy-start(f32[2,2,16]{2,1,0:T(2,128)} %param.9) | copy-start | bytes 772
  1.7 3.4 %copy-start.6 = (f32[4,128]{1,0:T(4,128)S(1)}, f32[4,128]{1,0:T(4,128)}, u32[]{:S(2)}) copy-start(f32[4,128]{1,0:T(4,128)} %param.11) | copy-start | bytes 6148
  1.7 3.5 %copy-start.3 = (f32[4,2,8,2,8,128]{5,4,3,2,1,0:T(8,128)S(1)}, f32[4,2,8,2,8,128]{5,4,3,2,1,0:T(8,128)}, u32[]{:S(2)}) copy-start(f32[4,2,8,2,8,128]{5,4,3,2,1,0:T(8,128)} %fields.3) | copy-start | bytes 1572868
  1.8 8.3 %copy-start = (bf16[3,256,256]{2,1,0:T(8,128)(2,1)S(1)}, bf16[3,256,256]{2,1,0:T(8,128)(2,1)}, u32[]{:S(2)}) copy-start(bf16[3,256,256]{2,1,0:T(8,128)(2,1)} %constant.5.clone.zmat) | copy-start | bytes 1179652
  1.9 4.3 %collective-permute-start = (f32[64,128]{1,0:T(8,128)S(1)}, f32[64,128]{1,0:T(8,128)S(1)}, u32[]{:S(2)}, u32[]{:S(2)}) collective-permute-start(f32[64,128]{1,0:T(8,128)S(1)} %get-tuple-element.44), channel_id=1, source_target_pairs={{0,3},{1,2},{2,1},{3,0},{4,7},{5,6},{6,5},{7,4},{8,11},{9,10},{10,... | collective-permute-start | bytes 98312 | tf_op jit(solution)/shard_map/ppermute | solution.py:1595
  4.3 1.8 %collective-permute-start.1 = (f32[64,128]{1,0:T(8,128)S(1)}, f32[64,128]{1,0:T(8,128)S(1)}, u32[]{:S(2)}, u32[]{:S(2)}) collective-permute-start(f32[64,128]{1,0:T(8,128)S(1)} %get-tuple-element.45), channel_id=1, source_target_pairs={{0,1},{1,0},{2,3},{3,2},{4,5},{5,4},{6,7},{7,6},{8,9},{9,8},{10,11... | collective-permute-start | bytes 98312 | tf_op jit(solution)/shard_map/ppermute | solution.py:1596
  5.1 5.0 %copy-start.4 = (f32[2,8,2,8,128]{4,3,2,1,0:T(8,128)S(1)}, f32[2,8,2,8,128]{4,3,2,1,0:T(8,128)}, u32[]{:S(2)}) copy-start(f32[2,8,2,8,128]{4,3,2,1,0:T(8,128)} %visc.3) | copy-start | bytes 393220
  5.5 4.6 %copy-start.1 = (f32[30,8,128]{2,1,0:T(8,128)S(1)}, f32[30,8,128]{2,1,0:T(8,128)}, u32[]{:S(2)}) copy-start(f32[30,8,128]{2,1,0:T(8,128)} %constant.4.clone.ctab) | copy-start | bytes 368644
  6.1 6.3 %collective-permute-start.2 = (f32[69,128]{1,0:T(8,128)S(1)}, f32[69,128]{1,0:T(8,128)S(1)}, u32[]{:S(2)}, u32[]{:S(2)}) collective-permute-start(f32[69,128]{1,0:T(8,128)S(1)} %get-tuple-element.51), channel_id=1, source_target_pairs={{0,1},{1,0},{2,3},{3,2},{4,8},{5,9},{6,10},{7,11},{8,4},{9,5},{10,... | collective-permute-start | bytes 105992 | tf_op jit(solution)/shard_map/ppermute | solution.py:1595
  6.7 5.8 %collective-permute-start.3 = (f32[69,128]{1,0:T(8,128)S(1)}, f32[69,128]{1,0:T(8,128)S(1)}, u32[]{:S(2)}, u32[]{:S(2)}) collective-permute-start(f32[69,128]{1,0:T(8,128)S(1)} %get-tuple-element.52), channel_id=1, source_target_pairs={{0,4},{1,5},{2,6},{3,7},{4,0},{5,1},{6,2},{7,3},{8,12},{9,13},{10,... | collective-permute-start | bytes 105992 | tf_op jit(solution)/shard_map/ppermute | solution.py:1596
  13.5 4.1 %collective-permute-start.4 = (f32[97,128]{1,0:T(8,128)S(1)}, f32[97,128]{1,0:T(8,128)S(1)}, u32[]{:S(2)}, u32[]{:S(2)}) collective-permute-start(f32[97,128]{1,0:T(8,128)S(1)} %get-tuple-element.54), channel_id=1, source_target_pairs={{0,3},{1,2},{2,1},{3,0},{4,7},{5,6},{6,5},{7,4},{8,11},{9,10},{10,... | collective-permute-start | bytes 149000 | tf_op jit(solution)/shard_map/ppermute | solution.py:1595
  14.4 3.3 %collective-permute-start.5 = (f32[97,128]{1,0:T(8,128)S(1)}, f32[97,128]{1,0:T(8,128)S(1)}, u32[]{:S(2)}, u32[]{:S(2)}) collective-permute-start(f32[97,128]{1,0:T(8,128)S(1)} %get-tuple-element.55), channel_id=1, source_target_pairs={{0,1},{1,0},{2,3},{3,2},{4,5},{5,4},{6,7},{7,6},{8,9},{9,8},{10,11... | collective-permute-start | bytes 149000 | tf_op jit(solution)/shard_map/ppermute | solution.py:1596
  17.6 4.1 %collective-permute-start.6 = (f32[82,128]{1,0:T(8,128)S(1)}, f32[82,128]{1,0:T(8,128)S(1)}, u32[]{:S(2)}, u32[]{:S(2)}) collective-permute-start(f32[82,128]{1,0:T(8,128)S(1)} %get-tuple-element.59), channel_id=1, source_target_pairs={{0,1},{1,0},{2,3},{3,2},{4,8},{5,9},{6,10},{7,11},{8,4},{9,5},{10,... | collective-permute-start | bytes 125960 | tf_op jit(solution)/shard_map/ppermute | solution.py:1595
  17.8 4.9 %collective-permute-start.7 = (f32[82,128]{1,0:T(8,128)S(1)}, f32[82,128]{1,0:T(8,128)S(1)}, u32[]{:S(2)}, u32[]{:S(2)}) collective-permute-start(f32[82,128]{1,0:T(8,128)S(1)} %get-tuple-element.60), channel_id=1, source_target_pairs={{0,4},{1,5},{2,6},{3,7},{4,0},{5,1},{6,2},{7,3},{8,12},{9,13},{10,... | collective-permute-start | bytes 125960 | tf_op jit(solution)/shard_map/ppermute | solution.py:1596
  36.4 1.3 %collective-permute-start.8 = (f32[42,128]{1,0:T(8,128)S(1)}, f32[42,128]{1,0:T(8,128)S(1)}, u32[]{:S(2)}, u32[]{:S(2)}) collective-permute-start(f32[42,128]{1,0:T(8,128)S(1)} %shard_map.95), channel_id=1, source_target_pairs={{0,1},{1,0},{2,3},{3,2},{4,5},{5,4},{6,7},{7,6},{8,9},{9,8},{10,11... | collective-permute-start | bytes 64520 | tf_op jit(solution)/shard_map/ppermute | solution.py:1668
  38.3 1.3 %collective-permute-start.10 = (f32[34,128]{1,0:T(8,128)S(1)}, f32[34,128]{1,0:T(8,128)S(1)}, u32[]{:S(2)}, u32[]{:S(2)}) collective-permute-start(f32[34,128]{1,0:T(8,128)S(1)} %get-tuple-element.73), channel_id=1, source_target_pairs={{0,1},{1,0},{2,3},{3,2},{4,5},{5,4},{6,7},{7,6},{8,9},{9,8},{10,11... | collective-permute-start | bytes 52232 | tf_op jit(solution)/shard_map/ppermute | solution.py:1596
  38.6 3.2 %collective-permute-start.9 = (f32[34,128]{1,0:T(8,128)S(1)}, f32[34,128]{1,0:T(8,128)S(1)}, u32[]{:S(2)}, u32[]{:S(2)}) collective-permute-start(f32[34,128]{1,0:T(8,128)S(1)} %get-tuple-element.72), channel_id=1, source_target_pairs={{0,3},{1,2},{2,1},{3,0},{4,7},{5,6},{6,5},{7,4},{8,11},{9,10},{10,... | collective-permute-start | bytes 52232 | tf_op jit(solution)/shard_map/ppermute | solution.py:1595
  41.9 3.3 %collective-permute-start.11 = (f32[34,128]{1,0:T(8,128)S(1)}, f32[34,128]{1,0:T(8,128)S(1)}, u32[]{:S(2)}, u32[]{:S(2)}) collective-permute-start(f32[34,128]{1,0:T(8,128)S(1)} %get-tuple-element.78), channel_id=1, source_target_pairs={{0,1},{1,0},{2,3},{3,2},{4,8},{5,9},{6,10},{7,11},{8,4},{9,5},{10,... | collective-permute-start | bytes 52232 | tf_op jit(solution)/shard_map/ppermute | solution.py:1595
  42.2 3.8 %collective-permute-start.12 = (f32[34,128]{1,0:T(8,128)S(1)}, f32[34,128]{1,0:T(8,128)S(1)}, u32[]{:S(2)}, u32[]{:S(2)}) collective-permute-start(f32[34,128]{1,0:T(8,128)S(1)} %get-tuple-element.79), channel_id=1, source_target_pairs={{0,4},{1,5},{2,6},{3,7},{4,0},{5,1},{6,2},{7,3},{8,12},{9,13},{10,... | collective-permute-start | bytes 52232 | tf_op jit(solution)/shard_map/ppermute | solution.py:1596

commit v14 on v13

--- a/solution.py
+++ b/solution.py
@@ -492,7 +492,7 @@
 
     def column(index, carry):
         ch, ey = index // 2, index % 2
-        coef = jnp.where(ch == 3, 1.0 / prandtl, 1.0)
+        coef = 1.0 / prandtl if ch == 3 else 1.0
         for ex in range(2):
             grad_x = along_x(DERIV, [start[ch, ex, a, ey] for a in range(8)], -1)
             flux_x = [
@@ -521,7 +521,8 @@
             back = along_x(DERIV.T, flux_x, -1)
             for a in range(8):
                 answer[ex, a, ey] = back[a]
-    lax.fori_loop(0, 8, column, 0)
+    for index in range(8):
+        column(index, 0)
     for ch in range(4):
         for ex in range(2):
             inner = pl.ds(1 - ex, 7)
@@ -587,7 +588,7 @@
 
     def side_of(ch, ex, a, ey):
         outer = OUTER[ex][1]
-        coef = jnp.where(ch == 3, 1.0 / prandtl, 1.0)
+        coef = 1.0 / prandtl if ch == 3 else 1.0
         extra = came[ch, ex, ey]
         node = float(WEIGHTS[a]) * weight
         turn = float(DERIV[a, outer])
@@ -613,7 +614,8 @@
                     share[ch, ex, a, ey] = part + tiles[ex][a][ey] * (inv_mass[ey] * scale)
         return carry
 
-    lax.fori_loop(0, 4, finish, 0)
+    for ch in range(4):
+        finish(ch, 0)
     for ch in range(4):
         store_y_faces(place, share, first, second, (ch,), ch * 16)
         for ey in range(2):
@@ -1503,20 +1505,21 @@
     row_lane = lax.broadcasted_iota(jnp.int32, (1, LANES), 1)
     rest = jnp.zeros((1, LANES), jnp.float32)
     dual = jnp.zeros((1, LANES), jnp.float32)
-    sums = [jnp.zeros((1, LANES), jnp.float32) for _ in range(4)]
+    scalars = jnp.zeros((1, LANES), jnp.float32)
     for i in range(per):
         line = got[i, :, pl.ds(0, LANES)]
         mine = row_lane // NCD == (i + AWAY) % per
         known = row_lane // NCD == (i + BEYOND) % per
         rest = jnp.where(mine, line, rest)
         dual = dual + jnp.where(mine | known, 0.0, line)
-        for c in range(4):
-            sums[c] = sums[c] + jnp.where(row_lane == ((i + BEYOND) % per) * NCD + c, line, 0.0)
+        scalars = jnp.where(known, line, scalars)
+        for c in range(NCD):
             block = got[i, :, pl.ds((2 + c) * LANES, LANES)]
             matrix[pl.ds(i * NCD + c, 1), :] = block
     rest = pltpu.roll(rest, (per - AWAY) * NCD, 1)
     energy, curvature, square, self_energy = [
-        jnp.sum(value, axis=1, keepdims=True) for value in sums
+        jnp.sum(jnp.where(row_lane % NCD == c, scalars, 0.0), axis=1, keepdims=True)
+        for c in range(4)
     ]
     values = exact_dot(jnp.broadcast_to(rest, TILE), matrix[...])
     line = values[0:1]

time: 59.4 us -> 59 us (level)
  Pallas kernels: 10 us -> 9.04 us
    pallas_call x1, Pallas kernels: 2.33 us -> 1.71 us  [per_device(): call(prepare_kernel, [four, four, edge_shape, one], [four, four], cost_es...]
  transfers between devices with their start and end apart: 13 -> 13, of which waited for: 7 -> 8; matrix products, arithmetic and copies ran while one was open for 0% -> 0% of each run, Pallas kernels for 8% -> 7%
where the time goes in v14:
time: 59 us; the launch traced here: 58.8 us
  blocking collectives  23.6 us (40%)
  starting transfers between devices  15.4 us (26%)
  Pallas kernels  9.04 us (15%)
  waiting for transfers between devices  8.81 us (15%)
  local copies, waits for them, and re-layouts  1.16 us (2%)
  between operations  0.81 us (1%)
    all_to_all x2, blocking collectives, exchange_all(): return lax.all_to_all(msg, BOTH, 0, 0, tiled=True)  23.6 us
    ppermute x6, starting transfers between devices, swap(): return (first_got, lax.ppermute(second, BOTH, pairs[1]))  10.6 us
    ppermute x6, waiting for transfers between devices, swap(): first_got = lax.ppermute(first, BOTH, pairs[0])  5.14 us
    ppermute x6, starting transfers between devices, swap(): first_got = lax.ppermute(first, BOTH, pairs[0])  4.51 us
    ppermute x6, waiting for transfers between devices, swap(): return (first_got, lax.ppermute(second, BOTH, pairs[1]))  2.69 us
    pallas_call x1, Pallas kernels, per_device(): call(prepare_kernel, [four, four, edge_shape, one], [four, four], cost_es...  1.71 us
    pallas_call x1, Pallas kernels, per_device(): call(finish_kernel, [one], [(LANES, LANES), (2,) + TILE, (2,) + TILE])  1.46 us
    pallas_call x1, Pallas kernels, per_device(): call(smooth_kernel, [one, one, (devices, 1, 6 * LANES) if grid_fits else...  1.28 us
  transfers between devices with their start and end apart: 13, of which 8 were waited for; matrix products, arithmetic and copies ran while one was open for 0% of the time, Pallas kernels for 7%

profile of v14, /device:TPU:0, one launch (start us, length us, event | category | flops | bytes accessed | tf_op | source)
XLA Modules:
  0.0 58.8 jit_solution(4198880761265439089)
XLA Ops:
  0.6 1.0 %copy-done.2 = f32[4,2,8,2,8,128]{5,4,3,2,1,0:T(8,128)S(1)} copy-done((f32[4,2,8,2,8,128]{5,4,3,2,1,0:T(8,128)S(1)}, f32[4,2,8,2,8,128]{5,4,3,2,1,0:T(8,128)}, u32[]{:S(2)}) %copy-start.2) | copy-done | bytes 524312
  1.9 2.5 %collective-permute-start = (f32[64,128]{1,0:T(8,128)S(1)}, f32[64,128]{1,0:T(8,128)S(1)}, u32[]{:S(2)}, u32[]{:S(2)}) collective-permute-start(f32[64,128]{1,0:T(8,128)S(1)} %get-tuple-element.44), channel_id=1, source_target_pairs={{0,3},{1,2},{2,1},{3,0},{4,7},{5,6},{6,5},{7,4},{8,11},{9,10},{10,... | collective-permute-start | bytes 98312 | tf_op jit(solution)/shard_map/ppermute | solution.py:1598
  4.3 0.7 %collective-permute-start.1 = (f32[64,128]{1,0:T(8,128)S(1)}, f32[64,128]{1,0:T(8,128)S(1)}, u32[]{:S(2)}, u32[]{:S(2)}) collective-permute-start(f32[64,128]{1,0:T(8,128)S(1)} %get-tuple-element.45), channel_id=1, source_target_pairs={{0,1},{1,0},{2,3},{3,2},{4,5},{5,4},{6,7},{7,6},{8,9},{9,8},{10,11... | collective-permute-start | bytes 98312 | tf_op jit(solution)/shard_map/ppermute | solution.py:1599
  5.2 0.3 shard_map.86
  5.5 0.6 collective-permute-done.y_first
  6.1 0.6 collective-permute-start.2
  6.7 3.4 %collective-permute-start.3 = (f32[69,128]{1,0:T(8,128)S(1)}, f32[69,128]{1,0:T(8,128)S(1)}, u32[]{:S(2)}, u32[]{:S(2)}) collective-permute-start(f32[69,128]{1,0:T(8,128)S(1)} %get-tuple-element.52), channel_id=1, source_target_pairs={{0,4},{1,5},{2,6},{3,7},{4,0},{5,1},{6,2},{7,3},{8,12},{9,13},{10,... | collective-permute-start | bytes 105992 | tf_op jit(solution)/shard_map/ppermute | solution.py:1599
  10.1 1.7 %shard_map.88 = (f32[4,2,8,2,8,128]{5,4,3,2,1,0:T(8,128)S(1)}, f32[4,2,8,2,8,128]{5,4,3,2,1,0:T(8,128)S(1)}, f32[4,2,2,8,128]{4,3,2,1,0:T(8,128)S(1)}, f32[2,8,2,8,128]{4,3,2,1,0:T(8,128)S(1)}) custom-call(f32[4,2,8,2,8,128]{5,4,3,2,1,0:T(8,128)S(1)} %get-tuple-element.43.summed, f32[2,8,2,8,128]{4,3,2,1,0:T(8,128)S(1)} %copy-done.4, ...), custom_call_target="tpu_custom_call" | custom-call | flops 10000000 | bytes 1000000 | tf_op jit(solution)/shard_map/pallas_call | solution.py:1641
  12.1 0.7 %shard_map.90 = (f32[4,2,8,2,8,128]{5,4,3,2,1,0:T(8,128)S(1)}, f32[2,4,2,8,128]{4,3,2,1,0:T(8,128)S(1)}, f32[2,2,8,128]{3,2,1,0:T(8,128)S(1)}, f32[97,128]{1,0:T(8,128)S(1)}, f32[97,128]{1,0:T(8,128)S(1)}) custom-call(f32[4,2,8,2,8,128]{5,4,3,2,1,0:T(8,128)S(1)} %get-tuple-element.46.begun, f32[4,2,8,2,8,128]{5,4,3,2,1,0:T(8,128)S(1)} %get-tuple-element.47.given, ...), custom_call_target="tpu_custom_call" | custom-call | tf_op jit(solution)/shard_map/pallas_call | solution.py:1644
  12.7 0.6 %collective-permute-start.4 = (f32[97,128]{1,0:T(8,128)S(1)}, f32[97,128]{1,0:T(8,128)S(1)}, u32[]{:S(2)}, u32[]{:S(2)}) collective-permute-start(f32[97,128]{1,0:T(8,128)S(1)} %get-tuple-element.54), channel_id=1, source_target_pairs={{0,3},{1,2},{2,1},{3,0},{4,7},{5,6},{6,5},{7,4},{8,11},{9,10},{10,... | collective-permute-start | bytes 149000 | tf_op jit(solution)/shard_map/ppermute | solution.py:1598
  13.3 1.1 %collective-permute-start.5 = (f32[97,128]{1,0:T(8,128)S(1)}, f32[97,128]{1,0:T(8,128)S(1)}, u32[]{:S(2)}, u32[]{:S(2)}) collective-permute-start(f32[97,128]{1,0:T(8,128)S(1)} %get-tuple-element.55), channel_id=1, source_target_pairs={{0,1},{1,0},{2,3},{3,2},{4,5},{5,4},{6,7},{7,6},{8,9},{9,8},{10,11... | collective-permute-start | bytes 149000 | tf_op jit(solution)/shard_map/ppermute | solution.py:1599
  14.5 2.3 %collective-permute-done.4.y_first = f32[97,128]{1,0:T(8,128)S(1)} collective-permute-done((f32[97,128]{1,0:T(8,128)S(1)}, f32[97,128]{1,0:T(8,128)S(1)}, u32[]{:S(2)}, u32[]{:S(2)}) %collective-permute-start.4) | collective-permute-done | bytes 49696 | tf_op jit(solution)/shard_map/ppermute | solution.py:1598
  17.0 3.3 %collective-permute-start.7 = (f32[82,128]{1,0:T(8,128)S(1)}, f32[82,128]{1,0:T(8,128)S(1)}, u32[]{:S(2)}, u32[]{:S(2)}) collective-permute-start(f32[82,128]{1,0:T(8,128)S(1)} %get-tuple-element.60), channel_id=1, source_target_pairs={{0,4},{1,5},{2,6},{3,7},{4,0},{5,1},{6,2},{7,3},{8,12},{9,13},{10,... | collective-permute-start | bytes 125960 | tf_op jit(solution)/shard_map/ppermute | solution.py:1599
  20.3 0.5 shard_map.93
  20.8 0.5 shard_map.91
  21.3 1.0 %collective-permute-done.7.x_second = f32[82,128]{1,0:T(8,128)S(1)} collective-permute-done((f32[82,128]{1,0:T(8,128)S(1)}, f32[82,128]{1,0:T(8,128)S(1)}, u32[]{:S(2)}, u32[]{:S(2)}) %collective-permute-start.7) | collective-permute-done | bytes 42016 | tf_op jit(solution)/shard_map/ppermute | solution.py:1599
  22.3 0.6 shard_map.94
  22.9 13.1 %all_to_all.10.got = f32[32,8,128]{2,1,0:T(8,128)S(1)} all-to-all(f32[32,8,128]{2,1,0:T(8,128)S(1)} %get-tuple-element.65), channel_id=1, replica_groups=mesh['gx'=8,'gy'=4] {'gx','gy'}, dimensions={0} | all-to-all | bytes 262144 | tf_op jit(solution)/shard_map/all_to_all | solution.py:1626
  36.0 0.3 collective-permute-start.8
  36.3 1.0 %collective-permute-done.8.relayed = f32[42,128]{1,0:T(8,128)S(1)} collective-permute-done((f32[42,128]{1,0:T(8,128)S(1)}, f32[42,128]{1,0:T(8,128)S(1)}, u32[]{:S(2)}, u32[]{:S(2)}) %collective-permute-start.8) | collective-permute-done | bytes 21536 | tf_op jit(solution)/shard_map/ppermute | solution.py:1671
  37.3 0.7 %shard_map.96 = (f32[2,8,2,8,128]{4,3,2,1,0:T(8,128)S(1)}, f32[2,8,2,8,128]{4,3,2,1,0:T(8,128)S(1)}, f32[2,2,8,128]{3,2,1,0:T(8,128)S(1)}, f32[34,128]{1,0:T(8,1...) custom-call(f32[32,8,128]{2,1,0:T(8,128)S(1)} %all_to_all.10.got, f32[42,128]{1,0:T(8,128)S(1)} %collective-permute-done.8.relayed, ...), custom_call_target="tpu_custom_call" | custom-call | tf_op jit(solution)/shard_map/pallas_call | solution.py:1674
  38.0 0.3 collective-permute-start.10
  38.3 0.3 collective-permute-start.9
  38.6 0.6 %collective-permute-done.10.y_second = f32[34,128]{1,0:T(8,128)S(1)} collective-permute-done((f32[34,128]{1,0:T(8,128)S(1)}, f32[34,128]{1,0:T(8,128)S(1)}, u32[]{:S(2)}, u32[]{:S(2)}) %collective-permute-start.10) | collective-permute-done | bytes 17440 | tf_op jit(solution)/shard_map/ppermute | solution.py:1599
  39.2 2.2 %collective-permute-done.9.y_first = f32[34,128]{1,0:T(8,128)S(1)} collective-permute-done((f32[34,128]{1,0:T(8,128)S(1)}, f32[34,128]{1,0:T(8,128)S(1)}, u32[]{:S(2)}, u32[]{:S(2)}) %collective-permute-start.9) | collective-permute-done | bytes 17440 | tf_op jit(solution)/shard_map/ppermute | solution.py:1598
  41.5 0.3 collective-permute-start.11
  41.8 1.8 %collective-permute-start.12 = (f32[34,128]{1,0:T(8,128)S(1)}, f32[34,128]{1,0:T(8,128)S(1)}, u32[]{:S(2)}, u32[]{:S(2)}) collective-permute-start(f32[34,128]{1,0:T(8,128)S(1)} %get-tuple-element.79), channel_id=1, source_target_pairs={{0,4},{1,5},{2,6},{3,7},{4,0},{5,1},{6,2},{7,3},{8,12},{9,13},{10,... | collective-permute-start | bytes 52232 | tf_op jit(solution)/shard_map/ppermute | solution.py:1599
  43.7 0.8 %shard_map.97 = (f32[4,2,8,2,8,128]{5,4,3,2,1,0:T(8,128)}, f32[1,128]{1,0:T(1,128)S(1)}) custom-call(f32[4,2,8,2,8,128]{5,4,3,2,1,0:T(8,128)S(1)} %get-tuple-element.56.begun, f32[82,128]{1,0:T(8,128)S(1)} %collective-permute-done.6.x_first, f32[82,128]{1,0:T(8,128)S(1)} %collective-permute-done.7.x_second, f32[1,128]{1,0:T(1,128)S(1)} %get-tuple-element.69.extra), custom_call_target="tpu_custom_call" | custom-call | flops 10000000 | bytes 1000000 | tf_op jit(solution)/shard_map/pallas_call | solution.py:1682
  44.8 0.8 %collective-permute-done.12.x_second = f32[34,128]{1,0:T(8,128)S(1)} collective-permute-done((f32[34,128]{1,0:T(8,128)S(1)}, f32[34,128]{1,0:T(8,128)S(1)}, u32[]{:S(2)}, u32[]{:S(2)}) %collective-permute-start.12) | collective-permute-done | bytes 17440 | tf_op jit(solution)/shard_map/ppermute | solution.py:1599
  45.6 1.3 %shard_map.101 = (f32[2,8,2,8,128]{4,3,2,1,0:T(8,128)}, f32[2,8,2,8,128]{4,3,2,1,0:T(8,128)S(1)}, f32[32,1,768]{2,1,0:T(1,128)S(1)}) custom-call(f32[2,8,2,8,128]{4,3,2,1,0:T(8,128)S(1)} %get-tuple-element.74.begun, f32[2,8,2,8,128]{4,3,2,1,0:T(8,128)S(1)} %get-tuple-element.75.begun_scaled, f32[2,8,2,8,128]{4,3,2,1,0:T(8,128)S(1)} %get-tuple-element.76.given, ...), custom_call_target="tpu_custom_call" | custom-call | tf_op jit(solution)/shard_map/pallas_call | solution.py:1688
  46.9 10.4 %all_to_all.11.got = f32[32,1,768]{2,1,0:T(1,128)S(1)} all-to-all(f32[32,1,768]{2,1,0:T(1,128)S(1)} %get-tuple-element.81), channel_id=1, replica_groups=mesh['gx'=8,'gy'=4] {'gx','gy'}, dimensions={0} | all-to-all | bytes 196608 | tf_op jit(solution)/shard_map/all_to_all | solution.py:1626
  57.3 1.5 %shard_map.102 = f32[2,8,2,8,128]{4,3,2,1,0:T(8,128)} custom-call(f32[32,1,768]{2,1,0:T(1,128)S(1)} %all_to_all.11.got, f32[16,128]{1,0:T(8,128)S(1)} %get-tuple-element.64.grp, f32[2,8,2,8,128]{4,3,2,1,0:T(8,128)S(1)} %get-tuple-element.82.direction, f32[2,8,2,8,128]{4,3,2,1,0:T(8,128)S(1)} %get-tuple-element.83.smoothed), custom_call_target="tpu_custom_call" | custom-call | tf_op jit(solution)/shard_map/pallas_call | solution.py:1697
  (34 shorter events, 1.1 us)
Async XLA Ops:
  0.6 1.0 %copy-start.2 = (f32[4,2,8,2,8,128]{5,4,3,2,1,0:T(8,128)S(1)}, f32[4,2,8,2,8,128]{5,4,3,2,1,0:T(8,128)}, u32[]{:S(2)}) copy-start(f32[4,2,8,2,8,128]{5,4,3,2,1,0:T(8,128)} %fields.3) | copy-start | bytes 1572868
  1.7 3.3 %copy-start.5 = (s32[2,2,16]{2,1,0:T(2,128)S(1)}, s32[2,2,16]{2,1,0:T(2,128)}, u32[]{:S(2)}) copy-start(s32[2,2,16]{2,1,0:T(2,128)} %param.10) | copy-start | bytes 772
  1.7 3.3 %copy-start.7 = (f32[2,2,16]{2,1,0:T(2,128)S(1)}, f32[2,2,16]{2,1,0:T(2,128)}, u32[]{:S(2)}) copy-start(f32[2,2,16]{2,1,0:T(2,128)} %param.9) | copy-start | bytes 772
  1.7 3.4 %copy-start.6 = (f32[4,128]{1,0:T(4,128)S(1)}, f32[4,128]{1,0:T(4,128)}, u32[]{:S(2)}) copy-start(f32[4,128]{1,0:T(4,128)} %param.11) | copy-start | bytes 6148
  1.7 3.5 %copy-start.3 = (f32[4,2,8,2,8,128]{5,4,3,2,1,0:T(8,128)S(1)}, f32[4,2,8,2,8,128]{5,4,3,2,1,0:T(8,128)}, u32[]{:S(2)}) copy-start(f32[4,2,8,2,8,128]{5,4,3,2,1,0:T(8,128)} %fields.3) | copy-start | bytes 1572868
  1.8 8.3 %copy-start = (bf16[3,256,256]{2,1,0:T(8,128)(2,1)S(1)}, bf16[3,256,256]{2,1,0:T(8,128)(2,1)}, u32[]{:S(2)}) copy-start(bf16[3,256,256]{2,1,0:T(8,128)(2,1)} %constant.5.clone.zmat) | copy-start | bytes 1179652
  1.9 4.3 %collective-permute-start = (f32[64,128]{1,0:T(8,128)S(1)}, f32[64,128]{1,0:T(8,128)S(1)}, u32[]{:S(2)}, u32[]{:S(2)}) collective-permute-start(f32[64,128]{1,0:T(8,128)S(1)} %get-tuple-element.44), channel_id=1, source_target_pairs={{0,3},{1,2},{2,1},{3,0},{4,7},{5,6},{6,5},{7,4},{8,11},{9,10},{10,... | collective-permute-start | bytes 98312 | tf_op jit(solution)/shard_map/ppermute | solution.py:1598
  4.3 1.8 %collective-permute-start.1 = (f32[64,128]{1,0:T(8,128)S(1)}, f32[64,128]{1,0:T(8,128)S(1)}, u32[]{:S(2)}, u32[]{:S(2)}) collective-permute-start(f32[64,128]{1,0:T(8,128)S(1)} %get-tuple-element.45), channel_id=1, source_target_pairs={{0,1},{1,0},{2,3},{3,2},{4,5},{5,4},{6,7},{7,6},{8,9},{9,8},{10,11... | collective-permute-start | bytes 98312 | tf_op jit(solution)/shard_map/ppermute | solution.py:1599
  5.1 5.0 %copy-start.4 = (f32[2,8,2,8,128]{4,3,2,1,0:T(8,128)S(1)}, f32[2,8,2,8,128]{4,3,2,1,0:T(8,128)}, u32[]{:S(2)}) copy-start(f32[2,8,2,8,128]{4,3,2,1,0:T(8,128)} %visc.3) | copy-start | bytes 393220
  5.5 4.6 %copy-start.1 = (f32[30,8,128]{2,1,0:T(8,128)S(1)}, f32[30,8,128]{2,1,0:T(8,128)}, u32[]{:S(2)}) copy-start(f32[30,8,128]{2,1,0:T(8,128)} %constant.4.clone.ctab) | copy-start | bytes 368644
  6.1 5.7 %collective-permute-start.2 = (f32[69,128]{1,0:T(8,128)S(1)}, f32[69,128]{1,0:T(8,128)S(1)}, u32[]{:S(2)}, u32[]{:S(2)}) collective-permute-start(f32[69,128]{1,0:T(8,128)S(1)} %get-tuple-element.51), channel_id=1, source_target_pairs={{0,1},{1,0},{2,3},{3,2},{4,8},{5,9},{6,10},{7,11},{8,4},{9,5},{10,... | collective-permute-start | bytes 105992 | tf_op jit(solution)/shard_map/ppermute | solution.py:1598
  6.7 5.4 %collective-permute-start.3 = (f32[69,128]{1,0:T(8,128)S(1)}, f32[69,128]{1,0:T(8,128)S(1)}, u32[]{:S(2)}, u32[]{:S(2)}) collective-permute-start(f32[69,128]{1,0:T(8,128)S(1)} %get-tuple-element.52), channel_id=1, source_target_pairs={{0,4},{1,5},{2,6},{3,7},{4,0},{5,1},{6,2},{7,3},{8,12},{9,13},{10,... | collective-permute-start | bytes 105992 | tf_op jit(solution)/shard_map/ppermute | solution.py:1599
  12.7 4.1 %collective-permute-start.4 = (f32[97,128]{1,0:T(8,128)S(1)}, f32[97,128]{1,0:T(8,128)S(1)}, u32[]{:S(2)}, u32[]{:S(2)}) collective-permute-start(f32[97,128]{1,0:T(8,128)S(1)} %get-tuple-element.54), channel_id=1, source_target_pairs={{0,3},{1,2},{2,1},{3,0},{4,7},{5,6},{6,5},{7,4},{8,11},{9,10},{10,... | collective-permute-start | bytes 149000 | tf_op jit(solution)/shard_map/ppermute | solution.py:1598
  13.3 3.4 %collective-permute-start.5 = (f32[97,128]{1,0:T(8,128)S(1)}, f32[97,128]{1,0:T(8,128)S(1)}, u32[]{:S(2)}, u32[]{:S(2)}) collective-permute-start(f32[97,128]{1,0:T(8,128)S(1)} %get-tuple-element.55), channel_id=1, source_target_pairs={{0,1},{1,0},{2,3},{3,2},{4,5},{5,4},{6,7},{7,6},{8,9},{9,8},{10,11... | collective-permute-start | bytes 149000 | tf_op jit(solution)/shard_map/ppermute | solution.py:1599
  16.8 4.5 %collective-permute-start.6 = (f32[82,128]{1,0:T(8,128)S(1)}, f32[82,128]{1,0:T(8,128)S(1)}, u32[]{:S(2)}, u32[]{:S(2)}) collective-permute-start(f32[82,128]{1,0:T(8,128)S(1)} %get-tuple-element.59), channel_id=1, source_target_pairs={{0,1},{1,0},{2,3},{3,2},{4,8},{5,9},{6,10},{7,11},{8,4},{9,5},{10,... | collective-permute-start | bytes 125960 | tf_op jit(solution)/shard_map/ppermute | solution.py:1598
  17.0 5.3 %collective-permute-start.7 = (f32[82,128]{1,0:T(8,128)S(1)}, f32[82,128]{1,0:T(8,128)S(1)}, u32[]{:S(2)}, u32[]{:S(2)}) collective-permute-start(f32[82,128]{1,0:T(8,128)S(1)} %get-tuple-element.60), channel_id=1, source_target_pairs={{0,4},{1,5},{2,6},{3,7},{4,0},{5,1},{6,2},{7,3},{8,12},{9,13},{10,... | collective-permute-start | bytes 125960 | tf_op jit(solution)/shard_map/ppermute | solution.py:1599
  36.0 1.3 %collective-permute-start.8 = (f32[42,128]{1,0:T(8,128)S(1)}, f32[42,128]{1,0:T(8,128)S(1)}, u32[]{:S(2)}, u32[]{:S(2)}) collective-permute-start(f32[42,128]{1,0:T(8,128)S(1)} %shard_map.95), channel_id=1, source_target_pairs={{0,1},{1,0},{2,3},{3,2},{4,5},{5,4},{6,7},{7,6},{8,9},{9,8},{10,11... | collective-permute-start | bytes 64520 | tf_op jit(solution)/shard_map/ppermute | solution.py:1671
  38.0 1.3 %collective-permute-start.10 = (f32[34,128]{1,0:T(8,128)S(1)}, f32[34,128]{1,0:T(8,128)S(1)}, u32[]{:S(2)}, u32[]{:S(2)}) collective-permute-start(f32[34,128]{1,0:T(8,128)S(1)} %get-tuple-element.73), channel_id=1, source_target_pairs={{0,1},{1,0},{2,3},{3,2},{4,5},{5,4},{6,7},{7,6},{8,9},{9,8},{10,11... | collective-permute-start | bytes 52232 | tf_op jit(solution)/shard_map/ppermute | solution.py:1599
  38.3 3.2 %collective-permute-start.9 = (f32[34,128]{1,0:T(8,128)S(1)}, f32[34,128]{1,0:T(8,128)S(1)}, u32[]{:S(2)}, u32[]{:S(2)}) collective-permute-start(f32[34,128]{1,0:T(8,128)S(1)} %get-tuple-element.72), channel_id=1, source_target_pairs={{0,3},{1,2},{2,1},{3,0},{4,7},{5,6},{6,5},{7,4},{8,11},{9,10},{10,... | collective-permute-start | bytes 52232 | tf_op jit(solution)/shard_map/ppermute | solution.py:1598
  41.5 3.3 %collective-permute-start.11 = (f32[34,128]{1,0:T(8,128)S(1)}, f32[34,128]{1,0:T(8,128)S(1)}, u32[]{:S(2)}, u32[]{:S(2)}) collective-permute-start(f32[34,128]{1,0:T(8,128)S(1)} %get-tuple-element.78), channel_id=1, source_target_pairs={{0,1},{1,0},{2,3},{3,2},{4,8},{5,9},{6,10},{7,11},{8,4},{9,5},{10,... | collective-permute-start | bytes 52232 | tf_op jit(solution)/shard_map/ppermute | solution.py:1598
  41.8 3.8 %collective-permute-start.12 = (f32[34,128]{1,0:T(8,128)S(1)}, f32[34,128]{1,0:T(8,128)S(1)}, u32[]{:S(2)}, u32[]{:S(2)}) collective-permute-start(f32[34,128]{1,0:T(8,128)S(1)} %get-tuple-element.79), channel_id=1, source_target_pairs={{0,4},{1,5},{2,6},{3,7},{4,0},{5,1},{6,2},{7,3},{8,12},{9,13},{10,... | collective-permute-start | bytes 52232 | tf_op jit(solution)/shard_map/ppermute | solution.py:1599

commit v15 on v14

--- a/solution.py
+++ b/solution.py
@@ -751,7 +751,6 @@
         rows = pl.ds(row, count)
         return place.after_x(x_first[rows, :], x_second[rows, :])
 
-    part[...] = given[...]
     for ch in range(3):
         for side, (ex, a) in enumerate(OUTER):
             for ey in range(2):
@@ -788,7 +787,8 @@
     for ex in range(2):
         for a in range(8):
             for ey in range(2):
-                div = slope[ex][ey][a] + part[ex, a, ey]
+                rest = part if (ex, a) in OUTER else given
+                div = slope[ex][ey][a] + rest[ex, a, ey]
                 value = div * (mass[ey] * (place.mult_x(ex, a) * float(-WEIGHTS[a])))
                 resid[ex, a, ey] = value
                 scaled[ex, a, ey] = value * inv_diag[ex, a, ey] * float(1.0 / THETA)
@@ -1034,8 +1034,8 @@
         rows = pl.ds(row, count)
         return place.after_x(x_first[rows, :], x_second[rows, :])
 
-    image[...] = begun[...]
-    scaled[...] = begun_scaled[...]
+    if msg.shape[2] == LANES:
+        image[...] = begun[...]
     for side, (ex, a) in enumerate(OUTER):
         for ey in range(2):
             tile = got_x_sum(place, begun[ex, a, ey], 0, ex, ey, x_first, x_second)
@@ -1052,7 +1052,7 @@
             place, y_first, y_second, before, after, ex, a_out, SMOOTH_Y, SMOOTH_EDGE
         )
         for ey in range(2):
-            values = [scaled[ex, a, ey] for a in range(8)]
+            values = [(scaled if a == a_out else begun_scaled)[ex, a, ey] for a in range(8)]
             slopes = along_x(SCALED, values, 1)
             far_row = beyond_y(place, ey)
             beside = kap[pl.ds((ex + 1) * 4 + 3 * ey, 1), :]
@@ -1082,9 +1082,10 @@
     for ex in range(2):
         for a in range(8):
             for ey in range(2):
-                value = image[ex, a, ey]
+                outer = (ex, a) in OUTER
+                value = (image if outer else begun)[ex, a, ey]
                 defect = (value - tiles[ex][a][ey]) * inv_diag[ex, a, ey]
-                update = scaled[ex, a, ey]
+                update = (scaled if outer else begun_scaled)[ex, a, ey]
                 result = (
                     float(1.0 + RHO_NEXT * RHO) * update + float(2.0 * RHO_NEXT / DELTA) * defect
                 )

time: 59 us -> 59 us (level)
  no operation moved by 1% of the time
where the time goes in v15:
time: 59 us; the launch traced here: 58.8 us
  blocking collectives  23.6 us (40%)
  starting transfers between devices  15.4 us (26%)
  Pallas kernels  9.02 us (15%)
  waiting for transfers between devices  8.81 us (15%)
  local copies, waits for them, and re-layouts  1.16 us (2%)
  between operations  0.81 us (1%)
    all_to_all x2, blocking collectives, exchange_all(): return lax.all_to_all(msg, BOTH, 0, 0, tiled=True)  23.6 us
    ppermute x6, starting transfers between devices, swap(): return (first_got, lax.ppermute(second, BOTH, pairs[1]))  10.6 us
    ppermute x6, waiting for transfers between devices, swap(): first_got = lax.ppermute(first, BOTH, pairs[0])  5.14 us
    ppermute x6, starting transfers between devices, swap(): first_got = lax.ppermute(first, BOTH, pairs[0])  4.52 us
    ppermute x6, waiting for transfers between devices, swap(): return (first_got, lax.ppermute(second, BOTH, pairs[1]))  2.69 us
    pallas_call x1, Pallas kernels, per_device(): call(prepare_kernel, [four, four, edge_shape, one], [four, four], cost_es...  1.71 us
    pallas_call x1, Pallas kernels, per_device(): call(finish_kernel, [one], [(LANES, LANES), (2,) + TILE, (2,) + TILE])  1.46 us
    pallas_call x1, Pallas kernels, per_device(): call(smooth_kernel, [one, one, (devices, 1, 6 * LANES) if grid_fits else...  1.26 us
  transfers between devices with their start and end apart: 13, of which 8 were waited for; matrix products, arithmetic and copies ran while one was open for 0% of the time, Pallas kernels for 7%

profile of v15, /device:TPU:0, one launch (start us, length us, event | category | flops | bytes accessed | tf_op | source)
XLA Modules:
  0.0 58.8 jit_solution(3976711079726981385)
XLA Ops:
  0.6 1.0 %copy-done.2 = f32[4,2,8,2,8,128]{5,4,3,2,1,0:T(8,128)S(1)} copy-done((f32[4,2,8,2,8,128]{5,4,3,2,1,0:T(8,128)S(1)}, f32[4,2,8,2,8,128]{5,4,3,2,1,0:T(8,128)}, u32[]{:S(2)}) %copy-start.2) | copy-done | bytes 524312
  1.9 2.5 %collective-permute-start = (f32[64,128]{1,0:T(8,128)S(1)}, f32[64,128]{1,0:T(8,128)S(1)}, u32[]{:S(2)}, u32[]{:S(2)}) collective-permute-start(f32[64,128]{1,0:T(8,128)S(1)} %get-tuple-element.44), channel_id=1, source_target_pairs={{0,3},{1,2},{2,1},{3,0},{4,7},{5,6},{6,5},{7,4},{8,11},{9,10},{10,... | collective-permute-start | bytes 98312 | tf_op jit(solution)/shard_map/ppermute | solution.py:1599
  4.3 0.7 %collective-permute-start.1 = (f32[64,128]{1,0:T(8,128)S(1)}, f32[64,128]{1,0:T(8,128)S(1)}, u32[]{:S(2)}, u32[]{:S(2)}) collective-permute-start(f32[64,128]{1,0:T(8,128)S(1)} %get-tuple-element.45), channel_id=1, source_target_pairs={{0,1},{1,0},{2,3},{3,2},{4,5},{5,4},{6,7},{7,6},{8,9},{9,8},{10,11... | collective-permute-start | bytes 98312 | tf_op jit(solution)/shard_map/ppermute | solution.py:1600
  5.2 0.3 shard_map.86
  5.5 0.6 collective-permute-done.y_first
  6.1 0.6 collective-permute-start.2
  6.7 3.4 %collective-permute-start.3 = (f32[69,128]{1,0:T(8,128)S(1)}, f32[69,128]{1,0:T(8,128)S(1)}, u32[]{:S(2)}, u32[]{:S(2)}) collective-permute-start(f32[69,128]{1,0:T(8,128)S(1)} %get-tuple-element.52), channel_id=1, source_target_pairs={{0,4},{1,5},{2,6},{3,7},{4,0},{5,1},{6,2},{7,3},{8,12},{9,13},{10,... | collective-permute-start | bytes 105992 | tf_op jit(solution)/shard_map/ppermute | solution.py:1600
  10.1 1.7 %shard_map.88 = (f32[4,2,8,2,8,128]{5,4,3,2,1,0:T(8,128)S(1)}, f32[4,2,8,2,8,128]{5,4,3,2,1,0:T(8,128)S(1)}, f32[4,2,2,8,128]{4,3,2,1,0:T(8,128)S(1)}, f32[2,8,2,8,128]{4,3,2,1,0:T(8,128)S(1)}) custom-call(f32[4,2,8,2,8,128]{5,4,3,2,1,0:T(8,128)S(1)} %get-tuple-element.43.summed, f32[2,8,2,8,128]{4,3,2,1,0:T(8,128)S(1)} %copy-done.4, ...), custom_call_target="tpu_custom_call" | custom-call | flops 10000000 | bytes 1000000 | tf_op jit(solution)/shard_map/pallas_call | solution.py:1642
  12.1 0.7 %shard_map.90 = (f32[4,2,8,2,8,128]{5,4,3,2,1,0:T(8,128)S(1)}, f32[2,4,2,8,128]{4,3,2,1,0:T(8,128)S(1)}, f32[2,2,8,128]{3,2,1,0:T(8,128)S(1)}, f32[97,128]{1,0:T(8,128)S(1)}, f32[97,128]{1,0:T(8,128)S(1)}) custom-call(f32[4,2,8,2,8,128]{5,4,3,2,1,0:T(8,128)S(1)} %get-tuple-element.46.begun, f32[4,2,8,2,8,128]{5,4,3,2,1,0:T(8,128)S(1)} %get-tuple-element.47.given, ...), custom_call_target="tpu_custom_call" | custom-call | tf_op jit(solution)/shard_map/pallas_call | solution.py:1645
  12.7 0.6 %collective-permute-start.4 = (f32[97,128]{1,0:T(8,128)S(1)}, f32[97,128]{1,0:T(8,128)S(1)}, u32[]{:S(2)}, u32[]{:S(2)}) collective-permute-start(f32[97,128]{1,0:T(8,128)S(1)} %get-tuple-element.54), channel_id=1, source_target_pairs={{0,3},{1,2},{2,1},{3,0},{4,7},{5,6},{6,5},{7,4},{8,11},{9,10},{10,... | collective-permute-start | bytes 149000 | tf_op jit(solution)/shard_map/ppermute | solution.py:1599
  13.3 1.1 %collective-permute-start.5 = (f32[97,128]{1,0:T(8,128)S(1)}, f32[97,128]{1,0:T(8,128)S(1)}, u32[]{:S(2)}, u32[]{:S(2)}) collective-permute-start(f32[97,128]{1,0:T(8,128)S(1)} %get-tuple-element.55), channel_id=1, source_target_pairs={{0,1},{1,0},{2,3},{3,2},{4,5},{5,4},{6,7},{7,6},{8,9},{9,8},{10,11... | collective-permute-start | bytes 149000 | tf_op jit(solution)/shard_map/ppermute | solution.py:1600
  14.5 2.3 %collective-permute-done.4.y_first = f32[97,128]{1,0:T(8,128)S(1)} collective-permute-done((f32[97,128]{1,0:T(8,128)S(1)}, f32[97,128]{1,0:T(8,128)S(1)}, u32[]{:S(2)}, u32[]{:S(2)}) %collective-permute-start.4) | collective-permute-done | bytes 49696 | tf_op jit(solution)/shard_map/ppermute | solution.py:1599
  17.0 3.3 %collective-permute-start.7 = (f32[82,128]{1,0:T(8,128)S(1)}, f32[82,128]{1,0:T(8,128)S(1)}, u32[]{:S(2)}, u32[]{:S(2)}) collective-permute-start(f32[82,128]{1,0:T(8,128)S(1)} %get-tuple-element.60), channel_id=1, source_target_pairs={{0,4},{1,5},{2,6},{3,7},{4,0},{5,1},{6,2},{7,3},{8,12},{9,13},{10,... | collective-permute-start | bytes 125960 | tf_op jit(solution)/shard_map/ppermute | solution.py:1600
  20.3 0.5 shard_map.93
  20.8 0.5 shard_map.91
  21.3 1.0 %collective-permute-done.7.x_second = f32[82,128]{1,0:T(8,128)S(1)} collective-permute-done((f32[82,128]{1,0:T(8,128)S(1)}, f32[82,128]{1,0:T(8,128)S(1)}, u32[]{:S(2)}, u32[]{:S(2)}) %collective-permute-start.7) | collective-permute-done | bytes 42016 | tf_op jit(solution)/shard_map/ppermute | solution.py:1600
  22.3 0.6 shard_map.94
  22.9 13.1 %all_to_all.10.got = f32[32,8,128]{2,1,0:T(8,128)S(1)} all-to-all(f32[32,8,128]{2,1,0:T(8,128)S(1)} %get-tuple-element.65), channel_id=1, replica_groups=mesh['gx'=8,'gy'=4] {'gx','gy'}, dimensions={0} | all-to-all | bytes 262144 | tf_op jit(solution)/shard_map/all_to_all | solution.py:1627
  36.0 0.3 collective-permute-start.8
  36.3 1.0 %collective-permute-done.8.relayed = f32[42,128]{1,0:T(8,128)S(1)} collective-permute-done((f32[42,128]{1,0:T(8,128)S(1)}, f32[42,128]{1,0:T(8,128)S(1)}, u32[]{:S(2)}, u32[]{:S(2)}) %collective-permute-start.8) | collective-permute-done | bytes 21536 | tf_op jit(solution)/shard_map/ppermute | solution.py:1672
  37.3 0.7 %shard_map.96 = (f32[2,8,2,8,128]{4,3,2,1,0:T(8,128)S(1)}, f32[2,8,2,8,128]{4,3,2,1,0:T(8,128)S(1)}, f32[2,2,8,128]{3,2,1,0:T(8,128)S(1)}, f32[34,128]{1,0:T(8,1...) custom-call(f32[32,8,128]{2,1,0:T(8,128)S(1)} %all_to_all.10.got, f32[42,128]{1,0:T(8,128)S(1)} %collective-permute-done.8.relayed, ...), custom_call_target="tpu_custom_call" | custom-call | tf_op jit(solution)/shard_map/pallas_call | solution.py:1675
  38.0 0.3 collective-permute-start.10
  38.3 0.3 collective-permute-start.9
  38.6 0.6 %collective-permute-done.10.y_second = f32[34,128]{1,0:T(8,128)S(1)} collective-permute-done((f32[34,128]{1,0:T(8,128)S(1)}, f32[34,128]{1,0:T(8,128)S(1)}, u32[]{:S(2)}, u32[]{:S(2)}) %collective-permute-start.10) | collective-permute-done | bytes 17440 | tf_op jit(solution)/shard_map/ppermute | solution.py:1600
  39.2 2.2 %collective-permute-done.9.y_first = f32[34,128]{1,0:T(8,128)S(1)} collective-permute-done((f32[34,128]{1,0:T(8,128)S(1)}, f32[34,128]{1,0:T(8,128)S(1)}, u32[]{:S(2)}, u32[]{:S(2)}) %collective-permute-start.9) | collective-permute-done | bytes 17440 | tf_op jit(solution)/shard_map/ppermute | solution.py:1599
  41.5 0.3 collective-permute-start.11
  41.8 1.8 %collective-permute-start.12 = (f32[34,128]{1,0:T(8,128)S(1)}, f32[34,128]{1,0:T(8,128)S(1)}, u32[]{:S(2)}, u32[]{:S(2)}) collective-permute-start(f32[34,128]{1,0:T(8,128)S(1)} %get-tuple-element.79), channel_id=1, source_target_pairs={{0,4},{1,5},{2,6},{3,7},{4,0},{5,1},{6,2},{7,3},{8,12},{9,13},{10,... | collective-permute-start | bytes 52232 | tf_op jit(solution)/shard_map/ppermute | solution.py:1600
  43.7 0.8 %shard_map.97 = (f32[4,2,8,2,8,128]{5,4,3,2,1,0:T(8,128)}, f32[1,128]{1,0:T(1,128)S(1)}) custom-call(f32[4,2,8,2,8,128]{5,4,3,2,1,0:T(8,128)S(1)} %get-tuple-element.56.begun, f32[82,128]{1,0:T(8,128)S(1)} %collective-permute-done.6.x_first, f32[82,128]{1,0:T(8,128)S(1)} %collective-permute-done.7.x_second, f32[1,128]{1,0:T(1,128)S(1)} %get-tuple-element.69.extra), custom_call_target="tpu_custom_call" | custom-call | flops 10000000 | bytes 1000000 | tf_op jit(solution)/shard_map/pallas_call | solution.py:1683
  44.8 0.8 %collective-permute-done.12.x_second = f32[34,128]{1,0:T(8,128)S(1)} collective-permute-done((f32[34,128]{1,0:T(8,128)S(1)}, f32[34,128]{1,0:T(8,128)S(1)}, u32[]{:S(2)}, u32[]{:S(2)}) %collective-permute-start.12) | collective-permute-done | bytes 17440 | tf_op jit(solution)/shard_map/ppermute | solution.py:1600
  45.6 1.3 %shard_map.101 = (f32[2,8,2,8,128]{4,3,2,1,0:T(8,128)}, f32[2,8,2,8,128]{4,3,2,1,0:T(8,128)S(1)}, f32[32,1,768]{2,1,0:T(1,128)S(1)}) custom-call(f32[2,8,2,8,128]{4,3,2,1,0:T(8,128)S(1)} %get-tuple-element.74.begun, f32[2,8,2,8,128]{4,3,2,1,0:T(8,128)S(1)} %get-tuple-element.75.begun_scaled, f32[2,8,2,8,128]{4,3,2,1,0:T(8,128)S(1)} %get-tuple-element.76.given, ...), custom_call_target="tpu_custom_call" | custom-call | tf_op jit(solution)/shard_map/pallas_call | solution.py:1689
  46.9 10.4 %all_to_all.11.got = f32[32,1,768]{2,1,0:T(1,128)S(1)} all-to-all(f32[32,1,768]{2,1,0:T(1,128)S(1)} %get-tuple-element.81), channel_id=1, replica_groups=mesh['gx'=8,'gy'=4] {'gx','gy'}, dimensions={0} | all-to-all | bytes 196608 | tf_op jit(solution)/shard_map/all_to_all | solution.py:1627
  57.3 1.5 %shard_map.102 = f32[2,8,2,8,128]{4,3,2,1,0:T(8,128)} custom-call(f32[32,1,768]{2,1,0:T(1,128)S(1)} %all_to_all.11.got, f32[16,128]{1,0:T(8,128)S(1)} %get-tuple-element.64.grp, f32[2,8,2,8,128]{4,3,2,1,0:T(8,128)S(1)} %get-tuple-element.82.direction, f32[2,8,2,8,128]{4,3,2,1,0:T(8,128)S(1)} %get-tuple-element.83.smoothed), custom_call_target="tpu_custom_call" | custom-call | tf_op jit(solution)/shard_map/pallas_call | solution.py:1698
  (34 shorter events, 1.1 us)
Async XLA Ops:
  0.6 1.0 %copy-start.2 = (f32[4,2,8,2,8,128]{5,4,3,2,1,0:T(8,128)S(1)}, f32[4,2,8,2,8,128]{5,4,3,2,1,0:T(8,128)}, u32[]{:S(2)}) copy-start(f32[4,2,8,2,8,128]{5,4,3,2,1,0:T(8,128)} %fields.3) | copy-start | bytes 1572868
  1.7 3.3 %copy-start.5 = (s32[2,2,16]{2,1,0:T(2,128)S(1)}, s32[2,2,16]{2,1,0:T(2,128)}, u32[]{:S(2)}) copy-start(s32[2,2,16]{2,1,0:T(2,128)} %param.10) | copy-start | bytes 772
  1.7 3.3 %copy-start.7 = (f32[2,2,16]{2,1,0:T(2,128)S(1)}, f32[2,2,16]{2,1,0:T(2,128)}, u32[]{:S(2)}) copy-start(f32[2,2,16]{2,1,0:T(2,128)} %param.9) | copy-start | bytes 772
  1.7 3.4 %copy-start.6 = (f32[4,128]{1,0:T(4,128)S(1)}, f32[4,128]{1,0:T(4,128)}, u32[]{:S(2)}) copy-start(f32[4,128]{1,0:T(4,128)} %param.11) | copy-start | bytes 6148
  1.7 3.5 %copy-start.3 = (f32[4,2,8,2,8,128]{5,4,3,2,1,0:T(8,128)S(1)}, f32[4,2,8,2,8,128]{5,4,3,2,1,0:T(8,128)}, u32[]{:S(2)}) copy-start(f32[4,2,8,2,8,128]{5,4,3,2,1,0:T(8,128)} %fields.3) | copy-start | bytes 1572868
  1.8 8.3 %copy-start = (bf16[3,256,256]{2,1,0:T(8,128)(2,1)S(1)}, bf16[3,256,256]{2,1,0:T(8,128)(2,1)}, u32[]{:S(2)}) copy-start(bf16[3,256,256]{2,1,0:T(8,128)(2,1)} %constant.5.clone.zmat) | copy-start | bytes 1179652
  1.9 4.3 %collective-permute-start = (f32[64,128]{1,0:T(8,128)S(1)}, f32[64,128]{1,0:T(8,128)S(1)}, u32[]{:S(2)}, u32[]{:S(2)}) collective-permute-start(f32[64,128]{1,0:T(8,128)S(1)} %get-tuple-element.44), channel_id=1, source_target_pairs={{0,3},{1,2},{2,1},{3,0},{4,7},{5,6},{6,5},{7,4},{8,11},{9,10},{10,... | collective-permute-start | bytes 98312 | tf_op jit(solution)/shard_map/ppermute | solution.py:1599
  4.3 1.8 %collective-permute-start.1 = (f32[64,128]{1,0:T(8,128)S(1)}, f32[64,128]{1,0:T(8,128)S(1)}, u32[]{:S(2)}, u32[]{:S(2)}) collective-permute-start(f32[64,128]{1,0:T(8,128)S(1)} %get-tuple-element.45), channel_id=1, source_target_pairs={{0,1},{1,0},{2,3},{3,2},{4,5},{5,4},{6,7},{7,6},{8,9},{9,8},{10,11... | collective-permute-start | bytes 98312 | tf_op jit(solution)/shard_map/ppermute | solution.py:1600
  5.1 5.0 %copy-start.4 = (f32[2,8,2,8,128]{4,3,2,1,0:T(8,128)S(1)}, f32[2,8,2,8,128]{4,3,2,1,0:T(8,128)}, u32[]{:S(2)}) copy-start(f32[2,8,2,8,128]{4,3,2,1,0:T(8,128)} %visc.3) | copy-start | bytes 393220
  5.5 4.6 %copy-start.1 = (f32[30,8,128]{2,1,0:T(8,128)S(1)}, f32[30,8,128]{2,1,0:T(8,128)}, u32[]{:S(2)}) copy-start(f32[30,8,128]{2,1,0:T(8,128)} %constant.4.clone.ctab) | copy-start | bytes 368644
  6.1 5.7 %collective-permute-start.2 = (f32[69,128]{1,0:T(8,128)S(1)}, f32[69,128]{1,0:T(8,128)S(1)}, u32[]{:S(2)}, u32[]{:S(2)}) collective-permute-start(f32[69,128]{1,0:T(8,128)S(1)} %get-tuple-element.51), channel_id=1, source_target_pairs={{0,1},{1,0},{2,3},{3,2},{4,8},{5,9},{6,10},{7,11},{8,4},{9,5},{10,... | collective-permute-start | bytes 105992 | tf_op jit(solution)/shard_map/ppermute | solution.py:1599
  6.7 5.4 %collective-permute-start.3 = (f32[69,128]{1,0:T(8,128)S(1)}, f32[69,128]{1,0:T(8,128)S(1)}, u32[]{:S(2)}, u32[]{:S(2)}) collective-permute-start(f32[69,128]{1,0:T(8,128)S(1)} %get-tuple-element.52), channel_id=1, source_target_pairs={{0,4},{1,5},{2,6},{3,7},{4,0},{5,1},{6,2},{7,3},{8,12},{9,13},{10,... | collective-permute-start | bytes 105992 | tf_op jit(solution)/shard_map/ppermute | solution.py:1600
  12.7 4.1 %collective-permute-start.4 = (f32[97,128]{1,0:T(8,128)S(1)}, f32[97,128]{1,0:T(8,128)S(1)}, u32[]{:S(2)}, u32[]{:S(2)}) collective-permute-start(f32[97,128]{1,0:T(8,128)S(1)} %get-tuple-element.54), channel_id=1, source_target_pairs={{0,3},{1,2},{2,1},{3,0},{4,7},{5,6},{6,5},{7,4},{8,11},{9,10},{10,... | collective-permute-start | bytes 149000 | tf_op jit(solution)/shard_map/ppermute | solution.py:1599
  13.3 3.4 %collective-permute-start.5 = (f32[97,128]{1,0:T(8,128)S(1)}, f32[97,128]{1,0:T(8,128)S(1)}, u32[]{:S(2)}, u32[]{:S(2)}) collective-permute-start(f32[97,128]{1,0:T(8,128)S(1)} %get-tuple-element.55), channel_id=1, source_target_pairs={{0,1},{1,0},{2,3},{3,2},{4,5},{5,4},{6,7},{7,6},{8,9},{9,8},{10,11... | collective-permute-start | bytes 149000 | tf_op jit(solution)/shard_map/ppermute | solution.py:1600
  16.8 4.5 %collective-permute-start.6 = (f32[82,128]{1,0:T(8,128)S(1)}, f32[82,128]{1,0:T(8,128)S(1)}, u32[]{:S(2)}, u32[]{:S(2)}) collective-permute-start(f32[82,128]{1,0:T(8,128)S(1)} %get-tuple-element.59), channel_id=1, source_target_pairs={{0,1},{1,0},{2,3},{3,2},{4,8},{5,9},{6,10},{7,11},{8,4},{9,5},{10,... | collective-permute-start | bytes 125960 | tf_op jit(solution)/shard_map/ppermute | solution.py:1599
  17.0 5.3 %collective-permute-start.7 = (f32[82,128]{1,0:T(8,128)S(1)}, f32[82,128]{1,0:T(8,128)S(1)}, u32[]{:S(2)}, u32[]{:S(2)}) collective-permute-start(f32[82,128]{1,0:T(8,128)S(1)} %get-tuple-element.60), channel_id=1, source_target_pairs={{0,4},{1,5},{2,6},{3,7},{4,0},{5,1},{6,2},{7,3},{8,12},{9,13},{10,... | collective-permute-start | bytes 125960 | tf_op jit(solution)/shard_map/ppermute | solution.py:1600
  36.0 1.3 %collective-permute-start.8 = (f32[42,128]{1,0:T(8,128)S(1)}, f32[42,128]{1,0:T(8,128)S(1)}, u32[]{:S(2)}, u32[]{:S(2)}) collective-permute-start(f32[42,128]{1,0:T(8,128)S(1)} %shard_map.95), channel_id=1, source_target_pairs={{0,1},{1,0},{2,3},{3,2},{4,5},{5,4},{6,7},{7,6},{8,9},{9,8},{10,11... | collective-permute-start | bytes 64520 | tf_op jit(solution)/shard_map/ppermute | solution.py:1672
  38.0 1.3 %collective-permute-start.10 = (f32[34,128]{1,0:T(8,128)S(1)}, f32[34,128]{1,0:T(8,128)S(1)}, u32[]{:S(2)}, u32[]{:S(2)}) collective-permute-start(f32[34,128]{1,0:T(8,128)S(1)} %get-tuple-element.73), channel_id=1, source_target_pairs={{0,1},{1,0},{2,3},{3,2},{4,5},{5,4},{6,7},{7,6},{8,9},{9,8},{10,11... | collective-permute-start | bytes 52232 | tf_op jit(solution)/shard_map/ppermute | solution.py:1600
  38.3 3.2 %collective-permute-start.9 = (f32[34,128]{1,0:T(8,128)S(1)}, f32[34,128]{1,0:T(8,128)S(1)}, u32[]{:S(2)}, u32[]{:S(2)}) collective-permute-start(f32[34,128]{1,0:T(8,128)S(1)} %get-tuple-element.72), channel_id=1, source_target_pairs={{0,3},{1,2},{2,1},{3,0},{4,7},{5,6},{6,5},{7,4},{8,11},{9,10},{10,... | collective-permute-start | bytes 52232 | tf_op jit(solution)/shard_map/ppermute | solution.py:1599
  41.5 3.3 %collective-permute-start.11 = (f32[34,128]{1,0:T(8,128)S(1)}, f32[34,128]{1,0:T(8,128)S(1)}, u32[]{:S(2)}, u32[]{:S(2)}) collective-permute-start(f32[34,128]{1,0:T(8,128)S(1)} %get-tuple-element.78), channel_id=1, source_target_pairs={{0,1},{1,0},{2,3},{3,2},{4,8},{5,9},{6,10},{7,11},{8,4},{9,5},{10,... | collective-permute-start | bytes 52232 | tf_op jit(solution)/shard_map/ppermute | solution.py:1599
  41.8 3.8 %collective-permute-start.12 = (f32[34,128]{1,0:T(8,128)S(1)}, f32[34,128]{1,0:T(8,128)S(1)}, u32[]{:S(2)}, u32[]{:S(2)}) collective-permute-start(f32[34,128]{1,0:T(8,128)S(1)} %get-tuple-element.79), channel_id=1, source_target_pairs={{0,4},{1,5},{2,6},{3,7},{4,0},{5,1},{6,2},{7,3},{8,12},{9,13},{10,... | collective-permute-start | bytes 52232 | tf_op jit(solution)/shard_map/ppermute | solution.py:1600
